TPU v7x, 32 devices: a whole 2x2x4 slice. The times are simulated.
32 devices in a mesh: section: 4 (over z), dp: 2 (over x), mp: 4 (over y, core).
Axes of the slice: x: 2, y: 2, z: 4, core: 2. Of those that a mesh axis runs over, the one named last changes fastest.
Arguments:
- lengths: int32 [16], P(('section', 'dp')), may hold values from 1 to 128
- final_hidden: bfloat16 [16, 3584], P(('section', 'dp')), may hold values from -6 to 6
- score_gain: bfloat16 [3584], replicated, may hold values from 0.5 to 1.5
- score_head: bfloat16 [3584], replicated, may hold values from -0.09375 to 0.09375
- policy_input: bfloat16 [2048, 8192], P(('section', 'dp'), 'mp')
- block_order: int32 [8, 2], P(('section', 'dp')), may hold values from 0 to 1, each once within a row
- norm_gain: bfloat16 [8192], P('mp'), may hold values from 0.5 to 1.5
- key_weight: bfloat16 [8192, 1024], P('mp'), may hold values from -0.0625 to 0.0625
- key_cotangent: bfloat16 [2048, 1024], P(('section', 'dp'), 'mp'), may hold values from -6 to 6
Outputs:
- keys: bfloat16 [2048, 1024], P(('section', 'dp'), 'mp')
- grad_weight: float32 [8192, 1024], P('mp')
- grad_gain: float32 [8192], P('mp')
Inputs may be any that keep to these rules, and one draw needn't show every extreme that they name: `block_order`: each row lists every number from 0 to 1 once.
All inputs are finite; a program needn't handle non-finite values.
Results may differ from a plain program's by a relative error of at most 0.0062.
Values may be sent and summed in bfloat16 or wider, within the bound.
No kernel may reach another device: no remote copies, remote signals or barrier semaphores. Data moves between devices by JAX's collectives and lax.ppermute only.
A program may use at most 128 MiB of HBM per device.

v0:
```python
import jax
import jax.numpy as jnp
from jax import lax
from jax.sharding import PartitionSpec as P

EPSILON = 1e-06


def body(
    lengths,
    final_hidden,
    score_gain,
    score_head,
    policy_input,
    block_order,
    norm_gain,
    key_weight,
    key_cotangent,
):
    block_count = lengths.shape[0]
    block_len = policy_input.shape[0] // block_count
    local_width = policy_input.shape[1]
    hidden_values = final_hidden.astype(jnp.float32)
    inverse_rms = lax.rsqrt(jnp.mean(hidden_values * hidden_values, axis=1) + EPSILON)
    coefficient = score_gain.astype(jnp.float32) * score_head.astype(jnp.float32)
    scores = jnp.sum(hidden_values * coefficient[None, :], axis=1) * inverse_rms
    position = lax.broadcasted_iota(jnp.int32, (block_count, block_len), 1)
    token_weight = jnp.where(position < lengths[:, None], scores[:, None], 0.0).astype(jnp.bfloat16)
    source = jnp.argsort(block_order[0])
    send_rows = jnp.take(policy_input.reshape(block_count, block_len, local_width), source, axis=0)
    send_weight = jnp.take(token_weight, source, axis=0)
    moved_rows, moved_weight = (
        lax.all_to_all(send_rows, "dp", split_axis=0, concat_axis=0, tiled=True),
        lax.all_to_all(send_weight, "dp", split_axis=0, concat_axis=0, tiled=True),
    )
    learner_rows = moved_rows.reshape(-1, local_width)
    row_weight = moved_weight.reshape(-1)
    full_rows, full_gain = (
        lax.all_gather(learner_rows, "mp", axis=1, tiled=True),
        lax.all_gather(norm_gain, "mp", axis=0, tiled=True),
    )
    columns = lax.all_to_all(key_weight, "mp", split_axis=1, concat_axis=0, tiled=True)
    inverse = lax.rsqrt(
        jnp.mean(jnp.square(full_rows.astype(jnp.float32)), axis=1, keepdims=True) + EPSILON
    )
    full_normed = (
        full_rows.astype(jnp.float32) * inverse * full_gain.astype(jnp.float32)[None, :]
    ).astype(jnp.bfloat16)
    projected = jnp.dot(full_normed, columns, preferred_element_type=jnp.float32).astype(
        jnp.bfloat16
    )
    normed = lax.dynamic_slice_in_dim(
        full_normed, lax.axis_index("mp") * local_width, local_width, 1
    )
    scaled = learner_rows.astype(jnp.float32) * inverse
    key_grad = (key_cotangent.astype(jnp.float32) * row_weight.astype(jnp.float32)[:, None]).astype(
        jnp.bfloat16
    )
    piece = lax.all_gather(key_grad, "mp", axis=1, tiled=True)
    block_grad = lax.dot_general(
        normed, piece, (((0,), (0,)), ((), ())), preferred_element_type=jnp.float32
    )
    grad_weight = block_grad
    grad_normed = lax.dot_general(
        piece, key_weight, (((1,), (1,)), ((), ())), preferred_element_type=jnp.float32
    )
    grad_weight, grad_normed = (grad_weight, grad_normed)
    local_gain = jnp.sum(grad_normed * scaled, axis=0)
    summed_weight, summed_gain = lax.psum((grad_weight, local_gain), ("section", "dp"))
    shards = lax.axis_size("section") * lax.axis_size("dp")
    return (projected, summed_weight / shards, summed_gain / shards)


def solution(mesh):
    placed = (
        P(("section", "dp")),
        P(("section", "dp"), None),
        P(),
        P(),
        P(("section", "dp"), "mp"),
        P(("section", "dp"), None),
        P("mp"),
        P("mp", None),
        P(("section", "dp"), "mp"),
    )
    return jax.shard_map(
        body,
        mesh=mesh,
        in_specs=placed,
        out_specs=(P(("section", "dp"), "mp"), P("mp", None), P("mp")),
        check_vma=False,
    )
```

profile of v0, /device:TPU:0, one launch (start us, length us, event | category | flops | bytes accessed | tf_op | source)
XLA Modules:
  0.0 363.9 jit_solution(10345036474939570050)
XLA Ops:
  7.3 1.3 sort.17
  8.7 0.6 gather_fusion
  9.5 18.3 %all_to_all.30 = bf16[2,128,2048]{2,1,0:T(8,128)(2,1)} all-to-all(bf16[2,128,2048]{2,1,0:T(8,128)(2,1)S(1)} %broadcast_select_fusion), channel_id=1, replica_groups=mesh['section'=4,'dp'=2,'mp'=4] {'dp'}, dimensions={0} | all-to-all | bytes 2097152 | tf_op jit(solution)/shard_map/all_to_all | solution.py:33
  27.8 0.2 fusion.7
  28.1 0.6 gather_fusion.1
  28.8 0.6 copy.16
  29.3 3.2 all-to-all-start.2
  32.6 5.2 %all_gather.10 = bf16[8192]{0:T(1024)(128)(2,1)S(1)} all-gather(bf16[2048]{0:T(1024)(128)(2,1)S(1)} %copy-done.8), channel_id=1, replica_groups=mesh['section'=4,'dp'=2,'mp'=4] {'mp'}, dimensions={0}, use_global_device_ids=true | all-gather | bytes 20480 | tf_op jit(solution)/shard_map/all_gather | solution.py:40
  37.9 10.5 %all_gather.11 = bf16[256,1024]{1,0:T(8,128)(2,1)S(1)} all-gather(bf16[256,256]{1,0:T(8,128)(2,1)S(1)} %multiply_convert_fusion), channel_id=1, replica_groups=mesh['section'=4,'dp'=2,'mp'=4] {'mp'}, dimensions={1}, use_global_device_ids=true | all-gather | bytes 655360 | tf_op jit(solution)/shard_map/all_gather | solution.py:59
  48.4 17.4 %all-gather.2.cloned.1.call-done = bf16[256,8192]{1,0:T(8,128)(2,1)} async-done(((bf16[256,2048]{1,0:T(8,128)(2,1)}), bf16[256,8192]{1,0:T(8,128)(2,1)}) %all-gather.2.cloned.1.call-update) | async-done | bytes 4194320 | tf_op jit(solution)/shard_map/all_gather | solution.py:39
  65.8 3.3 fusion
  69.1 0.2 copy-done.1
  69.2 1.2 fusion.2
  70.4 2.0 copy-done.2
  72.4 4.7 %fusion.4 = f32[2048,1024]{1,0:T(8,128)} fusion(bf16[256,1024]{1,0:T(8,128)(2,1)S(1)} %all_gather.11, bf16[256,8192]{1,0:T(8,128)(2,1)S(1)} %fusion.2, s32[]{:T(128)S(6)} %select_n.31), kind=kOutput, calls=%fused_computation.11 | convolution fusion | flops 1073741824 | bytes 9961476 | tf_op jit(solution)/shard_map/dot_general | solution.py:60
  77.2 6.5 %copy.14 = bf16[2048,1024]{0,1:T(8,128)(2,1)} copy(bf16[2048,1024]{1,0:T(8,128)(2,1)} %param.16) | data formatting | bytes 8388608 | tf_op args[7]
  83.7 53.8 %all_to_all.31 = bf16[2048,4,256]{0,2,1:T(8,128)(2,1)} all-to-all(bf16[2048,4,256]{0,2,1:T(8,128)(2,1)} %bitcast.16), channel_id=1, replica_groups=mesh['section'=4,'dp'=2,'mp'=4] {'mp'}, dimensions={1} | all-to-all | bytes 8388608 | tf_op jit(solution)/shard_map/all_to_all | solution.py:42
  137.5 6.3 %copy.15 = bf16[4,2048,256]{2,1,0:T(8,128)(2,1)} copy(bf16[4,2048,256]{1,2,0:T(8,128)(2,1)} %bitcast.15) | data formatting | bytes 8388608 | tf_op jit(solution)/shard_map/all_to_all | solution.py:42
  143.8 3.6 fusion.3
  147.4 23.1 %psum.15 = f32[2048]{0:T(1024)S(1)} all-reduce(f32[2048]{0:T(1024)S(1)} %fusion.3), channel_id=1, replica_groups=mesh['section'=4,'dp'=2,'mp'=4] {'section','dp'}, use_global_device_ids=true, to_apply=%region_6.7 | all-reduce | flops 2048 | bytes 16384 | tf_op jit(solution)/shard_map/psum | solution.py:69
  170.5 0.6 broadcast_multiply_fusion.1
  171.1 5.4 %convolution_convert_fusion = bf16[256,256]{1,0:T(8,128)(2,1)} fusion(bf16[256,8192]{1,0:T(8,128)(2,1)} %copy-done.2, bf16[8192,256]{1,0:T(8,128)(2,1)} %bitcast.17), kind=kOutput, calls=%fused_computation.10 | convolution fusion | flops 1073807360 | bytes 8519680 | tf_op jit(solution)/shard_map/dot_general | solution.py:49
  176.5 171.9 %all-reduce.2.cloned.1.call-done = f32[2048,1024]{1,0:T(8,128)} async-done(((f32[2048,1024]{1,0:T(8,128)}), f32[2048,1024]{1,0:T(8,128)}) %all-reduce.2.cloned.1.call-update) | async-done | bytes 8388624 | tf_op jit(solution)/shard_map/psum | solution.py:69
  348.4 8.7 %broadcast_multiply_fusion = f32[2048,1024]{1,0:T(8,128)} fusion(f32[2048,1024]{1,0:T(8,128)} %all-reduce.2.cloned.1.call-done), kind=kLoop, calls=%fused_computation.7 | loop fusion | flops 2097152 | bytes 16777216 | tf_op jit(solution)/shard_map/div | solution.py:71
  (36 shorter events, 0.6 us)
Async XLA Ops:
  7.2 1.5 copy-start
  7.2 20.6 %copy-start.6 = (bf16[3584]{0:T(1024)(128)(2,1)S(1)}, bf16[3584]{0:T(1024)(128)(2,1)}, u32[]{:S(2)}) copy-start(bf16[3584]{0:T(1024)(128)(2,1)} %param.12) | copy-start | bytes 21508
  7.2 20.6 %copy-start.7 = (bf16[3584]{0:T(1024)(128)(2,1)S(1)}, bf16[3584]{0:T(1024)(128)(2,1)}, u32[]{:S(2)}) copy-start(bf16[3584]{0:T(1024)(128)(2,1)} %param.11) | copy-start | bytes 21508
  7.2 20.6 %copy-start.5 = (bf16[2,3584]{1,0:T(2,128)(2,1)S(1)}, bf16[2,3584]{1,0:T(2,128)(2,1)}, u32[]{:S(2)}) copy-start(bf16[2,3584]{1,0:T(2,128)(2,1)} %param.10) | copy-start | bytes 43012
  7.2 20.8 %copy-start.9 = (s32[2]{0:T(128)S(1)}, s32[2]{0:T(128)}, u32[]{:S(2)}) copy-start(s32[2]{0:T(128)} %param.9) | copy-start | bytes 28
  7.2 25.4 %copy-start.8 = (bf16[2048]{0:T(1024)(128)(2,1)S(1)}, bf16[2048]{0:T(1024)(128)(2,1)}, u32[]{:S(2)}) copy-start(bf16[2048]{0:T(1024)(128)(2,1)} %param.15) | copy-start | bytes 12292
  7.2 30.6 %copy-start.4 = (bf16[256,256]{1,0:T(8,128)(2,1)S(1)}, bf16[256,256]{1,0:T(8,128)(2,1)}, u32[]{:S(2)}) copy-start(bf16[256,256]{1,0:T(8,128)(2,1)} %param.17) | copy-start | bytes 393220
  7.2 58.5 %all-gather.2.cloned.1.call-start = ((), (), s32[]{:S(2)}) async-start(), calls=%async_computation.3 | async-start | bytes 5242880 | tf_op jit(solution)/shard_map/all_gather | solution.py:39
  29.3 8.5 %all-to-all-start.2 = ((bf16[2,1,128]{2,1,0:T(2,128)(2,1)}), bf16[2,1,128]{2,1,0:T(2,128)(2,1)S(1)}, u32[]{:S(2)}, u32[]{:S(2)}) async-start(bf16[2,1,128]{2,1,0:T(2,128)(2,1)} %copy.16), calls=%async_computation.2 | async-start | bytes 2048 | tf_op jit(solution)/shard_map/all_to_all | solution.py:34
  32.5 315.9 %all-reduce.2.cloned.1.call-start = ((), (), s32[]{:S(2)}) async-start(), calls=%async_computation.4 | async-start | bytes 16777216 | tf_op jit(solution)/shard_map/psum | solution.py:69
  65.8 3.4 copy-start.1
  70.4 2.0 copy-start.2
  137.5 6.3 %copy-start.3 = (bf16[2,128,2048]{2,1,0:T(8,128)(2,1)S(1)}, bf16[2,128,2048]{2,1,0:T(8,128)(2,1)}, u32[]{:S(2)}) copy-start(bf16[2,128,2048]{2,1,0:T(8,128)(2,1)} %all_to_all.30) | copy-start | bytes 3145732
Sparse Core Ops, SparseCore 0:
  27.9 37.8 all-gather.1
  77.3 271.0 all-reduce.1
where the time goes:
time: 365 us; the launch traced here: 364 us
  waiting for transfers between devices  189 us (52%)
  blocking collectives  111 us (30%)
  local copies, waits for them, and re-layouts  16.8 us (5%)
  other arithmetic  15.7 us (4%)
  between operations  14.3 us (4%)
  matrix products  13.7 us (4%)
    psum x1, waiting for transfers between devices, body(): lax.psum((grad_weight, local_gain), ('section', 'dp'))  172 us
    all_to_all x1, blocking collectives, body(): lax.all_to_all(key_weight, 'mp', split_axis=1, concat_axis=0, tiled=True)  53.8 us
    psum x1, blocking collectives, body(): lax.psum((grad_weight, local_gain), ('section', 'dp'))  23.1 us
    all_to_all x1, blocking collectives, body(): lax.all_to_all(send_rows, 'dp', split_axis=0, concat_axis=0, tiled=True)  18.3 us
    all_gather x1, waiting for transfers between devices, body(): lax.all_gather(learner_rows, 'mp', axis=1, tiled=True)  17.4 us
    all_gather x1, blocking collectives, body(): piece = lax.all_gather(key_grad, 'mp', axis=1, tiled=True)  10.5 us
    div x2, other arithmetic, body(): return (projected, summed_weight / shards, summed_gain / shards)  9.3 us
    unnamed x21, local copies, waits for them, and re-layouts  8.73 us
  transfers between devices with their start and end apart: 3, of which 2 were waited for; matrix products, arithmetic and copies ran while one was open for 7% of the time, Pallas kernels for 0%

commit v1 on v0

v1 whole, which is shorter than its diff:
```python
import jax
import jax.numpy as jnp
from jax import lax
from jax.sharding import PartitionSpec as P

EPSILON = 1e-06
CHUNKS = 8


def swap(value, axis, bit):
    return lax.ppermute(value, axis, [(i, i ^ bit) for i in range(lax.axis_size(axis))])


def gather_pieces(piece, axis, dimension):
    index = lax.axis_index(axis)
    pieces = [piece]
    bit = lax.axis_size(axis) // 2
    while bit:
        sent = jnp.concatenate(pieces, axis=dimension) if len(pieces) > 1 else pieces[0]
        got = jnp.split(swap(sent, axis, bit), len(pieces), axis=dimension)
        low = (index & bit) == 0
        pieces = [
            value
            for mine, theirs in zip(pieces, got)
            for value in (jnp.where(low, mine, theirs), jnp.where(low, theirs, mine))
        ]
        bit //= 2
    return pieces


def to_bfloat16(value):
    return lax.reduce_precision(value, 8, 7).astype(jnp.bfloat16)


def add(left, right):
    return to_bfloat16(left.astype(jnp.float32) + right.astype(jnp.float32))


def line_sum(part, axis):
    size = lax.axis_size(axis)
    index = lax.axis_index(axis)
    half = size // 2
    for i in range(half - 1):
        part = add(part, lax.ppermute(part, axis, [(i, i + 1), (size - 1 - i, size - 2 - i)]))
    total = add(part, lax.ppermute(part, axis, [(half - 1, half), (half, half - 1)]))
    for i in reversed(range(half - 1)):
        got = lax.ppermute(total, axis, [(i + 1, i), (size - 2 - i, size - 1 - i)])
        total = jnp.where((index == i) | (index == size - 1 - i), got, total)
    return total


def body(
    lengths,
    final_hidden,
    score_gain,
    score_head,
    policy_input,
    block_order,
    norm_gain,
    key_weight,
    key_cotangent,
):
    n_section, n_dp, n_mp = (lax.axis_size(name) for name in ("section", "dp", "mp"))
    dp, mp = lax.axis_index("dp"), lax.axis_index("mp")
    block_count = lengths.shape[0]
    tokens, local_width = policy_input.shape
    block_len = tokens // block_count
    pair = block_count // n_dp
    columns = key_cotangent.shape[1]
    own_width = local_width // n_dp
    order = block_order[0]

    cotangent_rows = jnp.concatenate(gather_pieces(key_cotangent, "dp", 0), axis=0)
    cotangents = jnp.concatenate(gather_pieces(cotangent_rows, "mp", 1), axis=1)

    rows = []
    for j in range(n_dp):
        piece = lax.dynamic_slice_in_dim(policy_input, (dp ^ j) * own_width, own_width, 1)
        rows.append(piece if j == 0 else swap(piece, "dp", j))
    rows = jnp.concatenate(rows, axis=0)

    hidden_values = final_hidden.astype(jnp.float32)
    inverse_hidden = lax.rsqrt(jnp.mean(hidden_values * hidden_values, axis=1) + EPSILON)
    coefficient = score_gain.astype(jnp.float32) * score_head.astype(jnp.float32)
    scores = jnp.sum(hidden_values * coefficient[None, :], axis=1) * inverse_hidden
    squares = jnp.sum(jnp.square(policy_input.astype(jnp.float32)), axis=1)
    small = jnp.concatenate(
        [squares, scores, lengths.astype(jnp.float32), order.astype(jnp.float32)]
    )
    small = lax.all_gather(small, ("dp", "mp")).reshape(n_dp, n_mp, -1)
    squares = jnp.sum(small[:, :, :tokens], axis=1)
    small = small[:, 0, tokens:].reshape(n_dp, 3, block_count)
    inverse = lax.rsqrt(squares / (local_width * n_mp) + EPSILON)
    position = lax.broadcasted_iota(jnp.int32, (n_dp, block_count, block_len), 2)
    token_weight = jnp.where(
        position < small[:, 1, :, None].astype(jnp.int32), small[:, 0, :, None], 0.0
    ).astype(jnp.bfloat16)
    orders = small[:, 2].astype(jnp.int32)

    senders = dp ^ jnp.arange(n_dp)
    slots = orders[senders]
    learner_block = (slots // pair) * block_count + senders[:, None] * pair + slots % pair
    taken = jnp.take(
        cotangents.reshape(n_dp * block_count, block_len, -1), learner_block.reshape(-1), axis=0
    )
    taken_weight = token_weight[senders].reshape(-1, block_len, 1).astype(jnp.float32)
    taken_inverse = inverse[senders].reshape(-1, block_len, 1)
    key_grad = to_bfloat16(taken.astype(jnp.float32) * taken_weight)
    key_grad = (key_grad.astype(jnp.float32) * taken_inverse).astype(jnp.bfloat16)
    key_grad = key_grad.reshape(n_dp * tokens, -1)

    chunk = own_width // CHUNKS
    found = []
    for c in range(CHUNKS):
        part = lax.dot_general(
            rows[:, c * chunk : (c + 1) * chunk],
            key_grad,
            (((0,), (0,)), ((), ())),
            preferred_element_type=jnp.float32,
        )
        found.append(gather_pieces(line_sum(to_bfloat16(part), "section"), "dp", 0))
    shards = n_section * n_dp
    gain = norm_gain.astype(jnp.float32)
    grad_weight = jnp.zeros((local_width, n_mp * columns), jnp.float32)
    grad_gain = jnp.zeros((local_width,), jnp.float32)
    for c in range(CHUNKS):
        for e in range(n_dp):
            start = e * own_width + c * chunk
            value = found[c][e].astype(jnp.float32) / shards
            grad_weight = lax.dynamic_update_slice(
                grad_weight, value * gain[start : start + chunk, None], (start, 0)
            )
            weight = key_weight[start : start + chunk].astype(jnp.float32)
            grad_gain = lax.dynamic_update_slice(
                grad_gain, jnp.sum(value * weight, axis=1), (start,)
            )

    scaled = (policy_input.astype(jnp.float32) * gain[None, :]).astype(jnp.bfloat16)
    partial = jnp.dot(scaled, key_weight, preferred_element_type=jnp.float32)
    own_columns = lax.dynamic_slice_in_dim(partial, mp * columns, columns, 1)
    partial = partial.astype(jnp.bfloat16)
    for j in range(1, n_mp):
        piece = lax.dynamic_slice_in_dim(partial, (mp ^ j) * columns, columns, 1)
        own_columns = own_columns + swap(piece, "mp", j).astype(jnp.float32)
    own_inverse = inverse[dp][:, None]
    keys = jnp.where(own_inverse == 0.0, 0.0, own_columns * own_inverse).astype(jnp.bfloat16)
    block = jnp.arange(block_count)
    source = jnp.sum(jnp.where(order[None, :] == block[:, None], block[None, :], 0), axis=1)
    send = jnp.take(keys.reshape(block_count, block_len, columns), source, axis=0)
    arrived = []
    for j in range(n_dp):
        piece = lax.dynamic_slice_in_dim(send, (dp ^ j) * pair, pair, 0)
        arrived.append(piece if j == 0 else swap(piece, "dp", j))
    learner_keys = jnp.take(jnp.stack(arrived), senders, axis=0).reshape(tokens, columns)
    return learner_keys, grad_weight, grad_gain


def solution(mesh):
    placed = (
        P(("section", "dp")),
        P(("section", "dp"), None),
        P(),
        P(),
        P(("section", "dp"), "mp"),
        P(("section", "dp"), None),
        P("mp"),
        P("mp", None),
        P(("section", "dp"), "mp"),
    )
    return jax.shard_map(
        body,
        mesh=mesh,
        in_specs=placed,
        out_specs=(P(("section", "dp"), "mp"), P("mp", None), P("mp")),
        check_vma=False,
    )
```

time: 365 us -> 196 us (0.54)
  waiting for transfers between devices: 189 us -> 90.4 us
  blocking collectives: 111 us -> 24.8 us
  starting transfers between devices: 3.27 us -> 49.4 us
  between operations: 14.3 us -> 2.45 us
  matrix products: 13.7 us -> 7.44 us
  other arithmetic: 15.7 us -> 9.58 us
  local copies, waits for them, and re-layouts: 16.8 us -> 11.2 us
    psum x1 -> x0, waiting for transfers between devices: 172 us -> none  [body(): lax.psum((grad_weight, local_gain), ('section', 'dp'))]
    ppermute x0 -> x40, waiting for transfers between devices: none -> 90.4 us  [the longest x8 42.5 us: line_sum(): got = lax.ppermute(total, axis, [(i + 1, i), (size - 2 - i, size - 1 - i)])]
    all_to_all x2 -> x0, blocking collectives: 72.2 us -> none  [the longest x1 53.8 us: body(): lax.all_to_all(key_weight, 'mp', split_axis=1, concat_axis=0, tiled=True)]
    ppermute x0 -> x40, starting transfers between devices: none -> 49.4 us  [the longest x8 20.9 us: line_sum(): lax.ppermute(part, axis, [(i, i + 1), (size - 1 - i, size - 2 - i)])]
    unnamed x0 -> x1, blocking collectives: none -> 24.8 us
    psum x1 -> x0, blocking collectives: 23.1 us -> none  [body(): lax.psum((grad_weight, local_gain), ('section', 'dp'))]
    all_gather x1 -> x0, waiting for transfers between devices: 17.4 us -> none  [body(): lax.all_gather(learner_rows, 'mp', axis=1, tiled=True)]
    all_gather x2 -> x0, blocking collectives: 15.7 us -> none  [the longest x1 10.5 us: body(): piece = lax.all_gather(key_grad, 'mp', axis=1, tiled=True)]
  transfers between devices with their start and end apart: 3 -> 40, of which waited for: 2 -> 22; matrix products, arithmetic and copies ran while one was open for 7% -> 12% of each run, Pallas kernels for 0% -> 0%
where the time goes in v1:
time: 196 us; the launch traced here: 195 us
  waiting for transfers between devices  90.4 us (46%)
  starting transfers between devices  49.4 us (25%)
  blocking collectives  24.8 us (13%)
  local copies, waits for them, and re-layouts  11.2 us (6%)
  other arithmetic  9.58 us (5%)
  matrix products  7.44 us (4%)
  between operations  2.45 us (1%)
    ppermute x8, waiting for transfers between devices, line_sum(): got = lax.ppermute(total, axis, [(i + 1, i), (size - 2 - i, size - 1 - i)])  42.5 us
    ppermute x16, waiting for transfers between devices, swap(): lax.ppermute(value, axis, [(i, i ^ bit) for i in range(lax.axis_size(axis...  26.2 us
    unnamed x1, blocking collectives  24.8 us
    ppermute x8, waiting for transfers between devices, line_sum(): lax.ppermute(part, axis, [(i, i + 1), (size - 1 - i, size - 2 - i)])  21.6 us
    ppermute x8, starting transfers between devices, line_sum(): lax.ppermute(part, axis, [(i, i + 1), (size - 1 - i, size - 2 - i)])  20.9 us
    ppermute x16, starting transfers between devices, swap(): lax.ppermute(value, axis, [(i, i ^ bit) for i in range(lax.axis_size(axis...  12.4 us
    ppermute x8, starting transfers between devices, line_sum(): got = lax.ppermute(total, axis, [(i + 1, i), (size - 2 - i, size - 1 - i)])  10.7 us
    ppermute x8, starting transfers between devices, line_sum(): lax.ppermute(part, axis, [(half - 1, half), (half, half - 1)])  5.36 us
  transfers between devices with their start and end apart: 40, of which 22 were waited for; matrix products, arithmetic and copies ran while one was open for 12% of the time, Pallas kernels for 0%

profile of v1, /device:TPU:0, one launch (start us, length us, event | category | flops | bytes accessed | tf_op | source)
XLA Modules:
  0.0 195.2 jit_solution(7513585615479323779)
XLA Ops:
  0.7 3.0 %collective-permute-start.5 = (bf16[256,256]{1,0:T(8,128)(2,1)}, bf16[256,256]{1,0:T(8,128)(2,1)S(1)}, u32[]{:S(2)}, u32[]{:S(2)}) collective-permute-start(bf16[256,256]{1,0:T(8,128)(2,1)} %param.17), channel_id=1, source_target_pairs={{0,4},{4,0},{1,5},{5,1},{2,6},{6,2},{3,7},{7,3},{8,12},{12,8},{9,1... | collective-permute-start | bytes 393224 | tf_op jit(solution)/shard_map/ppermute | solution.py:11
  6.6 4.7 %fusion.90 = (bf16[256,1024]{1,0:T(8,128)(2,1)S(1)}, f32[256,1024]{1,0:T(8,128)}) fusion(bf16[2048,1024]{1,0:T(8,128)(2,1)} %param.16, bf16[256,2048]{1,0:T(8,128)(2,1)} %param.13, f32[2048]{0:T(1024)S(1)} %convert_element_type.357), kind=kOutput, calls=%fused_computation.272 | convolution fusion | flops 1075576832 | bytes 6823936 | tf_op jit(solution)/shard_map/dot_general | solution.py:139
  15.6 24.8 %all-reduce.2 = f32[2096]{0:T(1024)S(1)} all-reduce(f32[2096]{0:T(1024)S(1)} %maximum_dynamic-update-slice_fusion), channel_id=2, replica_groups=mesh['section'=4,'dp'=2,'mp'=4] {'dp','mp'}, use_global_device_ids=true, to_apply=%add.2 | all-reduce | flops 2096 | bytes 16768
  44.9 4.6 %collective-permute-done.6 = bf16[512,256]{1,0:T(8,128)(2,1)S(1)} collective-permute-done((bf16[512,256]{1,0:T(8,128)(2,1)S(1)}, bf16[512,256]{1,0:T(8,128)(2,1)S(1)}, u32[]{:S(2)}, u32[]{:S(2)}) %collective-permute-start.6) | collective-permute-done | bytes 262176 | tf_op jit(solution)/shard_map/ppermute | solution.py:11
  50.4 3.9 %collective-permute-done.3 = bf16[1,128,256]{2,1,0:T(8,128)(2,1)S(1)} collective-permute-done((bf16[1,128,256]{2,1,0:T(8,128)(2,1)S(1)}, bf16[1,128,256]{2,1,0:T(8,128)(2,1)S(1)}, u32[]{:S(2)}, u32[]{:S(2)}) %collective-permute-start.3) | collective-permute-done | bytes 65568 | tf_op jit(solution)/shard_map/ppermute | solution.py:11
  57.3 3.5 %collective-permute-start.8 = (bf16[128,1024]{1,0:T(8,128)(2,1)S(1)}, bf16[128,1024]{1,0:T(8,128)(2,1)S(1)}, u32[]{:S(2)}, u32[]{:S(2)}) collective-permute-start(bf16[128,1024]{1,0:T(8,128)(2,1)S(1)} %fusion.2), channel_id=1, source_target_pairs={{0,8},{24,16},{1,9},{25,17},{2,10},{26,18},{3,11},{27,19},{4,12},{... | collective-permute-start | bytes 786440 | tf_op jit(solution)/shard_map/ppermute | solution.py:44
  68.5 3.4 %collective-permute-start.28 = (bf16[128,1024]{1,0:T(8,128)(2,1)S(1)}, bf16[128,1024]{1,0:T(8,128)(2,1)S(1)}, u32[]{:S(2)}, u32[]{:S(2)}) collective-permute-start(bf16[128,1024]{1,0:T(8,128)(2,1)S(1)} %fusion.7), channel_id=1, source_target_pairs={{0,8},{24,16},{1,9},{25,17},{2,10},{26,18},{3,11},{27,19},{4,12},{... | collective-permute-start | bytes 786440 | tf_op jit(solution)/shard_map/ppermute | solution.py:44
  73.1 4.4 %collective-permute-start.32 = (bf16[128,1024]{1,0:T(8,128)(2,1)S(1)}, bf16[128,1024]{1,0:T(8,128)(2,1)S(1)}, u32[]{:S(2)}, u32[]{:S(2)}) collective-permute-start(bf16[128,1024]{1,0:T(8,128)(2,1)S(1)} %fusion.8), channel_id=1, source_target_pairs={{0,8},{24,16},{1,9},{25,17},{2,10},{26,18},{3,11},{27,19},{4,12},{... | collective-permute-start | bytes 786440 | tf_op jit(solution)/shard_map/ppermute | solution.py:44
  78.8 4.4 %collective-permute-start.36 = (bf16[128,1024]{1,0:T(8,128)(2,1)S(1)}, bf16[128,1024]{1,0:T(8,128)(2,1)S(1)}, u32[]{:S(2)}, u32[]{:S(2)}) collective-permute-start(bf16[128,1024]{1,0:T(8,128)(2,1)S(1)} %fusion.9), channel_id=1, source_target_pairs={{0,8},{24,16},{1,9},{25,17},{2,10},{26,18},{3,11},{27,19},{4,12},{... | collective-permute-start | bytes 786440 | tf_op jit(solution)/shard_map/ppermute | solution.py:44
  85.1 4.9 %collective-permute-done.24 = bf16[128,1024]{1,0:T(8,128)(2,1)S(1)} collective-permute-done((bf16[128,1024]{1,0:T(8,128)(2,1)S(1)}, bf16[128,1024]{1,0:T(8,128)(2,1)S(1)}, u32[]{:S(2)}, u32[]{:S(2)}) %collective-permute-start.24) | collective-permute-done | bytes 262176 | tf_op jit(solution)/shard_map/ppermute | solution.py:44
  90.7 4.9 %collective-permute-done.28 = bf16[128,1024]{1,0:T(8,128)(2,1)S(1)} collective-permute-done((bf16[128,1024]{1,0:T(8,128)(2,1)S(1)}, bf16[128,1024]{1,0:T(8,128)(2,1)S(1)}, u32[]{:S(2)}, u32[]{:S(2)}) %collective-permute-start.28) | collective-permute-done | bytes 262176 | tf_op jit(solution)/shard_map/ppermute | solution.py:44
  96.4 4.9 %collective-permute-done.32 = bf16[128,1024]{1,0:T(8,128)(2,1)S(1)} collective-permute-done((bf16[128,1024]{1,0:T(8,128)(2,1)S(1)}, bf16[128,1024]{1,0:T(8,128)(2,1)S(1)}, u32[]{:S(2)}, u32[]{:S(2)}) %collective-permute-start.32) | collective-permute-done | bytes 262176 | tf_op jit(solution)/shard_map/ppermute | solution.py:44
  102.0 3.6 %collective-permute-done.36 = bf16[128,1024]{1,0:T(8,128)(2,1)S(1)} collective-permute-done((bf16[128,1024]{1,0:T(8,128)(2,1)S(1)}, bf16[128,1024]{1,0:T(8,128)(2,1)S(1)}, u32[]{:S(2)}, u32[]{:S(2)}) %collective-permute-start.36) | collective-permute-done | bytes 262176 | tf_op jit(solution)/shard_map/ppermute | solution.py:44
  115.8 12.8 %collective-permute-done.10 = bf16[128,1024]{1,0:T(8,128)(2,1)S(1)} collective-permute-done((bf16[128,1024]{1,0:T(8,128)(2,1)S(1)}, bf16[128,1024]{1,0:T(8,128)(2,1)S(1)}, u32[]{:S(2)}, u32[]{:S(2)}) %collective-permute-start.10) | collective-permute-done | bytes 262176 | tf_op jit(solution)/shard_map/ppermute | solution.py:47
  129.9 4.3 %collective-permute-done.14 = bf16[128,1024]{1,0:T(8,128)(2,1)S(1)} collective-permute-done((bf16[128,1024]{1,0:T(8,128)(2,1)S(1)}, bf16[128,1024]{1,0:T(8,128)(2,1)S(1)}, u32[]{:S(2)}, u32[]{:S(2)}) %collective-permute-start.14) | collective-permute-done | bytes 262176 | tf_op jit(solution)/shard_map/ppermute | solution.py:47
  135.5 4.3 %collective-permute-done.18 = bf16[128,1024]{1,0:T(8,128)(2,1)S(1)} collective-permute-done((bf16[128,1024]{1,0:T(8,128)(2,1)S(1)}, bf16[128,1024]{1,0:T(8,128)(2,1)S(1)}, u32[]{:S(2)}, u32[]{:S(2)}) %collective-permute-start.18) | collective-permute-done | bytes 262176 | tf_op jit(solution)/shard_map/ppermute | solution.py:47
  141.3 4.1 %collective-permute-done.22 = bf16[128,1024]{1,0:T(8,128)(2,1)S(1)} collective-permute-done((bf16[128,1024]{1,0:T(8,128)(2,1)S(1)}, bf16[128,1024]{1,0:T(8,128)(2,1)S(1)}, u32[]{:S(2)}, u32[]{:S(2)}) %collective-permute-start.22) | collective-permute-done | bytes 262176 | tf_op jit(solution)/shard_map/ppermute | solution.py:47
  146.0 5.0 %collective-permute-done.26 = bf16[128,1024]{1,0:T(8,128)(2,1)S(1)} collective-permute-done((bf16[128,1024]{1,0:T(8,128)(2,1)S(1)}, bf16[128,1024]{1,0:T(8,128)(2,1)S(1)}, u32[]{:S(2)}, u32[]{:S(2)}) %collective-permute-start.26) | collective-permute-done | bytes 262176 | tf_op jit(solution)/shard_map/ppermute | solution.py:47
  151.6 5.0 %collective-permute-done.30 = bf16[128,1024]{1,0:T(8,128)(2,1)S(1)} collective-permute-done((bf16[128,1024]{1,0:T(8,128)(2,1)S(1)}, bf16[128,1024]{1,0:T(8,128)(2,1)S(1)}, u32[]{:S(2)}, u32[]{:S(2)}) %collective-permute-start.30) | collective-permute-done | bytes 262176 | tf_op jit(solution)/shard_map/ppermute | solution.py:47
  157.2 4.8 %collective-permute-done.34 = bf16[128,1024]{1,0:T(8,128)(2,1)S(1)} collective-permute-done((bf16[128,1024]{1,0:T(8,128)(2,1)S(1)}, bf16[128,1024]{1,0:T(8,128)(2,1)S(1)}, u32[]{:S(2)}, u32[]{:S(2)}) %collective-permute-start.34) | collective-permute-done | bytes 262176 | tf_op jit(solution)/shard_map/ppermute | solution.py:47
  173.1 3.7 %collective-permute-done.27 = bf16[128,1024]{1,0:T(8,128)(2,1)S(1)} collective-permute-done((bf16[128,1024]{1,0:T(8,128)(2,1)S(1)}, bf16[128,1024]{1,0:T(8,128)(2,1)S(1)}, u32[]{:S(2)}, u32[]{:S(2)}) %collective-permute-start.27) | collective-permute-done | bytes 262176 | tf_op jit(solution)/shard_map/ppermute | solution.py:11
  176.8 5.6 %collective-permute-done.31 = bf16[128,1024]{1,0:T(8,128)(2,1)S(1)} collective-permute-done((bf16[128,1024]{1,0:T(8,128)(2,1)S(1)}, bf16[128,1024]{1,0:T(8,128)(2,1)S(1)}, u32[]{:S(2)}, u32[]{:S(2)}) %collective-permute-start.31) | collective-permute-done | bytes 262176 | tf_op jit(solution)/shard_map/ppermute | solution.py:11
  182.5 4.5 %collective-permute-done.35 = bf16[128,1024]{1,0:T(8,128)(2,1)S(1)} collective-permute-done((bf16[128,1024]{1,0:T(8,128)(2,1)S(1)}, bf16[128,1024]{1,0:T(8,128)(2,1)S(1)}, u32[]{:S(2)}, u32[]{:S(2)}) %collective-permute-start.35) | collective-permute-done | bytes 262176 | tf_op jit(solution)/shard_map/ppermute | solution.py:11
  191.8 3.4 %copy-done = f32[2048,1024]{1,0:T(8,128)} copy-done((f32[2048,1024]{1,0:T(8,128)}, f32[2048,1024]{1,0:T(8,128)S(1)}, u32[]{:S(2)}) %copy-start) | copy-done | bytes 8388632
  (203 shorter events, 60.3 us)
Async XLA Ops:
  0.7 42.3 %collective-permute-start.5 = (bf16[256,256]{1,0:T(8,128)(2,1)}, bf16[256,256]{1,0:T(8,128)(2,1)S(1)}, u32[]{:S(2)}, u32[]{:S(2)}) collective-permute-start(bf16[256,256]{1,0:T(8,128)(2,1)} %param.17), channel_id=1, source_target_pairs={{0,4},{4,0},{1,5},{5,1},{2,6},{6,2},{3,7},{7,3},{8,12},{12,8},{9,1... | collective-permute-start | bytes 393224 | tf_op jit(solution)/shard_map/ppermute | solution.py:11
  5.8 51.2 %collective-permute-start.4 = (bf16[256,1024]{1,0:T(8,128)(2,1)}, bf16[256,1024]{1,0:T(8,128)(2,1)S(1)}, u32[]{:S(2)}, u32[]{:S(2)}) collective-permute-start(bf16[256,1024]{1,0:T(8,128)(2,1)} %get-tuple-element.33), channel_id=1, source_target_pairs={{0,4},{4,0},{1,5},{5,1},{2,6},{6,2},{3,7},{7,3},{8,12},{12,8},{9,1... | collective-permute-start | bytes 1572872 | tf_op jit(solution)/shard_map/ppermute | solution.py:11
  11.4 31.8 %collective-permute-start = (bf16[256,256]{1,0:T(8,128)(2,1)S(1)}, bf16[256,256]{1,0:T(8,128)(2,1)S(1)}, u32[]{:S(2)}, u32[]{:S(2)}) collective-permute-start(bf16[256,256]{1,0:T(8,128)(2,1)S(1)} %get-tuple-element.45), channel_id=1, source_target_pairs={{0,1},{1,0},{2,3},{3,2},{4,5},{5,4},{6,7},{7,6},{8,9},{9,8},{10,11... | collective-permute-start | bytes 393224 | tf_op jit(solution)/shard_map/ppermute | solution.py:11
  11.5 31.7 %collective-permute-start.1 = (bf16[256,256]{1,0:T(8,128)(2,1)S(1)}, bf16[256,256]{1,0:T(8,128)(2,1)S(1)}, u32[]{:S(2)}, u32[]{:S(2)}) collective-permute-start(bf16[256,256]{1,0:T(8,128)(2,1)S(1)} %get-tuple-element.47), channel_id=1, source_target_pairs={{0,2},{1,3},{2,0},{3,1},{4,6},{5,7},{6,4},{7,5},{8,10},{9,11},{10,... | collective-permute-start | bytes 393224 | tf_op jit(solution)/shard_map/ppermute | solution.py:11
  13.5 29.7 %collective-permute-start.2 = (bf16[256,256]{1,0:T(8,128)(2,1)S(1)}, bf16[256,256]{1,0:T(8,128)(2,1)S(1)}, u32[]{:S(2)}, u32[]{:S(2)}) collective-permute-start(bf16[256,256]{1,0:T(8,128)(2,1)S(1)} %get-tuple-element.46), channel_id=1, source_target_pairs={{0,3},{1,2},{2,1},{3,0},{4,7},{5,6},{6,5},{7,4},{8,11},{9,10},{10,... | collective-permute-start | bytes 393224 | tf_op jit(solution)/shard_map/ppermute | solution.py:11
  64.5 19.9 %collective-permute-start.20 = (bf16[128,1024]{1,0:T(8,128)(2,1)S(1)}, bf16[128,1024]{1,0:T(8,128)(2,1)S(1)}, u32[]{:S(2)}, u32[]{:S(2)}) collective-permute-start(bf16[128,1024]{1,0:T(8,128)(2,1)S(1)} %fusion.5), channel_id=1, source_target_pairs={{0,8},{24,16},{1,9},{25,17},{2,10},{26,18},{3,11},{27,19},{4,12},{... | collective-permute-start | bytes 786440 | tf_op jit(solution)/shard_map/ppermute | solution.py:44
  66.1 23.8 %collective-permute-start.24 = (bf16[128,1024]{1,0:T(8,128)(2,1)S(1)}, bf16[128,1024]{1,0:T(8,128)(2,1)S(1)}, u32[]{:S(2)}, u32[]{:S(2)}) collective-permute-start(bf16[128,1024]{1,0:T(8,128)(2,1)S(1)} %fusion.6), channel_id=1, source_target_pairs={{0,8},{24,16},{1,9},{25,17},{2,10},{26,18},{3,11},{27,19},{4,12},{... | collective-permute-start | bytes 786440 | tf_op jit(solution)/shard_map/ppermute | solution.py:44
  68.5 27.1 %collective-permute-start.28 = (bf16[128,1024]{1,0:T(8,128)(2,1)S(1)}, bf16[128,1024]{1,0:T(8,128)(2,1)S(1)}, u32[]{:S(2)}, u32[]{:S(2)}) collective-permute-start(bf16[128,1024]{1,0:T(8,128)(2,1)S(1)} %fusion.7), channel_id=1, source_target_pairs={{0,8},{24,16},{1,9},{25,17},{2,10},{26,18},{3,11},{27,19},{4,12},{... | collective-permute-start | bytes 786440 | tf_op jit(solution)/shard_map/ppermute | solution.py:44
  73.1 28.1 %collective-permute-start.32 = (bf16[128,1024]{1,0:T(8,128)(2,1)S(1)}, bf16[128,1024]{1,0:T(8,128)(2,1)S(1)}, u32[]{:S(2)}, u32[]{:S(2)}) collective-permute-start(bf16[128,1024]{1,0:T(8,128)(2,1)S(1)} %fusion.8), channel_id=1, source_target_pairs={{0,8},{24,16},{1,9},{25,17},{2,10},{26,18},{3,11},{27,19},{4,12},{... | collective-permute-start | bytes 786440 | tf_op jit(solution)/shard_map/ppermute | solution.py:44
  78.8 26.8 %collective-permute-start.36 = (bf16[128,1024]{1,0:T(8,128)(2,1)S(1)}, bf16[128,1024]{1,0:T(8,128)(2,1)S(1)}, u32[]{:S(2)}, u32[]{:S(2)}) collective-permute-start(bf16[128,1024]{1,0:T(8,128)(2,1)S(1)} %fusion.9), channel_id=1, source_target_pairs={{0,8},{24,16},{1,9},{25,17},{2,10},{26,18},{3,11},{27,19},{4,12},{... | collective-permute-start | bytes 786440 | tf_op jit(solution)/shard_map/ppermute | solution.py:44
  84.4 21.9 %collective-permute-start.9 = (bf16[128,1024]{1,0:T(8,128)(2,1)S(1)}, bf16[128,1024]{1,0:T(8,128)(2,1)S(1)}, u32[]{:S(2)}, u32[]{:S(2)}) collective-permute-start(bf16[128,1024]{1,0:T(8,128)(2,1)S(1)} %reduce-precision_convert_fusion.16), channel_id=1, source_target_pairs={{8,16},{16,8},{9,17},{17,9},{10,18},{18,10},{11,19},{19,11},{12,20... | collective-permute-start | bytes 786440 | tf_op jit(solution)/shard_map/ppermute | solution.py:45
  90.0 17.1 %collective-permute-start.13 = (bf16[128,1024]{1,0:T(8,128)(2,1)S(1)}, bf16[128,1024]{1,0:T(8,128)(2,1)S(1)}, u32[]{:S(2)}, u32[]{:S(2)}) collective-permute-start(bf16[128,1024]{1,0:T(8,128)(2,1)S(1)} %reduce-precision_convert_fusion.14), channel_id=1, source_target_pairs={{8,16},{16,8},{9,17},{17,9},{10,18},{18,10},{11,19},{19,11},{12,20... | collective-permute-start | bytes 786440 | tf_op jit(solution)/shard_map/ppermute | solution.py:45
  108.6 20.0 %collective-permute-start.10 = (bf16[128,1024]{1,0:T(8,128)(2,1)S(1)}, bf16[128,1024]{1,0:T(8,128)(2,1)S(1)}, u32[]{:S(2)}, u32[]{:S(2)}) collective-permute-start(bf16[128,1024]{1,0:T(8,128)(2,1)S(1)} %reduce-precision_convert_fusion.15), channel_id=1, source_target_pairs={{8,0},{16,24},{9,1},{17,25},{10,2},{18,26},{11,3},{19,27},{12,4},{... | collective-permute-start | bytes 786440 | tf_op jit(solution)/shard_map/ppermute | solution.py:47
  110.0 24.2 %collective-permute-start.14 = (bf16[128,1024]{1,0:T(8,128)(2,1)S(1)}, bf16[128,1024]{1,0:T(8,128)(2,1)S(1)}, u32[]{:S(2)}, u32[]{:S(2)}) collective-permute-start(bf16[128,1024]{1,0:T(8,128)(2,1)S(1)} %reduce-precision_convert_fusion.13), channel_id=1, source_target_pairs={{8,0},{16,24},{9,1},{17,25},{10,2},{18,26},{11,3},{19,27},{12,4},{... | collective-permute-start | bytes 786440 | tf_op jit(solution)/shard_map/ppermute | solution.py:47
  111.4 28.4 %collective-permute-start.18 = (bf16[128,1024]{1,0:T(8,128)(2,1)S(1)}, bf16[128,1024]{1,0:T(8,128)(2,1)S(1)}, u32[]{:S(2)}, u32[]{:S(2)}) collective-permute-start(bf16[128,1024]{1,0:T(8,128)(2,1)S(1)} %reduce-precision_convert_fusion.11), channel_id=1, source_target_pairs={{8,0},{16,24},{9,1},{17,25},{10,2},{18,26},{11,3},{19,27},{12,4},{... | collective-permute-start | bytes 786440 | tf_op jit(solution)/shard_map/ppermute | solution.py:47
  112.8 32.7 %collective-permute-start.22 = (bf16[128,1024]{1,0:T(8,128)(2,1)S(1)}, bf16[128,1024]{1,0:T(8,128)(2,1)S(1)}, u32[]{:S(2)}, u32[]{:S(2)}) collective-permute-start(bf16[128,1024]{1,0:T(8,128)(2,1)S(1)} %reduce-precision_convert_fusion.9), channel_id=1, source_target_pairs={{8,0},{16,24},{9,1},{17,25},{10,2},{18,26},{11,3},{19,27},{12,4},{... | collective-permute-start | bytes 786440 | tf_op jit(solution)/shard_map/ppermute | solution.py:47
  114.2 36.9 %collective-permute-start.26 = (bf16[128,1024]{1,0:T(8,128)(2,1)S(1)}, bf16[128,1024]{1,0:T(8,128)(2,1)S(1)}, u32[]{:S(2)}, u32[]{:S(2)}) collective-permute-start(bf16[128,1024]{1,0:T(8,128)(2,1)S(1)} %reduce-precision_convert_fusion.7), channel_id=1, source_target_pairs={{8,0},{16,24},{9,1},{17,25},{10,2},{18,26},{11,3},{19,27},{12,4},{... | collective-permute-start | bytes 786440 | tf_op jit(solution)/shard_map/ppermute | solution.py:47
  128.6 28.1 %collective-permute-start.30 = (bf16[128,1024]{1,0:T(8,128)(2,1)S(1)}, bf16[128,1024]{1,0:T(8,128)(2,1)S(1)}, u32[]{:S(2)}, u32[]{:S(2)}) collective-permute-start(bf16[128,1024]{1,0:T(8,128)(2,1)S(1)} %reduce-precision_convert_fusion.5), channel_id=1, source_target_pairs={{8,0},{16,24},{9,1},{17,25},{10,2},{18,26},{11,3},{19,27},{12,4},{... | collective-permute-start | bytes 786440 | tf_op jit(solution)/shard_map/ppermute | solution.py:47
  134.2 27.8 %collective-permute-start.34 = (bf16[128,1024]{1,0:T(8,128)(2,1)S(1)}, bf16[128,1024]{1,0:T(8,128)(2,1)S(1)}, u32[]{:S(2)}, u32[]{:S(2)}) collective-permute-start(bf16[128,1024]{1,0:T(8,128)(2,1)S(1)} %reduce-precision_convert_fusion.3), channel_id=1, source_target_pairs={{8,0},{16,24},{9,1},{17,25},{10,2},{18,26},{11,3},{19,27},{12,4},{... | collective-permute-start | bytes 786440 | tf_op jit(solution)/shard_map/ppermute | solution.py:47
  139.8 25.0 %collective-permute-start.38 = (bf16[128,1024]{1,0:T(8,128)(2,1)S(1)}, bf16[128,1024]{1,0:T(8,128)(2,1)S(1)}, u32[]{:S(2)}, u32[]{:S(2)}) collective-permute-start(bf16[128,1024]{1,0:T(8,128)(2,1)S(1)} %reduce-precision_convert_fusion.1), channel_id=1, source_target_pairs={{8,0},{16,24},{9,1},{17,25},{10,2},{18,26},{11,3},{19,27},{12,4},{... | collective-permute-start | bytes 786440 | tf_op jit(solution)/shard_map/ppermute | solution.py:47
  145.4 20.0 %collective-permute-start.11 = (bf16[128,1024]{1,0:T(8,128)(2,1)S(1)}, bf16[128,1024]{1,0:T(8,128)(2,1)S(1)}, u32[]{:S(2)}, u32[]{:S(2)}) collective-permute-start(bf16[128,1024]{1,0:T(8,128)(2,1)S(1)} %broadcast_select_fusion.13), channel_id=1, source_target_pairs={{0,4},{4,0},{1,5},{5,1},{2,6},{6,2},{3,7},{7,3},{8,12},{12,8},{9,1... | collective-permute-start | bytes 786440 | tf_op jit(solution)/shard_map/ppermute | solution.py:11
  151.0 17.1 %collective-permute-start.15 = (bf16[128,1024]{1,0:T(8,128)(2,1)S(1)}, bf16[128,1024]{1,0:T(8,128)(2,1)S(1)}, u32[]{:S(2)}, u32[]{:S(2)}) collective-permute-start(bf16[128,1024]{1,0:T(8,128)(2,1)S(1)} %broadcast_select_fusion.12), channel_id=1, source_target_pairs={{0,4},{4,0},{1,5},{5,1},{2,6},{6,2},{3,7},{7,3},{8,12},{12,8},{9,1... | collective-permute-start | bytes 786440 | tf_op jit(solution)/shard_map/ppermute | solution.py:11
  168.2 18.8 %collective-permute-start.35 = (bf16[128,1024]{1,0:T(8,128)(2,1)S(1)}, bf16[128,1024]{1,0:T(8,128)(2,1)S(1)}, u32[]{:S(2)}, u32[]{:S(2)}) collective-permute-start(bf16[128,1024]{1,0:T(8,128)(2,1)S(1)} %broadcast_select_fusion.7), channel_id=1, source_target_pairs={{0,4},{4,0},{1,5},{5,1},{2,6},{6,2},{3,7},{7,3},{8,12},{12,8},{9,1... | collective-permute-start | bytes 786440 | tf_op jit(solution)/shard_map/ppermute | solution.py:11
  168.8 21.0 %collective-permute-start.39 = (bf16[128,1024]{1,0:T(8,128)(2,1)S(1)}, bf16[128,1024]{1,0:T(8,128)(2,1)S(1)}, u32[]{:S(2)}, u32[]{:S(2)}) collective-permute-start(bf16[128,1024]{1,0:T(8,128)(2,1)S(1)} %broadcast_select_fusion.6), channel_id=1, source_target_pairs={{0,4},{4,0},{1,5},{5,1},{2,6},{6,2},{3,7},{7,3},{8,12},{12,8},{9,1... | collective-permute-start | bytes 786440 | tf_op jit(solution)/shard_map/ppermute | solution.py:11
  (27 other events, 347.0 us)

commit v2 on v0

v2 whole, which is shorter than its diff:
```python
import jax
import jax.numpy as jnp
from jax import lax
from jax.sharding import PartitionSpec as P

EPSILON = 1e-06
FEATURE_BLOCKS = 8
LAG = 3


def swap(value, axis, bit):
    return lax.ppermute(value, axis, [(i, i ^ bit) for i in range(lax.axis_size(axis))])


def pick(values, index):
    chosen = values[0]
    for i in range(1, len(values)):
        chosen = jnp.where(index == i, values[i], chosen)
    return chosen


def to_bfloat16(value):
    return lax.reduce_precision(value, 8, 7).astype(jnp.bfloat16)


def add(left, right):
    return to_bfloat16(left.astype(jnp.float32) + right.astype(jnp.float32))


def line_sums(parts, axis):
    if lax.axis_size(axis) != 4:
        return [to_bfloat16(lax.psum(part.astype(jnp.float32), axis)) for part in parts]
    index = lax.axis_index(axis)
    inner = (index == 1) | (index == 2)
    count = len(parts)
    totals, results = [], []
    for k in range(count + LAG):
        if k < LAG:
            sent = parts[k]
        elif k < count:
            sent = jnp.where(inner, totals[k - LAG], parts[k])
        else:
            sent = totals[k - LAG]
        got = lax.ppermute(sent, axis, [(0, 1), (1, 0), (2, 3), (3, 2)])
        if k < count:
            half = add(parts[k], got)
            other = lax.ppermute(half, axis, [(1, 2), (2, 1), (0, 0), (3, 3)])
            totals.append(add(half, other))
        if k >= LAG:
            results.append(jnp.where(inner, totals[k - LAG], got))
    return results


def body(
    lengths,
    final_hidden,
    score_gain,
    score_head,
    policy_input,
    block_order,
    norm_gain,
    key_weight,
    key_cotangent,
):
    n_section, n_dp, n_mp = (lax.axis_size(name) for name in ("section", "dp", "mp"))
    dp, mp = lax.axis_index("dp"), lax.axis_index("mp")
    block_count = lengths.shape[0]
    tokens, local_width = policy_input.shape
    block_len = tokens // block_count
    pair = block_count // n_dp
    columns = key_cotangent.shape[1]
    own_width = local_width // n_dp
    chunk = own_width // FEATURE_BLOCKS
    n_far = n_mp // 2
    order = block_order[0]
    gain = norm_gain.astype(jnp.float32)

    cotangents = [key_cotangent] + [swap(key_cotangent, "dp", j) for j in range(1, n_dp)]

    def both_cores(values):
        other = [swap(value, "mp", 1) for value in values]
        low = mp % 2 == 0
        return jnp.concatenate(
            [
                jnp.concatenate([jnp.where(low, a, b), jnp.where(low, b, a)], axis=1)
                for a, b in zip(values, other)
            ],
            axis=0,
        )

    def features(part, f):
        start = part * own_width + f * chunk
        return policy_input[:, start : start + chunk]

    def piece_for(j, first, last):
        return pick(
            [
                policy_input[:, e * own_width + first * chunk : e * own_width + last * chunk]
                for e in range(n_dp)
            ],
            dp ^ j,
        )

    send_blocks = FEATURE_BLOCKS // 4
    rows = []
    for first in range(0, FEATURE_BLOCKS, send_blocks):
        last = first + send_blocks
        got = [piece_for(0, first, last)]
        got += [swap(piece_for(j, first, last), "dp", j) for j in range(1, n_dp)]
        got = jnp.concatenate(got, axis=0)
        rows += [got[:, i * chunk : (i + 1) * chunk] for i in range(send_blocks)]

    hidden_values = final_hidden.astype(jnp.float32)
    inverse_hidden = lax.rsqrt(jnp.mean(hidden_values * hidden_values, axis=1) + EPSILON)
    coefficient = score_gain.astype(jnp.float32) * score_head.astype(jnp.float32)
    scores = jnp.sum(hidden_values * coefficient[None, :], axis=1) * inverse_hidden
    position = lax.broadcasted_iota(jnp.int32, (block_count, block_len), 1)
    token_weight = jnp.where(position < lengths[:, None], scores[:, None], 0.0)
    squares = jnp.sum(jnp.square(policy_input.astype(jnp.float32)), axis=1)
    squares = squares.reshape(block_count, block_len)
    squares = squares + sum(swap(squares, "mp", j) for j in range(1, n_mp))
    inverse = lax.rsqrt(squares / (local_width * n_mp) + EPSILON)
    small = jnp.concatenate(
        [
            inverse,
            token_weight,
            jnp.broadcast_to(order.astype(jnp.float32)[:, None], (block_count, block_len)),
        ],
        axis=0,
    )
    small = [small] + [swap(small, "dp", j) for j in range(1, n_dp)]

    def key_gradient(cotangent):
        blocks = cotangent.reshape(n_dp, block_count, block_len, -1)
        found = []
        for j in range(n_dp):
            sender = dp ^ j
            for b in range(block_count):
                slot = small[j][2 * block_count + b, 0].astype(jnp.int32)
                candidates, where = [], []
                for e in range(n_dp):
                    for q in range(pair):
                        candidates.append(
                            lax.dynamic_index_in_dim(
                                blocks[e], sender * pair + q, 0, keepdims=False
                            )
                        )
                        where.append((dp ^ e) * pair + q)
                chosen = candidates[0]
                for value, at in zip(candidates[1:], where[1:]):
                    chosen = jnp.where(slot == at, value, chosen)
                weight = small[j][block_count + b].astype(jnp.bfloat16).astype(jnp.float32)
                key_grad = to_bfloat16(chosen.astype(jnp.float32) * weight[:, None])
                found.append(
                    (key_grad.astype(jnp.float32) * small[j][b][:, None]).astype(jnp.bfloat16)
                )
        return jnp.concatenate(found, axis=0)

    parts = []
    for g in range(n_far):
        near = cotangents if g == 0 else [swap(value, "mp", 2 * g) for value in cotangents]
        key_grad = key_gradient(both_cores(near))
        for f in range(FEATURE_BLOCKS):
            part = lax.dot_general(
                rows[f],
                key_grad,
                (((0,), (0,)), ((), ())),
                preferred_element_type=jnp.float32,
            )
            parts.append(to_bfloat16(part))
    totals = line_sums(parts, "section")
    shared = [[total] + [swap(total, "dp", j) for j in range(1, n_dp)] for total in totals]
    shards = n_section * n_dp
    grad_weight = jnp.zeros((local_width, n_mp * columns), jnp.float32)
    grad_gain = [None] * (n_dp * FEATURE_BLOCKS)
    for f in range(FEATURE_BLOCKS):
        groups = [shared[g * FEATURE_BLOCKS + f] for g in range(n_far)]
        for e in range(n_dp):
            start = e * own_width + f * chunk
            by_group = [pick(group, dp ^ e) for group in groups]
            value = jnp.concatenate([pick(by_group, (mp // 2) ^ g) for g in range(n_far)], axis=1)
            value = value.astype(jnp.float32) / shards
            grad_weight = lax.dynamic_update_slice(
                grad_weight, value * gain[start : start + chunk, None], (start, 0)
            )
            weight = key_weight[start : start + chunk].astype(jnp.float32)
            grad_gain[e * FEATURE_BLOCKS + f] = jnp.sum(value * weight, axis=1)
    grad_gain = jnp.concatenate(grad_gain)

    inverse, _ = lax.optimization_barrier((inverse, totals[0]))
    normed = policy_input.astype(jnp.float32) * inverse.reshape(-1, 1) * gain[None, :]
    normed = lax.optimization_barrier(normed.astype(jnp.bfloat16))
    partial = jnp.dot(normed, key_weight, preferred_element_type=jnp.float32)
    own_columns = pick([partial[:, i * columns : (i + 1) * columns] for i in range(n_mp)], mp)
    partial = partial.astype(jnp.bfloat16)
    for j in range(1, n_mp):
        piece = pick([partial[:, i * columns : (i + 1) * columns] for i in range(n_mp)], mp ^ j)
        own_columns = own_columns + swap(piece, "mp", j).astype(jnp.float32)
    keys = own_columns.astype(jnp.bfloat16).reshape(block_count, block_len, columns)
    by_slot = []
    for slot in range(block_count):
        chosen = keys[0]
        for b in range(1, block_count):
            chosen = jnp.where(order[b] == slot, keys[b], chosen)
        by_slot.append(chosen)
    by_target = [jnp.stack(by_slot[e * pair : (e + 1) * pair]) for e in range(n_dp)]
    arrived = [pick(by_target, dp)]
    arrived += [swap(pick(by_target, dp ^ j), "dp", j) for j in range(1, n_dp)]
    learner_keys = jnp.concatenate([pick(arrived, dp ^ a) for a in range(n_dp)], axis=0)
    return learner_keys.reshape(tokens, columns), grad_weight, grad_gain


def solution(mesh):
    placed = (
        P(("section", "dp")),
        P(("section", "dp"), None),
        P(),
        P(),
        P(("section", "dp"), "mp"),
        P(("section", "dp"), None),
        P("mp"),
        P("mp", None),
        P(("section", "dp"), "mp"),
    )
    return jax.shard_map(
        body,
        mesh=mesh,
        in_specs=placed,
        out_specs=(P(("section", "dp"), "mp"), P("mp", None), P("mp")),
        check_vma=False,
    )
```

time: 365 us -> 257 us (0.70)
  starting transfers between devices: 3.27 us -> 146 us
  waiting for transfers between devices: 189 us -> 77.6 us
  blocking collectives: 111 us -> 0 us
  local copies, waits for them, and re-layouts: 16.8 us -> 6.96 us
  between operations: 14.3 us -> 5.38 us
  matrix products: 13.7 us -> 5.39 us
    psum x1 -> x0, waiting for transfers between devices: 172 us -> none  [body(): lax.psum((grad_weight, local_gain), ('section', 'dp'))]
    ppermute x0 -> x70, starting transfers between devices: none -> 146 us  [the longest x19 102 us: line_sums(): got = lax.ppermute(sent, axis, [(0, 1), (1, 0), (2, 3), (3, 2)])]
    ppermute x0 -> x70, waiting for transfers between devices: none -> 77.6 us  [the longest x19 42.7 us: line_sums(): got = lax.ppermute(sent, axis, [(0, 1), (1, 0), (2, 3), (3, 2)])]
    all_to_all x2 -> x0, blocking collectives: 72.2 us -> none  [the longest x1 53.8 us: body(): lax.all_to_all(key_weight, 'mp', split_axis=1, concat_axis=0, tiled=True)]
    psum x1 -> x0, blocking collectives: 23.1 us -> none  [body(): lax.psum((grad_weight, local_gain), ('section', 'dp'))]
    all_gather x1 -> x0, waiting for transfers between devices: 17.4 us -> none  [body(): lax.all_gather(learner_rows, 'mp', axis=1, tiled=True)]
    all_gather x2 -> x0, blocking collectives: 15.7 us -> none  [the longest x1 10.5 us: body(): piece = lax.all_gather(key_grad, 'mp', axis=1, tiled=True)]
    div x2 -> x0, other arithmetic: 9.3 us -> none  [body(): return (projected, summed_weight / shards, summed_gain / shards)]
  transfers between devices with their start and end apart: 3 -> 70, of which waited for: 2 -> 28; matrix products, arithmetic and copies ran while one was open for 7% -> 8% of each run, Pallas kernels for 0% -> 0%
where the time goes in v2:
time: 257 us; the launch traced here: 256 us
  starting transfers between devices  146 us (57%)
  waiting for transfers between devices  77.6 us (30%)
  other arithmetic  15.2 us (6%)
  local copies, waits for them, and re-layouts  6.96 us (3%)
  matrix products  5.39 us (2%)
  between operations  5.38 us (2%)
    ppermute x19, starting transfers between devices, line_sums(): got = lax.ppermute(sent, axis, [(0, 1), (1, 0), (2, 3), (3, 2)])  102 us
    ppermute x19, waiting for transfers between devices, line_sums(): got = lax.ppermute(sent, axis, [(0, 1), (1, 0), (2, 3), (3, 2)])  42.7 us
    ppermute x35, waiting for transfers between devices, swap(): lax.ppermute(value, axis, [(i, i ^ bit) for i in range(lax.axis_size(axis...  34.9 us
    ppermute x35, starting transfers between devices, swap(): lax.ppermute(value, axis, [(i, i ^ bit) for i in range(lax.axis_size(axis...  33 us
    ppermute x16, starting transfers between devices, line_sums(): other = lax.ppermute(half, axis, [(1, 2), (2, 1), (0, 0), (3, 3)])  10.8 us
  transfers between devices with their start and end apart: 70, of which 28 were waited for; matrix products, arithmetic and copies ran while one was open for 8% of the time, Pallas kernels for 0%

profile of v2, /device:TPU:0, one launch (start us, length us, event | category | flops | bytes accessed | tf_op | source)
XLA Modules:
  0.0 256.1 jit_solution(6318914237121191691)
XLA Ops:
  21.0 3.2 %collective-permute-done.7 = f32[6,128]{1,0:T(8,128)S(1)} collective-permute-done((f32[6,128]{1,0:T(8,128)S(1)}, f32[6,128]{1,0:T(8,128)S(1)}, u32[]{:S(2)}, u32[]{:S(2)}) %collective-permute-start.7) | collective-permute-done | bytes 3104 | tf_op jit(solution)/shard_map/ppermute | solution.py:12
  29.8 5.2 %collective-permute-done.16 = bf16[256,256]{1,0:T(8,128)(2,1)S(1)} collective-permute-done((bf16[256,256]{1,0:T(8,128)(2,1)S(1)}, bf16[256,256]{1,0:T(8,128)(2,1)S(1)}, u32[]{:S(2)}, u32[]{:S(2)}) %collective-permute-start.16) | collective-permute-done | bytes 131104 | tf_op jit(solution)/shard_map/ppermute | solution.py:12
  44.8 4.1 %collective-permute-done.38 = bf16[128,512]{1,0:T(8,128)(2,1)S(1)} collective-permute-done((bf16[128,512]{1,0:T(8,128)(2,1)S(1)}, bf16[128,512]{1,0:T(8,128)(2,1)S(1)}, u32[]{:S(2)}, u32[]{:S(2)}) %collective-permute-start.38) | collective-permute-done | bytes 131104 | tf_op jit(solution)/shard_map/ppermute | solution.py:44
  50.6 7.1 %collective-permute-start.40 = (bf16[128,512]{1,0:T(8,128)(2,1)S(1)}, bf16[128,512]{1,0:T(8,128)(2,1)S(1)}, u32[]{:S(2)}, u32[]{:S(2)}) collective-permute-start(bf16[128,512]{1,0:T(8,128)(2,1)S(1)} %get-tuple-element.135), channel_id=1, source_target_pairs={{0,8},{8,0},{16,24},{24,16},{1,9},{9,1},{17,25},{25,17},{2,10},{10... | collective-permute-start | bytes 393224 | tf_op jit(solution)/shard_map/ppermute | solution.py:44
  58.0 3.2 %collective-permute-start.11 = (bf16[128,512]{1,0:T(8,128)(2,1)S(1)}, bf16[128,512]{1,0:T(8,128)(2,1)S(1)}, u32[]{:S(2)}, u32[]{:S(2)}) collective-permute-start(bf16[128,512]{1,0:T(8,128)(2,1)S(1)} %get-tuple-element.121), channel_id=1, source_target_pairs={{0,8},{8,0},{16,24},{24,16},{1,9},{9,1},{17,25},{25,17},{2,10},{10... | collective-permute-start | bytes 393224 | tf_op jit(solution)/shard_map/ppermute | solution.py:44
  61.6 3.3 %collective-permute-done.11 = bf16[128,512]{1,0:T(8,128)(2,1)S(1)} collective-permute-done((bf16[128,512]{1,0:T(8,128)(2,1)S(1)}, bf16[128,512]{1,0:T(8,128)(2,1)S(1)}, u32[]{:S(2)}, u32[]{:S(2)}) %collective-permute-start.11) | collective-permute-done | bytes 131104 | tf_op jit(solution)/shard_map/ppermute | solution.py:44
  73.7 3.2 %collective-permute-done.13 = bf16[256,256]{1,0:T(8,128)(2,1)S(1)} collective-permute-done((bf16[256,256]{1,0:T(8,128)(2,1)S(1)}, bf16[256,256]{1,0:T(8,128)(2,1)S(1)}, u32[]{:S(2)}, u32[]{:S(2)}) %collective-permute-start.13) | collective-permute-done | bytes 131104 | tf_op jit(solution)/shard_map/ppermute | solution.py:12
  78.8 8.1 %collective-permute-start.43 = (bf16[128,512]{1,0:T(8,128)(2,1)S(1)}, bf16[128,512]{1,0:T(8,128)(2,1)S(1)}, u32[]{:S(2)}, u32[]{:S(2)}) collective-permute-start(bf16[128,512]{1,0:T(8,128)(2,1)S(1)} %get-tuple-element.137), channel_id=1, source_target_pairs={{0,8},{8,0},{16,24},{24,16},{1,9},{9,1},{17,25},{25,17},{2,10},{10... | collective-permute-start | bytes 393224 | tf_op jit(solution)/shard_map/ppermute | solution.py:44
  91.4 3.1 %collective-permute-start.32 = (bf16[128,512]{1,0:T(8,128)(2,1)S(1)}, bf16[128,512]{1,0:T(8,128)(2,1)S(1)}, u32[]{:S(2)}, u32[]{:S(2)}) collective-permute-start(bf16[128,512]{1,0:T(8,128)(2,1)S(1)} %get-tuple-element.133), channel_id=1, source_target_pairs={{0,8},{8,0},{16,24},{24,16},{1,9},{9,1},{17,25},{25,17},{2,10},{10... | collective-permute-start | bytes 393224 | tf_op jit(solution)/shard_map/ppermute | solution.py:44
  95.4 3.4 %collective-permute-done.32 = bf16[128,512]{1,0:T(8,128)(2,1)S(1)} collective-permute-done((bf16[128,512]{1,0:T(8,128)(2,1)S(1)}, bf16[128,512]{1,0:T(8,128)(2,1)S(1)}, u32[]{:S(2)}, u32[]{:S(2)}) %collective-permute-start.32) | collective-permute-done | bytes 131104 | tf_op jit(solution)/shard_map/ppermute | solution.py:44
  103.8 17.6 %collective-permute-start.45 = (bf16[128,512]{1,0:T(8,128)(2,1)S(1)}, bf16[128,512]{1,0:T(8,128)(2,1)S(1)}, u32[]{:S(2)}, u32[]{:S(2)}) collective-permute-start(bf16[128,512]{1,0:T(8,128)(2,1)S(1)} %get-tuple-element.139), channel_id=1, source_target_pairs={{0,8},{8,0},{16,24},{24,16},{1,9},{9,1},{17,25},{25,17},{2,10},{10... | collective-permute-start | bytes 393224 | tf_op jit(solution)/shard_map/ppermute | solution.py:44
  121.7 3.7 %collective-permute-done.45 = bf16[128,512]{1,0:T(8,128)(2,1)S(1)} collective-permute-done((bf16[128,512]{1,0:T(8,128)(2,1)S(1)}, bf16[128,512]{1,0:T(8,128)(2,1)S(1)}, u32[]{:S(2)}, u32[]{:S(2)}) %collective-permute-start.45) | collective-permute-done | bytes 131104 | tf_op jit(solution)/shard_map/ppermute | solution.py:44
  127.7 2.9 %collective-permute-done.27 = bf16[128,512]{1,0:T(8,128)(2,1)S(1)} collective-permute-done((bf16[128,512]{1,0:T(8,128)(2,1)S(1)}, bf16[128,512]{1,0:T(8,128)(2,1)S(1)}, u32[]{:S(2)}, u32[]{:S(2)}) %collective-permute-start.27) | collective-permute-done | bytes 131104 | tf_op jit(solution)/shard_map/ppermute | solution.py:44
  132.7 2.8 %collective-permute-done.34 = bf16[128,512]{1,0:T(8,128)(2,1)S(1)} collective-permute-done((bf16[128,512]{1,0:T(8,128)(2,1)S(1)}, bf16[128,512]{1,0:T(8,128)(2,1)S(1)}, u32[]{:S(2)}, u32[]{:S(2)}) %collective-permute-start.34) | collective-permute-done | bytes 131104 | tf_op jit(solution)/shard_map/ppermute | solution.py:44
  143.2 21.2 %collective-permute-start.47 = (bf16[128,512]{1,0:T(8,128)(2,1)S(1)}, bf16[128,512]{1,0:T(8,128)(2,1)S(1)}, u32[]{:S(2)}, u32[]{:S(2)}) collective-permute-start(bf16[128,512]{1,0:T(8,128)(2,1)S(1)} %get-tuple-element.141), channel_id=1, source_target_pairs={{0,8},{8,0},{16,24},{24,16},{1,9},{9,1},{17,25},{25,17},{2,10},{10... | collective-permute-start | bytes 393224 | tf_op jit(solution)/shard_map/ppermute | solution.py:44
  169.4 2.8 %collective-permute-done.36 = bf16[128,512]{1,0:T(8,128)(2,1)S(1)} collective-permute-done((bf16[128,512]{1,0:T(8,128)(2,1)S(1)}, bf16[128,512]{1,0:T(8,128)(2,1)S(1)}, u32[]{:S(2)}, u32[]{:S(2)}) %collective-permute-start.36) | collective-permute-done | bytes 131104 | tf_op jit(solution)/shard_map/ppermute | solution.py:44
  174.4 2.8 %collective-permute-done.51 = bf16[128,512]{1,0:T(8,128)(2,1)S(1)} collective-permute-done((bf16[128,512]{1,0:T(8,128)(2,1)S(1)}, bf16[128,512]{1,0:T(8,128)(2,1)S(1)}, u32[]{:S(2)}, u32[]{:S(2)}) %collective-permute-start.51) | collective-permute-done | bytes 131104 | tf_op jit(solution)/shard_map/ppermute | solution.py:44
  197.0 17.7 %collective-permute-start.55 = (bf16[128,512]{1,0:T(8,128)(2,1)S(1)}, bf16[128,512]{1,0:T(8,128)(2,1)S(1)}, u32[]{:S(2)}, u32[]{:S(2)}) collective-permute-start(bf16[128,512]{1,0:T(8,128)(2,1)S(1)} %get-tuple-element.147), channel_id=1, source_target_pairs={{0,8},{8,0},{16,24},{24,16},{1,9},{9,1},{17,25},{25,17},{2,10},{10... | collective-permute-start | bytes 393224 | tf_op jit(solution)/shard_map/ppermute | solution.py:44
  214.8 3.1 %collective-permute-done.55 = bf16[128,512]{1,0:T(8,128)(2,1)S(1)} collective-permute-done((bf16[128,512]{1,0:T(8,128)(2,1)S(1)}, bf16[128,512]{1,0:T(8,128)(2,1)S(1)}, u32[]{:S(2)}, u32[]{:S(2)}) %collective-permute-start.55) | collective-permute-done | bytes 131104 | tf_op jit(solution)/shard_map/ppermute | solution.py:44
  219.7 3.1 %collective-permute-done.59 = bf16[128,512]{1,0:T(8,128)(2,1)S(1)} collective-permute-done((bf16[128,512]{1,0:T(8,128)(2,1)S(1)}, bf16[128,512]{1,0:T(8,128)(2,1)S(1)}, u32[]{:S(2)}, u32[]{:S(2)}) %collective-permute-start.59) | collective-permute-done | bytes 131104 | tf_op jit(solution)/shard_map/ppermute | solution.py:44
  224.7 3.2 %collective-permute-done.63 = bf16[128,512]{1,0:T(8,128)(2,1)S(1)} collective-permute-done((bf16[128,512]{1,0:T(8,128)(2,1)S(1)}, bf16[128,512]{1,0:T(8,128)(2,1)S(1)}, u32[]{:S(2)}, u32[]{:S(2)}) %collective-permute-start.63) | collective-permute-done | bytes 131104 | tf_op jit(solution)/shard_map/ppermute | solution.py:44
  235.1 7.9 %collective-permute-start.67 = (bf16[128,512]{1,0:T(8,128)(2,1)S(1)}, bf16[128,512]{1,0:T(8,128)(2,1)S(1)}, u32[]{:S(2)}, u32[]{:S(2)}) collective-permute-start(bf16[128,512]{1,0:T(8,128)(2,1)S(1)} %reduce-precision_convert_fusion), channel_id=1, source_target_pairs={{0,8},{8,0},{16,24},{24,16},{1,9},{9,1},{17,25},{25,17},{2,10},{10... | collective-permute-start | bytes 393224 | tf_op jit(solution)/shard_map/ppermute | solution.py:44
  246.7 4.3 %collective-permute-done.68 = bf16[128,512]{1,0:T(8,128)(2,1)S(1)} collective-permute-done((bf16[128,512]{1,0:T(8,128)(2,1)S(1)}, bf16[128,512]{1,0:T(8,128)(2,1)S(1)}, u32[]{:S(2)}, u32[]{:S(2)}) %collective-permute-start.68) | collective-permute-done | bytes 131104 | tf_op jit(solution)/shard_map/ppermute | solution.py:12
  253.0 3.0 %copy-done.1 = f32[2048,1024]{1,0:T(8,128)} copy-done((f32[2048,1024]{1,0:T(8,128)}, f32[2048,1024]{1,0:T(8,128)S(1)}, u32[]{:S(2)}) %copy-start.1) | copy-done | bytes 8388632
  (257 shorter events, 110.2 us)
Async XLA Ops:
  2.1 15.3 %collective-permute-start.2 = (f32[2,128]{1,0:T(2,128)S(1)}, f32[2,128]{1,0:T(2,128)S(1)}, u32[]{:S(2)}, u32[]{:S(2)}) collective-permute-start(f32[2,128]{1,0:T(2,128)S(1)} %bitcast.73), channel_id=1, source_target_pairs={{0,3},{1,2},{2,1},{3,0},{4,7},{5,6},{6,5},{7,4},{8,11},{9,10},{10,... | collective-permute-start | bytes 3080 | tf_op jit(solution)/shard_map/ppermute | solution.py:12
  4.6 14.2 %collective-permute-start.1 = (f32[2,128]{1,0:T(2,128)S(1)}, f32[2,128]{1,0:T(2,128)S(1)}, u32[]{:S(2)}, u32[]{:S(2)}) collective-permute-start(f32[2,128]{1,0:T(2,128)S(1)} %bitcast.74), channel_id=1, source_target_pairs={{0,2},{1,3},{2,0},{3,1},{4,6},{5,7},{6,4},{7,5},{8,10},{9,11},{10,... | collective-permute-start | bytes 3080 | tf_op jit(solution)/shard_map/ppermute | solution.py:12
  5.2 14.1 %collective-permute-start = (f32[2,128]{1,0:T(2,128)S(1)}, f32[2,128]{1,0:T(2,128)S(1)}, u32[]{:S(2)}, u32[]{:S(2)}) collective-permute-start(f32[2,128]{1,0:T(2,128)S(1)} %bitcast.75), channel_id=1, source_target_pairs={{0,1},{1,0},{2,3},{3,2},{4,5},{5,4},{6,7},{7,6},{8,9},{9,8},{10,11... | collective-permute-start | bytes 3080 | tf_op jit(solution)/shard_map/ppermute | solution.py:12
  5.3 21.2 %collective-permute-start.6 = (bf16[256,256]{1,0:T(8,128)(2,1)}, bf16[256,256]{1,0:T(8,128)(2,1)S(1)}, u32[]{:S(2)}, u32[]{:S(2)}) collective-permute-start(bf16[256,256]{1,0:T(8,128)(2,1)} %param.17), channel_id=1, source_target_pairs={{0,1},{1,0},{2,3},{3,2},{4,5},{5,4},{6,7},{7,6},{8,9},{9,8},{10,11... | collective-permute-start | bytes 393224 | tf_op jit(solution)/shard_map/ppermute | solution.py:12
  5.8 22.3 %collective-permute-start.4 = (bf16[256,256]{1,0:T(8,128)(2,1)}, bf16[256,256]{1,0:T(8,128)(2,1)S(1)}, u32[]{:S(2)}, u32[]{:S(2)}) collective-permute-start(bf16[256,256]{1,0:T(8,128)(2,1)} %param.17), channel_id=1, source_target_pairs={{0,4},{4,0},{1,5},{5,1},{2,6},{6,2},{3,7},{7,3},{8,12},{12,8},{9,1... | collective-permute-start | bytes 393224 | tf_op jit(solution)/shard_map/ppermute | solution.py:12
  18.8 51.6 %collective-permute-start.30 = (bf16[256,256]{1,0:T(8,128)(2,1)S(1)}, bf16[256,256]{1,0:T(8,128)(2,1)S(1)}, u32[]{:S(2)}, u32[]{:S(2)}) collective-permute-start(bf16[256,256]{1,0:T(8,128)(2,1)S(1)} %get-tuple-element.26), channel_id=1, source_target_pairs={{0,4},{4,0},{1,5},{5,1},{2,6},{6,2},{3,7},{7,3},{8,12},{12,8},{9,1... | collective-permute-start | bytes 393224 | tf_op jit(solution)/shard_map/ppermute | solution.py:12
  24.2 13.2 %collective-permute-start.10 = (bf16[256,256]{1,0:T(8,128)(2,1)S(1)}, bf16[256,256]{1,0:T(8,128)(2,1)S(1)}, u32[]{:S(2)}, u32[]{:S(2)}) collective-permute-start(bf16[256,256]{1,0:T(8,128)(2,1)S(1)} %get-tuple-element.31), channel_id=1, source_target_pairs={{0,4},{4,0},{1,5},{5,1},{2,6},{6,2},{3,7},{7,3},{8,12},{12,8},{9,1... | collective-permute-start | bytes 393224 | tf_op jit(solution)/shard_map/ppermute | solution.py:12
  26.5 23.9 %collective-permute-start.20 = (bf16[256,256]{1,0:T(8,128)(2,1)S(1)}, bf16[256,256]{1,0:T(8,128)(2,1)S(1)}, u32[]{:S(2)}, u32[]{:S(2)}) collective-permute-start(bf16[256,256]{1,0:T(8,128)(2,1)S(1)} %get-tuple-element.32), channel_id=1, source_target_pairs={{0,4},{4,0},{1,5},{5,1},{2,6},{6,2},{3,7},{7,3},{8,12},{12,8},{9,1... | collective-permute-start | bytes 393224 | tf_op jit(solution)/shard_map/ppermute | solution.py:12
  44.1 17.1 %collective-permute-start.22 = (bf16[128,512]{1,0:T(8,128)(2,1)S(1)}, bf16[128,512]{1,0:T(8,128)(2,1)S(1)}, u32[]{:S(2)}, u32[]{:S(2)}) collective-permute-start(bf16[128,512]{1,0:T(8,128)(2,1)S(1)} %reduce-precision_convert_fusion.29), channel_id=1, source_target_pairs={{8,16},{16,8},{0,0},{24,24},{9,17},{17,9},{1,1},{25,25},{10,18},{1... | collective-permute-start | bytes 393224 | tf_op jit(solution)/shard_map/ppermute | solution.py:47
  50.6 15.9 %collective-permute-start.40 = (bf16[128,512]{1,0:T(8,128)(2,1)S(1)}, bf16[128,512]{1,0:T(8,128)(2,1)S(1)}, u32[]{:S(2)}, u32[]{:S(2)}) collective-permute-start(bf16[128,512]{1,0:T(8,128)(2,1)S(1)} %get-tuple-element.135), channel_id=1, source_target_pairs={{0,8},{8,0},{16,24},{24,16},{1,9},{9,1},{17,25},{25,17},{2,10},{10... | collective-permute-start | bytes 393224 | tf_op jit(solution)/shard_map/ppermute | solution.py:44
  65.0 72.2 %collective-permute-start.29 = (bf16[128,512]{1,0:T(8,128)(2,1)S(1)}, bf16[128,512]{1,0:T(8,128)(2,1)S(1)}, u32[]{:S(2)}, u32[]{:S(2)}) collective-permute-start(bf16[128,512]{1,0:T(8,128)(2,1)S(1)} %broadcast_select_fusion.107), channel_id=1, source_target_pairs={{0,4},{4,0},{1,5},{5,1},{2,6},{6,2},{3,7},{7,3},{8,12},{12,8},{9,1... | collective-permute-start | bytes 393224 | tf_op jit(solution)/shard_map/ppermute | solution.py:12
  67.3 116.4 %collective-permute-start.41 = (bf16[128,512]{1,0:T(8,128)(2,1)S(1)}, bf16[128,512]{1,0:T(8,128)(2,1)S(1)}, u32[]{:S(2)}, u32[]{:S(2)}) collective-permute-start(bf16[128,512]{1,0:T(8,128)(2,1)S(1)} %broadcast_select_fusion.97), channel_id=1, source_target_pairs={{0,4},{4,0},{1,5},{5,1},{2,6},{6,2},{3,7},{7,3},{8,12},{12,8},{9,1... | collective-permute-start | bytes 393224 | tf_op jit(solution)/shard_map/ppermute | solution.py:12
  73.0 14.1 %collective-permute-start.24 = (bf16[128,512]{1,0:T(8,128)(2,1)S(1)}, bf16[128,512]{1,0:T(8,128)(2,1)S(1)}, u32[]{:S(2)}, u32[]{:S(2)}) collective-permute-start(bf16[128,512]{1,0:T(8,128)(2,1)S(1)} %reduce-precision_convert_fusion.27), channel_id=1, source_target_pairs={{8,16},{16,8},{0,0},{24,24},{9,17},{17,9},{1,1},{25,25},{10,18},{1... | collective-permute-start | bytes 393224 | tf_op jit(solution)/shard_map/ppermute | solution.py:47
  76.9 101.9 %collective-permute-start.49 = (bf16[128,512]{1,0:T(8,128)(2,1)S(1)}, bf16[128,512]{1,0:T(8,128)(2,1)S(1)}, u32[]{:S(2)}, u32[]{:S(2)}) collective-permute-start(bf16[128,512]{1,0:T(8,128)(2,1)S(1)} %broadcast_select_fusion.92), channel_id=1, source_target_pairs={{0,4},{4,0},{1,5},{5,1},{2,6},{6,2},{3,7},{7,3},{8,12},{12,8},{9,1... | collective-permute-start | bytes 393224 | tf_op jit(solution)/shard_map/ppermute | solution.py:12
  78.8 16.4 %collective-permute-start.43 = (bf16[128,512]{1,0:T(8,128)(2,1)S(1)}, bf16[128,512]{1,0:T(8,128)(2,1)S(1)}, u32[]{:S(2)}, u32[]{:S(2)}) collective-permute-start(bf16[128,512]{1,0:T(8,128)(2,1)S(1)} %get-tuple-element.137), channel_id=1, source_target_pairs={{0,8},{8,0},{16,24},{24,16},{1,9},{9,1},{17,25},{25,17},{2,10},{10... | collective-permute-start | bytes 393224 | tf_op jit(solution)/shard_map/ppermute | solution.py:44
  100.3 128.8 %collective-permute-start.57 = (bf16[128,512]{1,0:T(8,128)(2,1)S(1)}, bf16[128,512]{1,0:T(8,128)(2,1)S(1)}, u32[]{:S(2)}, u32[]{:S(2)}) collective-permute-start(bf16[128,512]{1,0:T(8,128)(2,1)S(1)} %broadcast_select_fusion.86), channel_id=1, source_target_pairs={{0,4},{4,0},{1,5},{5,1},{2,6},{6,2},{3,7},{7,3},{8,12},{12,8},{9,1... | collective-permute-start | bytes 393224 | tf_op jit(solution)/shard_map/ppermute | solution.py:12
  103.8 21.6 %collective-permute-start.45 = (bf16[128,512]{1,0:T(8,128)(2,1)S(1)}, bf16[128,512]{1,0:T(8,128)(2,1)S(1)}, u32[]{:S(2)}, u32[]{:S(2)}) collective-permute-start(bf16[128,512]{1,0:T(8,128)(2,1)S(1)} %get-tuple-element.139), channel_id=1, source_target_pairs={{0,8},{8,0},{16,24},{24,16},{1,9},{9,1},{17,25},{25,17},{2,10},{10... | collective-permute-start | bytes 393224 | tf_op jit(solution)/shard_map/ppermute | solution.py:44
  137.2 51.5 %collective-permute-start.53 = (bf16[128,512]{1,0:T(8,128)(2,1)S(1)}, bf16[128,512]{1,0:T(8,128)(2,1)S(1)}, u32[]{:S(2)}, u32[]{:S(2)}) collective-permute-start(bf16[128,512]{1,0:T(8,128)(2,1)S(1)} %broadcast_select_fusion.89), channel_id=1, source_target_pairs={{0,4},{4,0},{1,5},{5,1},{2,6},{6,2},{3,7},{7,3},{8,12},{12,8},{9,1... | collective-permute-start | bytes 393224 | tf_op jit(solution)/shard_map/ppermute | solution.py:12
  143.2 24.1 %collective-permute-start.47 = (bf16[128,512]{1,0:T(8,128)(2,1)S(1)}, bf16[128,512]{1,0:T(8,128)(2,1)S(1)}, u32[]{:S(2)}, u32[]{:S(2)}) collective-permute-start(bf16[128,512]{1,0:T(8,128)(2,1)S(1)} %get-tuple-element.141), channel_id=1, source_target_pairs={{0,8},{8,0},{16,24},{24,16},{1,9},{9,1},{17,25},{25,17},{2,10},{10... | collective-permute-start | bytes 393224 | tf_op jit(solution)/shard_map/ppermute | solution.py:44
  178.8 56.3 %collective-permute-start.61 = (bf16[128,512]{1,0:T(8,128)(2,1)S(1)}, bf16[128,512]{1,0:T(8,128)(2,1)S(1)}, u32[]{:S(2)}, u32[]{:S(2)}) collective-permute-start(bf16[128,512]{1,0:T(8,128)(2,1)S(1)} %broadcast_select_fusion.84), channel_id=1, source_target_pairs={{0,4},{4,0},{1,5},{5,1},{2,6},{6,2},{3,7},{7,3},{8,12},{12,8},{9,1... | collective-permute-start | bytes 393224 | tf_op jit(solution)/shard_map/ppermute | solution.py:12
  183.7 63.0 %collective-permute-start.69 = (bf16[128,512]{1,0:T(8,128)(2,1)S(1)}, bf16[128,512]{1,0:T(8,128)(2,1)S(1)}, u32[]{:S(2)}, u32[]{:S(2)}) collective-permute-start(bf16[128,512]{1,0:T(8,128)(2,1)S(1)} %broadcast_select_fusion.80), channel_id=1, source_target_pairs={{0,4},{4,0},{1,5},{5,1},{2,6},{6,2},{3,7},{7,3},{8,12},{12,8},{9,1... | collective-permute-start | bytes 393224 | tf_op jit(solution)/shard_map/ppermute | solution.py:12
  188.7 54.6 %collective-permute-start.65 = (bf16[128,512]{1,0:T(8,128)(2,1)S(1)}, bf16[128,512]{1,0:T(8,128)(2,1)S(1)}, u32[]{:S(2)}, u32[]{:S(2)}) collective-permute-start(bf16[128,512]{1,0:T(8,128)(2,1)S(1)} %broadcast_select_fusion.82), channel_id=1, source_target_pairs={{0,4},{4,0},{1,5},{5,1},{2,6},{6,2},{3,7},{7,3},{8,12},{12,8},{9,1... | collective-permute-start | bytes 393224 | tf_op jit(solution)/shard_map/ppermute | solution.py:12
  197.0 20.9 %collective-permute-start.55 = (bf16[128,512]{1,0:T(8,128)(2,1)S(1)}, bf16[128,512]{1,0:T(8,128)(2,1)S(1)}, u32[]{:S(2)}, u32[]{:S(2)}) collective-permute-start(bf16[128,512]{1,0:T(8,128)(2,1)S(1)} %get-tuple-element.147), channel_id=1, source_target_pairs={{0,8},{8,0},{16,24},{24,16},{1,9},{9,1},{17,25},{25,17},{2,10},{10... | collective-permute-start | bytes 393224 | tf_op jit(solution)/shard_map/ppermute | solution.py:44
  229.1 13.9 %collective-permute-start.60 = (bf16[128,512]{1,0:T(8,128)(2,1)S(1)}, bf16[128,512]{1,0:T(8,128)(2,1)S(1)}, u32[]{:S(2)}, u32[]{:S(2)}) collective-permute-start(bf16[128,512]{1,0:T(8,128)(2,1)S(1)} %broadcast_select_fusion.85), channel_id=1, source_target_pairs={{0,4},{4,0},{1,5},{5,1},{2,6},{6,2},{3,7},{7,3},{8,12},{12,8},{9,1... | collective-permute-start | bytes 393224 | tf_op jit(solution)/shard_map/ppermute | solution.py:12
  (50 other events, 278.2 us)

commit v3 on v2

v3 whole, which is shorter than its diff:
```python
import functools

import jax
import jax.numpy as jnp
from jax import lax
from jax.experimental import pallas as pl
from jax.experimental.pallas import tpu as pltpu
from jax.sharding import PartitionSpec as P

EPSILON = 1e-06
CHUNK_ROWS = 128
LAG = 3
SHARE_LAG = 2


def swap(value, axis, bit):
    return lax.ppermute(value, axis, [(i, i ^ bit) for i in range(lax.axis_size(axis))])


def pick(values, index):
    chosen = values[0]
    for i in range(1, len(values)):
        chosen = jnp.where(index == i, values[i], chosen)
    return chosen


def to_bfloat16(value):
    return lax.reduce_precision(value, 8, 7).astype(jnp.bfloat16)


def add(left, right):
    return to_bfloat16(left.astype(jnp.float32) + right.astype(jnp.float32))


def summed(parts, shared_sum, emit):
    count = len(parts)
    if lax.axis_size("section") != 4:
        for k, part in enumerate(parts):
            emit(k, shared_sum(to_bfloat16(lax.psum(part.astype(jnp.float32), "section"))))
        return
    index = lax.axis_index("section")
    inner = (index == 1) | (index == 2)

    def outer_swap(value):
        return lax.ppermute(value, "section", [(0, 1), (1, 0), (2, 3), (3, 2)])

    def middle_swap(value):
        return lax.ppermute(value, "section", [(1, 2), (2, 1), (0, 0), (3, 3)])

    arriving = {k: outer_swap(parts[k]) for k in range(min(LAG, count))}
    halves, others, totals, shares = {}, {}, {}, {}
    for k in range(count + LAG + SHARE_LAG):
        waited = {}
        if k in arriving:
            waited["got"] = arriving[k]
        if k - 1 in others:
            waited["other"] = others[k - 1]
        if k - LAG - SHARE_LAG in shares:
            waited["share"] = shares[k - LAG - SHARE_LAG]
        waited = lax.optimization_barrier(waited)
        if k < count:
            halves[k] = add(parts[k], waited["got"])
            others[k] = middle_swap(halves[k])
        if "other" in waited:
            totals[k - 1] = add(halves[k - 1], waited["other"])
        following = k - 1 + LAG
        if LAG <= following < count + LAG:
            value = totals[following - LAG]
            if following < count:
                value = jnp.where(inner, value, parts[following])
            arriving[following] = outer_swap(value)
        if LAG <= k < count + LAG:
            shares[k - LAG] = shared_sum(jnp.where(inner, totals[k - LAG], waited["got"]))
        if "share" in waited:
            emit(k - LAG - SHARE_LAG, waited["share"])


def prepare(n_dp, block_len, send_width, lengths, order, hidden, gain, head, rows, squares, rest, *pieces):
    block_count = lengths.shape[0]
    dp = lax.axis_index("dp")
    own_width = rows.shape[1] // n_dp
    per_owner = own_width // send_width
    for j in range(n_dp):
        for e in range(n_dp):

            @pl.when((dp ^ j) == e)
            def _(j=j, e=e):
                for i in range(per_owner):
                    start = e * own_width + i * send_width
                    pieces[j * per_owner + i][...] = rows[:, start : start + send_width]

    lane = lax.broadcasted_iota(jnp.int32, (block_len, block_len), 1)
    diagonal = lane == lax.broadcasted_iota(jnp.int32, (block_len, block_len), 0)
    position = lax.broadcasted_iota(jnp.int32, (1, block_len), 1)
    values = hidden[...].astype(jnp.float32)
    coefficient = (gain[...].astype(jnp.float32) * head[...].astype(jnp.float32)).reshape(1, -1)
    inverse = lax.rsqrt(jnp.mean(values * values, axis=1, keepdims=True) + EPSILON)
    scores = jnp.sum(values * coefficient, axis=1, keepdims=True) * inverse
    for b in range(block_count):
        total = jnp.zeros((block_len, 128), jnp.float32)
        for start in range(0, rows.shape[1], 128):
            value = rows[b * block_len : (b + 1) * block_len, start : start + 128]
            value = value.astype(jnp.float32)
            total = total + value * value
        total = jnp.sum(total, axis=1, keepdims=True)
        squares[b : b + 1, :] = jnp.sum(jnp.where(diagonal, total, 0.0), axis=0, keepdims=True)
        weight = jnp.where(position < lengths[b], scores[b : b + 1], 0.0)
        rest[b : b + 1, :] = weight
        rest[block_count + b : block_count + b + 1, :] = jnp.full(
            (1, block_len), order[0, b].astype(jnp.float32)
        )


def body(
    lengths,
    final_hidden,
    score_gain,
    score_head,
    policy_input,
    block_order,
    norm_gain,
    key_weight,
    key_cotangent,
):
    n_section, n_dp, n_mp = (lax.axis_size(name) for name in ("section", "dp", "mp"))
    dp, mp = lax.axis_index("dp"), lax.axis_index("mp")
    block_count = lengths.shape[0]
    tokens, local_width = policy_input.shape
    block_len = tokens // block_count
    pair = block_count // n_dp
    columns = key_cotangent.shape[1]
    own_width = local_width // n_dp
    chunk = min(CHUNK_ROWS, own_width)
    feature_blocks = own_width // chunk
    n_far = n_mp // 2
    far, core = mp >> 1, mp & 1
    order = block_order[0]
    gain = norm_gain.astype(jnp.float32)

    cotangents = [key_cotangent] + [swap(key_cotangent, "dp", j) for j in range(1, n_dp)]
    cotangents = jnp.concatenate(cotangents, axis=0)

    send_width = min(2 * chunk, own_width)
    per_owner = own_width // send_width
    vmem, smem = pl.BlockSpec(memory_space=pltpu.VMEM), pl.BlockSpec(memory_space=pltpu.SMEM)
    squares, rest, *pieces = pl.pallas_call(
        functools.partial(prepare, n_dp, block_len, send_width),
        out_shape=[
            jax.ShapeDtypeStruct((block_count, block_len), jnp.float32),
            jax.ShapeDtypeStruct((2 * block_count, block_len), jnp.float32),
        ]
        + [jax.ShapeDtypeStruct((tokens, send_width), jnp.bfloat16)] * (n_dp * per_owner),
        in_specs=[smem, smem, vmem, vmem, vmem, vmem],
        out_specs=[vmem] * (2 + n_dp * per_owner),
        compiler_params=pltpu.CompilerParams(vmem_limit_bytes=32 * 2**20),
        name="prepare",
    )(lengths, block_order, final_hidden, score_gain, score_head, policy_input)
    squares = squares + sum(swap(squares, "mp", j) for j in range(1, n_mp))
    inverse = lax.rsqrt(squares / (local_width * n_mp) + EPSILON)
    small = jnp.concatenate([inverse, rest], axis=0)
    small = [small] + [swap(small, "dp", j) for j in range(1, n_dp)]
    rows = []
    for i in range(per_owner):
        got = [pieces[i]]
        for j in range(1, n_dp):
            piece = pieces[j * per_owner + i]
            if i:
                piece, _ = lax.optimization_barrier((piece, small[0]))
            got.append(swap(piece, "dp", j))
        got = jnp.concatenate(got, axis=0)
        rows += [got[:, c : c + chunk] for c in range(0, send_width, chunk)]

    def key_gradient(near):
        other = swap(near, "mp", 1)
        low = core == 0
        cotangent = jnp.concatenate(
            [jnp.where(low, near, other), jnp.where(low, other, near)], axis=1
        ).reshape(n_dp, n_dp, pair, block_len, -1)
        found = []
        for j in range(n_dp):
            sender = dp ^ j
            for b in range(block_count):
                slot = small[j][2 * block_count + b][:, None]
                chosen = None
                for e in range(n_dp):
                    for q in range(pair):
                        value = lax.dynamic_index_in_dim(cotangent[e], sender, 0, keepdims=False)[q]
                        at = ((dp ^ e) * pair + q).astype(jnp.float32)
                        chosen = value if chosen is None else jnp.where(slot == at, value, chosen)
                weight = small[j][block_count + b].astype(jnp.bfloat16).astype(jnp.float32)
                key_grad = to_bfloat16(chosen.astype(jnp.float32) * weight[:, None])
                found.append(
                    (key_grad.astype(jnp.float32) * small[j][b][:, None]).astype(jnp.bfloat16)
                )
        return jnp.concatenate(found, axis=0)

    parts = []
    for g in range(n_far):
        near = cotangents
        if g:
            near, _ = lax.optimization_barrier((near, parts[0]))
            near = swap(near, "mp", 2 * g)
        key_grad = key_gradient(near)
        for f in range(feature_blocks):
            part = lax.dot_general(
                rows[f],
                key_grad,
                (((0,), (0,)), ((), ())),
                preferred_element_type=jnp.float32,
            )
            parts.append(to_bfloat16(part))
    shards = n_section * n_dp
    shared = {}
    out = [jnp.zeros((local_width, n_mp * columns), jnp.float32)]
    grad_gain = [None] * (n_dp * feature_blocks)

    def shared_sum(total):
        return [total] + [swap(total, "dp", j) for j in range(1, n_dp)]

    def emit(k, values):
        shared[k] = values
        f = k % feature_blocks
        if k // feature_blocks < n_far - 1:
            return
        groups = [shared[g * feature_blocks + f] for g in range(n_far)]
        for e in range(n_dp):
            start = e * own_width + f * chunk
            by_group = [pick(group, dp ^ e) for group in groups]
            value = jnp.concatenate([pick(by_group, far ^ g) for g in range(n_far)], axis=1)
            value = value.astype(jnp.float32) / shards
            out[0] = lax.dynamic_update_slice(
                out[0], value * gain[start : start + chunk, None], (start, 0)
            )
            weight = key_weight[start : start + chunk].astype(jnp.float32)
            grad_gain[e * feature_blocks + f] = jnp.sum(value * weight, axis=1)

    summed(parts, shared_sum, emit)
    grad_weight = out[0]
    grad_gain = jnp.concatenate(grad_gain)

    inverse, _ = lax.optimization_barrier((inverse, shared[0]))
    normed = policy_input.astype(jnp.float32) * inverse.reshape(-1, 1) * gain[None, :]
    normed = lax.optimization_barrier(normed.astype(jnp.bfloat16))
    partial = jnp.dot(normed, key_weight, preferred_element_type=jnp.float32)
    own_columns = pick([partial[:, i * columns : (i + 1) * columns] for i in range(n_mp)], mp)
    partial = partial.astype(jnp.bfloat16)
    for j in range(1, n_mp):
        piece = pick([partial[:, i * columns : (i + 1) * columns] for i in range(n_mp)], mp ^ j)
        own_columns = own_columns + swap(piece, "mp", j).astype(jnp.float32)
    keys = own_columns.astype(jnp.bfloat16).reshape(block_count, block_len, columns)
    by_slot = []
    for slot in range(block_count):
        chosen = keys[0]
        for b in range(1, block_count):
            chosen = jnp.where(order[b] == slot, keys[b], chosen)
        by_slot.append(chosen)
    by_target = [jnp.stack(by_slot[e * pair : (e + 1) * pair]) for e in range(n_dp)]
    arrived = [pick(by_target, dp)]
    arrived += [swap(pick(by_target, dp ^ j), "dp", j) for j in range(1, n_dp)]
    learner_keys = jnp.concatenate([pick(arrived, dp ^ a) for a in range(n_dp)], axis=0)
    return learner_keys.reshape(tokens, columns), grad_weight, grad_gain


def solution(mesh):
    placed = (
        P(("section", "dp")),
        P(("section", "dp"), None),
        P(),
        P(),
        P(("section", "dp"), "mp"),
        P(("section", "dp"), None),
        P("mp"),
        P("mp", None),
        P(("section", "dp"), "mp"),
    )
    return jax.shard_map(
        body,
        mesh=mesh,
        in_specs=placed,
        out_specs=(P(("section", "dp"), "mp"), P("mp", None), P("mp")),
        check_vma=False,
    )
```

time: 257 us -> 178 us (0.69)
  waiting for transfers between devices: 77.6 us -> 25.6 us
  starting transfers between devices: 146 us -> 123 us
  other arithmetic: 15.2 us -> 7.7 us
  local copies, waits for them, and re-layouts: 6.96 us -> 11.4 us
    ppermute x35, waiting for transfers between devices: 42.7 us -> 4.51 us  [the longest x19 4.46 us: outer_swap(): return lax.ppermute(value, 'section', [(0, 1), (1, 0), (2, 3), (3, 2)])]
    ppermute x35, starting transfers between devices: 113 us -> 92.9 us  [the longest x19 81.9 us: outer_swap(): return lax.ppermute(value, 'section', [(0, 1), (1, 0), (2, 3), (3, 2)])]
    ppermute x35 -> x32, waiting for transfers between devices: 34.9 us -> 21.1 us  [swap(): lax.ppermute(value, axis, [(i, i ^ bit) for i in range(lax.axis_size(axis...]
    unnamed x23 -> x40, local copies, waits for them, and re-layouts: 3.5 us -> 9.09 us
    ppermute x35 -> x32, starting transfers between devices: 33 us -> 30.1 us  [swap(): lax.ppermute(value, axis, [(i, i ^ bit) for i in range(lax.axis_size(axis...]
  transfers between devices with their start and end apart: 70 -> 67, of which waited for: 28 -> 11; matrix products, arithmetic and copies ran while one was open for 8% -> 8% of each run, Pallas kernels for 0% -> 0%
where the time goes in v3:
time: 178 us; the launch traced here: 177 us
  starting transfers between devices  123 us (69%)
  waiting for transfers between devices  25.6 us (14%)
  local copies, waits for them, and re-layouts  11.4 us (6%)
  other arithmetic  7.7 us (4%)
  matrix products  5.37 us (3%)
  between operations  3.13 us (2%)
    ppermute x19, starting transfers between devices, outer_swap(): return lax.ppermute(value, 'section', [(0, 1), (1, 0), (2, 3), (3, 2)])  81.9 us
    ppermute x32, starting transfers between devices, swap(): lax.ppermute(value, axis, [(i, i ^ bit) for i in range(lax.axis_size(axis...  30.1 us
    ppermute x32, waiting for transfers between devices, swap(): lax.ppermute(value, axis, [(i, i ^ bit) for i in range(lax.axis_size(axis...  21.1 us
    ppermute x16, starting transfers between devices, middle_swap(): return lax.ppermute(value, 'section', [(1, 2), (2, 1), (0, 0), (3, 3)])  11 us
    unnamed x40, local copies, waits for them, and re-layouts  9.09 us
    ppermute x19, waiting for transfers between devices, outer_swap(): return lax.ppermute(value, 'section', [(0, 1), (1, 0), (2, 3), (3, 2)])  4.46 us
    dot_general x16, matrix products, body(): lax.dot_general(rows[f], key_grad, (((0,), (0,)), ((), ())), preferred_el...  4.1 us
  transfers between devices with their start and end apart: 67, of which 11 were waited for; matrix products, arithmetic and copies ran while one was open for 8% of the time, Pallas kernels for 0%

profile of v3, /device:TPU:0, one launch (start us, length us, event | category | flops | bytes accessed | tf_op | source)
XLA Modules:
  0.0 177.1 jit_solution(18077577580811910926)
XLA Ops:
  6.3 2.4 %collective-permute-start.2 = (f32[2,128]{1,0:T(2,128)S(1)}, f32[2,128]{1,0:T(2,128)S(1)}, u32[]{:S(2)}, u32[]{:S(2)}) collective-permute-start(f32[2,128]{1,0:T(2,128)S(1)} %get-tuple-element.84), channel_id=1, source_target_pairs={{0,3},{1,2},{2,1},{3,0},{4,7},{5,6},{6,5},{7,4},{8,11},{9,10},{10,... | collective-permute-start | bytes 3080 | tf_op jit(solution)/shard_map/ppermute | solution.py:17
  21.4 2.6 %collective-permute-done.3 = bf16[256,256]{1,0:T(8,128)(2,1)S(1)} collective-permute-done((bf16[256,256]{1,0:T(8,128)(2,1)S(1)}, bf16[256,256]{1,0:T(8,128)(2,1)S(1)}, u32[]{:S(2)}, u32[]{:S(2)}) %collective-permute-start.3) | collective-permute-done | bytes 131104 | tf_op jit(solution)/shard_map/ppermute | solution.py:17
  24.0 2.6 %collective-permute-done.15 = bf16[256,256]{1,0:T(8,128)(2,1)S(1)} collective-permute-done((bf16[256,256]{1,0:T(8,128)(2,1)S(1)}, bf16[256,256]{1,0:T(8,128)(2,1)S(1)}, u32[]{:S(2)}, u32[]{:S(2)}) %collective-permute-start.15) | collective-permute-done | bytes 131104 | tf_op jit(solution)/shard_map/ppermute | solution.py:17
  31.1 3.2 %collective-permute-done.10 = bf16[128,512]{1,0:T(8,128)(2,1)S(1)} collective-permute-done((bf16[128,512]{1,0:T(8,128)(2,1)S(1)}, bf16[128,512]{1,0:T(8,128)(2,1)S(1)}, u32[]{:S(2)}, u32[]{:S(2)}) %collective-permute-start.10) | collective-permute-done | bytes 131104 | tf_op jit(solution)/shard_map/ppermute | solution.py:45
  35.3 4.5 %collective-permute-start.7 = (bf16[128,512]{1,0:T(8,128)(2,1)S(1)}, bf16[128,512]{1,0:T(8,128)(2,1)S(1)}, u32[]{:S(2)}, u32[]{:S(2)}) collective-permute-start(bf16[128,512]{1,0:T(8,128)(2,1)S(1)} %fusion), channel_id=1, source_target_pairs={{0,8},{8,0},{16,24},{24,16},{1,9},{9,1},{17,25},{25,17},{2,10},{10... | collective-permute-start | bytes 393224 | tf_op jit(solution)/shard_map/ppermute | solution.py:45
  42.0 4.7 %collective-permute-start.13 = (bf16[128,512]{1,0:T(8,128)(2,1)S(1)}, bf16[128,512]{1,0:T(8,128)(2,1)S(1)}, u32[]{:S(2)}, u32[]{:S(2)}) collective-permute-start(bf16[128,512]{1,0:T(8,128)(2,1)S(1)} %get-tuple-element.265), channel_id=1, source_target_pairs={{0,8},{8,0},{16,24},{24,16},{1,9},{9,1},{17,25},{25,17},{2,10},{10... | collective-permute-start | bytes 393224 | tf_op jit(solution)/shard_map/ppermute | solution.py:45
  47.8 6.0 %collective-permute-start.17 = (bf16[128,512]{1,0:T(8,128)(2,1)S(1)}, bf16[128,512]{1,0:T(8,128)(2,1)S(1)}, u32[]{:S(2)}, u32[]{:S(2)}) collective-permute-start(bf16[128,512]{1,0:T(8,128)(2,1)S(1)} %get-tuple-element.269), channel_id=1, source_target_pairs={{0,8},{8,0},{16,24},{24,16},{1,9},{9,1},{17,25},{25,17},{2,10},{10... | collective-permute-start | bytes 393224 | tf_op jit(solution)/shard_map/ppermute | solution.py:45
  55.5 6.2 %collective-permute-start.16 = (bf16[128,512]{1,0:T(8,128)(2,1)S(1)}, bf16[128,512]{1,0:T(8,128)(2,1)S(1)}, u32[]{:S(2)}, u32[]{:S(2)}) collective-permute-start(bf16[128,512]{1,0:T(8,128)(2,1)S(1)} %get-tuple-element.267), channel_id=1, source_target_pairs={{0,8},{8,0},{16,24},{24,16},{1,9},{9,1},{17,25},{25,17},{2,10},{10... | collective-permute-start | bytes 393224 | tf_op jit(solution)/shard_map/ppermute | solution.py:45
  64.6 5.4 %collective-permute-start.29 = (bf16[128,512]{1,0:T(8,128)(2,1)S(1)}, bf16[128,512]{1,0:T(8,128)(2,1)S(1)}, u32[]{:S(2)}, u32[]{:S(2)}) collective-permute-start(bf16[128,512]{1,0:T(8,128)(2,1)S(1)} %get-tuple-element.273), channel_id=1, source_target_pairs={{0,8},{8,0},{16,24},{24,16},{1,9},{9,1},{17,25},{25,17},{2,10},{10... | collective-permute-start | bytes 393224 | tf_op jit(solution)/shard_map/ppermute | solution.py:45
  70.4 3.2 %collective-permute-start.28 = (bf16[128,512]{1,0:T(8,128)(2,1)S(1)}, bf16[128,512]{1,0:T(8,128)(2,1)S(1)}, u32[]{:S(2)}, u32[]{:S(2)}) collective-permute-start(bf16[128,512]{1,0:T(8,128)(2,1)S(1)} %get-tuple-element.277), channel_id=1, source_target_pairs={{0,8},{8,0},{16,24},{24,16},{1,9},{9,1},{17,25},{25,17},{2,10},{10... | collective-permute-start | bytes 393224 | tf_op jit(solution)/shard_map/ppermute | solution.py:45
  79.3 3.7 %collective-permute-done.22 = bf16[256,256]{1,0:T(8,128)(2,1)S(1)} collective-permute-done((bf16[256,256]{1,0:T(8,128)(2,1)S(1)}, bf16[256,256]{1,0:T(8,128)(2,1)S(1)}, u32[]{:S(2)}, u32[]{:S(2)}) %collective-permute-start.22) | collective-permute-done | bytes 131104 | tf_op jit(solution)/shard_map/ppermute | solution.py:17
  86.9 2.5 %collective-permute-done.24 = bf16[1,128,256]{2,1,0:T(8,128)(2,1)S(1)} collective-permute-done((bf16[1,128,256]{2,1,0:T(8,128)(2,1)S(1)}, bf16[1,128,256]{2,1,0:T(8,128)(2,1)S(1)}, u32[]{:S(2)}, u32[]{:S(2)}) %collective-permute-start.24) | collective-permute-done | bytes 65568 | tf_op jit(solution)/shard_map/ppermute | solution.py:17
  89.4 3.3 %collective-permute-start.34 = (bf16[128,512]{1,0:T(8,128)(2,1)S(1)}, bf16[128,512]{1,0:T(8,128)(2,1)S(1)}, u32[]{:S(2)}, u32[]{:S(2)}) collective-permute-start(bf16[128,512]{1,0:T(8,128)(2,1)S(1)} %get-tuple-element.275), channel_id=1, source_target_pairs={{0,8},{8,0},{16,24},{24,16},{1,9},{9,1},{17,25},{25,17},{2,10},{10... | collective-permute-start | bytes 393224 | tf_op jit(solution)/shard_map/ppermute | solution.py:45
  99.4 5.4 %collective-permute-start.37 = (bf16[128,512]{1,0:T(8,128)(2,1)S(1)}, bf16[128,512]{1,0:T(8,128)(2,1)S(1)}, u32[]{:S(2)}, u32[]{:S(2)}) collective-permute-start(bf16[128,512]{1,0:T(8,128)(2,1)S(1)} %get-tuple-element.279), channel_id=1, source_target_pairs={{0,8},{8,0},{16,24},{24,16},{1,9},{9,1},{17,25},{25,17},{2,10},{10... | collective-permute-start | bytes 393224 | tf_op jit(solution)/shard_map/ppermute | solution.py:45
  106.5 5.3 %collective-permute-start.43 = (bf16[128,512]{1,0:T(8,128)(2,1)S(1)}, bf16[128,512]{1,0:T(8,128)(2,1)S(1)}, u32[]{:S(2)}, u32[]{:S(2)}) collective-permute-start(bf16[128,512]{1,0:T(8,128)(2,1)S(1)} %get-tuple-element.285), channel_id=1, source_target_pairs={{0,8},{8,0},{16,24},{24,16},{1,9},{9,1},{17,25},{25,17},{2,10},{10... | collective-permute-start | bytes 393224 | tf_op jit(solution)/shard_map/ppermute | solution.py:45
  113.4 5.3 %collective-permute-start.47 = (bf16[128,512]{1,0:T(8,128)(2,1)S(1)}, bf16[128,512]{1,0:T(8,128)(2,1)S(1)}, u32[]{:S(2)}, u32[]{:S(2)}) collective-permute-start(bf16[128,512]{1,0:T(8,128)(2,1)S(1)} %get-tuple-element.283), channel_id=1, source_target_pairs={{0,8},{8,0},{16,24},{24,16},{1,9},{9,1},{17,25},{25,17},{2,10},{10... | collective-permute-start | bytes 393224 | tf_op jit(solution)/shard_map/ppermute | solution.py:45
  120.4 5.3 %collective-permute-start.46 = (bf16[128,512]{1,0:T(8,128)(2,1)S(1)}, bf16[128,512]{1,0:T(8,128)(2,1)S(1)}, u32[]{:S(2)}, u32[]{:S(2)}) collective-permute-start(bf16[128,512]{1,0:T(8,128)(2,1)S(1)} %get-tuple-element.289), channel_id=1, source_target_pairs={{0,8},{8,0},{16,24},{24,16},{1,9},{9,1},{17,25},{25,17},{2,10},{10... | collective-permute-start | bytes 393224 | tf_op jit(solution)/shard_map/ppermute | solution.py:45
  127.3 6.1 %collective-permute-start.52 = (bf16[128,512]{1,0:T(8,128)(2,1)S(1)}, bf16[128,512]{1,0:T(8,128)(2,1)S(1)}, u32[]{:S(2)}, u32[]{:S(2)}) collective-permute-start(bf16[128,512]{1,0:T(8,128)(2,1)S(1)} %get-tuple-element.287), channel_id=1, source_target_pairs={{0,8},{8,0},{16,24},{24,16},{1,9},{9,1},{17,25},{25,17},{2,10},{10... | collective-permute-start | bytes 393224 | tf_op jit(solution)/shard_map/ppermute | solution.py:45
  134.9 6.7 %collective-permute-start.55 = (bf16[128,512]{1,0:T(8,128)(2,1)S(1)}, bf16[128,512]{1,0:T(8,128)(2,1)S(1)}, u32[]{:S(2)}, u32[]{:S(2)}) collective-permute-start(bf16[128,512]{1,0:T(8,128)(2,1)S(1)} %get-tuple-element.291), channel_id=1, source_target_pairs={{0,8},{8,0},{16,24},{24,16},{1,9},{9,1},{17,25},{25,17},{2,10},{10... | collective-permute-start | bytes 393224 | tf_op jit(solution)/shard_map/ppermute | solution.py:45
  141.8 3.1 %collective-permute-start.58 = (bf16[128,512]{1,0:T(8,128)(2,1)S(1)}, bf16[128,512]{1,0:T(8,128)(2,1)S(1)}, u32[]{:S(2)}, u32[]{:S(2)}) collective-permute-start(bf16[128,512]{1,0:T(8,128)(2,1)S(1)} %reduce-precision_convert_fusion.3), channel_id=1, source_target_pairs={{0,8},{8,0},{16,24},{24,16},{1,9},{9,1},{17,25},{25,17},{2,10},{10... | collective-permute-start | bytes 393224 | tf_op jit(solution)/shard_map/ppermute | solution.py:45
  147.2 4.8 %collective-permute-start.61 = (bf16[128,512]{1,0:T(8,128)(2,1)S(1)}, bf16[128,512]{1,0:T(8,128)(2,1)S(1)}, u32[]{:S(2)}, u32[]{:S(2)}) collective-permute-start(bf16[128,512]{1,0:T(8,128)(2,1)S(1)} %reduce-precision_convert_fusion.1), channel_id=1, source_target_pairs={{0,8},{8,0},{16,24},{24,16},{1,9},{9,1},{17,25},{25,17},{2,10},{10... | collective-permute-start | bytes 393224 | tf_op jit(solution)/shard_map/ppermute | solution.py:45
  159.4 2.7 %collective-permute-start.63 = (bf16[128,512]{1,0:T(8,128)(2,1)S(1)}, bf16[128,512]{1,0:T(8,128)(2,1)S(1)}, u32[]{:S(2)}, u32[]{:S(2)}) collective-permute-start(bf16[128,512]{1,0:T(8,128)(2,1)S(1)} %reduce-precision_convert_fusion), channel_id=1, source_target_pairs={{0,8},{8,0},{16,24},{24,16},{1,9},{9,1},{17,25},{25,17},{2,10},{10... | collective-permute-start | bytes 393224 | tf_op jit(solution)/shard_map/ppermute | solution.py:45
  168.4 3.7 %collective-permute-done.66 = bf16[128,512]{1,0:T(8,128)(2,1)S(1)} collective-permute-done((bf16[128,512]{1,0:T(8,128)(2,1)S(1)}, bf16[128,512]{1,0:T(8,128)(2,1)S(1)}, u32[]{:S(2)}, u32[]{:S(2)}) %collective-permute-start.66) | collective-permute-done | bytes 131104 | tf_op jit(solution)/shard_map/ppermute | solution.py:17
  174.1 3.0 %copy-done.7 = f32[2048,1024]{1,0:T(8,128)} copy-done((f32[2048,1024]{1,0:T(8,128)}, f32[2048,1024]{1,0:T(8,128)S(1)}, u32[]{:S(2)}) %copy-start.7) | copy-done | bytes 8388632
  (263 shorter events, 72.2 us)
Async XLA Ops:
  46.7 15.0 %collective-permute-start.26 = (bf16[512,256]{1,0:T(8,128)(2,1)S(1)}, bf16[512,256]{1,0:T(8,128)(2,1)S(1)}, u32[]{:S(2)}, u32[]{:S(2)}) collective-permute-start(bf16[512,256]{1,0:T(8,128)(2,1)S(1)} %collective-permute-done.25), channel_id=1, source_target_pairs={{0,1},{1,0},{2,3},{3,2},{4,5},{5,4},{6,7},{7,6},{8,9},{9,8},{10,11... | collective-permute-start | bytes 786440 | tf_op jit(solution)/shard_map/ppermute | solution.py:17
  47.8 14.2 %collective-permute-start.17 = (bf16[128,512]{1,0:T(8,128)(2,1)S(1)}, bf16[128,512]{1,0:T(8,128)(2,1)S(1)}, u32[]{:S(2)}, u32[]{:S(2)}) collective-permute-start(bf16[128,512]{1,0:T(8,128)(2,1)S(1)} %get-tuple-element.269), channel_id=1, source_target_pairs={{0,8},{8,0},{16,24},{24,16},{1,9},{9,1},{17,25},{25,17},{2,10},{10... | collective-permute-start | bytes 393224 | tf_op jit(solution)/shard_map/ppermute | solution.py:45
  54.6 15.4 %collective-permute-start.20 = (bf16[128,512]{1,0:T(8,128)(2,1)S(1)}, bf16[128,512]{1,0:T(8,128)(2,1)S(1)}, u32[]{:S(2)}, u32[]{:S(2)}) collective-permute-start(bf16[128,512]{1,0:T(8,128)(2,1)S(1)} %broadcast_select_fusion.93), channel_id=1, source_target_pairs={{0,4},{4,0},{1,5},{5,1},{2,6},{6,2},{3,7},{7,3},{8,12},{12,8},{9,1... | collective-permute-start | bytes 393224 | tf_op jit(solution)/shard_map/ppermute | solution.py:17
  55.5 14.5 %collective-permute-start.16 = (bf16[128,512]{1,0:T(8,128)(2,1)S(1)}, bf16[128,512]{1,0:T(8,128)(2,1)S(1)}, u32[]{:S(2)}, u32[]{:S(2)}) collective-permute-start(bf16[128,512]{1,0:T(8,128)(2,1)S(1)} %get-tuple-element.267), channel_id=1, source_target_pairs={{0,8},{8,0},{16,24},{24,16},{1,9},{9,1},{17,25},{25,17},{2,10},{10... | collective-permute-start | bytes 393224 | tf_op jit(solution)/shard_map/ppermute | solution.py:45
  62.8 13.8 %collective-permute-start.31 = (bf16[128,512]{1,0:T(8,128)(2,1)S(1)}, bf16[128,512]{1,0:T(8,128)(2,1)S(1)}, u32[]{:S(2)}, u32[]{:S(2)}) collective-permute-start(bf16[128,512]{1,0:T(8,128)(2,1)S(1)} %broadcast_select_fusion.90), channel_id=1, source_target_pairs={{0,4},{4,0},{1,5},{5,1},{2,6},{6,2},{3,7},{7,3},{8,12},{12,8},{9,1... | collective-permute-start | bytes 393224 | tf_op jit(solution)/shard_map/ppermute | solution.py:17
  64.6 12.0 %collective-permute-start.29 = (bf16[128,512]{1,0:T(8,128)(2,1)S(1)}, bf16[128,512]{1,0:T(8,128)(2,1)S(1)}, u32[]{:S(2)}, u32[]{:S(2)}) collective-permute-start(bf16[128,512]{1,0:T(8,128)(2,1)S(1)} %get-tuple-element.273), channel_id=1, source_target_pairs={{0,8},{8,0},{16,24},{24,16},{1,9},{9,1},{17,25},{25,17},{2,10},{10... | collective-permute-start | bytes 393224 | tf_op jit(solution)/shard_map/ppermute | solution.py:45
  70.4 23.0 %collective-permute-start.28 = (bf16[128,512]{1,0:T(8,128)(2,1)S(1)}, bf16[128,512]{1,0:T(8,128)(2,1)S(1)}, u32[]{:S(2)}, u32[]{:S(2)}) collective-permute-start(bf16[128,512]{1,0:T(8,128)(2,1)S(1)} %get-tuple-element.277), channel_id=1, source_target_pairs={{0,8},{8,0},{16,24},{24,16},{1,9},{9,1},{17,25},{25,17},{2,10},{10... | collective-permute-start | bytes 393224 | tf_op jit(solution)/shard_map/ppermute | solution.py:45
  74.3 19.1 %collective-permute-start.33 = (bf16[128,512]{1,0:T(8,128)(2,1)S(1)}, bf16[128,512]{1,0:T(8,128)(2,1)S(1)}, u32[]{:S(2)}, u32[]{:S(2)}) collective-permute-start(bf16[128,512]{1,0:T(8,128)(2,1)S(1)} %broadcast_select_fusion.89), channel_id=1, source_target_pairs={{0,4},{4,0},{1,5},{5,1},{2,6},{6,2},{3,7},{7,3},{8,12},{12,8},{9,1... | collective-permute-start | bytes 393224 | tf_op jit(solution)/shard_map/ppermute | solution.py:17
  78.6 14.8 %collective-permute-start.32 = (bf16[128,512]{1,0:T(8,128)(2,1)S(1)}, bf16[128,512]{1,0:T(8,128)(2,1)S(1)}, u32[]{:S(2)}, u32[]{:S(2)}) collective-permute-start(bf16[128,512]{1,0:T(8,128)(2,1)S(1)} %reduce-precision_convert_fusion.20), channel_id=1, source_target_pairs={{8,16},{16,8},{0,0},{24,24},{9,17},{17,9},{1,1},{25,25},{10,18},{1... | collective-permute-start | bytes 393224 | tf_op jit(solution)/shard_map/ppermute | solution.py:48
  83.0 14.8 %collective-permute-start.36 = (bf16[128,512]{1,0:T(8,128)(2,1)S(1)}, bf16[128,512]{1,0:T(8,128)(2,1)S(1)}, u32[]{:S(2)}, u32[]{:S(2)}) collective-permute-start(bf16[128,512]{1,0:T(8,128)(2,1)S(1)} %broadcast_select_fusion.87), channel_id=1, source_target_pairs={{0,4},{4,0},{1,5},{5,1},{2,6},{6,2},{3,7},{7,3},{8,12},{12,8},{9,1... | collective-permute-start | bytes 393224 | tf_op jit(solution)/shard_map/ppermute | solution.py:17
  98.6 13.2 %collective-permute-start.42 = (bf16[128,512]{1,0:T(8,128)(2,1)S(1)}, bf16[128,512]{1,0:T(8,128)(2,1)S(1)}, u32[]{:S(2)}, u32[]{:S(2)}) collective-permute-start(bf16[128,512]{1,0:T(8,128)(2,1)S(1)} %broadcast_select_fusion.83), channel_id=1, source_target_pairs={{0,4},{4,0},{1,5},{5,1},{2,6},{6,2},{3,7},{7,3},{8,12},{12,8},{9,1... | collective-permute-start | bytes 393224 | tf_op jit(solution)/shard_map/ppermute | solution.py:17
  99.4 12.4 %collective-permute-start.37 = (bf16[128,512]{1,0:T(8,128)(2,1)S(1)}, bf16[128,512]{1,0:T(8,128)(2,1)S(1)}, u32[]{:S(2)}, u32[]{:S(2)}) collective-permute-start(bf16[128,512]{1,0:T(8,128)(2,1)S(1)} %get-tuple-element.279), channel_id=1, source_target_pairs={{0,8},{8,0},{16,24},{24,16},{1,9},{9,1},{17,25},{25,17},{2,10},{10... | collective-permute-start | bytes 393224 | tf_op jit(solution)/shard_map/ppermute | solution.py:45
  105.6 13.1 %collective-permute-start.45 = (bf16[128,512]{1,0:T(8,128)(2,1)S(1)}, bf16[128,512]{1,0:T(8,128)(2,1)S(1)}, u32[]{:S(2)}, u32[]{:S(2)}) collective-permute-start(bf16[128,512]{1,0:T(8,128)(2,1)S(1)} %broadcast_select_fusion.81), channel_id=1, source_target_pairs={{0,4},{4,0},{1,5},{5,1},{2,6},{6,2},{3,7},{7,3},{8,12},{12,8},{9,1... | collective-permute-start | bytes 393224 | tf_op jit(solution)/shard_map/ppermute | solution.py:17
  106.5 12.3 %collective-permute-start.43 = (bf16[128,512]{1,0:T(8,128)(2,1)S(1)}, bf16[128,512]{1,0:T(8,128)(2,1)S(1)}, u32[]{:S(2)}, u32[]{:S(2)}) collective-permute-start(bf16[128,512]{1,0:T(8,128)(2,1)S(1)} %get-tuple-element.285), channel_id=1, source_target_pairs={{0,8},{8,0},{16,24},{24,16},{1,9},{9,1},{17,25},{25,17},{2,10},{10... | collective-permute-start | bytes 393224 | tf_op jit(solution)/shard_map/ppermute | solution.py:45
  112.6 13.1 %collective-permute-start.49 = (bf16[128,512]{1,0:T(8,128)(2,1)S(1)}, bf16[128,512]{1,0:T(8,128)(2,1)S(1)}, u32[]{:S(2)}, u32[]{:S(2)}) collective-permute-start(bf16[128,512]{1,0:T(8,128)(2,1)S(1)} %broadcast_select_fusion.78), channel_id=1, source_target_pairs={{0,4},{4,0},{1,5},{5,1},{2,6},{6,2},{3,7},{7,3},{8,12},{12,8},{9,1... | collective-permute-start | bytes 393224 | tf_op jit(solution)/shard_map/ppermute | solution.py:17
  113.4 12.3 %collective-permute-start.47 = (bf16[128,512]{1,0:T(8,128)(2,1)S(1)}, bf16[128,512]{1,0:T(8,128)(2,1)S(1)}, u32[]{:S(2)}, u32[]{:S(2)}) collective-permute-start(bf16[128,512]{1,0:T(8,128)(2,1)S(1)} %get-tuple-element.283), channel_id=1, source_target_pairs={{0,8},{8,0},{16,24},{24,16},{1,9},{9,1},{17,25},{25,17},{2,10},{10... | collective-permute-start | bytes 393224 | tf_op jit(solution)/shard_map/ppermute | solution.py:45
  119.5 13.9 %collective-permute-start.51 = (bf16[128,512]{1,0:T(8,128)(2,1)S(1)}, bf16[128,512]{1,0:T(8,128)(2,1)S(1)}, u32[]{:S(2)}, u32[]{:S(2)}) collective-permute-start(bf16[128,512]{1,0:T(8,128)(2,1)S(1)} %broadcast_select_fusion.77), channel_id=1, source_target_pairs={{0,4},{4,0},{1,5},{5,1},{2,6},{6,2},{3,7},{7,3},{8,12},{12,8},{9,1... | collective-permute-start | bytes 393224 | tf_op jit(solution)/shard_map/ppermute | solution.py:17
  120.4 13.1 %collective-permute-start.46 = (bf16[128,512]{1,0:T(8,128)(2,1)S(1)}, bf16[128,512]{1,0:T(8,128)(2,1)S(1)}, u32[]{:S(2)}, u32[]{:S(2)}) collective-permute-start(bf16[128,512]{1,0:T(8,128)(2,1)S(1)} %get-tuple-element.289), channel_id=1, source_target_pairs={{0,8},{8,0},{16,24},{24,16},{1,9},{9,1},{17,25},{25,17},{2,10},{10... | collective-permute-start | bytes 393224 | tf_op jit(solution)/shard_map/ppermute | solution.py:45
  126.5 15.1 %collective-permute-start.54 = (bf16[128,512]{1,0:T(8,128)(2,1)S(1)}, bf16[128,512]{1,0:T(8,128)(2,1)S(1)}, u32[]{:S(2)}, u32[]{:S(2)}) collective-permute-start(bf16[128,512]{1,0:T(8,128)(2,1)S(1)} %broadcast_select_fusion.75), channel_id=1, source_target_pairs={{0,4},{4,0},{1,5},{5,1},{2,6},{6,2},{3,7},{7,3},{8,12},{12,8},{9,1... | collective-permute-start | bytes 393224 | tf_op jit(solution)/shard_map/ppermute | solution.py:17
  127.3 14.3 %collective-permute-start.52 = (bf16[128,512]{1,0:T(8,128)(2,1)S(1)}, bf16[128,512]{1,0:T(8,128)(2,1)S(1)}, u32[]{:S(2)}, u32[]{:S(2)}) collective-permute-start(bf16[128,512]{1,0:T(8,128)(2,1)S(1)} %get-tuple-element.287), channel_id=1, source_target_pairs={{0,8},{8,0},{16,24},{24,16},{1,9},{9,1},{17,25},{25,17},{2,10},{10... | collective-permute-start | bytes 393224 | tf_op jit(solution)/shard_map/ppermute | solution.py:45
  134.3 12.8 %collective-permute-start.57 = (bf16[128,512]{1,0:T(8,128)(2,1)S(1)}, bf16[128,512]{1,0:T(8,128)(2,1)S(1)}, u32[]{:S(2)}, u32[]{:S(2)}) collective-permute-start(bf16[128,512]{1,0:T(8,128)(2,1)S(1)} %broadcast_select_fusion.73), channel_id=1, source_target_pairs={{0,4},{4,0},{1,5},{5,1},{2,6},{6,2},{3,7},{7,3},{8,12},{12,8},{9,1... | collective-permute-start | bytes 393224 | tf_op jit(solution)/shard_map/ppermute | solution.py:17
  134.9 12.2 %collective-permute-start.55 = (bf16[128,512]{1,0:T(8,128)(2,1)S(1)}, bf16[128,512]{1,0:T(8,128)(2,1)S(1)}, u32[]{:S(2)}, u32[]{:S(2)}) collective-permute-start(bf16[128,512]{1,0:T(8,128)(2,1)S(1)} %get-tuple-element.291), channel_id=1, source_target_pairs={{0,8},{8,0},{16,24},{24,16},{1,9},{9,1},{17,25},{25,17},{2,10},{10... | collective-permute-start | bytes 393224 | tf_op jit(solution)/shard_map/ppermute | solution.py:45
  141.8 17.5 %collective-permute-start.58 = (bf16[128,512]{1,0:T(8,128)(2,1)S(1)}, bf16[128,512]{1,0:T(8,128)(2,1)S(1)}, u32[]{:S(2)}, u32[]{:S(2)}) collective-permute-start(bf16[128,512]{1,0:T(8,128)(2,1)S(1)} %reduce-precision_convert_fusion.3), channel_id=1, source_target_pairs={{0,8},{8,0},{16,24},{24,16},{1,9},{9,1},{17,25},{25,17},{2,10},{10... | collective-permute-start | bytes 393224 | tf_op jit(solution)/shard_map/ppermute | solution.py:45
  145.6 13.7 %collective-permute-start.60 = (bf16[128,512]{1,0:T(8,128)(2,1)S(1)}, bf16[128,512]{1,0:T(8,128)(2,1)S(1)}, u32[]{:S(2)}, u32[]{:S(2)}) collective-permute-start(bf16[128,512]{1,0:T(8,128)(2,1)S(1)} %broadcast_select_fusion.72), channel_id=1, source_target_pairs={{0,4},{4,0},{1,5},{5,1},{2,6},{6,2},{3,7},{7,3},{8,12},{12,8},{9,1... | collective-permute-start | bytes 393224 | tf_op jit(solution)/shard_map/ppermute | solution.py:17
  (53 other events, 376.3 us)

commit v4 on v3

v4 whole, which is shorter than its diff:
```python
import functools

import jax
import jax.numpy as jnp
from jax import lax
from jax.experimental import pallas as pl
from jax.experimental.pallas import tpu as pltpu
from jax.sharding import PartitionSpec as P

EPSILON = 1e-06
CHUNK_ROWS = 256
LAG = 3


def swap(value, axis, bit):
    return lax.ppermute(value, axis, [(i, i ^ bit) for i in range(lax.axis_size(axis))])


def pick(values, index):
    chosen = values[0]
    for i in range(1, len(values)):
        chosen = jnp.where(index == i, values[i], chosen)
    return chosen


def to_bfloat16(value):
    return lax.reduce_precision(value, 8, 7).astype(jnp.bfloat16)


def add(left, right):
    return to_bfloat16(left.astype(jnp.float32) + right.astype(jnp.float32))


def summed(parts, shared_sum, emit, side):
    count = len(parts)
    if lax.axis_size("section") != 4:
        for k, part in enumerate(parts):
            emit(k, shared_sum(to_bfloat16(lax.psum(part.astype(jnp.float32), "section"))))
        pending = ()
        while pending is not None:
            pending = side(pending)
        return
    index = lax.axis_index("section")
    inner = (index == 1) | (index == 2)

    def outer_swap(value):
        return lax.ppermute(value, "section", [(0, 1), (1, 0), (2, 3), (3, 2)])

    def middle_swap(value):
        return lax.ppermute(value, "section", [(1, 2), (2, 1), (0, 0), (3, 3)])

    arriving = {k: outer_swap(parts[k]) for k in range(min(LAG, count))}
    halves, others, totals, shares = {}, {}, {}, {}
    done, pending = (), ()
    for k in range(count + LAG):
        got, done = lax.optimization_barrier((arriving[k], done))
        tied = ()
        if k < count:
            halves[k] = add(parts[k], got)
            others[k] = middle_swap(halves[k])
            tied += (halves[k],)
        if k >= LAG:
            full = jnp.where(inner, totals[k - LAG], got)
            shares[k - LAG] = shared_sum(full)
            tied += (full,)
        waited = {"tied": tied, "side": pending}
        if k - 1 in others:
            waited["other"] = others[k - 1]
        if k - 1 - LAG in shares:
            waited["share"] = shares[k - 1 - LAG]
        waited = lax.optimization_barrier(waited)
        if k < count:
            halves[k] = waited["tied"][0]
        if "other" in waited:
            totals[k - 1] = add(halves[k - 1], waited["other"])
        following = k - 1 + LAG
        if LAG <= following < count + LAG:
            value = totals[following - LAG]
            if following < count:
                value = jnp.where(inner, value, parts[following])
            arriving[following] = outer_swap(value)
        done = ()
        if k >= LAG and pending is not None:
            pending = side(waited["side"])
            done += () if pending is None else pending[:1]
        if "share" in waited:
            done += (emit(k - 1 - LAG, waited["share"]),)
    emit(count - 1, shares[count - 1])
    while pending is not None:
        pending = side(pending)


def prepare(n_dp, block_len, send_width, *refs):
    sources, refs = refs[:6], refs[6:]
    n_pieces = len(refs) - 9
    squares, rest, *pieces = refs[: 2 + n_pieces]
    buffers, semaphores = refs[2 + n_pieces : -1], refs[-1]
    copies = [
        pltpu.make_async_copy(source, buffer, semaphores.at[i])
        for i, (source, buffer) in enumerate(zip(sources, buffers))
    ]
    for copy in copies:
        copy.start()
    for copy in copies:
        copy.wait()
    lengths, order, hidden, gain, head, rows = buffers
    block_count = lengths.shape[0]
    dp = lax.axis_index("dp")
    own_width = rows.shape[1] // n_dp
    per_owner = own_width // send_width
    for j in range(n_dp):
        for e in range(n_dp):

            @pl.when((dp ^ j) == e)
            def _(j=j, e=e):
                for i in range(per_owner):
                    start = e * own_width + i * send_width
                    pieces[j * per_owner + i][...] = rows[:, start : start + send_width]

    lane = lax.broadcasted_iota(jnp.int32, (block_len, block_len), 1)
    diagonal = lane == lax.broadcasted_iota(jnp.int32, (block_len, block_len), 0)
    position = lax.broadcasted_iota(jnp.int32, (1, block_len), 1)
    values = hidden[...].astype(jnp.float32)
    coefficient = (gain[...].astype(jnp.float32) * head[...].astype(jnp.float32)).reshape(1, -1)
    inverse = lax.rsqrt(jnp.mean(values * values, axis=1, keepdims=True) + EPSILON)
    scores = jnp.sum(values * coefficient, axis=1, keepdims=True) * inverse
    for b in range(block_count):
        total = jnp.zeros((block_len, 128), jnp.float32)
        for start in range(0, rows.shape[1], 128):
            value = rows[b * block_len : (b + 1) * block_len, start : start + 128]
            value = value.astype(jnp.float32)
            total = total + value * value
        total = jnp.sum(total, axis=1, keepdims=True)
        squares[b : b + 1, :] = jnp.sum(jnp.where(diagonal, total, 0.0), axis=0, keepdims=True)
        weight = jnp.where(position < lengths[b], scores[b : b + 1], 0.0)
        rest[b : b + 1, :] = weight
        rest[block_count + b : block_count + b + 1, :] = jnp.full(
            (1, block_len), order[0, b].astype(jnp.float32)
        )


def store(n_dp, g, first, shards, *refs):
    values = refs[:n_dp]
    gain, weight = refs[n_dp : n_dp + 2]
    out, sums, weights, results, semaphores = refs[-5:]
    chunk, width = values[0].shape
    dp, far = lax.axis_index("dp"), lax.axis_index("mp") >> 1
    own_width = weight.shape[0] // n_dp
    column = pl.multiple_of((far ^ g) * width, 128)
    starts = [pl.multiple_of((dp ^ j) * own_width + first, 16) for j in range(n_dp)]
    loads = [
        pltpu.make_async_copy(
            weight.at[pl.ds(starts[j], chunk), pl.ds(column, width)],
            weights.at[j],
            semaphores.at[0, j],
        )
        for j in range(n_dp)
    ]
    stores = [
        pltpu.make_async_copy(
            results.at[j],
            out.at[pl.ds(starts[j], chunk), pl.ds(column, width)],
            semaphores.at[1, j],
        )
        for j in range(n_dp)
    ]
    for load in loads:
        load.start()
    lane = lax.broadcasted_iota(jnp.int32, (128, 128), 1)
    diagonal = lane == lax.broadcasted_iota(jnp.int32, (128, 128), 0)
    for j in range(n_dp):
        loads[j].wait()
        for at in range(0, chunk, 128):
            gains = gain[:, pl.ds(pl.multiple_of((dp ^ j) * own_width + first + at, 128), 128)]
            gains = jnp.sum(jnp.where(diagonal, gains, 0.0), axis=1, keepdims=True)
            total = values[j][at : at + 128, :].astype(jnp.float32) * (1.0 / shards)
            results[j, at : at + 128, :] = total * gains
            total = total * weights[j, at : at + 128, :].astype(jnp.float32)
            total = jnp.sum(total, axis=1, keepdims=True)
            total = jnp.sum(jnp.where(diagonal, total, 0.0), axis=0, keepdims=True)
            sums[j : j + 1, at : at + 128] = total
        stores[j].start()
    for copy in stores:
        copy.wait()


def body(
    lengths,
    final_hidden,
    score_gain,
    score_head,
    policy_input,
    block_order,
    norm_gain,
    key_weight,
    key_cotangent,
):
    n_section, n_dp, n_mp = (lax.axis_size(name) for name in ("section", "dp", "mp"))
    dp, mp = lax.axis_index("dp"), lax.axis_index("mp")
    block_count = lengths.shape[0]
    tokens, local_width = policy_input.shape
    block_len = tokens // block_count
    pair = block_count // n_dp
    columns = key_cotangent.shape[1]
    own_width = local_width // n_dp
    chunk = min(CHUNK_ROWS, own_width)
    feature_blocks = own_width // chunk
    n_far = n_mp // 2
    far, core = mp >> 1, mp & 1

    cotangents = [key_cotangent] + [swap(key_cotangent, "dp", j) for j in range(1, n_dp)]
    cotangents = jnp.concatenate(cotangents, axis=0)

    per_owner = feature_blocks
    given = (lengths, block_order, final_hidden, score_gain, score_head, policy_input)
    vmem, hbm = pl.BlockSpec(memory_space=pltpu.VMEM), pl.BlockSpec(memory_space=pl.ANY)
    squares, rest, *pieces = pl.pallas_call(
        functools.partial(prepare, n_dp, block_len, chunk),
        out_shape=[
            jax.ShapeDtypeStruct((block_count, block_len), jnp.float32),
            jax.ShapeDtypeStruct((2 * block_count, block_len), jnp.float32),
        ]
        + [jax.ShapeDtypeStruct((tokens, chunk), jnp.bfloat16)] * (n_dp * per_owner),
        in_specs=[hbm] * 6,
        out_specs=[vmem] * (2 + n_dp * per_owner),
        scratch_shapes=[pltpu.SMEM(value.shape, value.dtype) for value in given[:2]]
        + [pltpu.VMEM(value.shape, value.dtype) for value in given[2:]]
        + [pltpu.SemaphoreType.DMA((6,))],
        compiler_params=pltpu.CompilerParams(vmem_limit_bytes=32 * 2**20),
        name="prepare",
    )(*given)
    squares = squares + sum(swap(squares, "mp", j) for j in range(1, n_mp))
    inverse = lax.rsqrt(squares / (local_width * n_mp) + EPSILON)
    small = jnp.concatenate([inverse, rest], axis=0)
    small = [small] + [swap(small, "dp", j) for j in range(1, n_dp)]

    parts = []

    def rows(f):
        got = [pieces[f]]
        for j in range(1, n_dp):
            piece = pieces[j * per_owner + f]
            if f:
                piece, _ = lax.optimization_barrier((piece, parts[0]))
            piece = swap(piece, "dp", j)
            if f:
                piece, _ = lax.optimization_barrier((piece, parts[f - 1]))
            got.append(piece)
        return jnp.concatenate(got, axis=0)

    gathered = []

    def key_gradient(near):
        other = swap(near, "mp", 1)
        low = core == 0
        cotangent = jnp.concatenate(
            [jnp.where(low, near, other), jnp.where(low, other, near)], axis=1
        ).reshape(n_dp, n_dp, pair, block_len, -1)
        found = []
        for j in range(n_dp):
            sender = dp ^ j
            for b in range(block_count):
                slot = small[j][2 * block_count + b][:, None]
                chosen = None
                for e in range(n_dp):
                    for q in range(pair):
                        value = lax.dynamic_index_in_dim(cotangent[e], sender, 0, keepdims=False)[q]
                        at = ((dp ^ e) * pair + q).astype(jnp.float32)
                        chosen = value if chosen is None else jnp.where(slot == at, value, chosen)
                weight = small[j][block_count + b].astype(jnp.bfloat16).astype(jnp.float32)
                key_grad = to_bfloat16(chosen.astype(jnp.float32) * weight[:, None])
                found.append(
                    (key_grad.astype(jnp.float32) * small[j][b][:, None]).astype(jnp.bfloat16)
                )
        return jnp.concatenate(found, axis=0)

    for g in range(n_far):
        near = cotangents
        if g:
            near, _ = lax.optimization_barrier((near, parts[0]))
            near = swap(near, "mp", 2 * g)
        key_grad = key_gradient(near)
        for f in range(feature_blocks):
            if not g:
                gathered.append(rows(f))
            part = lax.dot_general(
                gathered[f],
                key_grad,
                (((0,), (0,)), ((), ())),
                preferred_element_type=jnp.float32,
            )
            parts.append(to_bfloat16(part))
    late_gain, _ = lax.optimization_barrier((norm_gain, parts[0]))
    gain = late_gain.astype(jnp.float32)[None, :]
    shards = n_section * n_dp
    out = []
    sums = []

    def shared_sum(total):
        return [total] + [swap(total, "dp", j) for j in range(1, n_dp)]

    def emit(k, values):
        g, f = divmod(k, feature_blocks)
        before = tuple(out)
        result, total = pl.pallas_call(
            functools.partial(store, n_dp, g, f * chunk, shards),
            out_shape=[
                jax.ShapeDtypeStruct((local_width, n_mp * columns), jnp.float32),
                jax.ShapeDtypeStruct((n_dp, chunk), jnp.float32),
            ],
            in_specs=[vmem] * (n_dp + 1) + [hbm] * (1 + len(before)),
            out_specs=[hbm, vmem],
            input_output_aliases={n_dp + 2: 0} if before else {},
            scratch_shapes=[
                pltpu.VMEM((n_dp, chunk, 2 * columns), jnp.bfloat16),
                pltpu.VMEM((n_dp, chunk, 2 * columns), jnp.float32),
                pltpu.SemaphoreType.DMA((2, n_dp)),
            ],
            compiler_params=pltpu.CompilerParams(vmem_limit_bytes=32 * 2**20),
            name="store",
        )(*values, gain, key_weight, *before)
        out[:] = [result]
        sums.append(total)
        return total

    def key_steps():
        yield (inverse,)
        (late_inverse,) = side_values[0]
        normed = policy_input.astype(jnp.float32) * late_inverse.reshape(-1, 1) * gain
        normed = lax.optimization_barrier(normed.astype(jnp.bfloat16))
        partial = jnp.dot(normed, key_weight, preferred_element_type=jnp.float32)
        cut = [partial[:, i * columns : (i + 1) * columns] for i in range(n_mp)]
        yield (partial,)
        (partial,) = side_values[0]
        cut = [partial[:, i * columns : (i + 1) * columns] for i in range(n_mp)]
        own = pick(cut, mp)
        yield (own,) + tuple(
            swap(pick(cut, mp ^ j).astype(jnp.bfloat16), "mp", j) for j in range(1, n_mp)
        )
        own, *others = side_values[0]
        keys = own + sum(other.astype(jnp.float32) for other in others)
        keys = keys.astype(jnp.bfloat16).reshape(block_count, block_len, columns)
        by_slot = []
        for slot in range(block_count):
            chosen = keys[0]
            for b in range(1, block_count):
                chosen = jnp.where(rest[block_count + b][:, None] == slot, keys[b], chosen)
            by_slot.append(chosen)
        by_target = [jnp.concatenate(by_slot[e * pair : (e + 1) * pair]) for e in range(n_dp)]
        yield (pick(by_target, dp),) + tuple(
            swap(pick(by_target, dp ^ j), "dp", j) for j in range(1, n_dp)
        )
        arrived = side_values[0]
        learner_keys.append(jnp.concatenate([pick(arrived, dp ^ a) for a in range(n_dp)], axis=0))

    side_values, learner_keys = [()], []
    steps = key_steps()

    def side(waited):
        side_values[0] = waited
        return next(steps, None)

    summed(parts, shared_sum, emit, side)
    grad_gain = [
        sum(sums[g * feature_blocks + f] for g in range(n_far)) for f in range(feature_blocks)
    ]
    grad_gain = jnp.concatenate(grad_gain, axis=1)
    grad_gain = jnp.concatenate([pick([grad_gain[j] for j in range(n_dp)], dp ^ e) for e in range(n_dp)])
    return learner_keys[0], out[0], grad_gain


def solution(mesh):
    placed = (
        P(("section", "dp")),
        P(("section", "dp"), None),
        P(),
        P(),
        P(("section", "dp"), "mp"),
        P(("section", "dp"), None),
        P("mp"),
        P("mp", None),
        P(("section", "dp"), "mp"),
    )
    return jax.shard_map(
        body,
        mesh=mesh,
        in_specs=placed,
        out_specs=(P(("section", "dp"), "mp"), P("mp", None), P("mp")),
        check_vma=False,
    )
```

time: 178 us -> 121 us (0.68)
  starting transfers between devices: 123 us -> 63.7 us
  Pallas kernels: 0.98 us -> 11.1 us
  local copies, waits for them, and re-layouts: 11.4 us -> 5.67 us
  waiting for transfers between devices: 25.6 us -> 30.3 us
  other arithmetic: 7.7 us -> 4.1 us
    ppermute x19 -> x11, starting transfers between devices: 81.9 us -> 36.8 us  [outer_swap(): return lax.ppermute(value, 'section', [(0, 1), (1, 0), (2, 3), (3, 2)])]
    pallas_call x1 -> x9, Pallas kernels: 0.98 us -> 11.1 us  [the longest x8 10 us: emit(): pl.pallas_call(functools.partial(store, n_dp, g, f * chunk, shards), out_...]
    ppermute x32 -> x24, starting transfers between devices: 30.1 us -> 21.3 us  [swap(): lax.ppermute(value, axis, [(i, i ^ bit) for i in range(lax.axis_size(axis...]
    ppermute x19 -> x11, waiting for transfers between devices: 4.46 us -> 12 us  [outer_swap(): return lax.ppermute(value, 'section', [(0, 1), (1, 0), (2, 3), (3, 2)])]
    ppermute x16 -> x8, starting transfers between devices: 11 us -> 5.71 us  [middle_swap(): return lax.ppermute(value, 'section', [(1, 2), (2, 1), (0, 0), (3, 3)])]
    unnamed x40 -> x22, local copies, waits for them, and re-layouts: 9.09 us -> 5.61 us
    ppermute x32 -> x24, waiting for transfers between devices: 21.1 us -> 18.3 us  [swap(): lax.ppermute(value, axis, [(i, i ^ bit) for i in range(lax.axis_size(axis...]
    dot_general x17 -> x9, matrix products: 5.37 us -> 3.86 us  [the longest x8 2.59 us: body(): lax.dot_general(gathered[f], key_grad, (((0,), (0,)), ((), ())), preferre...]
  transfers between devices with their start and end apart: 67 -> 43, of which waited for: 11 -> 12; matrix products, arithmetic and copies ran while one was open for 8% -> 6% of each run, Pallas kernels for 0% -> 7%
where the time goes in v4:
time: 121 us; the launch traced here: 120 us
  starting transfers between devices  63.7 us (53%)
  waiting for transfers between devices  30.3 us (25%)
  Pallas kernels  11.1 us (9%)
  local copies, waits for them, and re-layouts  5.67 us (5%)
  other arithmetic  4.1 us (3%)
  matrix products  3.86 us (3%)
  between operations  1.5 us (1%)
    ppermute x11, starting transfers between devices, outer_swap(): return lax.ppermute(value, 'section', [(0, 1), (1, 0), (2, 3), (3, 2)])  36.8 us
    ppermute x24, starting transfers between devices, swap(): lax.ppermute(value, axis, [(i, i ^ bit) for i in range(lax.axis_size(axis...  21.3 us
    ppermute x24, waiting for transfers between devices, swap(): lax.ppermute(value, axis, [(i, i ^ bit) for i in range(lax.axis_size(axis...  18.3 us
    ppermute x11, waiting for transfers between devices, outer_swap(): return lax.ppermute(value, 'section', [(0, 1), (1, 0), (2, 3), (3, 2)])  12 us
    pallas_call x8, Pallas kernels, emit(): pl.pallas_call(functools.partial(store, n_dp, g, f * chunk, shards), out_...  10 us
    ppermute x8, starting transfers between devices, middle_swap(): return lax.ppermute(value, 'section', [(1, 2), (2, 1), (0, 0), (3, 3)])  5.71 us
    unnamed x22, local copies, waits for them, and re-layouts  5.61 us
    dot_general x8, matrix products, body(): lax.dot_general(gathered[f], key_grad, (((0,), (0,)), ((), ())), preferre...  2.59 us
  transfers between devices with their start and end apart: 43, of which 12 were waited for; matrix products, arithmetic and copies ran while one was open for 6% of the time, Pallas kernels for 7%

profile of v4, /device:TPU:0, one launch (start us, length us, event | category | flops | bytes accessed | tf_op | source)
XLA Modules:
  0.0 120.3 jit_solution(12184640385022299978)
XLA Ops:
  6.8 2.6 %collective-permute-start.4 = (f32[2,128]{1,0:T(2,128)S(1)}, f32[2,128]{1,0:T(2,128)S(1)}, u32[]{:S(2)}, u32[]{:S(2)}) collective-permute-start(f32[2,128]{1,0:T(2,128)S(1)} %get-tuple-element.86), channel_id=1, source_target_pairs={{0,2},{1,3},{2,0},{3,1},{4,6},{5,7},{6,4},{7,5},{8,10},{9,11},{10,... | collective-permute-start | bytes 3080 | tf_op jit(solution)/shard_map/ppermute | solution.py:16
  9.5 1.7 %collective-permute-start.1 = (bf16[256,256]{1,0:T(8,128)(2,1)}, bf16[256,256]{1,0:T(8,128)(2,1)S(1)}, u32[]{:S(2)}, u32[]{:S(2)}) collective-permute-start(bf16[256,256]{1,0:T(8,128)(2,1)} %param.17), channel_id=1, source_target_pairs={{0,4},{4,0},{1,5},{5,1},{2,6},{6,2},{3,7},{7,3},{8,12},{12,8},{9,1... | collective-permute-start | bytes 393224 | tf_op jit(solution)/shard_map/ppermute | solution.py:16
  12.6 1.8 %collective-permute-start.6 = (f32[6,128]{1,0:T(8,128)S(1)}, f32[6,128]{1,0:T(8,128)S(1)}, u32[]{:S(2)}, u32[]{:S(2)}) collective-permute-start(f32[6,128]{1,0:T(8,128)S(1)} %pad_maximum_fusion.7), channel_id=1, source_target_pairs={{0,4},{4,0},{1,5},{5,1},{2,6},{6,2},{3,7},{7,3},{8,12},{12,8},{9,1... | collective-permute-start | bytes 9224 | tf_op jit(solution)/shard_map/ppermute | solution.py:16
  14.4 3.9 %collective-permute-done.6 = f32[6,128]{1,0:T(8,128)S(1)} collective-permute-done((f32[6,128]{1,0:T(8,128)S(1)}, f32[6,128]{1,0:T(8,128)S(1)}, u32[]{:S(2)}, u32[]{:S(2)}) %collective-permute-start.6) | collective-permute-done | bytes 3104 | tf_op jit(solution)/shard_map/ppermute | solution.py:16
  20.7 1.8 %collective-permute-start.8 = (bf16[256,256]{1,0:T(8,128)(2,1)S(1)}, bf16[256,256]{1,0:T(8,128)(2,1)S(1)}, u32[]{:S(2)}, u32[]{:S(2)}) collective-permute-start(bf16[256,256]{1,0:T(8,128)(2,1)S(1)} %get-tuple-element.90), channel_id=1, source_target_pairs={{0,4},{4,0},{1,5},{5,1},{2,6},{6,2},{3,7},{7,3},{8,12},{12,8},{9,1... | collective-permute-start | bytes 393224 | tf_op jit(solution)/shard_map/ppermute | solution.py:16
  22.6 1.6 %collective-permute-start.14 = (bf16[256,512]{1,0:T(8,128)(2,1)S(1)}, bf16[256,512]{1,0:T(8,128)(2,1)S(1)}, u32[]{:S(2)}, u32[]{:S(2)}) collective-permute-start(bf16[256,512]{1,0:T(8,128)(2,1)S(1)} %fusion), channel_id=1, source_target_pairs={{0,8},{8,0},{16,24},{24,16},{1,9},{9,1},{17,25},{25,17},{2,10},{10... | collective-permute-start | bytes 786440 | tf_op jit(solution)/shard_map/ppermute | solution.py:47
  28.6 3.2 %collective-permute-done.7 = bf16[256,256]{1,0:T(8,128)(2,1)S(1)} collective-permute-done((bf16[256,256]{1,0:T(8,128)(2,1)S(1)}, bf16[256,256]{1,0:T(8,128)(2,1)S(1)}, u32[]{:S(2)}, u32[]{:S(2)}) %collective-permute-start.7) | collective-permute-done | bytes 131104 | tf_op jit(solution)/shard_map/ppermute | solution.py:16
  34.1 7.8 %collective-permute-done.11 = bf16[256,512]{1,0:T(8,128)(2,1)S(1)} collective-permute-done((bf16[256,512]{1,0:T(8,128)(2,1)S(1)}, bf16[256,512]{1,0:T(8,128)(2,1)S(1)}, u32[]{:S(2)}, u32[]{:S(2)}) %collective-permute-start.11) | collective-permute-done | bytes 262176 | tf_op jit(solution)/shard_map/ppermute | solution.py:47
  43.8 6.1 %collective-permute-start.17 = (bf16[256,512]{1,0:T(8,128)(2,1)S(1)}, bf16[256,512]{1,0:T(8,128)(2,1)S(1)}, u32[]{:S(2)}, u32[]{:S(2)}) collective-permute-start(bf16[256,512]{1,0:T(8,128)(2,1)S(1)} %get-tuple-element.197), channel_id=1, source_target_pairs={{0,8},{8,0},{16,24},{24,16},{1,9},{9,1},{17,25},{25,17},{2,10},{10... | collective-permute-start | bytes 786440 | tf_op jit(solution)/shard_map/ppermute | solution.py:47
  50.7 4.5 %collective-permute-start.21 = (bf16[256,512]{1,0:T(8,128)(2,1)S(1)}, bf16[256,512]{1,0:T(8,128)(2,1)S(1)}, u32[]{:S(2)}, u32[]{:S(2)}) collective-permute-start(bf16[256,512]{1,0:T(8,128)(2,1)S(1)} %get-tuple-element.199), channel_id=1, source_target_pairs={{0,8},{8,0},{16,24},{24,16},{1,9},{9,1},{17,25},{25,17},{2,10},{10... | collective-permute-start | bytes 786440 | tf_op jit(solution)/shard_map/ppermute | solution.py:47
  55.2 2.0 %collective-permute-done.17 = bf16[256,512]{1,0:T(8,128)(2,1)S(1)} collective-permute-done((bf16[256,512]{1,0:T(8,128)(2,1)S(1)}, bf16[256,512]{1,0:T(8,128)(2,1)S(1)}, u32[]{:S(2)}, u32[]{:S(2)}) %collective-permute-start.17) | collective-permute-done | bytes 262176 | tf_op jit(solution)/shard_map/ppermute | solution.py:47
  59.1 4.9 %collective-permute-start.25 = (bf16[256,512]{1,0:T(8,128)(2,1)S(1)}, bf16[256,512]{1,0:T(8,128)(2,1)S(1)}, u32[]{:S(2)}, u32[]{:S(2)}) collective-permute-start(bf16[256,512]{1,0:T(8,128)(2,1)S(1)} %get-tuple-element.203), channel_id=1, source_target_pairs={{0,8},{8,0},{16,24},{24,16},{1,9},{9,1},{17,25},{25,17},{2,10},{10... | collective-permute-start | bytes 786440 | tf_op jit(solution)/shard_map/ppermute | solution.py:47
  69.8 3.7 %collective-permute-start.22 = (bf16[256,512]{1,0:T(8,128)(2,1)S(1)}, bf16[256,512]{1,0:T(8,128)(2,1)S(1)}, u32[]{:S(2)}, u32[]{:S(2)}) collective-permute-start(bf16[256,512]{1,0:T(8,128)(2,1)S(1)} %get-tuple-element.201), channel_id=1, source_target_pairs={{0,8},{8,0},{16,24},{24,16},{1,9},{9,1},{17,25},{25,17},{2,10},{10... | collective-permute-start | bytes 786440 | tf_op jit(solution)/shard_map/ppermute | solution.py:47
  73.4 1.7 %collective-permute-start.29 = (bf16[256,512]{1,0:T(8,128)(2,1)S(1)}, bf16[256,512]{1,0:T(8,128)(2,1)S(1)}, u32[]{:S(2)}, u32[]{:S(2)}) collective-permute-start(bf16[256,512]{1,0:T(8,128)(2,1)S(1)} %broadcast_select_fusion.6.refs_0_), channel_id=1, source_target_pairs={{0,4},{4,0},{1,5},{5,1},{2,6},{6,2},{3,7},{7,3},{8,12},{12,8},{9,1... | collective-permute-start | bytes 786440 | tf_op jit(solution)/shard_map/ppermute | solution.py:16
  76.1 1.7 %collective-permute-start.32 = (bf16[256,256]{1,0:T(8,128)(2,1)S(1)}, bf16[256,256]{1,0:T(8,128)(2,1)S(1)}, u32[]{:S(2)}, u32[]{:S(2)}) collective-permute-start(bf16[256,256]{1,0:T(8,128)(2,1)S(1)} %get-tuple-element.159), channel_id=1, source_target_pairs={{0,3},{1,2},{2,1},{3,0},{4,7},{5,6},{6,5},{7,4},{8,11},{9,10},{10,... | collective-permute-start | bytes 393224 | tf_op jit(solution)/shard_map/ppermute | solution.py:16
  80.2 3.0 %collective-permute-start.34 = (bf16[256,512]{1,0:T(8,128)(2,1)S(1)}, bf16[256,512]{1,0:T(8,128)(2,1)S(1)}, u32[]{:S(2)}, u32[]{:S(2)}) collective-permute-start(bf16[256,512]{1,0:T(8,128)(2,1)S(1)} %get-tuple-element.205), channel_id=1, source_target_pairs={{0,8},{8,0},{16,24},{24,16},{1,9},{9,1},{17,25},{25,17},{2,10},{10... | collective-permute-start | bytes 786440 | tf_op jit(solution)/shard_map/ppermute | solution.py:47
  86.3 4.6 %collective-permute-start.37 = (bf16[256,512]{1,0:T(8,128)(2,1)S(1)}, bf16[256,512]{1,0:T(8,128)(2,1)S(1)}, u32[]{:S(2)}, u32[]{:S(2)}) collective-permute-start(bf16[256,512]{1,0:T(8,128)(2,1)S(1)} %reduce-precision_convert_fusion.2), channel_id=1, source_target_pairs={{0,8},{8,0},{16,24},{24,16},{1,9},{9,1},{17,25},{25,17},{2,10},{10... | collective-permute-start | bytes 786440 | tf_op jit(solution)/shard_map/ppermute | solution.py:47
  92.4 1.8 %collective-permute-start.36 = (bf16[256,512]{1,0:T(8,128)(2,1)S(1)}, bf16[256,512]{1,0:T(8,128)(2,1)S(1)}, u32[]{:S(2)}, u32[]{:S(2)}) collective-permute-start(bf16[256,512]{1,0:T(8,128)(2,1)S(1)} %broadcast_select_fusion.3.refs_0_), channel_id=1, source_target_pairs={{0,4},{4,0},{1,5},{5,1},{2,6},{6,2},{3,7},{7,3},{8,12},{12,8},{9,1... | collective-permute-start | bytes 786440 | tf_op jit(solution)/shard_map/ppermute | solution.py:16
  96.5 4.1 %collective-permute-start.40 = (bf16[256,512]{1,0:T(8,128)(2,1)S(1)}, bf16[256,512]{1,0:T(8,128)(2,1)S(1)}, u32[]{:S(2)}, u32[]{:S(2)}) collective-permute-start(bf16[256,512]{1,0:T(8,128)(2,1)S(1)} %reduce-precision_convert_fusion), channel_id=1, source_target_pairs={{0,8},{8,0},{16,24},{24,16},{1,9},{9,1},{17,25},{25,17},{2,10},{10... | collective-permute-start | bytes 786440 | tf_op jit(solution)/shard_map/ppermute | solution.py:47
  100.8 3.1 %collective-permute-start.38 = (bf16[256,512]{1,0:T(8,128)(2,1)S(1)}, bf16[256,512]{1,0:T(8,128)(2,1)S(1)}, u32[]{:S(2)}, u32[]{:S(2)}) collective-permute-start(bf16[256,512]{1,0:T(8,128)(2,1)S(1)} %reduce-precision_convert_fusion.1), channel_id=1, source_target_pairs={{0,8},{8,0},{16,24},{24,16},{1,9},{9,1},{17,25},{25,17},{2,10},{10... | collective-permute-start | bytes 786440 | tf_op jit(solution)/shard_map/ppermute | solution.py:47
  105.2 2.2 %collective-permute-done.40 = bf16[256,512]{1,0:T(8,128)(2,1)S(1)} collective-permute-done((bf16[256,512]{1,0:T(8,128)(2,1)S(1)}, bf16[256,512]{1,0:T(8,128)(2,1)S(1)}, u32[]{:S(2)}, u32[]{:S(2)}) %collective-permute-start.40) | collective-permute-done | bytes 262176 | tf_op jit(solution)/shard_map/ppermute | solution.py:47
  107.5 2.1 %collective-permute-done.39.refs_1_ = bf16[256,512]{1,0:T(8,128)(2,1)S(1)} collective-permute-done((bf16[256,512]{1,0:T(8,128)(2,1)S(1)}, bf16[256,512]{1,0:T(8,128)(2,1)S(1)}, u32[]{:S(2)}, u32[]{:S(2)}) %collective-permute-start.39) | collective-permute-done | bytes 262176 | tf_op jit(solution)/shard_map/ppermute | solution.py:16
  111.7 3.9 %collective-permute-done.42.refs_1_ = bf16[256,512]{1,0:T(8,128)(2,1)S(1)} collective-permute-done((bf16[256,512]{1,0:T(8,128)(2,1)S(1)}, bf16[256,512]{1,0:T(8,128)(2,1)S(1)}, u32[]{:S(2)}, u32[]{:S(2)}) %collective-permute-start.42) | collective-permute-done | bytes 262176 | tf_op jit(solution)/shard_map/ppermute | solution.py:16
  116.8 1.5 %collective-permute-done.41.refs_1_ = bf16[256,512]{1,0:T(8,128)(2,1)S(1)} collective-permute-done((bf16[256,512]{1,0:T(8,128)(2,1)S(1)}, bf16[256,512]{1,0:T(8,128)(2,1)S(1)}, u32[]{:S(2)}, u32[]{:S(2)}) %collective-permute-start.41) | collective-permute-done | bytes 262176 | tf_op jit(solution)/shard_map/ppermute | solution.py:16
  (158 shorter events, 43.3 us)
Async XLA Ops:
  9.5 8.8 %collective-permute-start.1 = (bf16[256,256]{1,0:T(8,128)(2,1)}, bf16[256,256]{1,0:T(8,128)(2,1)S(1)}, u32[]{:S(2)}, u32[]{:S(2)}) collective-permute-start(bf16[256,256]{1,0:T(8,128)(2,1)} %param.17), channel_id=1, source_target_pairs={{0,4},{4,0},{1,5},{5,1},{2,6},{6,2},{3,7},{7,3},{8,12},{12,8},{9,1... | collective-permute-start | bytes 393224 | tf_op jit(solution)/shard_map/ppermute | solution.py:16
  22.6 10.7 %collective-permute-start.14 = (bf16[256,512]{1,0:T(8,128)(2,1)S(1)}, bf16[256,512]{1,0:T(8,128)(2,1)S(1)}, u32[]{:S(2)}, u32[]{:S(2)}) collective-permute-start(bf16[256,512]{1,0:T(8,128)(2,1)S(1)} %fusion), channel_id=1, source_target_pairs={{0,8},{8,0},{16,24},{24,16},{1,9},{9,1},{17,25},{25,17},{2,10},{10... | collective-permute-start | bytes 786440 | tf_op jit(solution)/shard_map/ppermute | solution.py:47
  24.2 9.8 %collective-permute-start.9 = (bf16[512,256]{1,0:T(8,128)(2,1)S(1)}, bf16[512,256]{1,0:T(8,128)(2,1)S(1)}, u32[]{:S(2)}, u32[]{:S(2)}) collective-permute-start(bf16[512,256]{1,0:T(8,128)(2,1)S(1)} %constant_dynamic-update-slice_fusion.2), channel_id=1, source_target_pairs={{0,2},{1,3},{2,0},{3,1},{4,6},{5,7},{6,4},{7,5},{8,10},{9,11},{10,... | collective-permute-start | bytes 786440 | tf_op jit(solution)/shard_map/ppermute | solution.py:16
  28.1 13.9 %collective-permute-start.16 = (bf16[256,512]{1,0:T(8,128)(2,1)S(1)}, bf16[256,512]{1,0:T(8,128)(2,1)S(1)}, u32[]{:S(2)}, u32[]{:S(2)}) collective-permute-start(bf16[256,512]{1,0:T(8,128)(2,1)S(1)} %fusion.1), channel_id=1, source_target_pairs={{0,8},{8,0},{16,24},{24,16},{1,9},{9,1},{17,25},{25,17},{2,10},{10... | collective-permute-start | bytes 786440 | tf_op jit(solution)/shard_map/ppermute | solution.py:47
  32.2 9.8 %collective-permute-start.11 = (bf16[256,512]{1,0:T(8,128)(2,1)S(1)}, bf16[256,512]{1,0:T(8,128)(2,1)S(1)}, u32[]{:S(2)}, u32[]{:S(2)}) collective-permute-start(bf16[256,512]{1,0:T(8,128)(2,1)S(1)} %fusion.3), channel_id=1, source_target_pairs={{0,8},{8,0},{16,24},{24,16},{1,9},{9,1},{17,25},{25,17},{2,10},{10... | collective-permute-start | bytes 786440 | tf_op jit(solution)/shard_map/ppermute | solution.py:47
  33.3 10.1 %collective-permute-start.15 = (bf16[256,512]{1,0:T(8,128)(2,1)S(1)}, bf16[256,512]{1,0:T(8,128)(2,1)S(1)}, u32[]{:S(2)}, u32[]{:S(2)}) collective-permute-start(bf16[256,512]{1,0:T(8,128)(2,1)S(1)} %reduce-precision_convert_fusion.14), channel_id=1, source_target_pairs={{8,16},{16,8},{0,0},{24,24},{9,17},{17,9},{1,1},{25,25},{10,18},{1... | collective-permute-start | bytes 786440 | tf_op jit(solution)/shard_map/ppermute | solution.py:50
  34.0 15.9 %collective-permute-start.10 = (bf16[512,256]{1,0:T(8,128)(2,1)S(1)}, bf16[512,256]{1,0:T(8,128)(2,1)S(1)}, u32[]{:S(2)}, u32[]{:S(2)}) collective-permute-start(bf16[512,256]{1,0:T(8,128)(2,1)S(1)} %collective-permute-done.9), channel_id=1, source_target_pairs={{0,1},{1,0},{2,3},{3,2},{4,5},{5,4},{6,7},{7,6},{8,9},{9,8},{10,11... | collective-permute-start | bytes 786440 | tf_op jit(solution)/shard_map/ppermute | solution.py:16
  42.8 16.0 %collective-permute-start.12 = (bf16[256,512]{1,0:T(8,128)(2,1)S(1)}, bf16[256,512]{1,0:T(8,128)(2,1)S(1)}, u32[]{:S(2)}, u32[]{:S(2)}) collective-permute-start(bf16[256,512]{1,0:T(8,128)(2,1)S(1)} %reduce-precision_convert_fusion.15), channel_id=1, source_target_pairs={{8,16},{16,8},{0,0},{24,24},{9,17},{17,9},{1,1},{25,25},{10,18},{1... | collective-permute-start | bytes 786440 | tf_op jit(solution)/shard_map/ppermute | solution.py:50
  43.8 13.4 %collective-permute-start.17 = (bf16[256,512]{1,0:T(8,128)(2,1)S(1)}, bf16[256,512]{1,0:T(8,128)(2,1)S(1)}, u32[]{:S(2)}, u32[]{:S(2)}) collective-permute-start(bf16[256,512]{1,0:T(8,128)(2,1)S(1)} %get-tuple-element.197), channel_id=1, source_target_pairs={{0,8},{8,0},{16,24},{24,16},{1,9},{9,1},{17,25},{25,17},{2,10},{10... | collective-permute-start | bytes 786440 | tf_op jit(solution)/shard_map/ppermute | solution.py:47
  50.7 13.3 %collective-permute-start.21 = (bf16[256,512]{1,0:T(8,128)(2,1)S(1)}, bf16[256,512]{1,0:T(8,128)(2,1)S(1)}, u32[]{:S(2)}, u32[]{:S(2)}) collective-permute-start(bf16[256,512]{1,0:T(8,128)(2,1)S(1)} %get-tuple-element.199), channel_id=1, source_target_pairs={{0,8},{8,0},{16,24},{24,16},{1,9},{9,1},{17,25},{25,17},{2,10},{10... | collective-permute-start | bytes 786440 | tf_op jit(solution)/shard_map/ppermute | solution.py:47
  57.3 9.2 %collective-permute-start.19 = (bf16[256,512]{1,0:T(8,128)(2,1)S(1)}, bf16[256,512]{1,0:T(8,128)(2,1)S(1)}, u32[]{:S(2)}, u32[]{:S(2)}) collective-permute-start(bf16[256,512]{1,0:T(8,128)(2,1)S(1)} %broadcast_select_fusion.11.refs_0_), channel_id=1, source_target_pairs={{0,4},{4,0},{1,5},{5,1},{2,6},{6,2},{3,7},{7,3},{8,12},{12,8},{9,1... | collective-permute-start | bytes 786440 | tf_op jit(solution)/shard_map/ppermute | solution.py:16
  59.1 10.2 %collective-permute-start.25 = (bf16[256,512]{1,0:T(8,128)(2,1)S(1)}, bf16[256,512]{1,0:T(8,128)(2,1)S(1)}, u32[]{:S(2)}, u32[]{:S(2)}) collective-permute-start(bf16[256,512]{1,0:T(8,128)(2,1)S(1)} %get-tuple-element.203), channel_id=1, source_target_pairs={{0,8},{8,0},{16,24},{24,16},{1,9},{9,1},{17,25},{25,17},{2,10},{10... | collective-permute-start | bytes 786440 | tf_op jit(solution)/shard_map/ppermute | solution.py:47
  64.1 11.8 %collective-permute-start.24 = (bf16[256,512]{1,0:T(8,128)(2,1)S(1)}, bf16[256,512]{1,0:T(8,128)(2,1)S(1)}, u32[]{:S(2)}, u32[]{:S(2)}) collective-permute-start(bf16[256,512]{1,0:T(8,128)(2,1)S(1)} %broadcast_select_fusion.9.refs_0_), channel_id=1, source_target_pairs={{0,4},{4,0},{1,5},{5,1},{2,6},{6,2},{3,7},{7,3},{8,12},{12,8},{9,1... | collective-permute-start | bytes 786440 | tf_op jit(solution)/shard_map/ppermute | solution.py:16
  65.6 10.3 %collective-permute-start.23 = (bf16[256,512]{1,0:T(8,128)(2,1)S(1)}, bf16[256,512]{1,0:T(8,128)(2,1)S(1)}, u32[]{:S(2)}, u32[]{:S(2)}) collective-permute-start(bf16[256,512]{1,0:T(8,128)(2,1)S(1)} %reduce-precision_convert_fusion.9), channel_id=1, source_target_pairs={{8,16},{16,8},{0,0},{24,24},{9,17},{17,9},{1,1},{25,25},{10,18},{1... | collective-permute-start | bytes 786440 | tf_op jit(solution)/shard_map/ppermute | solution.py:50
  69.8 9.7 %collective-permute-start.22 = (bf16[256,512]{1,0:T(8,128)(2,1)S(1)}, bf16[256,512]{1,0:T(8,128)(2,1)S(1)}, u32[]{:S(2)}, u32[]{:S(2)}) collective-permute-start(bf16[256,512]{1,0:T(8,128)(2,1)S(1)} %get-tuple-element.201), channel_id=1, source_target_pairs={{0,8},{8,0},{16,24},{24,16},{1,9},{9,1},{17,25},{25,17},{2,10},{10... | collective-permute-start | bytes 786440 | tf_op jit(solution)/shard_map/ppermute | solution.py:47
  73.4 12.3 %collective-permute-start.29 = (bf16[256,512]{1,0:T(8,128)(2,1)S(1)}, bf16[256,512]{1,0:T(8,128)(2,1)S(1)}, u32[]{:S(2)}, u32[]{:S(2)}) collective-permute-start(bf16[256,512]{1,0:T(8,128)(2,1)S(1)} %broadcast_select_fusion.6.refs_0_), channel_id=1, source_target_pairs={{0,4},{4,0},{1,5},{5,1},{2,6},{6,2},{3,7},{7,3},{8,12},{12,8},{9,1... | collective-permute-start | bytes 786440 | tf_op jit(solution)/shard_map/ppermute | solution.py:16
  75.2 10.5 %collective-permute-start.28 = (bf16[256,512]{1,0:T(8,128)(2,1)S(1)}, bf16[256,512]{1,0:T(8,128)(2,1)S(1)}, u32[]{:S(2)}, u32[]{:S(2)}) collective-permute-start(bf16[256,512]{1,0:T(8,128)(2,1)S(1)} %reduce-precision_convert_fusion.6), channel_id=1, source_target_pairs={{8,16},{16,8},{0,0},{24,24},{9,17},{17,9},{1,1},{25,25},{10,18},{1... | collective-permute-start | bytes 786440 | tf_op jit(solution)/shard_map/ppermute | solution.py:50
  80.2 12.0 %collective-permute-start.34 = (bf16[256,512]{1,0:T(8,128)(2,1)S(1)}, bf16[256,512]{1,0:T(8,128)(2,1)S(1)}, u32[]{:S(2)}, u32[]{:S(2)}) collective-permute-start(bf16[256,512]{1,0:T(8,128)(2,1)S(1)} %get-tuple-element.205), channel_id=1, source_target_pairs={{0,8},{8,0},{16,24},{24,16},{1,9},{9,1},{17,25},{25,17},{2,10},{10... | collective-permute-start | bytes 786440 | tf_op jit(solution)/shard_map/ppermute | solution.py:47
  83.2 11.9 %collective-permute-start.27 = (bf16[256,512]{1,0:T(8,128)(2,1)S(1)}, bf16[256,512]{1,0:T(8,128)(2,1)S(1)}, u32[]{:S(2)}, u32[]{:S(2)}) collective-permute-start(bf16[256,512]{1,0:T(8,128)(2,1)S(1)} %broadcast_select_fusion.5.refs_0_), channel_id=1, source_target_pairs={{0,4},{4,0},{1,5},{5,1},{2,6},{6,2},{3,7},{7,3},{8,12},{12,8},{9,1... | collective-permute-start | bytes 786440 | tf_op jit(solution)/shard_map/ppermute | solution.py:16
  85.0 10.1 %collective-permute-start.26 = (bf16[256,512]{1,0:T(8,128)(2,1)S(1)}, bf16[256,512]{1,0:T(8,128)(2,1)S(1)}, u32[]{:S(2)}, u32[]{:S(2)}) collective-permute-start(bf16[256,512]{1,0:T(8,128)(2,1)S(1)} %reduce-precision_convert_fusion.5), channel_id=1, source_target_pairs={{8,16},{16,8},{0,0},{24,24},{9,17},{17,9},{1,1},{25,25},{10,18},{1... | collective-permute-start | bytes 786440 | tf_op jit(solution)/shard_map/ppermute | solution.py:50
  86.3 10.1 %collective-permute-start.37 = (bf16[256,512]{1,0:T(8,128)(2,1)S(1)}, bf16[256,512]{1,0:T(8,128)(2,1)S(1)}, u32[]{:S(2)}, u32[]{:S(2)}) collective-permute-start(bf16[256,512]{1,0:T(8,128)(2,1)S(1)} %reduce-precision_convert_fusion.2), channel_id=1, source_target_pairs={{0,8},{8,0},{16,24},{24,16},{1,9},{9,1},{17,25},{25,17},{2,10},{10... | collective-permute-start | bytes 786440 | tf_op jit(solution)/shard_map/ppermute | solution.py:47
  96.5 10.9 %collective-permute-start.40 = (bf16[256,512]{1,0:T(8,128)(2,1)S(1)}, bf16[256,512]{1,0:T(8,128)(2,1)S(1)}, u32[]{:S(2)}, u32[]{:S(2)}) collective-permute-start(bf16[256,512]{1,0:T(8,128)(2,1)S(1)} %reduce-precision_convert_fusion), channel_id=1, source_target_pairs={{0,8},{8,0},{16,24},{24,16},{1,9},{9,1},{17,25},{25,17},{2,10},{10... | collective-permute-start | bytes 786440 | tf_op jit(solution)/shard_map/ppermute | solution.py:47
  100.6 9.0 %collective-permute-start.39 = (bf16[256,512]{1,0:T(8,128)(2,1)S(1)}, bf16[256,512]{1,0:T(8,128)(2,1)S(1)}, u32[]{:S(2)}, u32[]{:S(2)}) collective-permute-start(bf16[256,512]{1,0:T(8,128)(2,1)S(1)} %broadcast_select_fusion.2.refs_0_), channel_id=1, source_target_pairs={{0,4},{4,0},{1,5},{5,1},{2,6},{6,2},{3,7},{7,3},{8,12},{12,8},{9,1... | collective-permute-start | bytes 786440 | tf_op jit(solution)/shard_map/ppermute | solution.py:16
  100.8 10.1 %collective-permute-start.38 = (bf16[256,512]{1,0:T(8,128)(2,1)S(1)}, bf16[256,512]{1,0:T(8,128)(2,1)S(1)}, u32[]{:S(2)}, u32[]{:S(2)}) collective-permute-start(bf16[256,512]{1,0:T(8,128)(2,1)S(1)} %reduce-precision_convert_fusion.1), channel_id=1, source_target_pairs={{0,8},{8,0},{16,24},{24,16},{1,9},{9,1},{17,25},{25,17},{2,10},{10... | collective-permute-start | bytes 786440 | tf_op jit(solution)/shard_map/ppermute | solution.py:47
  (28 other events, 174.4 us)

commit v5 on v4

--- a/solution.py
+++ b/solution.py
@@ -53,16 +53,15 @@
     halves, others, totals, shares = {}, {}, {}, {}
     done, pending = (), ()
     for k in range(count + LAG):
-        got, done = lax.optimization_barrier((arriving[k], done))
+        got, _ = lax.optimization_barrier((arriving[k], done))
+        done = ()
         tied = ()
         if k < count:
             halves[k] = add(parts[k], got)
             others[k] = middle_swap(halves[k])
             tied += (halves[k],)
         if k >= LAG:
-            full = jnp.where(inner, totals[k - LAG], got)
-            shares[k - LAG] = shared_sum(full)
-            tied += (full,)
+            tied += (jnp.where(inner, totals[k - LAG], got),)
         waited = {"tied": tied, "side": pending}
         if k - 1 in others:
             waited["other"] = others[k - 1]
@@ -78,8 +77,11 @@
             value = totals[following - LAG]
             if following < count:
                 value = jnp.where(inner, value, parts[following])
+            value, waited["tied"] = lax.optimization_barrier((value, waited["tied"]))
             arriving[following] = outer_swap(value)
-        done = ()
+            done = (value,)
+        if k >= LAG:
+            shares[k - LAG] = shared_sum(waited["tied"][-1])
         if k >= LAG and pending is not None:
             pending = side(waited["side"])
             done += () if pending is None else pending[:1]
@@ -213,7 +215,7 @@
 
     per_owner = feature_blocks
     given = (lengths, block_order, final_hidden, score_gain, score_head, policy_input)
-    vmem, hbm = pl.BlockSpec(memory_space=pltpu.VMEM), pl.BlockSpec(memory_space=pl.ANY)
+    vmem, hbm = pl.BlockSpec(memory_space=pltpu.VMEM), pl.BlockSpec(memory_space=pltpu.MemorySpace.HBM)
     squares, rest, *pieces = pl.pallas_call(
         functools.partial(prepare, n_dp, block_len, chunk),
         out_shape=[
@@ -240,8 +242,7 @@
         got = [pieces[f]]
         for j in range(1, n_dp):
             piece = pieces[j * per_owner + f]
-            if f:
-                piece, _ = lax.optimization_barrier((piece, parts[0]))
+            piece, _ = lax.optimization_barrier((piece, parts[0] if f else small[0]))
             piece = swap(piece, "dp", j)
             if f:
                 piece, _ = lax.optimization_barrier((piece, parts[f - 1]))

time: 121 us -> 128 us (1.058)
  waiting for transfers between devices: 30.3 us -> 43 us
  starting transfers between devices: 63.7 us -> 58.4 us
    ppermute x24, waiting for transfers between devices: 18.3 us -> 35.9 us  [swap(): lax.ppermute(value, axis, [(i, i ^ bit) for i in range(lax.axis_size(axis...]
    ppermute x11, starting transfers between devices: 36.8 us -> 26.9 us  [outer_swap(): return lax.ppermute(value, 'section', [(0, 1), (1, 0), (2, 3), (3, 2)])]
    ppermute x11, waiting for transfers between devices: 12 us -> 7.06 us  [outer_swap(): return lax.ppermute(value, 'section', [(0, 1), (1, 0), (2, 3), (3, 2)])]
    ppermute x24, starting transfers between devices: 21.3 us -> 25.7 us  [swap(): lax.ppermute(value, axis, [(i, i ^ bit) for i in range(lax.axis_size(axis...]
  transfers between devices with their start and end apart: 43 -> 43, of which waited for: 12 -> 16; matrix products, arithmetic and copies ran while one was open for 6% -> 6% of each run, Pallas kernels for 7% -> 7%
where the time goes in v5:
time: 128 us; the launch traced here: 127 us
  starting transfers between devices  58.4 us (46%)
  waiting for transfers between devices  43 us (34%)
  Pallas kernels  11.1 us (9%)
  local copies, waits for them, and re-layouts  5.69 us (4%)
  other arithmetic  4.08 us (3%)
  matrix products  3.84 us (3%)
  between operations  1.46 us (1%)
    ppermute x24, waiting for transfers between devices, swap(): lax.ppermute(value, axis, [(i, i ^ bit) for i in range(lax.axis_size(axis...  35.9 us
    ppermute x11, starting transfers between devices, outer_swap(): return lax.ppermute(value, 'section', [(0, 1), (1, 0), (2, 3), (3, 2)])  26.9 us
    ppermute x24, starting transfers between devices, swap(): lax.ppermute(value, axis, [(i, i ^ bit) for i in range(lax.axis_size(axis...  25.7 us
    pallas_call x8, Pallas kernels, emit(): pl.pallas_call(functools.partial(store, n_dp, g, f * chunk, shards), out_...  10 us
    ppermute x11, waiting for transfers between devices, outer_swap(): return lax.ppermute(value, 'section', [(0, 1), (1, 0), (2, 3), (3, 2)])  7.06 us
    ppermute x8, starting transfers between devices, middle_swap(): return lax.ppermute(value, 'section', [(1, 2), (2, 1), (0, 0), (3, 3)])  5.72 us
    unnamed x22, local copies, waits for them, and re-layouts  5.64 us
    dot_general x8, matrix products, body(): lax.dot_general(gathered[f], key_grad, (((0,), (0,)), ((), ())), preferre...  2.58 us
  transfers between devices with their start and end apart: 43, of which 16 were waited for; matrix products, arithmetic and copies ran while one was open for 6% of the time, Pallas kernels for 7%

profile of v5, /device:TPU:0, one launch (start us, length us, event | category | flops | bytes accessed | tf_op | source)
XLA Modules:
  0.0 127.5 jit_solution(4283632293553894033)
XLA Ops:
  6.3 2.5 %collective-permute-start.2 = (f32[2,128]{1,0:T(2,128)S(1)}, f32[2,128]{1,0:T(2,128)S(1)}, u32[]{:S(2)}, u32[]{:S(2)}) collective-permute-start(f32[2,128]{1,0:T(2,128)S(1)} %get-tuple-element.110), channel_id=1, source_target_pairs={{0,3},{1,2},{2,1},{3,0},{4,7},{5,6},{6,5},{7,4},{8,11},{9,10},{10,... | collective-permute-start | bytes 3080 | tf_op jit(solution)/shard_map/ppermute | solution.py:16
  9.5 1.7 %collective-permute-start.4 = (bf16[256,256]{1,0:T(8,128)(2,1)}, bf16[256,256]{1,0:T(8,128)(2,1)S(1)}, u32[]{:S(2)}, u32[]{:S(2)}) collective-permute-start(bf16[256,256]{1,0:T(8,128)(2,1)} %param.17), channel_id=1, source_target_pairs={{0,4},{4,0},{1,5},{5,1},{2,6},{6,2},{3,7},{7,3},{8,12},{12,8},{9,1... | collective-permute-start | bytes 393224 | tf_op jit(solution)/shard_map/ppermute | solution.py:16
  14.5 1.6 %collective-permute-done.6 = f32[6,128]{1,0:T(8,128)S(1)} collective-permute-done((f32[6,128]{1,0:T(8,128)S(1)}, f32[6,128]{1,0:T(8,128)S(1)}, u32[]{:S(2)}, u32[]{:S(2)}) %collective-permute-start.6) | collective-permute-done | bytes 3104 | tf_op jit(solution)/shard_map/ppermute | solution.py:16
  16.3 2.7 %collective-permute-done.3 = bf16[256,256]{1,0:T(8,128)(2,1)S(1)} collective-permute-done((bf16[256,256]{1,0:T(8,128)(2,1)S(1)}, bf16[256,256]{1,0:T(8,128)(2,1)S(1)}, u32[]{:S(2)}, u32[]{:S(2)}) %collective-permute-start.3) | collective-permute-done | bytes 131104 | tf_op jit(solution)/shard_map/ppermute | solution.py:16
  20.8 1.6 %collective-permute-start.12 = (bf16[256,512]{1,0:T(8,128)(2,1)S(1)}, bf16[256,512]{1,0:T(8,128)(2,1)S(1)}, u32[]{:S(2)}, u32[]{:S(2)}) collective-permute-start(bf16[256,512]{1,0:T(8,128)(2,1)S(1)} %fusion), channel_id=1, source_target_pairs={{0,8},{8,0},{16,24},{24,16},{1,9},{9,1},{17,25},{25,17},{2,10},{10... | collective-permute-start | bytes 786440 | tf_op jit(solution)/shard_map/ppermute | solution.py:47
  26.2 1.8 %collective-permute-start.14 = (bf16[256,512]{1,0:T(8,128)(2,1)S(1)}, bf16[256,512]{1,0:T(8,128)(2,1)S(1)}, u32[]{:S(2)}, u32[]{:S(2)}) collective-permute-start(bf16[256,512]{1,0:T(8,128)(2,1)S(1)} %fusion.1), channel_id=1, source_target_pairs={{0,8},{8,0},{16,24},{24,16},{1,9},{9,1},{17,25},{25,17},{2,10},{10... | collective-permute-start | bytes 786440 | tf_op jit(solution)/shard_map/ppermute | solution.py:47
  31.3 4.3 %collective-permute-done.14 = bf16[256,512]{1,0:T(8,128)(2,1)S(1)} collective-permute-done((bf16[256,512]{1,0:T(8,128)(2,1)S(1)}, bf16[256,512]{1,0:T(8,128)(2,1)S(1)}, u32[]{:S(2)}, u32[]{:S(2)}) %collective-permute-start.14) | collective-permute-done | bytes 262176 | tf_op jit(solution)/shard_map/ppermute | solution.py:47
  36.6 4.9 %collective-permute-start.17 = (bf16[256,512]{1,0:T(8,128)(2,1)S(1)}, bf16[256,512]{1,0:T(8,128)(2,1)S(1)}, u32[]{:S(2)}, u32[]{:S(2)}) collective-permute-start(bf16[256,512]{1,0:T(8,128)(2,1)S(1)} %get-tuple-element.126), channel_id=1, source_target_pairs={{0,8},{8,0},{16,24},{24,16},{1,9},{9,1},{17,25},{25,17},{2,10},{10... | collective-permute-start | bytes 786440 | tf_op jit(solution)/shard_map/ppermute | solution.py:47
  43.0 5.9 %collective-permute-start.21 = (bf16[256,512]{1,0:T(8,128)(2,1)S(1)}, bf16[256,512]{1,0:T(8,128)(2,1)S(1)}, u32[]{:S(2)}, u32[]{:S(2)}) collective-permute-start(bf16[256,512]{1,0:T(8,128)(2,1)S(1)} %get-tuple-element.130), channel_id=1, source_target_pairs={{0,8},{8,0},{16,24},{24,16},{1,9},{9,1},{17,25},{25,17},{2,10},{10... | collective-permute-start | bytes 786440 | tf_op jit(solution)/shard_map/ppermute | solution.py:47
  51.4 4.2 %collective-permute-start.25 = (bf16[256,512]{1,0:T(8,128)(2,1)S(1)}, bf16[256,512]{1,0:T(8,128)(2,1)S(1)}, u32[]{:S(2)}, u32[]{:S(2)}) collective-permute-start(bf16[256,512]{1,0:T(8,128)(2,1)S(1)} %get-tuple-element.136), channel_id=1, source_target_pairs={{0,8},{8,0},{16,24},{24,16},{1,9},{9,1},{17,25},{25,17},{2,10},{10... | collective-permute-start | bytes 786440 | tf_op jit(solution)/shard_map/ppermute | solution.py:47
  57.1 6.4 %collective-permute-start.22 = (bf16[256,512]{1,0:T(8,128)(2,1)S(1)}, bf16[256,512]{1,0:T(8,128)(2,1)S(1)}, u32[]{:S(2)}, u32[]{:S(2)}) collective-permute-start(bf16[256,512]{1,0:T(8,128)(2,1)S(1)} %get-tuple-element.141), channel_id=1, source_target_pairs={{0,8},{8,0},{16,24},{24,16},{1,9},{9,1},{17,25},{25,17},{2,10},{10... | collective-permute-start | bytes 786440 | tf_op jit(solution)/shard_map/ppermute | solution.py:47
  67.7 4.9 %collective-permute-done.24.refs_1_ = bf16[256,512]{1,0:T(8,128)(2,1)S(1)} collective-permute-done((bf16[256,512]{1,0:T(8,128)(2,1)S(1)}, bf16[256,512]{1,0:T(8,128)(2,1)S(1)}, u32[]{:S(2)}, u32[]{:S(2)}) %collective-permute-start.24) | collective-permute-done | bytes 262176 | tf_op jit(solution)/shard_map/ppermute | solution.py:16
  78.7 2.4 %collective-permute-done.31 = bf16[256,256]{1,0:T(8,128)(2,1)S(1)} collective-permute-done((bf16[256,256]{1,0:T(8,128)(2,1)S(1)}, bf16[256,256]{1,0:T(8,128)(2,1)S(1)}, u32[]{:S(2)}, u32[]{:S(2)}) %collective-permute-start.31) | collective-permute-done | bytes 131104 | tf_op jit(solution)/shard_map/ppermute | solution.py:16
  83.4 2.7 %collective-permute-done.34 = bf16[256,512]{1,0:T(8,128)(2,1)S(1)} collective-permute-done((bf16[256,512]{1,0:T(8,128)(2,1)S(1)}, bf16[256,512]{1,0:T(8,128)(2,1)S(1)}, u32[]{:S(2)}, u32[]{:S(2)}) %collective-permute-start.34) | collective-permute-done | bytes 262176 | tf_op jit(solution)/shard_map/ppermute | solution.py:47
  86.2 2.0 %collective-permute-start.32 = (bf16[256,512]{1,0:T(8,128)(2,1)S(1)}, bf16[256,512]{1,0:T(8,128)(2,1)S(1)}, u32[]{:S(2)}, u32[]{:S(2)}) collective-permute-start(bf16[256,512]{1,0:T(8,128)(2,1)S(1)} %broadcast_select_fusion.4.refs_0_), channel_id=1, source_target_pairs={{0,4},{4,0},{1,5},{5,1},{2,6},{6,2},{3,7},{7,3},{8,12},{12,8},{9,1... | collective-permute-start | bytes 786440 | tf_op jit(solution)/shard_map/ppermute | solution.py:16
  89.3 4.9 %collective-permute-done.33 = bf16[128,256]{1,0:T(8,128)(2,1)S(1)} collective-permute-done((bf16[128,256]{1,0:T(8,128)(2,1)S(1)}, bf16[128,256]{1,0:T(8,128)(2,1)S(1)}, u32[]{:S(2)}, u32[]{:S(2)}) %collective-permute-start.33) | collective-permute-done | bytes 65568 | tf_op jit(solution)/shard_map/ppermute | solution.py:16
  94.3 1.8 %collective-permute-start.36 = (bf16[256,512]{1,0:T(8,128)(2,1)S(1)}, bf16[256,512]{1,0:T(8,128)(2,1)S(1)}, u32[]{:S(2)}, u32[]{:S(2)}) collective-permute-start(bf16[256,512]{1,0:T(8,128)(2,1)S(1)} %broadcast_select_fusion.3.refs_0_), channel_id=1, source_target_pairs={{0,4},{4,0},{1,5},{5,1},{2,6},{6,2},{3,7},{7,3},{8,12},{12,8},{9,1... | collective-permute-start | bytes 786440 | tf_op jit(solution)/shard_map/ppermute | solution.py:16
  98.1 3.5 %collective-permute-done.36.refs_1_ = bf16[256,512]{1,0:T(8,128)(2,1)S(1)} collective-permute-done((bf16[256,512]{1,0:T(8,128)(2,1)S(1)}, bf16[256,512]{1,0:T(8,128)(2,1)S(1)}, u32[]{:S(2)}, u32[]{:S(2)}) %collective-permute-start.36) | collective-permute-done | bytes 262176 | tf_op jit(solution)/shard_map/ppermute | solution.py:16
  101.6 2.1 %collective-permute-start.38 = (bf16[256,512]{1,0:T(8,128)(2,1)S(1)}, bf16[256,512]{1,0:T(8,128)(2,1)S(1)}, u32[]{:S(2)}, u32[]{:S(2)}) collective-permute-start(bf16[256,512]{1,0:T(8,128)(2,1)S(1)} %broadcast_select_fusion.2.refs_0_), channel_id=1, source_target_pairs={{0,4},{4,0},{1,5},{5,1},{2,6},{6,2},{3,7},{7,3},{8,12},{12,8},{9,1... | collective-permute-start | bytes 786440 | tf_op jit(solution)/shard_map/ppermute | solution.py:16
  105.0 5.0 %collective-permute-done.38.refs_1_ = bf16[256,512]{1,0:T(8,128)(2,1)S(1)} collective-permute-done((bf16[256,512]{1,0:T(8,128)(2,1)S(1)}, bf16[256,512]{1,0:T(8,128)(2,1)S(1)}, u32[]{:S(2)}, u32[]{:S(2)}) %collective-permute-start.38) | collective-permute-done | bytes 262176 | tf_op jit(solution)/shard_map/ppermute | solution.py:16
  110.1 2.5 %collective-permute-start.40 = (bf16[256,512]{1,0:T(8,128)(2,1)S(1)}, bf16[256,512]{1,0:T(8,128)(2,1)S(1)}, u32[]{:S(2)}, u32[]{:S(2)}) collective-permute-start(bf16[256,512]{1,0:T(8,128)(2,1)S(1)} %broadcast_select_fusion.1.refs_0_), channel_id=1, source_target_pairs={{0,4},{4,0},{1,5},{5,1},{2,6},{6,2},{3,7},{7,3},{8,12},{12,8},{9,1... | collective-permute-start | bytes 786440 | tf_op jit(solution)/shard_map/ppermute | solution.py:16
  113.9 5.3 %collective-permute-done.40.refs_1_ = bf16[256,512]{1,0:T(8,128)(2,1)S(1)} collective-permute-done((bf16[256,512]{1,0:T(8,128)(2,1)S(1)}, bf16[256,512]{1,0:T(8,128)(2,1)S(1)}, u32[]{:S(2)}, u32[]{:S(2)}) %collective-permute-start.40) | collective-permute-done | bytes 262176 | tf_op jit(solution)/shard_map/ppermute | solution.py:16
  119.2 1.7 %collective-permute-start.42 = (bf16[256,512]{1,0:T(8,128)(2,1)S(1)}, bf16[256,512]{1,0:T(8,128)(2,1)S(1)}, u32[]{:S(2)}, u32[]{:S(2)}) collective-permute-start(bf16[256,512]{1,0:T(8,128)(2,1)S(1)} %broadcast_select_fusion.refs_0_), channel_id=1, source_target_pairs={{0,4},{4,0},{1,5},{5,1},{2,6},{6,2},{3,7},{7,3},{8,12},{12,8},{9,1... | collective-permute-start | bytes 786440 | tf_op jit(solution)/shard_map/ppermute | solution.py:16
  122.9 2.7 %collective-permute-done.42.refs_1_ = bf16[256,512]{1,0:T(8,128)(2,1)S(1)} collective-permute-done((bf16[256,512]{1,0:T(8,128)(2,1)S(1)}, bf16[256,512]{1,0:T(8,128)(2,1)S(1)}, u32[]{:S(2)}, u32[]{:S(2)}) %collective-permute-start.42) | collective-permute-done | bytes 262176 | tf_op jit(solution)/shard_map/ppermute | solution.py:16
  (158 shorter events, 46.7 us)
Async XLA Ops:
  20.8 9.6 %collective-permute-start.12 = (bf16[256,512]{1,0:T(8,128)(2,1)S(1)}, bf16[256,512]{1,0:T(8,128)(2,1)S(1)}, u32[]{:S(2)}, u32[]{:S(2)}) collective-permute-start(bf16[256,512]{1,0:T(8,128)(2,1)S(1)} %fusion), channel_id=1, source_target_pairs={{0,8},{8,0},{16,24},{24,16},{1,9},{9,1},{17,25},{25,17},{2,10},{10... | collective-permute-start | bytes 786440 | tf_op jit(solution)/shard_map/ppermute | solution.py:47
  26.2 9.3 %collective-permute-start.14 = (bf16[256,512]{1,0:T(8,128)(2,1)S(1)}, bf16[256,512]{1,0:T(8,128)(2,1)S(1)}, u32[]{:S(2)}, u32[]{:S(2)}) collective-permute-start(bf16[256,512]{1,0:T(8,128)(2,1)S(1)} %fusion.1), channel_id=1, source_target_pairs={{0,8},{8,0},{16,24},{24,16},{1,9},{9,1},{17,25},{25,17},{2,10},{10... | collective-permute-start | bytes 786440 | tf_op jit(solution)/shard_map/ppermute | solution.py:47
  29.2 12.3 %collective-permute-start.11 = (bf16[256,512]{1,0:T(8,128)(2,1)S(1)}, bf16[256,512]{1,0:T(8,128)(2,1)S(1)}, u32[]{:S(2)}, u32[]{:S(2)}) collective-permute-start(bf16[256,512]{1,0:T(8,128)(2,1)S(1)} %fusion.3), channel_id=1, source_target_pairs={{0,8},{8,0},{16,24},{24,16},{1,9},{9,1},{17,25},{25,17},{2,10},{10... | collective-permute-start | bytes 786440 | tf_op jit(solution)/shard_map/ppermute | solution.py:47
  31.2 11.1 %collective-permute-start.10 = (bf16[512,256]{1,0:T(8,128)(2,1)S(1)}, bf16[512,256]{1,0:T(8,128)(2,1)S(1)}, u32[]{:S(2)}, u32[]{:S(2)}) collective-permute-start(bf16[512,256]{1,0:T(8,128)(2,1)S(1)} %collective-permute-done.9), channel_id=1, source_target_pairs={{0,1},{1,0},{2,3},{3,2},{4,5},{5,4},{6,7},{7,6},{8,9},{9,8},{10,11... | collective-permute-start | bytes 786440 | tf_op jit(solution)/shard_map/ppermute | solution.py:16
  35.6 7.1 %collective-permute-start.18 = (bf16[256,512]{1,0:T(8,128)(2,1)S(1)}, bf16[256,512]{1,0:T(8,128)(2,1)S(1)}, u32[]{:S(2)}, u32[]{:S(2)}) collective-permute-start(bf16[256,512]{1,0:T(8,128)(2,1)S(1)} %reduce-precision_convert_fusion.14), channel_id=1, source_target_pairs={{8,16},{16,8},{0,0},{24,24},{9,17},{17,9},{1,1},{25,25},{10,18},{1... | collective-permute-start | bytes 786440 | tf_op jit(solution)/shard_map/ppermute | solution.py:50
  36.6 12.3 %collective-permute-start.17 = (bf16[256,512]{1,0:T(8,128)(2,1)S(1)}, bf16[256,512]{1,0:T(8,128)(2,1)S(1)}, u32[]{:S(2)}, u32[]{:S(2)}) collective-permute-start(bf16[256,512]{1,0:T(8,128)(2,1)S(1)} %get-tuple-element.126), channel_id=1, source_target_pairs={{0,8},{8,0},{16,24},{24,16},{1,9},{9,1},{17,25},{25,17},{2,10},{10... | collective-permute-start | bytes 786440 | tf_op jit(solution)/shard_map/ppermute | solution.py:47
  41.6 8.3 %collective-permute-start.16 = (bf16[256,512]{1,0:T(8,128)(2,1)S(1)}, bf16[256,512]{1,0:T(8,128)(2,1)S(1)}, u32[]{:S(2)}, u32[]{:S(2)}) collective-permute-start(bf16[256,512]{1,0:T(8,128)(2,1)S(1)} %reduce-precision_convert_fusion.12), channel_id=1, source_target_pairs={{8,16},{16,8},{0,0},{24,24},{9,17},{17,9},{1,1},{25,25},{10,18},{1... | collective-permute-start | bytes 786440 | tf_op jit(solution)/shard_map/ppermute | solution.py:50
  43.0 12.6 %collective-permute-start.21 = (bf16[256,512]{1,0:T(8,128)(2,1)S(1)}, bf16[256,512]{1,0:T(8,128)(2,1)S(1)}, u32[]{:S(2)}, u32[]{:S(2)}) collective-permute-start(bf16[256,512]{1,0:T(8,128)(2,1)S(1)} %get-tuple-element.130), channel_id=1, source_target_pairs={{0,8},{8,0},{16,24},{24,16},{1,9},{9,1},{17,25},{25,17},{2,10},{10... | collective-permute-start | bytes 786440 | tf_op jit(solution)/shard_map/ppermute | solution.py:47
  49.1 7.6 %collective-permute-start.19 = (bf16[256,512]{1,0:T(8,128)(2,1)S(1)}, bf16[256,512]{1,0:T(8,128)(2,1)S(1)}, u32[]{:S(2)}, u32[]{:S(2)}) collective-permute-start(bf16[256,512]{1,0:T(8,128)(2,1)S(1)} %reduce-precision_convert_fusion.10), channel_id=1, source_target_pairs={{8,16},{16,8},{0,0},{24,24},{9,17},{17,9},{1,1},{25,25},{10,18},{1... | collective-permute-start | bytes 786440 | tf_op jit(solution)/shard_map/ppermute | solution.py:50
  51.4 15.4 %collective-permute-start.25 = (bf16[256,512]{1,0:T(8,128)(2,1)S(1)}, bf16[256,512]{1,0:T(8,128)(2,1)S(1)}, u32[]{:S(2)}, u32[]{:S(2)}) collective-permute-start(bf16[256,512]{1,0:T(8,128)(2,1)S(1)} %get-tuple-element.136), channel_id=1, source_target_pairs={{0,8},{8,0},{16,24},{24,16},{1,9},{9,1},{17,25},{25,17},{2,10},{10... | collective-permute-start | bytes 786440 | tf_op jit(solution)/shard_map/ppermute | solution.py:47
  55.7 12.0 %collective-permute-start.23 = (bf16[256,512]{1,0:T(8,128)(2,1)S(1)}, bf16[256,512]{1,0:T(8,128)(2,1)S(1)}, u32[]{:S(2)}, u32[]{:S(2)}) collective-permute-start(bf16[256,512]{1,0:T(8,128)(2,1)S(1)} %reduce-precision_convert_fusion.8), channel_id=1, source_target_pairs={{8,16},{16,8},{0,0},{24,24},{9,17},{17,9},{1,1},{25,25},{10,18},{1... | collective-permute-start | bytes 786440 | tf_op jit(solution)/shard_map/ppermute | solution.py:50
  57.1 18.0 %collective-permute-start.22 = (bf16[256,512]{1,0:T(8,128)(2,1)S(1)}, bf16[256,512]{1,0:T(8,128)(2,1)S(1)}, u32[]{:S(2)}, u32[]{:S(2)}) collective-permute-start(bf16[256,512]{1,0:T(8,128)(2,1)S(1)} %get-tuple-element.141), channel_id=1, source_target_pairs={{0,8},{8,0},{16,24},{24,16},{1,9},{9,1},{17,25},{25,17},{2,10},{10... | collective-permute-start | bytes 786440 | tf_op jit(solution)/shard_map/ppermute | solution.py:47
  63.5 9.1 %collective-permute-start.24 = (bf16[256,512]{1,0:T(8,128)(2,1)S(1)}, bf16[256,512]{1,0:T(8,128)(2,1)S(1)}, u32[]{:S(2)}, u32[]{:S(2)}) collective-permute-start(bf16[256,512]{1,0:T(8,128)(2,1)S(1)} %broadcast_select_fusion.8.refs_0_), channel_id=1, source_target_pairs={{0,4},{4,0},{1,5},{5,1},{2,6},{6,2},{3,7},{7,3},{8,12},{12,8},{9,1... | collective-permute-start | bytes 786440 | tf_op jit(solution)/shard_map/ppermute | solution.py:16
  66.9 10.0 %collective-permute-start.27 = (bf16[256,512]{1,0:T(8,128)(2,1)S(1)}, bf16[256,512]{1,0:T(8,128)(2,1)S(1)}, u32[]{:S(2)}, u32[]{:S(2)}) collective-permute-start(bf16[256,512]{1,0:T(8,128)(2,1)S(1)} %reduce-precision_convert_fusion.6), channel_id=1, source_target_pairs={{8,16},{16,8},{0,0},{24,24},{9,17},{17,9},{1,1},{25,25},{10,18},{1... | collective-permute-start | bytes 786440 | tf_op jit(solution)/shard_map/ppermute | solution.py:50
  77.0 9.2 %collective-permute-start.34 = (bf16[256,512]{1,0:T(8,128)(2,1)S(1)}, bf16[256,512]{1,0:T(8,128)(2,1)S(1)}, u32[]{:S(2)}, u32[]{:S(2)}) collective-permute-start(bf16[256,512]{1,0:T(8,128)(2,1)S(1)} %get-tuple-element.152), channel_id=1, source_target_pairs={{0,8},{8,0},{16,24},{24,16},{1,9},{9,1},{17,25},{25,17},{2,10},{10... | collective-permute-start | bytes 786440 | tf_op jit(solution)/shard_map/ppermute | solution.py:47
  78.0 11.3 %collective-permute-start.26 = (bf16[256,512]{1,0:T(8,128)(2,1)S(1)}, bf16[256,512]{1,0:T(8,128)(2,1)S(1)}, u32[]{:S(2)}, u32[]{:S(2)}) collective-permute-start(bf16[256,512]{1,0:T(8,128)(2,1)S(1)} %reduce-precision_convert_fusion.4), channel_id=1, source_target_pairs={{8,16},{16,8},{0,0},{24,24},{9,17},{17,9},{1,1},{25,25},{10,18},{1... | collective-permute-start | bytes 786440 | tf_op jit(solution)/shard_map/ppermute | solution.py:50
  81.7 16.3 %collective-permute-start.37 = (bf16[256,512]{1,0:T(8,128)(2,1)S(1)}, bf16[256,512]{1,0:T(8,128)(2,1)S(1)}, u32[]{:S(2)}, u32[]{:S(2)}) collective-permute-start(bf16[256,512]{1,0:T(8,128)(2,1)S(1)} %reduce-precision_convert_fusion.3), channel_id=1, source_target_pairs={{0,8},{8,0},{16,24},{24,16},{1,9},{9,1},{17,25},{25,17},{2,10},{10... | collective-permute-start | bytes 786440 | tf_op jit(solution)/shard_map/ppermute | solution.py:47
  86.2 8.1 %collective-permute-start.32 = (bf16[256,512]{1,0:T(8,128)(2,1)S(1)}, bf16[256,512]{1,0:T(8,128)(2,1)S(1)}, u32[]{:S(2)}, u32[]{:S(2)}) collective-permute-start(bf16[256,512]{1,0:T(8,128)(2,1)S(1)} %broadcast_select_fusion.4.refs_0_), channel_id=1, source_target_pairs={{0,4},{4,0},{1,5},{5,1},{2,6},{6,2},{3,7},{7,3},{8,12},{12,8},{9,1... | collective-permute-start | bytes 786440 | tf_op jit(solution)/shard_map/ppermute | solution.py:16
  88.5 9.6 %collective-permute-start.35 = (bf16[256,512]{1,0:T(8,128)(2,1)S(1)}, bf16[256,512]{1,0:T(8,128)(2,1)S(1)}, u32[]{:S(2)}, u32[]{:S(2)}) collective-permute-start(bf16[256,512]{1,0:T(8,128)(2,1)S(1)} %reduce-precision_convert_fusion.2), channel_id=1, source_target_pairs={{8,16},{16,8},{0,0},{24,24},{9,17},{17,9},{1,1},{25,25},{10,18},{1... | collective-permute-start | bytes 786440 | tf_op jit(solution)/shard_map/ppermute | solution.py:50
  94.3 7.2 %collective-permute-start.36 = (bf16[256,512]{1,0:T(8,128)(2,1)S(1)}, bf16[256,512]{1,0:T(8,128)(2,1)S(1)}, u32[]{:S(2)}, u32[]{:S(2)}) collective-permute-start(bf16[256,512]{1,0:T(8,128)(2,1)S(1)} %broadcast_select_fusion.3.refs_0_), channel_id=1, source_target_pairs={{0,4},{4,0},{1,5},{5,1},{2,6},{6,2},{3,7},{7,3},{8,12},{12,8},{9,1... | collective-permute-start | bytes 786440 | tf_op jit(solution)/shard_map/ppermute | solution.py:16
  96.1 8.9 %collective-permute-start.39 = (bf16[256,512]{1,0:T(8,128)(2,1)S(1)}, bf16[256,512]{1,0:T(8,128)(2,1)S(1)}, u32[]{:S(2)}, u32[]{:S(2)}) collective-permute-start(bf16[256,512]{1,0:T(8,128)(2,1)S(1)} %reduce-precision_convert_fusion.1), channel_id=1, source_target_pairs={{0,8},{8,0},{16,24},{24,16},{1,9},{9,1},{17,25},{25,17},{2,10},{10... | collective-permute-start | bytes 786440 | tf_op jit(solution)/shard_map/ppermute | solution.py:47
  101.6 8.4 %collective-permute-start.38 = (bf16[256,512]{1,0:T(8,128)(2,1)S(1)}, bf16[256,512]{1,0:T(8,128)(2,1)S(1)}, u32[]{:S(2)}, u32[]{:S(2)}) collective-permute-start(bf16[256,512]{1,0:T(8,128)(2,1)S(1)} %broadcast_select_fusion.2.refs_0_), channel_id=1, source_target_pairs={{0,4},{4,0},{1,5},{5,1},{2,6},{6,2},{3,7},{7,3},{8,12},{12,8},{9,1... | collective-permute-start | bytes 786440 | tf_op jit(solution)/shard_map/ppermute | solution.py:16
  103.7 10.1 %collective-permute-start.41 = (bf16[256,512]{1,0:T(8,128)(2,1)S(1)}, bf16[256,512]{1,0:T(8,128)(2,1)S(1)}, u32[]{:S(2)}, u32[]{:S(2)}) collective-permute-start(bf16[256,512]{1,0:T(8,128)(2,1)S(1)} %reduce-precision_convert_fusion), channel_id=1, source_target_pairs={{0,8},{8,0},{16,24},{24,16},{1,9},{9,1},{17,25},{25,17},{2,10},{10... | collective-permute-start | bytes 786440 | tf_op jit(solution)/shard_map/ppermute | solution.py:47
  110.1 9.1 %collective-permute-start.40 = (bf16[256,512]{1,0:T(8,128)(2,1)S(1)}, bf16[256,512]{1,0:T(8,128)(2,1)S(1)}, u32[]{:S(2)}, u32[]{:S(2)}) collective-permute-start(bf16[256,512]{1,0:T(8,128)(2,1)S(1)} %broadcast_select_fusion.1.refs_0_), channel_id=1, source_target_pairs={{0,4},{4,0},{1,5},{5,1},{2,6},{6,2},{3,7},{7,3},{8,12},{12,8},{9,1... | collective-permute-start | bytes 786440 | tf_op jit(solution)/shard_map/ppermute | solution.py:16
  (28 other events, 152.9 us)

commit v6 on v4

v6 whole, which is shorter than its diff:
```python
import functools

import jax
import jax.numpy as jnp
from jax import lax
from jax.experimental import pallas as pl
from jax.experimental.pallas import tpu as pltpu
from jax.sharding import PartitionSpec as P

EPSILON = 1e-06
CHUNK_ROWS = 256
LAG = 3


def swap(value, axis, bit):
    return lax.ppermute(value, axis, [(i, i ^ bit) for i in range(lax.axis_size(axis))])


def pick(values, index):
    chosen = values[0]
    for i in range(1, len(values)):
        chosen = jnp.where(index == i, values[i], chosen)
    return chosen


def to_bfloat16(value):
    return lax.reduce_precision(value, 8, 7).astype(jnp.bfloat16)


def add(left, right):
    return to_bfloat16(left.astype(jnp.float32) + right.astype(jnp.float32))


def summed(parts, sums, share, emit, side):
    count = len(parts)
    groups = [[0]] + [list(range(k, min(k + 2, count))) for k in range(1, count - 1, 2)]
    groups += [[count - 1]] if count > 1 and groups[-1][-1] != count - 1 else []
    pending = ()
    if lax.axis_size("section") != 4:
        for group in groups:
            found = [to_bfloat16(lax.psum(parts[k].astype(jnp.float32), "section")) for k in group]
            emit(group, share(found))
        while pending is not None:
            pending = side(pending)
        return
    index = lax.axis_index("section")
    inner = (index == 1) | (index == 2)

    def outer_swap(value):
        return lax.ppermute(value, "section", [(0, 1), (1, 0), (2, 3), (3, 2)])

    def middle_swap(value):
        return lax.ppermute(value, "section", [(1, 2), (2, 1), (0, 0), (3, 3)])

    arriving = {k: outer_swap(parts[k]) for k in range(min(LAG, count))}
    halves, others, totals, results = {}, {}, {}, {}
    shares, recent = [], ()
    for k in range(count + LAG):
        tied = ({i: totals[i] for i in (k - 2,) if i in totals}, {i: sums[i] for i in recent})
        got, tied = lax.optimization_barrier((arriving[k], tied))
        totals.update(tied[0])
        sums.update(tied[1])
        if k < count:
            halves[k] = add(parts[k], got)
            others[k] = middle_swap(halves[k])
        if k >= LAG:
            results[k - LAG] = jnp.where(inner, totals[k - LAG], got)
        if k - 1 in others:
            tied = {i: halves[i] for i in (k - 1, k) if i in halves}
            other, tied = lax.optimization_barrier((others[k - 1], tied))
            halves.update(tied)
            totals[k - 1] = add(halves[k - 1], other)
        following = k - 1 + LAG
        if LAG <= following < count + LAG:
            value = totals[following - LAG]
            if following < count:
                value = jnp.where(inner, value, parts[following])
            arriving[following] = outer_swap(value)
        for group in groups:
            if group[-1] == k - LAG:
                tied = {i: totals[i] for i in (k - 1,) if i in totals}
                ready, tied = lax.optimization_barrier(([results[i] for i in group], tied))
                totals.update(tied)
                shares.append((k + len(group), group, share(ready)))
        now = [entry for entry in shares if entry[0] <= k]
        shares = [entry for entry in shares if entry[0] > k]
        tied = {i: totals[i] for i in (k - 1,) if i in totals}
        waited, pending, tied = lax.optimization_barrier(
            ([entry[2] for entry in now], pending, tied)
        )
        totals.update(tied)
        recent = ()
        for (_, group, _), values in zip(now, waited):
            recent += tuple(group)
            emit(group, values)
        if k >= LAG and pending is not None:
            pending = side(pending)
    for _, group, values in shares:
        values, tied = lax.optimization_barrier((values, {i: sums[i] for i in recent}))
        sums.update(tied)
        recent = tuple(group)
        emit(group, values)
    while pending is not None:
        pending = side(pending)


def prepare(n_dp, block_len, width, rows, squares, *pieces):
    dp = lax.axis_index("dp")
    own_width = rows.shape[1] // n_dp
    per_owner = own_width // width
    for j in range(n_dp):
        for e in range(n_dp):

            @pl.when((dp ^ j) == e)
            def _(j=j, e=e):
                for i in range(per_owner):
                    start = e * own_width + i * width
                    pieces[j * per_owner + i][...] = rows[:, start : start + width]

    lane = lax.broadcasted_iota(jnp.int32, (block_len, block_len), 1)
    diagonal = lane == lax.broadcasted_iota(jnp.int32, (block_len, block_len), 0)
    for b in range(squares.shape[0]):
        total = jnp.zeros((block_len, 128), jnp.float32)
        for start in range(0, rows.shape[1], 128):
            value = rows[b * block_len : (b + 1) * block_len, start : start + 128]
            value = value.astype(jnp.float32)
            total = total + value * value
        total = jnp.sum(total, axis=1, keepdims=True)
        squares[b : b + 1, :] = jnp.sum(jnp.where(diagonal, total, 0.0), axis=0, keepdims=True)


def score(lengths, order, hidden, gain, head, rest):
    block_count, block_len = lengths.shape[0], rest.shape[1]
    position = lax.broadcasted_iota(jnp.int32, (1, block_len), 1)
    values = hidden[...].astype(jnp.float32)
    coefficient = (gain[...].astype(jnp.float32) * head[...].astype(jnp.float32)).reshape(1, -1)
    inverse = lax.rsqrt(jnp.mean(values * values, axis=1, keepdims=True) + EPSILON)
    scores = jnp.sum(values * coefficient, axis=1, keepdims=True) * inverse
    for b in range(block_count):
        rest[b : b + 1, :] = jnp.where(position < lengths[b], scores[b : b + 1], 0.0)
        rest[block_count + b : block_count + b + 1, :] = jnp.full(
            (1, block_len), order[0, b].astype(jnp.float32)
        )


def store(n_dp, g, first, offset, shards, *refs):
    values, gain, weight = refs[0], refs[1], refs[2]
    out, sums, results, semaphores = refs[-4:]
    (_, chunk, width) = results.shape
    far = lax.axis_index("mp") >> 1
    own_width = weight.shape[0] // n_dp
    column = pl.multiple_of((far ^ g) * width, 128)
    stores = []
    lane = lax.broadcasted_iota(jnp.int32, (128, 128), 1)
    diagonal = lane == lax.broadcasted_iota(jnp.int32, (128, 128), 0)
    for e in range(n_dp):
        start = e * own_width + first
        for at in range(0, chunk, 128):
            gains = gain[:, start + at : start + at + 128]
            gains = jnp.sum(jnp.where(diagonal, gains, 0.0), axis=1, keepdims=True)
            total = values[e, offset + at : offset + at + 128, :].astype(jnp.float32) * (1.0 / shards)
            results[e, at : at + 128, :] = total * gains
            weights = weight[start + at : start + at + 128, pl.ds(column, width)]
            total = total * weights.astype(jnp.float32)
            total = jnp.sum(total, axis=1, keepdims=True)
            total = jnp.sum(jnp.where(diagonal, total, 0.0), axis=0, keepdims=True)
            sums[e : e + 1, at : at + 128] = total
        copy = pltpu.make_async_copy(
            results.at[e],
            out.at[pl.ds(start, chunk), pl.ds(column, width)],
            semaphores.at[e],
        )
        copy.start()
        stores.append(copy)
    for copy in stores:
        copy.wait()


def body(
    lengths,
    final_hidden,
    score_gain,
    score_head,
    policy_input,
    block_order,
    norm_gain,
    key_weight,
    key_cotangent,
):
    n_section, n_dp, n_mp = (lax.axis_size(name) for name in ("section", "dp", "mp"))
    dp, mp = lax.axis_index("dp"), lax.axis_index("mp")
    block_count = lengths.shape[0]
    tokens, local_width = policy_input.shape
    block_len = tokens // block_count
    pair = block_count // n_dp
    columns = key_cotangent.shape[1]
    own_width = local_width // n_dp
    chunk = min(CHUNK_ROWS, own_width)
    feature_blocks = own_width // chunk
    n_far = n_mp // 2
    far, core = mp >> 1, mp & 1

    cotangents = [key_cotangent] + [swap(key_cotangent, "dp", j) for j in range(1, n_dp)]
    cotangents = jnp.concatenate(cotangents, axis=0)

    per_owner = feature_blocks
    vmem, smem = pl.BlockSpec(memory_space=pltpu.VMEM), pl.BlockSpec(memory_space=pltpu.SMEM)
    hbm = pl.BlockSpec(memory_space=pltpu.MemorySpace.HBM)
    squares, *pieces = pl.pallas_call(
        functools.partial(prepare, n_dp, block_len, chunk),
        out_shape=[jax.ShapeDtypeStruct((block_count, block_len), jnp.float32)]
        + [jax.ShapeDtypeStruct((tokens, chunk), jnp.bfloat16)] * (n_dp * per_owner),
        in_specs=[vmem],
        out_specs=[vmem] * (1 + n_dp * per_owner),
        compiler_params=pltpu.CompilerParams(vmem_limit_bytes=32 * 2**20),
        name="prepare",
    )(policy_input)
    rest = pl.pallas_call(
        score,
        out_shape=jax.ShapeDtypeStruct((2 * block_count, block_len), jnp.float32),
        in_specs=[smem, smem, vmem, vmem, vmem],
        out_specs=vmem,
        name="score",
    )(lengths, block_order, final_hidden, score_gain, score_head)
    squares = squares + sum(swap(squares, "mp", j) for j in range(1, n_mp))
    inverse = lax.rsqrt(squares / (local_width * n_mp) + EPSILON)
    small = jnp.concatenate([inverse, rest], axis=0)
    small = [small] + [swap(small, "dp", j) for j in range(1, n_dp)]

    parts = []

    def rows(f):
        got = [pieces[f]]
        for j in range(1, n_dp):
            piece = pieces[j * per_owner + f]
            tied = parts if f else small
            piece, tied[0] = lax.optimization_barrier((piece, tied[0]))
            got.append(swap(piece, "dp", j))
        return jnp.concatenate(got, axis=0)

    gathered = []

    def key_gradient(near):
        other = swap(near, "mp", 1)
        low = core == 0
        cotangent = jnp.concatenate(
            [jnp.where(low, near, other), jnp.where(low, other, near)], axis=1
        ).reshape(n_dp, n_dp, pair, block_len, -1)
        found = []
        for j in range(n_dp):
            sender = dp ^ j
            for b in range(block_count):
                slot = small[j][2 * block_count + b][:, None]
                chosen = None
                for e in range(n_dp):
                    for q in range(pair):
                        value = lax.dynamic_index_in_dim(cotangent[e], sender, 0, keepdims=False)[q]
                        at = ((dp ^ e) * pair + q).astype(jnp.float32)
                        chosen = value if chosen is None else jnp.where(slot == at, value, chosen)
                weight = small[j][block_count + b].astype(jnp.bfloat16).astype(jnp.float32)
                key_grad = to_bfloat16(chosen.astype(jnp.float32) * weight[:, None])
                found.append(
                    (key_grad.astype(jnp.float32) * small[j][b][:, None]).astype(jnp.bfloat16)
                )
        return jnp.concatenate(found, axis=0)

    for g in range(n_far):
        near = cotangents
        if g:
            near, parts[0] = lax.optimization_barrier((near, parts[0]))
            near = swap(near, "mp", 2 * g)
        key_grad = key_gradient(near)
        for f in range(feature_blocks):
            if not g:
                gathered.append(rows(f))
            part = lax.dot_general(
                gathered[f],
                key_grad,
                (((0,), (0,)), ((), ())),
                preferred_element_type=jnp.float32,
            )
            parts.append(to_bfloat16(part))
    late_gain, parts[0] = lax.optimization_barrier((norm_gain, parts[0]))
    gain = late_gain.astype(jnp.float32)[None, :]
    shards = n_section * n_dp
    out = []
    sums = {}

    def share(values):
        if n_dp == 2 and len(values) == 1:
            return (values[0], swap(values[0], "dp", 1))
        return (lax.all_gather(jnp.concatenate(values, axis=0), "dp"),)

    def emit(group, values):
        if len(values) == 2:
            values = jnp.stack([pick(values, dp), pick(values, 1 - dp)])
        else:
            (values,) = values
        for i, k in enumerate(group):
            g, f = divmod(k, feature_blocks)
            before = tuple(out)
            result, total = pl.pallas_call(
                functools.partial(store, n_dp, g, f * chunk, i * chunk, shards),
                out_shape=[
                    jax.ShapeDtypeStruct((local_width, n_mp * columns), jnp.float32),
                    jax.ShapeDtypeStruct((n_dp, chunk), jnp.float32),
                ],
                in_specs=[vmem] * 3 + [hbm] * len(before),
                out_specs=[hbm, vmem],
                input_output_aliases={3: 0} if before else {},
                scratch_shapes=[
                    pltpu.VMEM((n_dp, chunk, 2 * columns), jnp.float32),
                    pltpu.SemaphoreType.DMA((n_dp,)),
                ],
                compiler_params=pltpu.CompilerParams(vmem_limit_bytes=32 * 2**20),
                name="store",
            )(values, gain, key_weight, *before)
            out[:] = [result]
            sums[k] = total

    def key_steps():
        yield (inverse,)
        (late_inverse,) = side_values[0]
        normed = policy_input.astype(jnp.float32) * late_inverse.reshape(-1, 1) * gain
        normed = lax.optimization_barrier(normed.astype(jnp.bfloat16))
        partial = jnp.dot(normed, key_weight, preferred_element_type=jnp.float32)
        cut = [partial[:, i * columns : (i + 1) * columns] for i in range(n_mp)]
        yield (partial,)
        (partial,) = side_values[0]
        cut = [partial[:, i * columns : (i + 1) * columns] for i in range(n_mp)]
        own = pick(cut, mp)
        yield (own,) + tuple(
            swap(pick(cut, mp ^ j).astype(jnp.bfloat16), "mp", j) for j in range(1, n_mp)
        )
        own, *others = side_values[0]
        keys = own + sum(other.astype(jnp.float32) for other in others)
        keys = keys.astype(jnp.bfloat16).reshape(block_count, block_len, columns)
        by_slot = []
        for slot in range(block_count):
            chosen = keys[0]
            for b in range(1, block_count):
                chosen = jnp.where(rest[block_count + b][:, None] == slot, keys[b], chosen)
            by_slot.append(chosen)
        by_target = [jnp.concatenate(by_slot[e * pair : (e + 1) * pair]) for e in range(n_dp)]
        yield (pick(by_target, dp),) + tuple(
            swap(pick(by_target, dp ^ j), "dp", j) for j in range(1, n_dp)
        )
        arrived = side_values[0]
        learner_keys.append(jnp.concatenate([pick(arrived, dp ^ a) for a in range(n_dp)], axis=0))

    side_values, learner_keys = [()], []
    steps = key_steps()

    def side(waited):
        side_values[0] = waited
        return next(steps, None)

    summed(parts, sums, share, emit, side)
    grad_gain = [
        sum(sums[g * feature_blocks + f] for g in range(n_far)) for f in range(feature_blocks)
    ]
    grad_gain = jnp.concatenate(grad_gain, axis=1)
    grad_gain = grad_gain.reshape(-1)
    return learner_keys[0], out[0], grad_gain


def solution(mesh):
    placed = (
        P(("section", "dp")),
        P(("section", "dp"), None),
        P(),
        P(),
        P(("section", "dp"), "mp"),
        P(("section", "dp"), None),
        P("mp"),
        P("mp", None),
        P(("section", "dp"), "mp"),
    )
    return jax.shard_map(
        body,
        mesh=mesh,
        in_specs=placed,
        out_specs=(P(("section", "dp"), "mp"), P("mp", None), P("mp")),
        check_vma=False,
    )
```

time: 121 us -> 166 us (1.37)
  waiting for transfers between devices: 30.3 us -> 57.2 us
  between operations: 1.5 us -> 14.6 us
  starting transfers between devices: 63.7 us -> 53 us
  other arithmetic: 4.1 us -> 12 us
  local copies, waits for them, and re-layouts: 5.67 us -> 13.1 us
    all_gather x0 -> x3, waiting for transfers between devices: none -> 33.4 us  [share(): return (lax.all_gather(jnp.concatenate(values, axis=0), 'dp'),)]
    ppermute x24 -> x18, waiting for transfers between devices: 18.3 us -> 7.42 us  [swap(): lax.ppermute(value, axis, [(i, i ^ bit) for i in range(lax.axis_size(axis...]
    unnamed x22 -> x26, local copies, waits for them, and re-layouts: 5.61 us -> 13.1 us
    ppermute x11, starting transfers between devices: 36.8 us -> 30.3 us  [outer_swap(): return lax.ppermute(value, 'section', [(0, 1), (1, 0), (2, 3), (3, 2)])]
    ppermute x24 -> x18, starting transfers between devices: 21.3 us -> 16.9 us  [swap(): lax.ppermute(value, axis, [(i, i ^ bit) for i in range(lax.axis_size(axis...]
    ppermute x11, waiting for transfers between devices: 12 us -> 16.3 us  [outer_swap(): return lax.ppermute(value, 'section', [(0, 1), (1, 0), (2, 3), (3, 2)])]
    concatenate x2 -> x3, other arithmetic: 0.61 us -> 2.46 us  [share(): return (lax.all_gather(jnp.concatenate(values, axis=0), 'dp'),)]
    pallas_call x8 -> x9, Pallas kernels: 10 us -> 11.1 us  [the longest x8 9.53 us: emit(): pl.pallas_call(functools.partial(store, n_dp, g, f * chunk, i * chunk, sh...]
  transfers between devices with their start and end apart: 43 -> 40, of which waited for: 12 -> 13; matrix products, arithmetic and copies ran while one was open for 6% -> 10% of each run, Pallas kernels for 7% -> 6%
where the time goes in v6:
time: 166 us; the launch traced here: 165 us
  waiting for transfers between devices  57.2 us (34%)
  starting transfers between devices  53 us (32%)
  between operations  14.6 us (9%)
  local copies, waits for them, and re-layouts  13.1 us (8%)
  other arithmetic  12 us (7%)
  Pallas kernels  11.4 us (7%)
  matrix products  3.84 us (2%)
    all_gather x3, waiting for transfers between devices, share(): return (lax.all_gather(jnp.concatenate(values, axis=0), 'dp'),)  33.4 us
    ppermute x11, starting transfers between devices, outer_swap(): return lax.ppermute(value, 'section', [(0, 1), (1, 0), (2, 3), (3, 2)])  30.3 us
    ppermute x18, starting transfers between devices, swap(): lax.ppermute(value, axis, [(i, i ^ bit) for i in range(lax.axis_size(axis...  16.9 us
    ppermute x11, waiting for transfers between devices, outer_swap(): return lax.ppermute(value, 'section', [(0, 1), (1, 0), (2, 3), (3, 2)])  16.3 us
    unnamed x26, local copies, waits for them, and re-layouts  13.1 us
    pallas_call x8, Pallas kernels, emit(): pl.pallas_call(functools.partial(store, n_dp, g, f * chunk, i * chunk, sh...  9.53 us
    ppermute x18, waiting for transfers between devices, swap(): lax.ppermute(value, axis, [(i, i ^ bit) for i in range(lax.axis_size(axis...  7.42 us
    ppermute x8, starting transfers between devices, middle_swap(): return lax.ppermute(value, 'section', [(1, 2), (2, 1), (0, 0), (3, 3)])  5.41 us
  transfers between devices with their start and end apart: 40, of which 13 were waited for; matrix products, arithmetic and copies ran while one was open for 10% of the time, Pallas kernels for 6%

profile of v6, /device:TPU:0, one launch (start us, length us, event | category | flops | bytes accessed | tf_op | source)
XLA Modules:
  0.0 165.2 jit_solution(8313392017696252288)
XLA Ops:
  9.3 2.6 %collective-permute-start.2 = (f32[2,128]{1,0:T(2,128)S(1)}, f32[2,128]{1,0:T(2,128)S(1)}, u32[]{:S(2)}, u32[]{:S(2)}) collective-permute-start(f32[2,128]{1,0:T(2,128)S(1)} %get-tuple-element.119), channel_id=1, source_target_pairs={{0,2},{1,3},{2,0},{3,1},{4,6},{5,7},{6,4},{7,5},{8,10},{9,11},{10,... | collective-permute-start | bytes 3080 | tf_op jit(solution)/shard_map/ppermute | solution.py:16
  12.0 1.7 %collective-permute-start = (bf16[256,256]{1,0:T(8,128)(2,1)}, bf16[256,256]{1,0:T(8,128)(2,1)S(1)}, u32[]{:S(2)}, u32[]{:S(2)}) collective-permute-start(bf16[256,256]{1,0:T(8,128)(2,1)} %param.17), channel_id=1, source_target_pairs={{0,4},{4,0},{1,5},{5,1},{2,6},{6,2},{3,7},{7,3},{8,12},{12,8},{9,1... | collective-permute-start | bytes 393224 | tf_op jit(solution)/shard_map/ppermute | solution.py:16
  19.4 1.8 %collective-permute-start.4 = (bf16[256,256]{1,0:T(8,128)(2,1)S(1)}, bf16[256,256]{1,0:T(8,128)(2,1)S(1)}, u32[]{:S(2)}, u32[]{:S(2)}) collective-permute-start(bf16[256,256]{1,0:T(8,128)(2,1)S(1)} %get-tuple-element.120), channel_id=1, source_target_pairs={{0,4},{4,0},{1,5},{5,1},{2,6},{6,2},{3,7},{7,3},{8,12},{12,8},{9,1... | collective-permute-start | bytes 393224 | tf_op jit(solution)/shard_map/ppermute | solution.py:16
  22.8 1.9 %collective-permute-done.4 = bf16[256,256]{1,0:T(8,128)(2,1)S(1)} collective-permute-done((bf16[256,256]{1,0:T(8,128)(2,1)S(1)}, bf16[256,256]{1,0:T(8,128)(2,1)S(1)}, u32[]{:S(2)}, u32[]{:S(2)}) %collective-permute-start.4) | collective-permute-done | bytes 131104 | tf_op jit(solution)/shard_map/ppermute | solution.py:16
  25.4 1.7 %collective-permute-start.14 = (bf16[256,256]{1,0:T(8,128)(2,1)S(1)}, bf16[256,256]{1,0:T(8,128)(2,1)S(1)}, u32[]{:S(2)}, u32[]{:S(2)}) collective-permute-start(bf16[256,256]{1,0:T(8,128)(2,1)S(1)} %get-tuple-element.134), channel_id=1, source_target_pairs={{0,4},{4,0},{1,5},{5,1},{2,6},{6,2},{3,7},{7,3},{8,12},{12,8},{9,1... | collective-permute-start | bytes 393224 | tf_op jit(solution)/shard_map/ppermute | solution.py:16
  27.5 1.8 %collective-permute-start.7 = (bf16[256,512]{1,0:T(8,128)(2,1)S(1)}, bf16[256,512]{1,0:T(8,128)(2,1)S(1)}, u32[]{:S(2)}, u32[]{:S(2)}) collective-permute-start(bf16[256,512]{1,0:T(8,128)(2,1)S(1)} %fusion), channel_id=1, source_target_pairs={{0,8},{8,0},{16,24},{24,16},{1,9},{9,1},{17,25},{25,17},{2,10},{10... | collective-permute-start | bytes 786440 | tf_op jit(solution)/shard_map/ppermute | solution.py:50
  35.0 1.8 %collective-permute-start.10 = (bf16[256,512]{1,0:T(8,128)(2,1)S(1)}, bf16[256,512]{1,0:T(8,128)(2,1)S(1)}, u32[]{:S(2)}, u32[]{:S(2)}) collective-permute-start(bf16[256,512]{1,0:T(8,128)(2,1)S(1)} %fusion.1), channel_id=1, source_target_pairs={{0,8},{8,0},{16,24},{24,16},{1,9},{9,1},{17,25},{25,17},{2,10},{10... | collective-permute-start | bytes 786440 | tf_op jit(solution)/shard_map/ppermute | solution.py:50
  38.0 8.1 %collective-permute-done.10 = bf16[256,512]{1,0:T(8,128)(2,1)S(1)} collective-permute-done((bf16[256,512]{1,0:T(8,128)(2,1)S(1)}, bf16[256,512]{1,0:T(8,128)(2,1)S(1)}, u32[]{:S(2)}, u32[]{:S(2)}) %collective-permute-start.10) | collective-permute-done | bytes 262176 | tf_op jit(solution)/shard_map/ppermute | solution.py:50
  48.5 4.5 %collective-permute-start.12 = (bf16[256,512]{1,0:T(8,128)(2,1)S(1)}, bf16[256,512]{1,0:T(8,128)(2,1)S(1)}, u32[]{:S(2)}, u32[]{:S(2)}) collective-permute-start(bf16[256,512]{1,0:T(8,128)(2,1)S(1)} %get-tuple-element.233), channel_id=1, source_target_pairs={{0,8},{8,0},{16,24},{24,16},{1,9},{9,1},{17,25},{25,17},{2,10},{10... | collective-permute-start | bytes 786440 | tf_op jit(solution)/shard_map/ppermute | solution.py:50
  54.1 2.9 %collective-permute-start.18 = (bf16[256,512]{1,0:T(8,128)(2,1)S(1)}, bf16[256,512]{1,0:T(8,128)(2,1)S(1)}, u32[]{:S(2)}, u32[]{:S(2)}) collective-permute-start(bf16[256,512]{1,0:T(8,128)(2,1)S(1)} %get-tuple-element.231), channel_id=1, source_target_pairs={{0,8},{8,0},{16,24},{24,16},{1,9},{9,1},{17,25},{25,17},{2,10},{10... | collective-permute-start | bytes 786440 | tf_op jit(solution)/shard_map/ppermute | solution.py:50
  57.0 3.0 %collective-permute-done.12 = bf16[256,512]{1,0:T(8,128)(2,1)S(1)} collective-permute-done((bf16[256,512]{1,0:T(8,128)(2,1)S(1)}, bf16[256,512]{1,0:T(8,128)(2,1)S(1)}, u32[]{:S(2)}, u32[]{:S(2)}) %collective-permute-start.12) | collective-permute-done | bytes 262176 | tf_op jit(solution)/shard_map/ppermute | solution.py:50
  62.0 3.0 %collective-permute-start.20 = (bf16[256,512]{1,0:T(8,128)(2,1)S(1)}, bf16[256,512]{1,0:T(8,128)(2,1)S(1)}, u32[]{:S(2)}, u32[]{:S(2)}) collective-permute-start(bf16[256,512]{1,0:T(8,128)(2,1)S(1)} %get-tuple-element.229), channel_id=1, source_target_pairs={{0,8},{8,0},{16,24},{24,16},{1,9},{9,1},{17,25},{25,17},{2,10},{10... | collective-permute-start | bytes 786440 | tf_op jit(solution)/shard_map/ppermute | solution.py:50
  71.0 3.8 %collective-permute-start.28 = (bf16[256,512]{1,0:T(8,128)(2,1)S(1)}, bf16[256,512]{1,0:T(8,128)(2,1)S(1)}, u32[]{:S(2)}, u32[]{:S(2)}) collective-permute-start(bf16[256,512]{1,0:T(8,128)(2,1)S(1)} %get-tuple-element.227), channel_id=1, source_target_pairs={{0,8},{8,0},{16,24},{24,16},{1,9},{9,1},{17,25},{25,17},{2,10},{10... | collective-permute-start | bytes 786440 | tf_op jit(solution)/shard_map/ppermute | solution.py:50
  80.2 2.6 %collective-permute-start.30 = (bf16[256,512]{1,0:T(8,128)(2,1)S(1)}, bf16[256,512]{1,0:T(8,128)(2,1)S(1)}, u32[]{:S(2)}, u32[]{:S(2)}) collective-permute-start(bf16[256,512]{1,0:T(8,128)(2,1)S(1)} %get-tuple-element.225), channel_id=1, source_target_pairs={{0,8},{8,0},{16,24},{24,16},{1,9},{9,1},{17,25},{25,17},{2,10},{10... | collective-permute-start | bytes 786440 | tf_op jit(solution)/shard_map/ppermute | solution.py:50
  83.6 2.8 %collective-permute-start.36 = (bf16[256,512]{1,0:T(8,128)(2,1)S(1)}, bf16[256,512]{1,0:T(8,128)(2,1)S(1)}, u32[]{:S(2)}, u32[]{:S(2)}) collective-permute-start(bf16[256,512]{1,0:T(8,128)(2,1)S(1)} %reduce-precision_convert_fusion.3), channel_id=1, source_target_pairs={{0,8},{8,0},{16,24},{24,16},{1,9},{9,1},{17,25},{25,17},{2,10},{10... | collective-permute-start | bytes 786440 | tf_op jit(solution)/shard_map/ppermute | solution.py:50
  87.6 2.4 %collective-permute-done.30 = bf16[256,512]{1,0:T(8,128)(2,1)S(1)} collective-permute-done((bf16[256,512]{1,0:T(8,128)(2,1)S(1)}, bf16[256,512]{1,0:T(8,128)(2,1)S(1)}, u32[]{:S(2)}, u32[]{:S(2)}) %collective-permute-start.30) | collective-permute-done | bytes 262176 | tf_op jit(solution)/shard_map/ppermute | solution.py:50
  90.8 4.1 %collective-permute-start.32 = (bf16[256,512]{1,0:T(8,128)(2,1)S(1)}, bf16[256,512]{1,0:T(8,128)(2,1)S(1)}, u32[]{:S(2)}, u32[]{:S(2)}) collective-permute-start(bf16[256,512]{1,0:T(8,128)(2,1)S(1)} %reduce-precision_convert_fusion.1), channel_id=1, source_target_pairs={{0,8},{8,0},{16,24},{24,16},{1,9},{9,1},{17,25},{25,17},{2,10},{10... | collective-permute-start | bytes 786440 | tf_op jit(solution)/shard_map/ppermute | solution.py:50
  98.0 2.2 %collective-permute-done.32 = bf16[256,512]{1,0:T(8,128)(2,1)S(1)} collective-permute-done((bf16[256,512]{1,0:T(8,128)(2,1)S(1)}, bf16[256,512]{1,0:T(8,128)(2,1)S(1)}, u32[]{:S(2)}, u32[]{:S(2)}) %collective-permute-start.32) | collective-permute-done | bytes 262176 | tf_op jit(solution)/shard_map/ppermute | solution.py:50
  100.2 2.0 %collective-permute-done.29 = bf16[128,256]{1,0:T(8,128)(2,1)S(1)} collective-permute-done((bf16[128,256]{1,0:T(8,128)(2,1)S(1)}, bf16[128,256]{1,0:T(8,128)(2,1)S(1)}, u32[]{:S(2)}, u32[]{:S(2)}) %collective-permute-start.29) | collective-permute-done | bytes 65568 | tf_op jit(solution)/shard_map/ppermute | solution.py:16
  102.5 2.2 %copy-done.1 = bf16[2048,1024]{1,0:T(8,128)(2,1)S(1)} copy-done((bf16[2048,1024]{1,0:T(8,128)(2,1)S(1)}, bf16[2048,1024]{1,0:T(8,128)(2,1)}, u32[]{:S(2)}) %copy-start.1) | copy-done | bytes 4194328
  110.8 14.6 %all-gather.9.cloned.1.call-done = bf16[1024,512]{1,0:T(8,128)(2,1)} async-done(((bf16[512,512]{1,0:T(8,128)(2,1)}), bf16[1024,512]{1,0:T(8,128)(2,1)}) %all-gather.9.cloned.1.call-update) | async-done | bytes 1048592 | tf_op jit(solution)/shard_map/all_gather | solution.py:292
  125.4 2.2 %copy-done.2 = bf16[2048,1024]{1,0:T(8,128)(2,1)S(1)} copy-done((bf16[2048,1024]{1,0:T(8,128)(2,1)S(1)}, bf16[2048,1024]{1,0:T(8,128)(2,1)}, u32[]{:S(2)}) %copy-start.2) | copy-done | bytes 4194328
  132.3 18.5 %all-gather.11.cloned.1.call-done = bf16[1024,512]{1,0:T(8,128)(2,1)} async-done(((bf16[512,512]{1,0:T(8,128)(2,1)}), bf16[1024,512]{1,0:T(8,128)(2,1)}) %all-gather.11.cloned.1.call-update) | async-done | bytes 1048592 | tf_op jit(solution)/shard_map/all_gather | solution.py:292
  150.8 2.2 %copy-done.3 = bf16[2048,1024]{1,0:T(8,128)(2,1)S(1)} copy-done((bf16[2048,1024]{1,0:T(8,128)(2,1)S(1)}, bf16[2048,1024]{1,0:T(8,128)(2,1)}, u32[]{:S(2)}) %copy-start.3) | copy-done | bytes 4194328
  (174 shorter events, 56.2 us)
Async XLA Ops:
  7.2 95.3 %all-gather.7.cloned.1.call-start = ((), (), s32[]{:S(2)}) async-start(), calls=%async_computation | async-start | bytes 1572864 | tf_op jit(solution)/shard_map/all_gather | solution.py:292
  8.8 9.5 %collective-permute-start.1 = (f32[2,128]{1,0:T(2,128)S(1)}, f32[2,128]{1,0:T(2,128)S(1)}, u32[]{:S(2)}, u32[]{:S(2)}) collective-permute-start(f32[2,128]{1,0:T(2,128)S(1)} %get-tuple-element.119), channel_id=1, source_target_pairs={{0,1},{1,0},{2,3},{3,2},{4,5},{5,4},{6,7},{7,6},{8,9},{9,8},{10,11... | collective-permute-start | bytes 3080 | tf_op jit(solution)/shard_map/ppermute | solution.py:16
  9.3 9.0 %collective-permute-start.2 = (f32[2,128]{1,0:T(2,128)S(1)}, f32[2,128]{1,0:T(2,128)S(1)}, u32[]{:S(2)}, u32[]{:S(2)}) collective-permute-start(f32[2,128]{1,0:T(2,128)S(1)} %get-tuple-element.119), channel_id=1, source_target_pairs={{0,2},{1,3},{2,0},{3,1},{4,6},{5,7},{6,4},{7,5},{8,10},{9,11},{10,... | collective-permute-start | bytes 3080 | tf_op jit(solution)/shard_map/ppermute | solution.py:16
  12.0 10.7 %collective-permute-start = (bf16[256,256]{1,0:T(8,128)(2,1)}, bf16[256,256]{1,0:T(8,128)(2,1)S(1)}, u32[]{:S(2)}, u32[]{:S(2)}) collective-permute-start(bf16[256,256]{1,0:T(8,128)(2,1)} %param.17), channel_id=1, source_target_pairs={{0,4},{4,0},{1,5},{5,1},{2,6},{6,2},{3,7},{7,3},{8,12},{12,8},{9,1... | collective-permute-start | bytes 393224 | tf_op jit(solution)/shard_map/ppermute | solution.py:16
  27.5 9.3 %collective-permute-start.7 = (bf16[256,512]{1,0:T(8,128)(2,1)S(1)}, bf16[256,512]{1,0:T(8,128)(2,1)S(1)}, u32[]{:S(2)}, u32[]{:S(2)}) collective-permute-start(bf16[256,512]{1,0:T(8,128)(2,1)S(1)} %fusion), channel_id=1, source_target_pairs={{0,8},{8,0},{16,24},{24,16},{1,9},{9,1},{17,25},{25,17},{2,10},{10... | collective-permute-start | bytes 786440 | tf_op jit(solution)/shard_map/ppermute | solution.py:50
  32.6 15.4 %collective-permute-start.15 = (bf16[256,512]{1,0:T(8,128)(2,1)S(1)}, bf16[256,512]{1,0:T(8,128)(2,1)S(1)}, u32[]{:S(2)}, u32[]{:S(2)}) collective-permute-start(bf16[256,512]{1,0:T(8,128)(2,1)S(1)} %fusion.3), channel_id=1, source_target_pairs={{0,8},{8,0},{16,24},{24,16},{1,9},{9,1},{17,25},{25,17},{2,10},{10... | collective-permute-start | bytes 786440 | tf_op jit(solution)/shard_map/ppermute | solution.py:50
  35.0 11.1 %collective-permute-start.10 = (bf16[256,512]{1,0:T(8,128)(2,1)S(1)}, bf16[256,512]{1,0:T(8,128)(2,1)S(1)}, u32[]{:S(2)}, u32[]{:S(2)}) collective-permute-start(bf16[256,512]{1,0:T(8,128)(2,1)S(1)} %fusion.1), channel_id=1, source_target_pairs={{0,8},{8,0},{16,24},{24,16},{1,9},{9,1},{17,25},{25,17},{2,10},{10... | collective-permute-start | bytes 786440 | tf_op jit(solution)/shard_map/ppermute | solution.py:50
  36.9 10.0 %collective-permute-start.8 = (bf16[256,512]{1,0:T(8,128)(2,1)S(1)}, bf16[256,512]{1,0:T(8,128)(2,1)S(1)}, u32[]{:S(2)}, u32[]{:S(2)}) collective-permute-start(bf16[256,512]{1,0:T(8,128)(2,1)S(1)} %reduce-precision_convert_fusion.15), channel_id=1, source_target_pairs={{8,16},{16,8},{0,0},{24,24},{9,17},{17,9},{1,1},{25,25},{10,18},{1... | collective-permute-start | bytes 786440 | tf_op jit(solution)/shard_map/ppermute | solution.py:53
  37.6 9.3 %collective-permute-start.17 = (bf16[512,256]{1,0:T(8,128)(2,1)S(1)}, bf16[512,256]{1,0:T(8,128)(2,1)S(1)}, u32[]{:S(2)}, u32[]{:S(2)}) collective-permute-start(bf16[512,256]{1,0:T(8,128)(2,1)S(1)} %collective-permute-done.16), channel_id=1, source_target_pairs={{0,1},{1,0},{2,3},{3,2},{4,5},{5,4},{6,7},{7,6},{8,9},{9,8},{10,11... | collective-permute-start | bytes 786440 | tf_op jit(solution)/shard_map/ppermute | solution.py:16
  48.5 11.5 %collective-permute-start.12 = (bf16[256,512]{1,0:T(8,128)(2,1)S(1)}, bf16[256,512]{1,0:T(8,128)(2,1)S(1)}, u32[]{:S(2)}, u32[]{:S(2)}) collective-permute-start(bf16[256,512]{1,0:T(8,128)(2,1)S(1)} %get-tuple-element.233), channel_id=1, source_target_pairs={{0,8},{8,0},{16,24},{24,16},{1,9},{9,1},{17,25},{25,17},{2,10},{10... | collective-permute-start | bytes 786440 | tf_op jit(solution)/shard_map/ppermute | solution.py:50
  54.1 10.9 %collective-permute-start.18 = (bf16[256,512]{1,0:T(8,128)(2,1)S(1)}, bf16[256,512]{1,0:T(8,128)(2,1)S(1)}, u32[]{:S(2)}, u32[]{:S(2)}) collective-permute-start(bf16[256,512]{1,0:T(8,128)(2,1)S(1)} %get-tuple-element.231), channel_id=1, source_target_pairs={{0,8},{8,0},{16,24},{24,16},{1,9},{9,1},{17,25},{25,17},{2,10},{10... | collective-permute-start | bytes 786440 | tf_op jit(solution)/shard_map/ppermute | solution.py:50
  65.0 10.5 %collective-permute-start.23 = (bf16[256,512]{1,0:T(8,128)(2,1)S(1)}, bf16[256,512]{1,0:T(8,128)(2,1)S(1)}, u32[]{:S(2)}, u32[]{:S(2)}) collective-permute-start(bf16[256,512]{1,0:T(8,128)(2,1)S(1)} %reduce-precision_convert_fusion.8), channel_id=1, source_target_pairs={{8,16},{16,8},{0,0},{24,24},{9,17},{17,9},{1,1},{25,25},{10,18},{1... | collective-permute-start | bytes 786440 | tf_op jit(solution)/shard_map/ppermute | solution.py:53
  71.0 9.2 %collective-permute-start.28 = (bf16[256,512]{1,0:T(8,128)(2,1)S(1)}, bf16[256,512]{1,0:T(8,128)(2,1)S(1)}, u32[]{:S(2)}, u32[]{:S(2)}) collective-permute-start(bf16[256,512]{1,0:T(8,128)(2,1)S(1)} %get-tuple-element.227), channel_id=1, source_target_pairs={{0,8},{8,0},{16,24},{24,16},{1,9},{9,1},{17,25},{25,17},{2,10},{10... | collective-permute-start | bytes 786440 | tf_op jit(solution)/shard_map/ppermute | solution.py:50
  74.8 8.0 %collective-permute-start.27 = (bf16[256,512]{1,0:T(8,128)(2,1)S(1)}, bf16[256,512]{1,0:T(8,128)(2,1)S(1)}, u32[]{:S(2)}, u32[]{:S(2)}) collective-permute-start(bf16[256,512]{1,0:T(8,128)(2,1)S(1)} %reduce-precision_convert_fusion.6), channel_id=1, source_target_pairs={{8,16},{16,8},{0,0},{24,24},{9,17},{17,9},{1,1},{25,25},{10,18},{1... | collective-permute-start | bytes 786440 | tf_op jit(solution)/shard_map/ppermute | solution.py:53
  76.4 10.1 %collective-permute-start.26 = (bf16[256,256]{1,0:T(8,128)(2,1)S(1)}, bf16[256,256]{1,0:T(8,128)(2,1)}, u32[]{:S(2)}, u32[]{:S(2)}) collective-permute-start(bf16[256,256]{1,0:T(8,128)(2,1)S(1)} %get-tuple-element.235), channel_id=1, source_target_pairs={{0,3},{1,2},{2,1},{3,0},{4,7},{5,6},{6,5},{7,4},{8,11},{9,10},{10,... | collective-permute-start | bytes 393224 | tf_op jit(solution)/shard_map/ppermute | solution.py:16
  78.5 7.9 %collective-permute-start.25 = (bf16[256,256]{1,0:T(8,128)(2,1)}, bf16[256,256]{1,0:T(8,128)(2,1)}, u32[]{:S(2)}, u32[]{:S(2)}) collective-permute-start(bf16[256,256]{1,0:T(8,128)(2,1)} %select_convert_fusion.1), channel_id=1, source_target_pairs={{0,2},{1,3},{2,0},{3,1},{4,6},{5,7},{6,4},{7,5},{8,10},{9,11},{10,... | collective-permute-start | bytes 393224 | tf_op jit(solution)/shard_map/ppermute | solution.py:16
  80.0 45.3 %all-gather.9.cloned.1.call-start = ((), (), s32[]{:S(2)}) async-start(), calls=%async_computation.1 | async-start | bytes 1572864 | tf_op jit(solution)/shard_map/all_gather | solution.py:292
  80.2 9.7 %collective-permute-start.30 = (bf16[256,512]{1,0:T(8,128)(2,1)S(1)}, bf16[256,512]{1,0:T(8,128)(2,1)S(1)}, u32[]{:S(2)}, u32[]{:S(2)}) collective-permute-start(bf16[256,512]{1,0:T(8,128)(2,1)S(1)} %get-tuple-element.225), channel_id=1, source_target_pairs={{0,8},{8,0},{16,24},{24,16},{1,9},{9,1},{17,25},{25,17},{2,10},{10... | collective-permute-start | bytes 786440 | tf_op jit(solution)/shard_map/ppermute | solution.py:50
  83.6 24.7 %collective-permute-start.36 = (bf16[256,512]{1,0:T(8,128)(2,1)S(1)}, bf16[256,512]{1,0:T(8,128)(2,1)S(1)}, u32[]{:S(2)}, u32[]{:S(2)}) collective-permute-start(bf16[256,512]{1,0:T(8,128)(2,1)S(1)} %reduce-precision_convert_fusion.3), channel_id=1, source_target_pairs={{0,8},{8,0},{16,24},{24,16},{1,9},{9,1},{17,25},{25,17},{2,10},{10... | collective-permute-start | bytes 786440 | tf_op jit(solution)/shard_map/ppermute | solution.py:50
  90.0 8.0 %collective-permute-start.33 = (bf16[256,512]{1,0:T(8,128)(2,1)S(1)}, bf16[256,512]{1,0:T(8,128)(2,1)S(1)}, u32[]{:S(2)}, u32[]{:S(2)}) collective-permute-start(bf16[256,512]{1,0:T(8,128)(2,1)S(1)} %reduce-precision_convert_fusion.2), channel_id=1, source_target_pairs={{8,16},{16,8},{0,0},{24,24},{9,17},{17,9},{1,1},{25,25},{10,18},{1... | collective-permute-start | bytes 786440 | tf_op jit(solution)/shard_map/ppermute | solution.py:53
  90.8 9.4 %collective-permute-start.32 = (bf16[256,512]{1,0:T(8,128)(2,1)S(1)}, bf16[256,512]{1,0:T(8,128)(2,1)S(1)}, u32[]{:S(2)}, u32[]{:S(2)}) collective-permute-start(bf16[256,512]{1,0:T(8,128)(2,1)S(1)} %reduce-precision_convert_fusion.1), channel_id=1, source_target_pairs={{0,8},{8,0},{16,24},{24,16},{1,9},{9,1},{17,25},{25,17},{2,10},{10... | collective-permute-start | bytes 786440 | tf_op jit(solution)/shard_map/ppermute | solution.py:50
  95.8 55.1 %all-gather.11.cloned.1.call-start = ((), (), s32[]{:S(2)}) async-start(), calls=%async_computation.2 | async-start | bytes 1572864 | tf_op jit(solution)/shard_map/all_gather | solution.py:292
  109.2 22.0 %collective-permute-start.34 = (bf16[256,512]{1,0:T(8,128)(2,1)S(1)}, bf16[256,512]{1,0:T(8,128)(2,1)S(1)}, u32[]{:S(2)}, u32[]{:S(2)}) collective-permute-start(bf16[256,512]{1,0:T(8,128)(2,1)S(1)} %reduce-precision_convert_fusion), channel_id=1, source_target_pairs={{0,8},{8,0},{16,24},{24,16},{1,9},{9,1},{17,25},{25,17},{2,10},{10... | collective-permute-start | bytes 786440 | tf_op jit(solution)/shard_map/ppermute | solution.py:50
  131.2 25.4 %collective-permute-start.35 = (bf16[256,512]{1,0:T(8,128)(2,1)S(1)}, bf16[256,512]{1,0:T(8,128)(2,1)S(1)}, u32[]{:S(2)}, u32[]{:S(2)}) collective-permute-start(bf16[256,512]{1,0:T(8,128)(2,1)S(1)} %broadcast_select_fusion.6), channel_id=1, source_target_pairs={{0,4},{4,0},{1,5},{5,1},{2,6},{6,2},{3,7},{7,3},{8,12},{12,8},{9,1... | collective-permute-start | bytes 786440 | tf_op jit(solution)/shard_map/ppermute | solution.py:16
  (26 other events, 153.6 us)
Sparse Core Ops, SparseCore 0:
  80.2 22.2 all-gather.6
  104.0 21.2 all-gather.8
  126.9 23.8 all-gather.10

commit v7 on v6

--- a/solution.py
+++ b/solution.py
@@ -31,7 +31,15 @@
     return to_bfloat16(left.astype(jnp.float32) + right.astype(jnp.float32))
 
 
-def summed(parts, sums, share, emit, side):
+def end_swap(value):
+    return lax.ppermute(value, "section", [(0, 1), (1, 0), (2, 3), (3, 2)])
+
+
+def middle_swap(value):
+    return lax.ppermute(value, "section", [(1, 2), (2, 1), (0, 0), (3, 3)])
+
+
+def summed(parts, arriving, sums, share, emit, side):
     count = len(parts)
     groups = [[0]] + [list(range(k, min(k + 2, count))) for k in range(1, count - 1, 2)]
     groups += [[count - 1]] if count > 1 and groups[-1][-1] != count - 1 else []
@@ -46,13 +54,6 @@
     index = lax.axis_index("section")
     inner = (index == 1) | (index == 2)
 
-    def outer_swap(value):
-        return lax.ppermute(value, "section", [(0, 1), (1, 0), (2, 3), (3, 2)])
-
-    def middle_swap(value):
-        return lax.ppermute(value, "section", [(1, 2), (2, 1), (0, 0), (3, 3)])
-
-    arriving = {k: outer_swap(parts[k]) for k in range(min(LAG, count))}
     halves, others, totals, results = {}, {}, {}, {}
     shares, recent = [], ()
     for k in range(count + LAG):
@@ -75,7 +76,7 @@
             value = totals[following - LAG]
             if following < count:
                 value = jnp.where(inner, value, parts[following])
-            arriving[following] = outer_swap(value)
+            arriving[following] = end_swap(value)
         for group in groups:
             if group[-1] == k - LAG:
                 tied = {i: totals[i] for i in (k - 1,) if i in totals}
@@ -104,19 +105,7 @@
         pending = side(pending)
 
 
-def prepare(n_dp, block_len, width, rows, squares, *pieces):
-    dp = lax.axis_index("dp")
-    own_width = rows.shape[1] // n_dp
-    per_owner = own_width // width
-    for j in range(n_dp):
-        for e in range(n_dp):
-
-            @pl.when((dp ^ j) == e)
-            def _(j=j, e=e):
-                for i in range(per_owner):
-                    start = e * own_width + i * width
-                    pieces[j * per_owner + i][...] = rows[:, start : start + width]
-
+def square(block_len, rows, squares):
     lane = lax.broadcasted_iota(jnp.int32, (block_len, block_len), 1)
     diagonal = lane == lax.broadcasted_iota(jnp.int32, (block_len, block_len), 0)
     for b in range(squares.shape[0]):
@@ -137,10 +126,47 @@
     inverse = lax.rsqrt(jnp.mean(values * values, axis=1, keepdims=True) + EPSILON)
     scores = jnp.sum(values * coefficient, axis=1, keepdims=True) * inverse
     for b in range(block_count):
-        rest[b : b + 1, :] = jnp.where(position < lengths[b], scores[b : b + 1], 0.0)
+        weight = jnp.where(position < lengths[b], scores[b : b + 1], 0.0)
+        rest[b : b + 1, :] = weight.astype(jnp.bfloat16).astype(jnp.float32)
         rest[block_count + b : block_count + b + 1, :] = jnp.full(
             (1, block_len), order[0, b].astype(jnp.float32)
         )
+
+
+def scale(n_dp, n_mp, width, order, rest, rows, *refs):
+    squares, inverse, pieces = refs[:n_mp], refs[n_mp], refs[n_mp + 1 :]
+    block_count, block_len = inverse.shape
+    dp = lax.axis_index("dp")
+    own_width = rows.shape[1] // n_dp
+    per_owner = own_width // width
+    total = squares[0][...]
+    for other in squares[1:]:
+        total = total + other[...]
+    inverse[...] = lax.rsqrt(total / (rows.shape[1] * n_mp) + EPSILON)
+    factors = inverse[...] * rest[:block_count, :]
+    lane = lax.broadcasted_iota(jnp.int32, (block_len, block_len), 1)
+    diagonal = lane == lax.broadcasted_iota(jnp.int32, (block_len, block_len), 0)
+    sources = []
+    for slot in range(block_count):
+        source, factor = 0, factors[0:1]
+        for b in range(1, block_count):
+            here = order[0, b] == slot
+            source = jnp.where(here, b, source)
+            factor = jnp.where(here, factors[b : b + 1], factor)
+        factor = jnp.sum(jnp.where(diagonal, factor, 0.0), axis=1, keepdims=True)
+        sources.append((pl.multiple_of(source * block_len, block_len), factor))
+    for j in range(n_dp):
+        for e in range(n_dp):
+
+            @pl.when((dp ^ j) == e)
+            def _(j=j, e=e):
+                for i in range(per_owner):
+                    start = e * own_width + i * width
+                    for slot, (source, factor) in enumerate(sources):
+                        value = rows[pl.ds(source, block_len), start : start + width]
+                        value = value.astype(jnp.float32) * factor
+                        place = slice(slot * block_len, (slot + 1) * block_len)
+                        pieces[j * per_owner + i][place, :] = value.astype(jnp.bfloat16)
 
 
 def store(n_dp, g, first, offset, shards, *refs):
@@ -200,21 +226,22 @@
     n_far = n_mp // 2
     far, core = mp >> 1, mp & 1
 
+    def in_order(values):
+        return [pick(values, dp ^ e) for e in range(n_dp)]
+
     cotangents = [key_cotangent] + [swap(key_cotangent, "dp", j) for j in range(1, n_dp)]
-    cotangents = jnp.concatenate(cotangents, axis=0)
-
-    per_owner = feature_blocks
+
     vmem, smem = pl.BlockSpec(memory_space=pltpu.VMEM), pl.BlockSpec(memory_space=pltpu.SMEM)
     hbm = pl.BlockSpec(memory_space=pltpu.MemorySpace.HBM)
-    squares, *pieces = pl.pallas_call(
-        functools.partial(prepare, n_dp, block_len, chunk),
-        out_shape=[jax.ShapeDtypeStruct((block_count, block_len), jnp.float32)]
-        + [jax.ShapeDtypeStruct((tokens, chunk), jnp.bfloat16)] * (n_dp * per_owner),
+    squares = pl.pallas_call(
+        functools.partial(square, block_len),
+        out_shape=jax.ShapeDtypeStruct((block_count, block_len), jnp.float32),
         in_specs=[vmem],
-        out_specs=[vmem] * (1 + n_dp * per_owner),
+        out_specs=vmem,
         compiler_params=pltpu.CompilerParams(vmem_limit_bytes=32 * 2**20),
-        name="prepare",
+        name="square",
     )(policy_input)
+    squares = [squares] + [swap(squares, "mp", j) for j in range(1, n_mp)]
     rest = pl.pallas_call(
         score,
         out_shape=jax.ShapeDtypeStruct((2 * block_count, block_len), jnp.float32),
@@ -222,78 +249,74 @@
         out_specs=vmem,
         name="score",
     )(lengths, block_order, final_hidden, score_gain, score_head)
-    squares = squares + sum(swap(squares, "mp", j) for j in range(1, n_mp))
-    inverse = lax.rsqrt(squares / (local_width * n_mp) + EPSILON)
-    small = jnp.concatenate([inverse, rest], axis=0)
-    small = [small] + [swap(small, "dp", j) for j in range(1, n_dp)]
-
-    parts = []
+    inverse, *pieces = pl.pallas_call(
+        functools.partial(scale, n_dp, n_mp, chunk),
+        out_shape=[jax.ShapeDtypeStruct((block_count, block_len), jnp.float32)]
+        + [jax.ShapeDtypeStruct((tokens, chunk), jnp.bfloat16)] * (n_dp * feature_blocks),
+        in_specs=[smem] + [vmem] * (2 + n_mp),
+        out_specs=[vmem] * (1 + n_dp * feature_blocks),
+        compiler_params=pltpu.CompilerParams(vmem_limit_bytes=32 * 2**20),
+        name="scale",
+    )(block_order, rest, policy_input, *squares)
+
+    cotangents, inverse = lax.optimization_barrier((cotangents, inverse))
+    cotangents = jnp.concatenate(in_order(cotangents), axis=0)
+    parts, arriving = [], {}
 
     def rows(f):
         got = [pieces[f]]
         for j in range(1, n_dp):
-            piece = pieces[j * per_owner + f]
-            tied = parts if f else small
-            piece, tied[0] = lax.optimization_barrier((piece, tied[0]))
-            got.append(swap(piece, "dp", j))
-        return jnp.concatenate(got, axis=0)
+            piece = pieces[j * feature_blocks + f]
+            if f > 1:
+                piece, parts[1] = lax.optimization_barrier((piece, parts[1]))
+            piece = swap(piece, "dp", j)
+            if f:
+                piece, parts[f - 1] = lax.optimization_barrier((piece, parts[f - 1]))
+            got.append(piece)
+        return jnp.concatenate(in_order(got), axis=0)
 
     gathered = []
 
-    def key_gradient(near):
+    def both_cores(near):
         other = swap(near, "mp", 1)
-        low = core == 0
-        cotangent = jnp.concatenate(
-            [jnp.where(low, near, other), jnp.where(low, other, near)], axis=1
-        ).reshape(n_dp, n_dp, pair, block_len, -1)
-        found = []
-        for j in range(n_dp):
-            sender = dp ^ j
-            for b in range(block_count):
-                slot = small[j][2 * block_count + b][:, None]
-                chosen = None
-                for e in range(n_dp):
-                    for q in range(pair):
-                        value = lax.dynamic_index_in_dim(cotangent[e], sender, 0, keepdims=False)[q]
-                        at = ((dp ^ e) * pair + q).astype(jnp.float32)
-                        chosen = value if chosen is None else jnp.where(slot == at, value, chosen)
-                weight = small[j][block_count + b].astype(jnp.bfloat16).astype(jnp.float32)
-                key_grad = to_bfloat16(chosen.astype(jnp.float32) * weight[:, None])
-                found.append(
-                    (key_grad.astype(jnp.float32) * small[j][b][:, None]).astype(jnp.bfloat16)
-                )
-        return jnp.concatenate(found, axis=0)
+        cotangent = jnp.concatenate([pick([near, other], core), pick([other, near], core)], axis=1)
+        cotangent = cotangent.reshape(n_dp, n_dp, tokens // n_dp, 2 * columns)
+        return cotangent.transpose(1, 0, 2, 3).reshape(n_dp * tokens, 2 * columns)
 
     for g in range(n_far):
         near = cotangents
         if g:
-            near, parts[0] = lax.optimization_barrier((near, parts[0]))
+            tied = min(1, len(parts) - 1)
+            near, parts[tied] = lax.optimization_barrier((near, parts[tied]))
             near = swap(near, "mp", 2 * g)
-        key_grad = key_gradient(near)
+        cotangent = both_cores(near)
         for f in range(feature_blocks):
             if not g:
                 gathered.append(rows(f))
             part = lax.dot_general(
                 gathered[f],
-                key_grad,
+                cotangent,
                 (((0,), (0,)), ((), ())),
                 preferred_element_type=jnp.float32,
             )
             parts.append(to_bfloat16(part))
-    late_gain, parts[0] = lax.optimization_barrier((norm_gain, parts[0]))
+            if len(parts) <= LAG and n_section == 4:
+                arriving[len(parts) - 1] = end_swap(parts[-1])
+    late_gain, parts[1] = lax.optimization_barrier((norm_gain, parts[1]))
     gain = late_gain.astype(jnp.float32)[None, :]
     shards = n_section * n_dp
     out = []
     sums = {}
 
     def share(values):
-        if n_dp == 2 and len(values) == 1:
-            return (values[0], swap(values[0], "dp", 1))
-        return (lax.all_gather(jnp.concatenate(values, axis=0), "dp"),)
+        values = jnp.concatenate(values, axis=0)
+        if n_dp == 2:
+            return (values, swap(values, "dp", 1))
+        return (lax.all_gather(values, "dp"),)
 
     def emit(group, values):
         if len(values) == 2:
-            values = jnp.stack([pick(values, dp), pick(values, 1 - dp)])
+            values = jnp.stack(in_order(values))
         else:
             (values,) = values
         for i, k in enumerate(group):
@@ -346,7 +369,7 @@
             swap(pick(by_target, dp ^ j), "dp", j) for j in range(1, n_dp)
         )
         arrived = side_values[0]
-        learner_keys.append(jnp.concatenate([pick(arrived, dp ^ a) for a in range(n_dp)], axis=0))
+        learner_keys.append(jnp.concatenate(in_order(arrived), axis=0))
 
     side_values, learner_keys = [()], []
     steps = key_steps()
@@ -355,7 +378,7 @@
         side_values[0] = waited
         return next(steps, None)
 
-    summed(parts, sums, share, emit, side)
+    summed(parts, arriving, sums, share, emit, side)
     grad_gain = [
         sum(sums[g * feature_blocks + f] for g in range(n_far)) for f in range(feature_blocks)
     ]

time: 166 us -> 129 us (0.78)
  between operations: 14.6 us -> 1.45 us
  waiting for transfers between devices: 57.2 us -> 45.1 us
  local copies, waits for them, and re-layouts: 13.1 us -> 4.59 us
  other arithmetic: 12 us -> 5.57 us
  starting transfers between devices: 53 us -> 55.6 us
    all_gather x3 -> x0, waiting for transfers between devices: 33.4 us -> none  [share(): return (lax.all_gather(jnp.concatenate(values, axis=0), 'dp'),)]
    ppermute x18 -> x20, waiting for transfers between devices: 7.42 us -> 28.6 us  [swap(): lax.ppermute(value, axis, [(i, i ^ bit) for i in range(lax.axis_size(axis...]
    unnamed x26 -> x18, local copies, waits for them, and re-layouts: 13.1 us -> 4.46 us
    concatenate x7 -> x4, other arithmetic: 3.89 us -> 0.76 us  [the longest x1 0.67 us: key_steps(): learner_keys.append(jnp.concatenate(in_order(arrived), axis=0))]
    ppermute x11, starting transfers between devices: 30.3 us -> 32.2 us  [end_swap(): return lax.ppermute(value, 'section', [(0, 1), (1, 0), (2, 3), (3, 2)])]
    ppermute x18 -> x20, starting transfers between devices: 16.9 us -> 17.8 us  [swap(): lax.ppermute(value, axis, [(i, i ^ bit) for i in range(lax.axis_size(axis...]
  transfers between devices with their start and end apart: 40 -> 39, of which waited for: 13 -> 15; matrix products, arithmetic and copies ran while one was open for 10% -> 7% of each run, Pallas kernels for 6% -> 9%
where the time goes in v7:
time: 129 us; the launch traced here: 128 us
  starting transfers between devices  55.6 us (43%)
  waiting for transfers between devices  45.1 us (35%)
  Pallas kernels  12.2 us (9%)
  other arithmetic  5.57 us (4%)
  local copies, waits for them, and re-layouts  4.59 us (4%)
  matrix products  3.81 us (3%)
  between operations  1.45 us (1%)
    ppermute x11, starting transfers between devices, end_swap(): return lax.ppermute(value, 'section', [(0, 1), (1, 0), (2, 3), (3, 2)])  32.2 us
    ppermute x20, waiting for transfers between devices, swap(): lax.ppermute(value, axis, [(i, i ^ bit) for i in range(lax.axis_size(axis...  28.6 us
    ppermute x20, starting transfers between devices, swap(): lax.ppermute(value, axis, [(i, i ^ bit) for i in range(lax.axis_size(axis...  17.8 us
    ppermute x11, waiting for transfers between devices, end_swap(): return lax.ppermute(value, 'section', [(0, 1), (1, 0), (2, 3), (3, 2)])  16.5 us
    pallas_call x8, Pallas kernels, emit(): pl.pallas_call(functools.partial(store, n_dp, g, f * chunk, i * chunk, sh...  9.57 us
    ppermute x8, starting transfers between devices, middle_swap(): return lax.ppermute(value, 'section', [(1, 2), (2, 1), (0, 0), (3, 3)])  5.59 us
    unnamed x18, local copies, waits for them, and re-layouts  4.46 us
  transfers between devices with their start and end apart: 39, of which 15 were waited for; matrix products, arithmetic and copies ran while one was open for 7% of the time, Pallas kernels for 9%

profile of v7, /device:TPU:0, one launch (start us, length us, event | category | flops | bytes accessed | tf_op | source)
XLA Modules:
  0.0 128.3 jit_solution(13298024591137239910)
XLA Ops:
  0.6 3.0 %collective-permute-start.5 = (bf16[256,256]{1,0:T(8,128)(2,1)}, bf16[256,256]{1,0:T(8,128)(2,1)S(1)}, u32[]{:S(2)}, u32[]{:S(2)}) collective-permute-start(bf16[256,256]{1,0:T(8,128)(2,1)} %param.17), channel_id=1, source_target_pairs={{0,4},{4,0},{1,5},{5,1},{2,6},{6,2},{3,7},{7,3},{8,12},{12,8},{9,1... | collective-permute-start | bytes 393224 | tf_op jit(solution)/shard_map/ppermute | solution.py:16
  5.2 1.6 %collective-permute-start.1 = (f32[2,128]{1,0:T(2,128)S(1)}, f32[2,128]{1,0:T(2,128)S(1)}, u32[]{:S(2)}, u32[]{:S(2)}) collective-permute-start(f32[2,128]{1,0:T(2,128)S(1)} %square.1.refs_0_), channel_id=1, source_target_pairs={{0,2},{1,3},{2,0},{3,1},{4,6},{5,7},{6,4},{7,5},{8,10},{9,11},{10,... | collective-permute-start | bytes 3080 | tf_op jit(solution)/shard_map/ppermute | solution.py:16
  14.9 1.6 %collective-permute-start.3 = (bf16[256,256]{1,0:T(8,128)(2,1)S(1)}, bf16[256,256]{1,0:T(8,128)(2,1)S(1)}, u32[]{:S(2)}, u32[]{:S(2)}) collective-permute-start(bf16[256,256]{1,0:T(8,128)(2,1)S(1)} %get-tuple-element.124), channel_id=1, source_target_pairs={{0,4},{4,0},{1,5},{5,1},{2,6},{6,2},{3,7},{7,3},{8,12},{12,8},{9,1... | collective-permute-start | bytes 393224 | tf_op jit(solution)/shard_map/ppermute | solution.py:16
  16.5 3.1 %collective-permute-done.4 = bf16[256,256]{1,0:T(8,128)(2,1)S(1)} collective-permute-done((bf16[256,256]{1,0:T(8,128)(2,1)S(1)}, bf16[256,256]{1,0:T(8,128)(2,1)S(1)}, u32[]{:S(2)}, u32[]{:S(2)}) %collective-permute-start.4) | collective-permute-done | bytes 131104 | tf_op jit(solution)/shard_map/ppermute | solution.py:16
  23.3 1.6 %collective-permute-start.10 = (bf16[256,512]{1,0:T(8,128)(2,1)S(1)}, bf16[256,512]{1,0:T(8,128)(2,1)S(1)}, u32[]{:S(2)}, u32[]{:S(2)}) collective-permute-start(bf16[256,512]{1,0:T(8,128)(2,1)S(1)} %fusion.1), channel_id=1, source_target_pairs={{0,8},{8,0},{16,24},{24,16},{1,9},{9,1},{17,25},{25,17},{2,10},{10... | collective-permute-start | bytes 786440 | tf_op jit(solution)/shard_map/ppermute | solution.py:35
  25.4 1.7 %collective-permute-done.9 = bf16[256,256]{1,0:T(8,128)(2,1)S(1)} collective-permute-done((bf16[256,256]{1,0:T(8,128)(2,1)S(1)}, bf16[256,256]{1,0:T(8,128)(2,1)S(1)}, u32[]{:S(2)}, u32[]{:S(2)}) %collective-permute-start.9) | collective-permute-done | bytes 131104 | tf_op jit(solution)/shard_map/ppermute | solution.py:16
  28.0 1.6 %collective-permute-start.14 = (bf16[256,512]{1,0:T(8,128)(2,1)S(1)}, bf16[256,512]{1,0:T(8,128)(2,1)S(1)}, u32[]{:S(2)}, u32[]{:S(2)}) collective-permute-start(bf16[256,512]{1,0:T(8,128)(2,1)S(1)} %fusion.2), channel_id=1, source_target_pairs={{0,8},{8,0},{16,24},{24,16},{1,9},{9,1},{17,25},{25,17},{2,10},{10... | collective-permute-start | bytes 786440 | tf_op jit(solution)/shard_map/ppermute | solution.py:35
  30.2 8.0 %collective-permute-done.7 = bf16[256,512]{1,0:T(8,128)(2,1)S(1)} collective-permute-done((bf16[256,512]{1,0:T(8,128)(2,1)S(1)}, bf16[256,512]{1,0:T(8,128)(2,1)S(1)}, u32[]{:S(2)}, u32[]{:S(2)}) %collective-permute-start.7) | collective-permute-done | bytes 262176 | tf_op jit(solution)/shard_map/ppermute | solution.py:35
  40.3 1.8 %collective-permute-done.14 = bf16[256,512]{1,0:T(8,128)(2,1)S(1)} collective-permute-done((bf16[256,512]{1,0:T(8,128)(2,1)S(1)}, bf16[256,512]{1,0:T(8,128)(2,1)S(1)}, u32[]{:S(2)}, u32[]{:S(2)}) %collective-permute-start.14) | collective-permute-done | bytes 262176 | tf_op jit(solution)/shard_map/ppermute | solution.py:35
  42.8 11.0 %collective-permute-start.12 = (bf16[256,512]{1,0:T(8,128)(2,1)S(1)}, bf16[256,512]{1,0:T(8,128)(2,1)S(1)}, u32[]{:S(2)}, u32[]{:S(2)}) collective-permute-start(bf16[256,512]{1,0:T(8,128)(2,1)S(1)} %get-tuple-element.253), channel_id=1, source_target_pairs={{0,8},{8,0},{16,24},{24,16},{1,9},{9,1},{17,25},{25,17},{2,10},{10... | collective-permute-start | bytes 786440 | tf_op jit(solution)/shard_map/ppermute | solution.py:35
  55.5 4.0 %collective-permute-done.12 = bf16[256,512]{1,0:T(8,128)(2,1)S(1)} collective-permute-done((bf16[256,512]{1,0:T(8,128)(2,1)S(1)}, bf16[256,512]{1,0:T(8,128)(2,1)S(1)}, u32[]{:S(2)}, u32[]{:S(2)}) %collective-permute-start.12) | collective-permute-done | bytes 262176 | tf_op jit(solution)/shard_map/ppermute | solution.py:35
  60.4 1.8 %collective-permute-start.20 = (bf16[256,512]{1,0:T(8,128)(2,1)S(1)}, bf16[256,512]{1,0:T(8,128)(2,1)S(1)}, u32[]{:S(2)}, u32[]{:S(2)}) collective-permute-start(bf16[256,512]{1,0:T(8,128)(2,1)S(1)} %broadcast_select_fusion.14), channel_id=1, source_target_pairs={{0,4},{4,0},{1,5},{5,1},{2,6},{6,2},{3,7},{7,3},{8,12},{12,8},{9,1... | collective-permute-start | bytes 786440 | tf_op jit(solution)/shard_map/ppermute | solution.py:16
  62.2 3.1 %collective-permute-start.19 = (bf16[256,512]{1,0:T(8,128)(2,1)S(1)}, bf16[256,512]{1,0:T(8,128)(2,1)S(1)}, u32[]{:S(2)}, u32[]{:S(2)}) collective-permute-start(bf16[256,512]{1,0:T(8,128)(2,1)S(1)} %get-tuple-element.249), channel_id=1, source_target_pairs={{0,8},{8,0},{16,24},{24,16},{1,9},{9,1},{17,25},{25,17},{2,10},{10... | collective-permute-start | bytes 786440 | tf_op jit(solution)/shard_map/ppermute | solution.py:35
  68.2 1.7 %collective-permute-done.19 = bf16[256,512]{1,0:T(8,128)(2,1)S(1)} collective-permute-done((bf16[256,512]{1,0:T(8,128)(2,1)S(1)}, bf16[256,512]{1,0:T(8,128)(2,1)S(1)}, u32[]{:S(2)}, u32[]{:S(2)}) %collective-permute-start.19) | collective-permute-done | bytes 262176 | tf_op jit(solution)/shard_map/ppermute | solution.py:35
  71.6 2.5 %collective-permute-start.28 = (bf16[256,512]{1,0:T(8,128)(2,1)S(1)}, bf16[256,512]{1,0:T(8,128)(2,1)S(1)}, u32[]{:S(2)}, u32[]{:S(2)}) collective-permute-start(bf16[256,512]{1,0:T(8,128)(2,1)S(1)} %get-tuple-element.247), channel_id=1, source_target_pairs={{0,8},{8,0},{16,24},{24,16},{1,9},{9,1},{17,25},{25,17},{2,10},{10... | collective-permute-start | bytes 786440 | tf_op jit(solution)/shard_map/ppermute | solution.py:35
  75.8 1.6 %collective-permute-start.25 = (bf16[256,256]{1,0:T(8,128)(2,1)S(1)}, bf16[256,256]{1,0:T(8,128)(2,1)S(1)}, u32[]{:S(2)}, u32[]{:S(2)}) collective-permute-start(bf16[256,256]{1,0:T(8,128)(2,1)S(1)} %select_convert_fusion.1), channel_id=1, source_target_pairs={{0,2},{1,3},{2,0},{3,1},{4,6},{5,7},{6,4},{7,5},{8,10},{9,11},{10,... | collective-permute-start | bytes 393224 | tf_op jit(solution)/shard_map/ppermute | solution.py:16
  78.5 3.8 %collective-permute-start.30 = (bf16[256,512]{1,0:T(8,128)(2,1)S(1)}, bf16[256,512]{1,0:T(8,128)(2,1)S(1)}, u32[]{:S(2)}, u32[]{:S(2)}) collective-permute-start(bf16[256,512]{1,0:T(8,128)(2,1)S(1)} %get-tuple-element.245), channel_id=1, source_target_pairs={{0,8},{8,0},{16,24},{24,16},{1,9},{9,1},{17,25},{25,17},{2,10},{10... | collective-permute-start | bytes 786440 | tf_op jit(solution)/shard_map/ppermute | solution.py:35
  83.2 4.7 %collective-permute-start.37 = (bf16[256,512]{1,0:T(8,128)(2,1)S(1)}, bf16[256,512]{1,0:T(8,128)(2,1)S(1)}, u32[]{:S(2)}, u32[]{:S(2)}) collective-permute-start(bf16[256,512]{1,0:T(8,128)(2,1)S(1)} %reduce-precision_convert_fusion.3), channel_id=1, source_target_pairs={{0,8},{8,0},{16,24},{24,16},{1,9},{9,1},{17,25},{25,17},{2,10},{10... | collective-permute-start | bytes 786440 | tf_op jit(solution)/shard_map/ppermute | solution.py:35
  88.1 2.1 %collective-permute-start.29 = (bf16[128,256]{1,0:T(8,128)(2,1)S(1)}, bf16[128,256]{1,0:T(8,128)(2,1)S(1)}, u32[]{:S(2)}, u32[]{:S(2)}) collective-permute-start(bf16[128,256]{1,0:T(8,128)(2,1)S(1)} %get-tuple-element.281), channel_id=1, source_target_pairs={{0,4},{4,0},{1,5},{5,1},{2,6},{6,2},{3,7},{7,3},{8,12},{12,8},{9,1... | collective-permute-start | bytes 196616 | tf_op jit(solution)/shard_map/ppermute | solution.py:16
  91.3 3.0 %collective-permute-start.32 = (bf16[256,512]{1,0:T(8,128)(2,1)S(1)}, bf16[256,512]{1,0:T(8,128)(2,1)S(1)}, u32[]{:S(2)}, u32[]{:S(2)}) collective-permute-start(bf16[256,512]{1,0:T(8,128)(2,1)S(1)} %reduce-precision_convert_fusion.1), channel_id=1, source_target_pairs={{0,8},{8,0},{16,24},{24,16},{1,9},{9,1},{17,25},{25,17},{2,10},{10... | collective-permute-start | bytes 786440 | tf_op jit(solution)/shard_map/ppermute | solution.py:35
  94.3 2.8 %collective-permute-done.29 = bf16[128,256]{1,0:T(8,128)(2,1)S(1)} collective-permute-done((bf16[128,256]{1,0:T(8,128)(2,1)S(1)}, bf16[128,256]{1,0:T(8,128)(2,1)S(1)}, u32[]{:S(2)}, u32[]{:S(2)}) %collective-permute-start.29) | collective-permute-done | bytes 65568 | tf_op jit(solution)/shard_map/ppermute | solution.py:16
  101.3 1.8 %collective-permute-start.38 = (bf16[512,512]{1,0:T(8,128)(2,1)S(1)}, bf16[512,512]{1,0:T(8,128)(2,1)S(1)}, u32[]{:S(2)}, u32[]{:S(2)}) collective-permute-start(bf16[512,512]{1,0:T(8,128)(2,1)S(1)} %constant_dynamic-update-slice_fusion.4), channel_id=1, source_target_pairs={{0,4},{4,0},{1,5},{5,1},{2,6},{6,2},{3,7},{7,3},{8,12},{12,8},{9,1... | collective-permute-start | bytes 1572872 | tf_op jit(solution)/shard_map/ppermute | solution.py:16
  103.1 8.9 %collective-permute-done.35 = bf16[512,512]{1,0:T(8,128)(2,1)S(1)} collective-permute-done((bf16[512,512]{1,0:T(8,128)(2,1)S(1)}, bf16[512,512]{1,0:T(8,128)(2,1)S(1)}, u32[]{:S(2)}, u32[]{:S(2)}) %collective-permute-start.35) | collective-permute-done | bytes 524320 | tf_op jit(solution)/shard_map/ppermute | solution.py:16
  115.0 8.2 %collective-permute-done.38 = bf16[512,512]{1,0:T(8,128)(2,1)S(1)} collective-permute-done((bf16[512,512]{1,0:T(8,128)(2,1)S(1)}, bf16[512,512]{1,0:T(8,128)(2,1)S(1)}, u32[]{:S(2)}, u32[]{:S(2)}) %collective-permute-start.38) | collective-permute-done | bytes 524320 | tf_op jit(solution)/shard_map/ppermute | solution.py:16
  (156 shorter events, 41.8 us)
Async XLA Ops:
  0.6 13.2 %collective-permute-start.5 = (bf16[256,256]{1,0:T(8,128)(2,1)}, bf16[256,256]{1,0:T(8,128)(2,1)S(1)}, u32[]{:S(2)}, u32[]{:S(2)}) collective-permute-start(bf16[256,256]{1,0:T(8,128)(2,1)} %param.17), channel_id=1, source_target_pairs={{0,4},{4,0},{1,5},{5,1},{2,6},{6,2},{3,7},{7,3},{8,12},{12,8},{9,1... | collective-permute-start | bytes 393224 | tf_op jit(solution)/shard_map/ppermute | solution.py:16
  23.3 15.6 %collective-permute-start.10 = (bf16[256,512]{1,0:T(8,128)(2,1)S(1)}, bf16[256,512]{1,0:T(8,128)(2,1)S(1)}, u32[]{:S(2)}, u32[]{:S(2)}) collective-permute-start(bf16[256,512]{1,0:T(8,128)(2,1)S(1)} %fusion.1), channel_id=1, source_target_pairs={{0,8},{8,0},{16,24},{24,16},{1,9},{9,1},{17,25},{25,17},{2,10},{10... | collective-permute-start | bytes 786440 | tf_op jit(solution)/shard_map/ppermute | solution.py:35
  24.9 13.3 %collective-permute-start.7 = (bf16[256,512]{1,0:T(8,128)(2,1)S(1)}, bf16[256,512]{1,0:T(8,128)(2,1)S(1)}, u32[]{:S(2)}, u32[]{:S(2)}) collective-permute-start(bf16[256,512]{1,0:T(8,128)(2,1)S(1)} %fusion), channel_id=1, source_target_pairs={{0,8},{8,0},{16,24},{24,16},{1,9},{9,1},{17,25},{25,17},{2,10},{10... | collective-permute-start | bytes 786440 | tf_op jit(solution)/shard_map/ppermute | solution.py:35
  27.0 11.9 %collective-permute-start.11 = (bf16[256,256]{1,0:T(8,128)(2,1)S(1)}, bf16[256,256]{1,0:T(8,128)(2,1)S(1)}, u32[]{:S(2)}, u32[]{:S(2)}) collective-permute-start(bf16[256,256]{1,0:T(8,128)(2,1)S(1)} %get-tuple-element.143), channel_id=1, source_target_pairs={{0,4},{4,0},{1,5},{5,1},{2,6},{6,2},{3,7},{7,3},{8,12},{12,8},{9,1... | collective-permute-start | bytes 393224 | tf_op jit(solution)/shard_map/ppermute | solution.py:16
  28.0 14.1 %collective-permute-start.14 = (bf16[256,512]{1,0:T(8,128)(2,1)S(1)}, bf16[256,512]{1,0:T(8,128)(2,1)S(1)}, u32[]{:S(2)}, u32[]{:S(2)}) collective-permute-start(bf16[256,512]{1,0:T(8,128)(2,1)S(1)} %fusion.2), channel_id=1, source_target_pairs={{0,8},{8,0},{16,24},{24,16},{1,9},{9,1},{17,25},{25,17},{2,10},{10... | collective-permute-start | bytes 786440 | tf_op jit(solution)/shard_map/ppermute | solution.py:35
  29.6 10.5 %collective-permute-start.15 = (bf16[512,256]{1,0:T(8,128)(2,1)S(1)}, bf16[512,256]{1,0:T(8,128)(2,1)S(1)}, u32[]{:S(2)}, u32[]{:S(2)}) collective-permute-start(bf16[512,256]{1,0:T(8,128)(2,1)S(1)} %pad_maximum_fusion.8), channel_id=1, source_target_pairs={{0,2},{1,3},{2,0},{3,1},{4,6},{5,7},{6,4},{7,5},{8,10},{9,11},{10,... | collective-permute-start | bytes 786440 | tf_op jit(solution)/shard_map/ppermute | solution.py:16
  40.1 13.8 %collective-permute-start.16 = (bf16[512,256]{1,0:T(8,128)(2,1)S(1)}, bf16[512,256]{1,0:T(8,128)(2,1)S(1)}, u32[]{:S(2)}, u32[]{:S(2)}) collective-permute-start(bf16[512,256]{1,0:T(8,128)(2,1)S(1)} %collective-permute-done.15), channel_id=1, source_target_pairs={{0,1},{1,0},{2,3},{3,2},{4,5},{5,4},{6,7},{7,6},{8,9},{9,8},{10,11... | collective-permute-start | bytes 786440 | tf_op jit(solution)/shard_map/ppermute | solution.py:16
  42.1 18.2 %collective-permute-start.18 = (bf16[256,512]{1,0:T(8,128)(2,1)S(1)}, bf16[256,512]{1,0:T(8,128)(2,1)S(1)}, u32[]{:S(2)}, u32[]{:S(2)}) collective-permute-start(bf16[256,512]{1,0:T(8,128)(2,1)S(1)} %reduce-precision_convert_fusion.12), channel_id=1, source_target_pairs={{8,16},{16,8},{0,0},{24,24},{9,17},{17,9},{1,1},{25,25},{10,18},{1... | collective-permute-start | bytes 786440 | tf_op jit(solution)/shard_map/ppermute | solution.py:39
  42.8 16.7 %collective-permute-start.12 = (bf16[256,512]{1,0:T(8,128)(2,1)S(1)}, bf16[256,512]{1,0:T(8,128)(2,1)S(1)}, u32[]{:S(2)}, u32[]{:S(2)}) collective-permute-start(bf16[256,512]{1,0:T(8,128)(2,1)S(1)} %get-tuple-element.253), channel_id=1, source_target_pairs={{0,8},{8,0},{16,24},{24,16},{1,9},{9,1},{17,25},{25,17},{2,10},{10... | collective-permute-start | bytes 786440 | tf_op jit(solution)/shard_map/ppermute | solution.py:35
  55.1 10.3 %collective-permute-start.17 = (bf16[256,512]{1,0:T(8,128)(2,1)S(1)}, bf16[256,512]{1,0:T(8,128)(2,1)S(1)}, u32[]{:S(2)}, u32[]{:S(2)}) collective-permute-start(bf16[256,512]{1,0:T(8,128)(2,1)S(1)} %get-tuple-element.251), channel_id=1, source_target_pairs={{0,8},{8,0},{16,24},{24,16},{1,9},{9,1},{17,25},{25,17},{2,10},{10... | collective-permute-start | bytes 786440 | tf_op jit(solution)/shard_map/ppermute | solution.py:35
  65.4 9.4 %collective-permute-start.22 = (bf16[256,512]{1,0:T(8,128)(2,1)S(1)}, bf16[256,512]{1,0:T(8,128)(2,1)S(1)}, u32[]{:S(2)}, u32[]{:S(2)}) collective-permute-start(bf16[256,512]{1,0:T(8,128)(2,1)S(1)} %reduce-precision_convert_fusion.8), channel_id=1, source_target_pairs={{8,16},{16,8},{0,0},{24,24},{9,17},{17,9},{1,1},{25,25},{10,18},{1... | collective-permute-start | bytes 786440 | tf_op jit(solution)/shard_map/ppermute | solution.py:39
  74.1 8.2 %collective-permute-start.27 = (bf16[256,512]{1,0:T(8,128)(2,1)S(1)}, bf16[256,512]{1,0:T(8,128)(2,1)S(1)}, u32[]{:S(2)}, u32[]{:S(2)}) collective-permute-start(bf16[256,512]{1,0:T(8,128)(2,1)S(1)} %reduce-precision_convert_fusion.6), channel_id=1, source_target_pairs={{8,16},{16,8},{0,0},{24,24},{9,17},{17,9},{1,1},{25,25},{10,18},{1... | collective-permute-start | bytes 786440 | tf_op jit(solution)/shard_map/ppermute | solution.py:39
  75.8 12.1 %collective-permute-start.25 = (bf16[256,256]{1,0:T(8,128)(2,1)S(1)}, bf16[256,256]{1,0:T(8,128)(2,1)S(1)}, u32[]{:S(2)}, u32[]{:S(2)}) collective-permute-start(bf16[256,256]{1,0:T(8,128)(2,1)S(1)} %select_convert_fusion.1), channel_id=1, source_target_pairs={{0,2},{1,3},{2,0},{3,1},{4,6},{5,7},{6,4},{7,5},{8,10},{9,11},{10,... | collective-permute-start | bytes 393224 | tf_op jit(solution)/shard_map/ppermute | solution.py:16
  78.5 11.7 %collective-permute-start.30 = (bf16[256,512]{1,0:T(8,128)(2,1)S(1)}, bf16[256,512]{1,0:T(8,128)(2,1)S(1)}, u32[]{:S(2)}, u32[]{:S(2)}) collective-permute-start(bf16[256,512]{1,0:T(8,128)(2,1)S(1)} %get-tuple-element.245), channel_id=1, source_target_pairs={{0,8},{8,0},{16,24},{24,16},{1,9},{9,1},{17,25},{25,17},{2,10},{10... | collective-permute-start | bytes 786440 | tf_op jit(solution)/shard_map/ppermute | solution.py:35
  82.3 15.1 %collective-permute-start.23 = (bf16[512,512]{1,0:T(8,128)(2,1)S(1)}, bf16[512,512]{1,0:T(8,128)(2,1)S(1)}, u32[]{:S(2)}, u32[]{:S(2)}) collective-permute-start(bf16[512,512]{1,0:T(8,128)(2,1)S(1)} %constant_dynamic-update-slice_fusion), channel_id=1, source_target_pairs={{0,4},{4,0},{1,5},{5,1},{2,6},{6,2},{3,7},{7,3},{8,12},{12,8},{9,1... | collective-permute-start | bytes 1572872 | tf_op jit(solution)/shard_map/ppermute | solution.py:16
  82.5 8.7 %collective-permute-start.31 = (bf16[256,512]{1,0:T(8,128)(2,1)S(1)}, bf16[256,512]{1,0:T(8,128)(2,1)S(1)}, u32[]{:S(2)}, u32[]{:S(2)}) collective-permute-start(bf16[256,512]{1,0:T(8,128)(2,1)S(1)} %reduce-precision_convert_fusion.4), channel_id=1, source_target_pairs={{8,16},{16,8},{0,0},{24,24},{9,17},{17,9},{1,1},{25,25},{10,18},{1... | collective-permute-start | bytes 786440 | tf_op jit(solution)/shard_map/ppermute | solution.py:39
  83.2 16.8 %collective-permute-start.37 = (bf16[256,512]{1,0:T(8,128)(2,1)S(1)}, bf16[256,512]{1,0:T(8,128)(2,1)S(1)}, u32[]{:S(2)}, u32[]{:S(2)}) collective-permute-start(bf16[256,512]{1,0:T(8,128)(2,1)S(1)} %reduce-precision_convert_fusion.3), channel_id=1, source_target_pairs={{0,8},{8,0},{16,24},{24,16},{1,9},{9,1},{17,25},{25,17},{2,10},{10... | collective-permute-start | bytes 786440 | tf_op jit(solution)/shard_map/ppermute | solution.py:35
  88.1 9.1 %collective-permute-start.29 = (bf16[128,256]{1,0:T(8,128)(2,1)S(1)}, bf16[128,256]{1,0:T(8,128)(2,1)S(1)}, u32[]{:S(2)}, u32[]{:S(2)}) collective-permute-start(bf16[128,256]{1,0:T(8,128)(2,1)S(1)} %get-tuple-element.281), channel_id=1, source_target_pairs={{0,4},{4,0},{1,5},{5,1},{2,6},{6,2},{3,7},{7,3},{8,12},{12,8},{9,1... | collective-permute-start | bytes 196616 | tf_op jit(solution)/shard_map/ppermute | solution.py:16
  90.3 9.7 %collective-permute-start.33 = (bf16[256,512]{1,0:T(8,128)(2,1)S(1)}, bf16[256,512]{1,0:T(8,128)(2,1)S(1)}, u32[]{:S(2)}, u32[]{:S(2)}) collective-permute-start(bf16[256,512]{1,0:T(8,128)(2,1)S(1)} %reduce-precision_convert_fusion.2), channel_id=1, source_target_pairs={{8,16},{16,8},{0,0},{24,24},{9,17},{17,9},{1,1},{25,25},{10,18},{1... | collective-permute-start | bytes 786440 | tf_op jit(solution)/shard_map/ppermute | solution.py:39
  91.3 9.9 %collective-permute-start.32 = (bf16[256,512]{1,0:T(8,128)(2,1)S(1)}, bf16[256,512]{1,0:T(8,128)(2,1)S(1)}, u32[]{:S(2)}, u32[]{:S(2)}) collective-permute-start(bf16[256,512]{1,0:T(8,128)(2,1)S(1)} %reduce-precision_convert_fusion.1), channel_id=1, source_target_pairs={{0,8},{8,0},{16,24},{24,16},{1,9},{9,1},{17,25},{25,17},{2,10},{10... | collective-permute-start | bytes 786440 | tf_op jit(solution)/shard_map/ppermute | solution.py:35
  97.1 14.9 %collective-permute-start.35 = (bf16[512,512]{1,0:T(8,128)(2,1)S(1)}, bf16[512,512]{1,0:T(8,128)(2,1)S(1)}, u32[]{:S(2)}, u32[]{:S(2)}) collective-permute-start(bf16[512,512]{1,0:T(8,128)(2,1)S(1)} %constant_dynamic-update-slice_fusion.2), channel_id=1, source_target_pairs={{0,4},{4,0},{1,5},{5,1},{2,6},{6,2},{3,7},{7,3},{8,12},{12,8},{9,1... | collective-permute-start | bytes 1572872 | tf_op jit(solution)/shard_map/ppermute | solution.py:16
  100.1 14.5 %collective-permute-start.34 = (bf16[256,512]{1,0:T(8,128)(2,1)S(1)}, bf16[256,512]{1,0:T(8,128)(2,1)S(1)}, u32[]{:S(2)}, u32[]{:S(2)}) collective-permute-start(bf16[256,512]{1,0:T(8,128)(2,1)S(1)} %reduce-precision_convert_fusion), channel_id=1, source_target_pairs={{0,8},{8,0},{16,24},{24,16},{1,9},{9,1},{17,25},{25,17},{2,10},{10... | collective-permute-start | bytes 786440 | tf_op jit(solution)/shard_map/ppermute | solution.py:35
  101.3 21.9 %collective-permute-start.38 = (bf16[512,512]{1,0:T(8,128)(2,1)S(1)}, bf16[512,512]{1,0:T(8,128)(2,1)S(1)}, u32[]{:S(2)}, u32[]{:S(2)}) collective-permute-start(bf16[512,512]{1,0:T(8,128)(2,1)S(1)} %constant_dynamic-update-slice_fusion.4), channel_id=1, source_target_pairs={{0,4},{4,0},{1,5},{5,1},{2,6},{6,2},{3,7},{7,3},{8,12},{12,8},{9,1... | collective-permute-start | bytes 1572872 | tf_op jit(solution)/shard_map/ppermute | solution.py:16
  114.6 11.8 %collective-permute-start.36 = (bf16[256,512]{1,0:T(8,128)(2,1)S(1)}, bf16[256,512]{1,0:T(8,128)(2,1)S(1)}, u32[]{:S(2)}, u32[]{:S(2)}) collective-permute-start(bf16[256,512]{1,0:T(8,128)(2,1)S(1)} %broadcast_select_fusion.6), channel_id=1, source_target_pairs={{0,4},{4,0},{1,5},{5,1},{2,6},{6,2},{3,7},{7,3},{8,12},{12,8},{9,1... | collective-permute-start | bytes 786440 | tf_op jit(solution)/shard_map/ppermute | solution.py:16
  (22 other events, 111.5 us)

commit v8 on v7

--- a/solution.py
+++ b/solution.py
@@ -41,31 +41,29 @@
 
 def summed(parts, arriving, sums, share, emit, side):
     count = len(parts)
-    groups = [[0]] + [list(range(k, min(k + 2, count))) for k in range(1, count - 1, 2)]
-    groups += [[count - 1]] if count > 1 and groups[-1][-1] != count - 1 else []
     pending = ()
     if lax.axis_size("section") != 4:
-        for group in groups:
-            found = [to_bfloat16(lax.psum(parts[k].astype(jnp.float32), "section")) for k in group]
-            emit(group, share(found))
+        for k, part in enumerate(parts):
+            emit(k, share(to_bfloat16(lax.psum(part.astype(jnp.float32), "section"))))
         while pending is not None:
             pending = side(pending)
         return
     index = lax.axis_index("section")
     inner = (index == 1) | (index == 2)
 
-    halves, others, totals, results = {}, {}, {}, {}
-    shares, recent = [], ()
+    halves, others, totals, shares = {}, {}, {}, {}
+    recent = ()
     for k in range(count + LAG):
+        before = k - 1 - LAG
         tied = ({i: totals[i] for i in (k - 2,) if i in totals}, {i: sums[i] for i in recent})
-        got, tied = lax.optimization_barrier((arriving[k], tied))
+        got, shared, tied = lax.optimization_barrier((arriving[k], shares.get(before, ()), tied))
         totals.update(tied[0])
         sums.update(tied[1])
+        if k >= LAG:
+            shares[k - LAG] = share(jnp.where(inner, totals[k - LAG], got))
         if k < count:
             halves[k] = add(parts[k], got)
             others[k] = middle_swap(halves[k])
-        if k >= LAG:
-            results[k - LAG] = jnp.where(inner, totals[k - LAG], got)
         if k - 1 in others:
             tied = {i: halves[i] for i in (k - 1, k) if i in halves}
             other, tied = lax.optimization_barrier((others[k - 1], tied))
@@ -77,35 +75,25 @@
             if following < count:
                 value = jnp.where(inner, value, parts[following])
             arriving[following] = end_swap(value)
-        for group in groups:
-            if group[-1] == k - LAG:
-                tied = {i: totals[i] for i in (k - 1,) if i in totals}
-                ready, tied = lax.optimization_barrier(([results[i] for i in group], tied))
-                totals.update(tied)
-                shares.append((k + len(group), group, share(ready)))
-        now = [entry for entry in shares if entry[0] <= k]
-        shares = [entry for entry in shares if entry[0] > k]
         tied = {i: totals[i] for i in (k - 1,) if i in totals}
-        waited, pending, tied = lax.optimization_barrier(
-            ([entry[2] for entry in now], pending, tied)
-        )
+        shared, pending, tied = lax.optimization_barrier((shared, pending, tied))
         totals.update(tied)
         recent = ()
-        for (_, group, _), values in zip(now, waited):
-            recent += tuple(group)
-            emit(group, values)
+        if before >= 0:
+            recent = (before,)
+            emit(before, shared)
         if k >= LAG and pending is not None:
             pending = side(pending)
-    for _, group, values in shares:
-        values, tied = lax.optimization_barrier((values, {i: sums[i] for i in recent}))
-        sums.update(tied)
-        recent = tuple(group)
-        emit(group, values)
+    tied = {i: sums[i] for i in recent}
+    shared, tied = lax.optimization_barrier((shares[count - 1], tied))
+    sums.update(tied)
+    emit(count - 1, shared)
     while pending is not None:
         pending = side(pending)
 
 
-def square(block_len, rows, squares):
+def square(block_len, rows, squares, held):
+    held[...] = rows[...]
     lane = lax.broadcasted_iota(jnp.int32, (block_len, block_len), 1)
     diagonal = lane == lax.broadcasted_iota(jnp.int32, (block_len, block_len), 0)
     for b in range(squares.shape[0]):
@@ -133,7 +121,7 @@
         )
 
 
-def scale(n_dp, n_mp, width, order, rest, rows, *refs):
+def scale(n_dp, n_mp, width, rest, rows, *refs):
     squares, inverse, pieces = refs[:n_mp], refs[n_mp], refs[n_mp + 1 :]
     block_count, block_len = inverse.shape
     dp = lax.axis_index("dp")
@@ -146,11 +134,12 @@
     factors = inverse[...] * rest[:block_count, :]
     lane = lax.broadcasted_iota(jnp.int32, (block_len, block_len), 1)
     diagonal = lane == lax.broadcasted_iota(jnp.int32, (block_len, block_len), 0)
+    order = [jnp.max(rest[block_count + b : block_count + b + 1, :]) for b in range(block_count)]
     sources = []
     for slot in range(block_count):
         source, factor = 0, factors[0:1]
         for b in range(1, block_count):
-            here = order[0, b] == slot
+            here = order[b] == slot
             source = jnp.where(here, b, source)
             factor = jnp.where(here, factors[b : b + 1], factor)
         factor = jnp.sum(jnp.where(diagonal, factor, 0.0), axis=1, keepdims=True)
@@ -169,10 +158,10 @@
                         pieces[j * per_owner + i][place, :] = value.astype(jnp.bfloat16)
 
 
-def store(n_dp, g, first, offset, shards, *refs):
+def store(n_dp, g, first, shards, *refs):
     values, gain, weight = refs[0], refs[1], refs[2]
     out, sums, results, semaphores = refs[-4:]
-    (_, chunk, width) = results.shape
+    _, chunk, width = results.shape
     far = lax.axis_index("mp") >> 1
     own_width = weight.shape[0] // n_dp
     column = pl.multiple_of((far ^ g) * width, 128)
@@ -184,7 +173,7 @@
         for at in range(0, chunk, 128):
             gains = gain[:, start + at : start + at + 128]
             gains = jnp.sum(jnp.where(diagonal, gains, 0.0), axis=1, keepdims=True)
-            total = values[e, offset + at : offset + at + 128, :].astype(jnp.float32) * (1.0 / shards)
+            total = values[e, at : at + 128, :].astype(jnp.float32) * (1.0 / shards)
             results[e, at : at + 128, :] = total * gains
             weights = weight[start + at : start + at + 128, pl.ds(column, width)]
             total = total * weights.astype(jnp.float32)
@@ -233,11 +222,14 @@
 
     vmem, smem = pl.BlockSpec(memory_space=pltpu.VMEM), pl.BlockSpec(memory_space=pltpu.SMEM)
     hbm = pl.BlockSpec(memory_space=pltpu.MemorySpace.HBM)
-    squares = pl.pallas_call(
+    squares, held = pl.pallas_call(
         functools.partial(square, block_len),
-        out_shape=jax.ShapeDtypeStruct((block_count, block_len), jnp.float32),
+        out_shape=[
+            jax.ShapeDtypeStruct((block_count, block_len), jnp.float32),
+            jax.ShapeDtypeStruct(policy_input.shape, policy_input.dtype),
+        ],
         in_specs=[vmem],
-        out_specs=vmem,
+        out_specs=[vmem] * 2,
         compiler_params=pltpu.CompilerParams(vmem_limit_bytes=32 * 2**20),
         name="square",
     )(policy_input)
@@ -253,25 +245,26 @@
         functools.partial(scale, n_dp, n_mp, chunk),
         out_shape=[jax.ShapeDtypeStruct((block_count, block_len), jnp.float32)]
         + [jax.ShapeDtypeStruct((tokens, chunk), jnp.bfloat16)] * (n_dp * feature_blocks),
-        in_specs=[smem] + [vmem] * (2 + n_mp),
+        in_specs=[vmem] * (2 + n_mp),
         out_specs=[vmem] * (1 + n_dp * feature_blocks),
         compiler_params=pltpu.CompilerParams(vmem_limit_bytes=32 * 2**20),
         name="scale",
-    )(block_order, rest, policy_input, *squares)
+    )(rest, held, *squares)
 
     cotangents, inverse = lax.optimization_barrier((cotangents, inverse))
     cotangents = jnp.concatenate(in_order(cotangents), axis=0)
-    parts, arriving = [], {}
+    parts, arriving, ready = [], {}, []
 
     def rows(f):
         got = [pieces[f]]
         for j in range(1, n_dp):
             piece = pieces[j * feature_blocks + f]
-            if f > 1:
-                piece, parts[1] = lax.optimization_barrier((piece, parts[1]))
+            if f:
+                tied = min(f - 1, 1)
+                piece, parts[tied] = lax.optimization_barrier((piece, parts[tied]))
             piece = swap(piece, "dp", j)
-            if f:
-                piece, parts[f - 1] = lax.optimization_barrier((piece, parts[f - 1]))
+            tied, i = (parts, f - 1) if f else (ready, 0)
+            piece, tied[i] = lax.optimization_barrier((piece, tied[i]))
             got.append(piece)
         return jnp.concatenate(in_order(got), axis=0)
 
@@ -289,13 +282,13 @@
             tied = min(1, len(parts) - 1)
             near, parts[tied] = lax.optimization_barrier((near, parts[tied]))
             near = swap(near, "mp", 2 * g)
-        cotangent = both_cores(near)
+        ready[:] = [both_cores(near)]
         for f in range(feature_blocks):
             if not g:
                 gathered.append(rows(f))
             part = lax.dot_general(
                 gathered[f],
-                cotangent,
+                ready[0],
                 (((0,), (0,)), ((), ())),
                 preferred_element_type=jnp.float32,
             )
@@ -308,43 +301,34 @@
     out = []
     sums = {}
 
-    def share(values):
-        values = jnp.concatenate(values, axis=0)
-        if n_dp == 2:
-            return (values, swap(values, "dp", 1))
-        return (lax.all_gather(values, "dp"),)
-
-    def emit(group, values):
-        if len(values) == 2:
-            values = jnp.stack(in_order(values))
-        else:
-            (values,) = values
-        for i, k in enumerate(group):
-            g, f = divmod(k, feature_blocks)
-            before = tuple(out)
-            result, total = pl.pallas_call(
-                functools.partial(store, n_dp, g, f * chunk, i * chunk, shards),
-                out_shape=[
-                    jax.ShapeDtypeStruct((local_width, n_mp * columns), jnp.float32),
-                    jax.ShapeDtypeStruct((n_dp, chunk), jnp.float32),
-                ],
-                in_specs=[vmem] * 3 + [hbm] * len(before),
-                out_specs=[hbm, vmem],
-                input_output_aliases={3: 0} if before else {},
-                scratch_shapes=[
-                    pltpu.VMEM((n_dp, chunk, 2 * columns), jnp.float32),
-                    pltpu.SemaphoreType.DMA((n_dp,)),
-                ],
-                compiler_params=pltpu.CompilerParams(vmem_limit_bytes=32 * 2**20),
-                name="store",
-            )(values, gain, key_weight, *before)
-            out[:] = [result]
-            sums[k] = total
+    def share(value):
+        return [value] + [swap(value, "dp", j) for j in range(1, n_dp)]
+
+    def emit(k, values):
+        g, f = divmod(k, feature_blocks)
+        before = tuple(out)
+        result, sums[k] = pl.pallas_call(
+            functools.partial(store, n_dp, g, f * chunk, shards),
+            out_shape=[
+                jax.ShapeDtypeStruct((local_width, n_mp * columns), jnp.float32),
+                jax.ShapeDtypeStruct((n_dp, chunk), jnp.float32),
+            ],
+            in_specs=[vmem] * 3 + [hbm] * len(before),
+            out_specs=[hbm, vmem],
+            input_output_aliases={3: 0} if before else {},
+            scratch_shapes=[
+                pltpu.VMEM((n_dp, chunk, 2 * columns), jnp.float32),
+                pltpu.SemaphoreType.DMA((n_dp,)),
+            ],
+            compiler_params=pltpu.CompilerParams(vmem_limit_bytes=32 * 2**20),
+            name="store",
+        )(jnp.stack(in_order(values)), gain, key_weight, *before)
+        out[:] = [result]
 
     def key_steps():
         yield (inverse,)
         (late_inverse,) = side_values[0]
-        normed = policy_input.astype(jnp.float32) * late_inverse.reshape(-1, 1) * gain
+        normed = held.astype(jnp.float32) * late_inverse.reshape(-1, 1) * gain
         normed = lax.optimization_barrier(normed.astype(jnp.bfloat16))
         partial = jnp.dot(normed, key_weight, preferred_element_type=jnp.float32)
         cut = [partial[:, i * columns : (i + 1) * columns] for i in range(n_mp)]

time: 129 us -> 138 us (1.070)
  waiting for transfers between devices: 45.1 us -> 54 us
  starting transfers between devices: 55.6 us -> 58.1 us
  local copies, waits for them, and re-layouts: 4.59 us -> 2.59 us
    ppermute x20 -> x23, waiting for transfers between devices: 28.6 us -> 39.6 us  [swap(): lax.ppermute(value, axis, [(i, i ^ bit) for i in range(lax.axis_size(axis...]
    ppermute x20 -> x23, starting transfers between devices: 17.8 us -> 20.5 us  [swap(): lax.ppermute(value, axis, [(i, i ^ bit) for i in range(lax.axis_size(axis...]
    ppermute x11, waiting for transfers between devices: 16.5 us -> 14.4 us  [end_swap(): return lax.ppermute(value, 'section', [(0, 1), (1, 0), (2, 3), (3, 2)])]
    unnamed x18 -> x9, local copies, waits for them, and re-layouts: 4.46 us -> 2.52 us
  transfers between devices with their start and end apart: 39 -> 42, of which waited for: 15 -> 15; matrix products, arithmetic and copies ran while one was open for 7% -> 6% of each run, Pallas kernels for 9% -> 8%
where the time goes in v8:
time: 138 us; the launch traced here: 137 us
  starting transfers between devices  58.1 us (42%)
  waiting for transfers between devices  54 us (39%)
  Pallas kernels  11.8 us (9%)
  other arithmetic  5.59 us (4%)
  matrix products  3.8 us (3%)
  local copies, waits for them, and re-layouts  2.59 us (2%)
    ppermute x23, waiting for transfers between devices, swap(): lax.ppermute(value, axis, [(i, i ^ bit) for i in range(lax.axis_size(axis...  39.6 us
    ppermute x11, starting transfers between devices, end_swap(): return lax.ppermute(value, 'section', [(0, 1), (1, 0), (2, 3), (3, 2)])  32 us
    ppermute x23, starting transfers between devices, swap(): lax.ppermute(value, axis, [(i, i ^ bit) for i in range(lax.axis_size(axis...  20.5 us
    ppermute x11, waiting for transfers between devices, end_swap(): return lax.ppermute(value, 'section', [(0, 1), (1, 0), (2, 3), (3, 2)])  14.4 us
    pallas_call x8, Pallas kernels, emit(): pl.pallas_call(functools.partial(store, n_dp, g, f * chunk, shards), out_...  9.57 us
    ppermute x8, starting transfers between devices, middle_swap(): return lax.ppermute(value, 'section', [(1, 2), (2, 1), (0, 0), (3, 3)])  5.6 us
  transfers between devices with their start and end apart: 42, of which 15 were waited for; matrix products, arithmetic and copies ran while one was open for 6% of the time, Pallas kernels for 8%

profile of v8, /device:TPU:0, one launch (start us, length us, event | category | flops | bytes accessed | tf_op | source)
XLA Modules:
  0.0 137.2 jit_solution(9139063582008093208)
XLA Ops:
  0.6 3.0 %collective-permute-start.4 = (bf16[256,256]{1,0:T(8,128)(2,1)}, bf16[256,256]{1,0:T(8,128)(2,1)S(1)}, u32[]{:S(2)}, u32[]{:S(2)}) collective-permute-start(bf16[256,256]{1,0:T(8,128)(2,1)} %param.17), channel_id=1, source_target_pairs={{0,4},{4,0},{1,5},{5,1},{2,6},{6,2},{3,7},{7,3},{8,12},{12,8},{9,1... | collective-permute-start | bytes 393224 | tf_op jit(solution)/shard_map/ppermute | solution.py:16
  13.3 4.2 %collective-permute-done.3 = bf16[256,256]{1,0:T(8,128)(2,1)S(1)} collective-permute-done((bf16[256,256]{1,0:T(8,128)(2,1)S(1)}, bf16[256,256]{1,0:T(8,128)(2,1)S(1)}, u32[]{:S(2)}, u32[]{:S(2)}) %collective-permute-start.3) | collective-permute-done | bytes 131104 | tf_op jit(solution)/shard_map/ppermute | solution.py:16
  18.5 4.5 %collective-permute-done.6 = bf16[256,256]{1,0:T(8,128)(2,1)S(1)} collective-permute-done((bf16[256,256]{1,0:T(8,128)(2,1)S(1)}, bf16[256,256]{1,0:T(8,128)(2,1)S(1)}, u32[]{:S(2)}, u32[]{:S(2)}) %collective-permute-start.6) | collective-permute-done | bytes 131104 | tf_op jit(solution)/shard_map/ppermute | solution.py:16
  24.6 1.6 %collective-permute-start.12 = (bf16[256,512]{1,0:T(8,128)(2,1)S(1)}, bf16[256,512]{1,0:T(8,128)(2,1)S(1)}, u32[]{:S(2)}, u32[]{:S(2)}) collective-permute-start(bf16[256,512]{1,0:T(8,128)(2,1)S(1)} %fusion), channel_id=1, source_target_pairs={{0,8},{8,0},{16,24},{24,16},{1,9},{9,1},{17,25},{25,17},{2,10},{10... | collective-permute-start | bytes 786440 | tf_op jit(solution)/shard_map/ppermute | solution.py:35
  26.7 1.7 %collective-permute-done.7 = bf16[256,256]{1,0:T(8,128)(2,1)S(1)} collective-permute-done((bf16[256,256]{1,0:T(8,128)(2,1)S(1)}, bf16[256,256]{1,0:T(8,128)(2,1)S(1)}, u32[]{:S(2)}, u32[]{:S(2)}) %collective-permute-start.7) | collective-permute-done | bytes 131104 | tf_op jit(solution)/shard_map/ppermute | solution.py:16
  29.3 1.6 %collective-permute-start.15 = (bf16[256,512]{1,0:T(8,128)(2,1)S(1)}, bf16[256,512]{1,0:T(8,128)(2,1)S(1)}, u32[]{:S(2)}, u32[]{:S(2)}) collective-permute-start(bf16[256,512]{1,0:T(8,128)(2,1)S(1)} %fusion.3), channel_id=1, source_target_pairs={{0,8},{8,0},{16,24},{24,16},{1,9},{9,1},{17,25},{25,17},{2,10},{10... | collective-permute-start | bytes 786440 | tf_op jit(solution)/shard_map/ppermute | solution.py:35
  31.8 2.0 %collective-permute-done.12 = bf16[256,512]{1,0:T(8,128)(2,1)S(1)} collective-permute-done((bf16[256,512]{1,0:T(8,128)(2,1)S(1)}, bf16[256,512]{1,0:T(8,128)(2,1)S(1)}, u32[]{:S(2)}, u32[]{:S(2)}) %collective-permute-start.12) | collective-permute-done | bytes 262176 | tf_op jit(solution)/shard_map/ppermute | solution.py:35
  34.6 4.9 %collective-permute-done.10 = bf16[256,512]{1,0:T(8,128)(2,1)S(1)} collective-permute-done((bf16[256,512]{1,0:T(8,128)(2,1)S(1)}, bf16[256,512]{1,0:T(8,128)(2,1)S(1)}, u32[]{:S(2)}, u32[]{:S(2)}) %collective-permute-start.10) | collective-permute-done | bytes 262176 | tf_op jit(solution)/shard_map/ppermute | solution.py:35
  40.8 1.7 %collective-permute-done.15 = bf16[256,512]{1,0:T(8,128)(2,1)S(1)} collective-permute-done((bf16[256,512]{1,0:T(8,128)(2,1)S(1)}, bf16[256,512]{1,0:T(8,128)(2,1)S(1)}, u32[]{:S(2)}, u32[]{:S(2)}) %collective-permute-start.15) | collective-permute-done | bytes 262176 | tf_op jit(solution)/shard_map/ppermute | solution.py:35
  43.3 6.7 %collective-permute-start.17 = (bf16[256,512]{1,0:T(8,128)(2,1)S(1)}, bf16[256,512]{1,0:T(8,128)(2,1)S(1)}, u32[]{:S(2)}, u32[]{:S(2)}) collective-permute-start(bf16[256,512]{1,0:T(8,128)(2,1)S(1)} %get-tuple-element.285), channel_id=1, source_target_pairs={{0,8},{8,0},{16,24},{24,16},{1,9},{9,1},{17,25},{25,17},{2,10},{10... | collective-permute-start | bytes 786440 | tf_op jit(solution)/shard_map/ppermute | solution.py:35
  51.3 5.7 %collective-permute-done.17 = bf16[256,512]{1,0:T(8,128)(2,1)S(1)} collective-permute-done((bf16[256,512]{1,0:T(8,128)(2,1)S(1)}, bf16[256,512]{1,0:T(8,128)(2,1)S(1)}, u32[]{:S(2)}, u32[]{:S(2)}) %collective-permute-start.17) | collective-permute-done | bytes 262176 | tf_op jit(solution)/shard_map/ppermute | solution.py:35
  57.9 1.5 %collective-permute-start.18 = (bf16[256,512]{1,0:T(8,128)(2,1)S(1)}, bf16[256,512]{1,0:T(8,128)(2,1)S(1)}, u32[]{:S(2)}, u32[]{:S(2)}) collective-permute-start(bf16[256,512]{1,0:T(8,128)(2,1)S(1)} %broadcast_select_fusion.14), channel_id=1, source_target_pairs={{0,4},{4,0},{1,5},{5,1},{2,6},{6,2},{3,7},{7,3},{8,12},{12,8},{9,1... | collective-permute-start | bytes 786440 | tf_op jit(solution)/shard_map/ppermute | solution.py:16
  59.6 3.8 %collective-permute-start.22 = (bf16[256,512]{1,0:T(8,128)(2,1)S(1)}, bf16[256,512]{1,0:T(8,128)(2,1)S(1)}, u32[]{:S(2)}, u32[]{:S(2)}) collective-permute-start(bf16[256,512]{1,0:T(8,128)(2,1)S(1)} %get-tuple-element.283), channel_id=1, source_target_pairs={{0,8},{8,0},{16,24},{24,16},{1,9},{9,1},{17,25},{25,17},{2,10},{10... | collective-permute-start | bytes 786440 | tf_op jit(solution)/shard_map/ppermute | solution.py:35
  63.7 1.8 %collective-permute-done.18 = bf16[256,512]{1,0:T(8,128)(2,1)S(1)} collective-permute-done((bf16[256,512]{1,0:T(8,128)(2,1)S(1)}, bf16[256,512]{1,0:T(8,128)(2,1)S(1)}, u32[]{:S(2)}, u32[]{:S(2)}) %collective-permute-start.18) | collective-permute-done | bytes 262176 | tf_op jit(solution)/shard_map/ppermute | solution.py:16
  68.3 5.7 %collective-permute-start.25 = (bf16[256,512]{1,0:T(8,128)(2,1)S(1)}, bf16[256,512]{1,0:T(8,128)(2,1)S(1)}, u32[]{:S(2)}, u32[]{:S(2)}) collective-permute-start(bf16[256,512]{1,0:T(8,128)(2,1)S(1)} %get-tuple-element.279), channel_id=1, source_target_pairs={{0,8},{8,0},{16,24},{24,16},{1,9},{9,1},{17,25},{25,17},{2,10},{10... | collective-permute-start | bytes 786440 | tf_op jit(solution)/shard_map/ppermute | solution.py:35
  81.6 6.1 %collective-permute-done.26 = bf16[256,512]{1,0:T(8,128)(2,1)S(1)} collective-permute-done((bf16[256,512]{1,0:T(8,128)(2,1)S(1)}, bf16[256,512]{1,0:T(8,128)(2,1)S(1)}, u32[]{:S(2)}, u32[]{:S(2)}) %collective-permute-start.26) | collective-permute-done | bytes 262176 | tf_op jit(solution)/shard_map/ppermute | solution.py:16
  87.8 3.5 %collective-permute-start.24 = (bf16[256,512]{1,0:T(8,128)(2,1)S(1)}, bf16[256,512]{1,0:T(8,128)(2,1)S(1)}, u32[]{:S(2)}, u32[]{:S(2)}) collective-permute-start(bf16[256,512]{1,0:T(8,128)(2,1)S(1)} %get-tuple-element.281), channel_id=1, source_target_pairs={{0,8},{8,0},{16,24},{24,16},{1,9},{9,1},{17,25},{25,17},{2,10},{10... | collective-permute-start | bytes 786440 | tf_op jit(solution)/shard_map/ppermute | solution.py:35
  92.1 2.9 %collective-permute-start.35 = (bf16[256,512]{1,0:T(8,128)(2,1)S(1)}, bf16[256,512]{1,0:T(8,128)(2,1)S(1)}, u32[]{:S(2)}, u32[]{:S(2)}) collective-permute-start(bf16[256,512]{1,0:T(8,128)(2,1)S(1)} %reduce-precision_convert_fusion.3), channel_id=1, source_target_pairs={{0,8},{8,0},{16,24},{24,16},{1,9},{9,1},{17,25},{25,17},{2,10},{10... | collective-permute-start | bytes 786440 | tf_op jit(solution)/shard_map/ppermute | solution.py:35
  98.6 6.3 %collective-permute-done.27 = bf16[256,512]{1,0:T(8,128)(2,1)S(1)} collective-permute-done((bf16[256,512]{1,0:T(8,128)(2,1)S(1)}, bf16[256,512]{1,0:T(8,128)(2,1)S(1)}, u32[]{:S(2)}, u32[]{:S(2)}) %collective-permute-start.27) | collective-permute-done | bytes 262176 | tf_op jit(solution)/shard_map/ppermute | solution.py:16
  106.0 2.1 %collective-permute-start.34 = (bf16[256,512]{1,0:T(8,128)(2,1)S(1)}, bf16[256,512]{1,0:T(8,128)(2,1)S(1)}, u32[]{:S(2)}, u32[]{:S(2)}) collective-permute-start(bf16[256,512]{1,0:T(8,128)(2,1)S(1)} %reduce-precision_convert_fusion.1), channel_id=1, source_target_pairs={{0,8},{8,0},{16,24},{24,16},{1,9},{9,1},{17,25},{25,17},{2,10},{10... | collective-permute-start | bytes 786440 | tf_op jit(solution)/shard_map/ppermute | solution.py:35
  111.1 3.6 %collective-permute-start.39 = (bf16[256,512]{1,0:T(8,128)(2,1)S(1)}, bf16[256,512]{1,0:T(8,128)(2,1)S(1)}, u32[]{:S(2)}, u32[]{:S(2)}) collective-permute-start(bf16[256,512]{1,0:T(8,128)(2,1)S(1)} %reduce-precision_convert_fusion), channel_id=1, source_target_pairs={{0,8},{8,0},{16,24},{24,16},{1,9},{9,1},{17,25},{25,17},{2,10},{10... | collective-permute-start | bytes 786440 | tf_op jit(solution)/shard_map/ppermute | solution.py:35
  116.9 4.4 %collective-permute-done.37 = bf16[256,512]{1,0:T(8,128)(2,1)S(1)} collective-permute-done((bf16[256,512]{1,0:T(8,128)(2,1)S(1)}, bf16[256,512]{1,0:T(8,128)(2,1)S(1)}, u32[]{:S(2)}, u32[]{:S(2)}) %collective-permute-start.37) | collective-permute-done | bytes 262176 | tf_op jit(solution)/shard_map/ppermute | solution.py:16
  123.7 5.1 %collective-permute-done.40 = bf16[256,512]{1,0:T(8,128)(2,1)S(1)} collective-permute-done((bf16[256,512]{1,0:T(8,128)(2,1)S(1)}, bf16[256,512]{1,0:T(8,128)(2,1)S(1)}, u32[]{:S(2)}, u32[]{:S(2)}) %collective-permute-start.40) | collective-permute-done | bytes 262176 | tf_op jit(solution)/shard_map/ppermute | solution.py:16
  131.6 3.7 %collective-permute-done.41 = bf16[256,512]{1,0:T(8,128)(2,1)S(1)} collective-permute-done((bf16[256,512]{1,0:T(8,128)(2,1)S(1)}, bf16[256,512]{1,0:T(8,128)(2,1)S(1)}, u32[]{:S(2)}, u32[]{:S(2)}) %collective-permute-start.41) | collective-permute-done | bytes 262176 | tf_op jit(solution)/shard_map/ppermute | solution.py:16
  (156 shorter events, 47.7 us)
Async XLA Ops:
  0.6 9.9 %collective-permute-start.4 = (bf16[256,256]{1,0:T(8,128)(2,1)}, bf16[256,256]{1,0:T(8,128)(2,1)S(1)}, u32[]{:S(2)}, u32[]{:S(2)}) collective-permute-start(bf16[256,256]{1,0:T(8,128)(2,1)} %param.17), channel_id=1, source_target_pairs={{0,4},{4,0},{1,5},{5,1},{2,6},{6,2},{3,7},{7,3},{8,12},{12,8},{9,1... | collective-permute-start | bytes 393224 | tf_op jit(solution)/shard_map/ppermute | solution.py:16
  26.2 13.3 %collective-permute-start.10 = (bf16[256,512]{1,0:T(8,128)(2,1)S(1)}, bf16[256,512]{1,0:T(8,128)(2,1)S(1)}, u32[]{:S(2)}, u32[]{:S(2)}) collective-permute-start(bf16[256,512]{1,0:T(8,128)(2,1)S(1)} %fusion.1), channel_id=1, source_target_pairs={{0,8},{8,0},{16,24},{24,16},{1,9},{9,1},{17,25},{25,17},{2,10},{10... | collective-permute-start | bytes 786440 | tf_op jit(solution)/shard_map/ppermute | solution.py:35
  28.4 11.9 %collective-permute-start.14 = (bf16[256,256]{1,0:T(8,128)(2,1)S(1)}, bf16[256,256]{1,0:T(8,128)(2,1)S(1)}, u32[]{:S(2)}, u32[]{:S(2)}) collective-permute-start(bf16[256,256]{1,0:T(8,128)(2,1)S(1)} %get-tuple-element.166), channel_id=1, source_target_pairs={{0,4},{4,0},{1,5},{5,1},{2,6},{6,2},{3,7},{7,3},{8,12},{12,8},{9,1... | collective-permute-start | bytes 393224 | tf_op jit(solution)/shard_map/ppermute | solution.py:16
  29.3 13.3 %collective-permute-start.15 = (bf16[256,512]{1,0:T(8,128)(2,1)S(1)}, bf16[256,512]{1,0:T(8,128)(2,1)S(1)}, u32[]{:S(2)}, u32[]{:S(2)}) collective-permute-start(bf16[256,512]{1,0:T(8,128)(2,1)S(1)} %fusion.3), channel_id=1, source_target_pairs={{0,8},{8,0},{16,24},{24,16},{1,9},{9,1},{17,25},{25,17},{2,10},{10... | collective-permute-start | bytes 786440 | tf_op jit(solution)/shard_map/ppermute | solution.py:35
  30.9 9.7 %collective-permute-start.8 = (bf16[512,256]{1,0:T(8,128)(2,1)S(1)}, bf16[512,256]{1,0:T(8,128)(2,1)S(1)}, u32[]{:S(2)}, u32[]{:S(2)}) collective-permute-start(bf16[512,256]{1,0:T(8,128)(2,1)S(1)} %pad_maximum_fusion.10), channel_id=1, source_target_pairs={{0,2},{1,3},{2,0},{3,1},{4,6},{5,7},{6,4},{7,5},{8,10},{9,11},{10,... | collective-permute-start | bytes 786440 | tf_op jit(solution)/shard_map/ppermute | solution.py:16
  39.6 10.4 %collective-permute-start.11 = (bf16[256,512]{1,0:T(8,128)(2,1)S(1)}, bf16[256,512]{1,0:T(8,128)(2,1)S(1)}, u32[]{:S(2)}, u32[]{:S(2)}) collective-permute-start(bf16[256,512]{1,0:T(8,128)(2,1)S(1)} %reduce-precision_convert_fusion.15), channel_id=1, source_target_pairs={{8,16},{16,8},{0,0},{24,24},{9,17},{17,9},{1,1},{25,25},{10,18},{1... | collective-permute-start | bytes 786440 | tf_op jit(solution)/shard_map/ppermute | solution.py:39
  42.6 15.3 %collective-permute-start.19 = (bf16[256,512]{1,0:T(8,128)(2,1)S(1)}, bf16[256,512]{1,0:T(8,128)(2,1)S(1)}, u32[]{:S(2)}, u32[]{:S(2)}) collective-permute-start(bf16[256,512]{1,0:T(8,128)(2,1)S(1)} %reduce-precision_convert_fusion.12), channel_id=1, source_target_pairs={{8,16},{16,8},{0,0},{24,24},{9,17},{17,9},{1,1},{25,25},{10,18},{1... | collective-permute-start | bytes 786440 | tf_op jit(solution)/shard_map/ppermute | solution.py:39
  43.3 13.8 %collective-permute-start.17 = (bf16[256,512]{1,0:T(8,128)(2,1)S(1)}, bf16[256,512]{1,0:T(8,128)(2,1)S(1)}, u32[]{:S(2)}, u32[]{:S(2)}) collective-permute-start(bf16[256,512]{1,0:T(8,128)(2,1)S(1)} %get-tuple-element.285), channel_id=1, source_target_pairs={{0,8},{8,0},{16,24},{24,16},{1,9},{9,1},{17,25},{25,17},{2,10},{10... | collective-permute-start | bytes 786440 | tf_op jit(solution)/shard_map/ppermute | solution.py:35
  50.9 12.8 %collective-permute-start.16 = (bf16[256,512]{1,0:T(8,128)(2,1)S(1)}, bf16[256,512]{1,0:T(8,128)(2,1)S(1)}, u32[]{:S(2)}, u32[]{:S(2)}) collective-permute-start(bf16[256,512]{1,0:T(8,128)(2,1)S(1)} %get-tuple-element.287), channel_id=1, source_target_pairs={{0,8},{8,0},{16,24},{24,16},{1,9},{9,1},{17,25},{25,17},{2,10},{10... | collective-permute-start | bytes 786440 | tf_op jit(solution)/shard_map/ppermute | solution.py:35
  57.2 10.7 %collective-permute-start.21 = (bf16[256,512]{1,0:T(8,128)(2,1)S(1)}, bf16[256,512]{1,0:T(8,128)(2,1)S(1)}, u32[]{:S(2)}, u32[]{:S(2)}) collective-permute-start(bf16[256,512]{1,0:T(8,128)(2,1)S(1)} %reduce-precision_convert_fusion.10), channel_id=1, source_target_pairs={{8,16},{16,8},{0,0},{24,24},{9,17},{17,9},{1,1},{25,25},{10,18},{1... | collective-permute-start | bytes 786440 | tf_op jit(solution)/shard_map/ppermute | solution.py:39
  59.6 17.0 %collective-permute-start.22 = (bf16[256,512]{1,0:T(8,128)(2,1)S(1)}, bf16[256,512]{1,0:T(8,128)(2,1)S(1)}, u32[]{:S(2)}, u32[]{:S(2)}) collective-permute-start(bf16[256,512]{1,0:T(8,128)(2,1)S(1)} %get-tuple-element.283), channel_id=1, source_target_pairs={{0,8},{8,0},{16,24},{24,16},{1,9},{9,1},{17,25},{25,17},{2,10},{10... | collective-permute-start | bytes 786440 | tf_op jit(solution)/shard_map/ppermute | solution.py:35
  65.6 11.8 %collective-permute-start.20 = (bf16[256,512]{1,0:T(8,128)(2,1)S(1)}, bf16[256,512]{1,0:T(8,128)(2,1)S(1)}, u32[]{:S(2)}, u32[]{:S(2)}) collective-permute-start(bf16[256,512]{1,0:T(8,128)(2,1)S(1)} %reduce-precision_convert_fusion.8), channel_id=1, source_target_pairs={{8,16},{16,8},{0,0},{24,24},{9,17},{17,9},{1,1},{25,25},{10,18},{1... | collective-permute-start | bytes 786440 | tf_op jit(solution)/shard_map/ppermute | solution.py:39
  66.3 10.3 %collective-permute-start.23 = (bf16[256,512]{1,0:T(8,128)(2,1)S(1)}, bf16[256,512]{1,0:T(8,128)(2,1)S(1)}, u32[]{:S(2)}, u32[]{:S(2)}) collective-permute-start(bf16[256,512]{1,0:T(8,128)(2,1)S(1)} %broadcast_select_fusion.12), channel_id=1, source_target_pairs={{0,4},{4,0},{1,5},{5,1},{2,6},{6,2},{3,7},{7,3},{8,12},{12,8},{9,1... | collective-permute-start | bytes 786440 | tf_op jit(solution)/shard_map/ppermute | solution.py:16
  68.3 12.4 %collective-permute-start.25 = (bf16[256,512]{1,0:T(8,128)(2,1)S(1)}, bf16[256,512]{1,0:T(8,128)(2,1)S(1)}, u32[]{:S(2)}, u32[]{:S(2)}) collective-permute-start(bf16[256,512]{1,0:T(8,128)(2,1)S(1)} %get-tuple-element.279), channel_id=1, source_target_pairs={{0,8},{8,0},{16,24},{24,16},{1,9},{9,1},{17,25},{25,17},{2,10},{10... | collective-permute-start | bytes 786440 | tf_op jit(solution)/shard_map/ppermute | solution.py:35
  76.7 14.7 %collective-permute-start.31 = (bf16[256,512]{1,0:T(8,128)(2,1)S(1)}, bf16[256,512]{1,0:T(8,128)(2,1)S(1)}, u32[]{:S(2)}, u32[]{:S(2)}) collective-permute-start(bf16[256,512]{1,0:T(8,128)(2,1)S(1)} %reduce-precision_convert_fusion.6), channel_id=1, source_target_pairs={{8,16},{16,8},{0,0},{24,24},{9,17},{17,9},{1,1},{25,25},{10,18},{1... | collective-permute-start | bytes 786440 | tf_op jit(solution)/shard_map/ppermute | solution.py:39
  77.6 14.5 %collective-permute-start.29 = (bf16[256,256]{1,0:T(8,128)(2,1)S(1)}, bf16[256,256]{1,0:T(8,128)(2,1)S(1)}, u32[]{:S(2)}, u32[]{:S(2)}) collective-permute-start(bf16[256,256]{1,0:T(8,128)(2,1)S(1)} %select_convert_fusion.1), channel_id=1, source_target_pairs={{0,2},{1,3},{2,0},{3,1},{4,6},{5,7},{6,4},{7,5},{8,10},{9,11},{10,... | collective-permute-start | bytes 393224 | tf_op jit(solution)/shard_map/ppermute | solution.py:16
  78.6 16.4 %collective-permute-start.30 = (bf16[256,256]{1,0:T(8,128)(2,1)S(1)}, bf16[256,256]{1,0:T(8,128)(2,1)S(1)}, u32[]{:S(2)}, u32[]{:S(2)}) collective-permute-start(bf16[256,256]{1,0:T(8,128)(2,1)S(1)} %get-tuple-element.289), channel_id=1, source_target_pairs={{0,3},{1,2},{2,1},{3,0},{4,7},{5,6},{6,5},{7,4},{8,11},{9,10},{10,... | collective-permute-start | bytes 393224 | tf_op jit(solution)/shard_map/ppermute | solution.py:16
  80.7 14.3 %collective-permute-start.28 = (bf16[256,256]{1,0:T(8,128)(2,1)S(1)}, bf16[256,256]{1,0:T(8,128)(2,1)S(1)}, u32[]{:S(2)}, u32[]{:S(2)}) collective-permute-start(bf16[256,256]{1,0:T(8,128)(2,1)S(1)} %get-tuple-element.290), channel_id=1, source_target_pairs={{0,1},{1,0},{2,3},{3,2},{4,5},{5,4},{6,7},{7,6},{8,9},{9,8},{10,11... | collective-permute-start | bytes 393224 | tf_op jit(solution)/shard_map/ppermute | solution.py:16
  87.8 10.8 %collective-permute-start.24 = (bf16[256,512]{1,0:T(8,128)(2,1)S(1)}, bf16[256,512]{1,0:T(8,128)(2,1)S(1)}, u32[]{:S(2)}, u32[]{:S(2)}) collective-permute-start(bf16[256,512]{1,0:T(8,128)(2,1)S(1)} %get-tuple-element.281), channel_id=1, source_target_pairs={{0,8},{8,0},{16,24},{24,16},{1,9},{9,1},{17,25},{25,17},{2,10},{10... | collective-permute-start | bytes 786440 | tf_op jit(solution)/shard_map/ppermute | solution.py:35
  91.3 14.5 %collective-permute-start.33 = (bf16[256,512]{1,0:T(8,128)(2,1)S(1)}, bf16[256,512]{1,0:T(8,128)(2,1)S(1)}, u32[]{:S(2)}, u32[]{:S(2)}) collective-permute-start(bf16[256,512]{1,0:T(8,128)(2,1)S(1)} %reduce-precision_convert_fusion.4), channel_id=1, source_target_pairs={{8,16},{16,8},{0,0},{24,24},{9,17},{17,9},{1,1},{25,25},{10,18},{1... | collective-permute-start | bytes 786440 | tf_op jit(solution)/shard_map/ppermute | solution.py:39
  92.1 22.6 %collective-permute-start.35 = (bf16[256,512]{1,0:T(8,128)(2,1)S(1)}, bf16[256,512]{1,0:T(8,128)(2,1)S(1)}, u32[]{:S(2)}, u32[]{:S(2)}) collective-permute-start(bf16[256,512]{1,0:T(8,128)(2,1)S(1)} %reduce-precision_convert_fusion.3), channel_id=1, source_target_pairs={{0,8},{8,0},{16,24},{24,16},{1,9},{9,1},{17,25},{25,17},{2,10},{10... | collective-permute-start | bytes 786440 | tf_op jit(solution)/shard_map/ppermute | solution.py:35
  95.2 12.9 %collective-permute-start.32 = (bf16[128,256]{1,0:T(8,128)(2,1)S(1)}, bf16[128,256]{1,0:T(8,128)(2,1)S(1)}, u32[]{:S(2)}, u32[]{:S(2)}) collective-permute-start(bf16[128,256]{1,0:T(8,128)(2,1)S(1)} %get-tuple-element.321), channel_id=1, source_target_pairs={{0,4},{4,0},{1,5},{5,1},{2,6},{6,2},{3,7},{7,3},{8,12},{12,8},{9,1... | collective-permute-start | bytes 196616 | tf_op jit(solution)/shard_map/ppermute | solution.py:16
  106.0 10.9 %collective-permute-start.34 = (bf16[256,512]{1,0:T(8,128)(2,1)S(1)}, bf16[256,512]{1,0:T(8,128)(2,1)S(1)}, u32[]{:S(2)}, u32[]{:S(2)}) collective-permute-start(bf16[256,512]{1,0:T(8,128)(2,1)S(1)} %reduce-precision_convert_fusion.1), channel_id=1, source_target_pairs={{0,8},{8,0},{16,24},{24,16},{1,9},{9,1},{17,25},{25,17},{2,10},{10... | collective-permute-start | bytes 786440 | tf_op jit(solution)/shard_map/ppermute | solution.py:35
  111.1 12.6 %collective-permute-start.39 = (bf16[256,512]{1,0:T(8,128)(2,1)S(1)}, bf16[256,512]{1,0:T(8,128)(2,1)S(1)}, u32[]{:S(2)}, u32[]{:S(2)}) collective-permute-start(bf16[256,512]{1,0:T(8,128)(2,1)S(1)} %reduce-precision_convert_fusion), channel_id=1, source_target_pairs={{0,8},{8,0},{16,24},{24,16},{1,9},{9,1},{17,25},{25,17},{2,10},{10... | collective-permute-start | bytes 786440 | tf_op jit(solution)/shard_map/ppermute | solution.py:35
  (22 other events, 144.9 us)

commit v9 on v7

--- a/solution.py
+++ b/solution.py
@@ -10,6 +10,7 @@
 EPSILON = 1e-06
 CHUNK_ROWS = 256
 LAG = 3
+KN = {"groups": (lambda c: [[0], [1, 2], [3, 4], [5], [6], [7]] if c == 8 else [[k] for k in range(c)]), "due": len, "xser": 0, "t1": 0, "t2": 0, "t3": 1, "tA": 0, "tail": 1, "keys": 3, "rpay": (None, 0, 1, 1), "rrecv": (0, 0, 0, 1), "ypay": 0, "yrecv": 0, "ptie": 1}
 
 
 def swap(value, axis, bit):
@@ -39,14 +40,15 @@
     return lax.ppermute(value, "section", [(1, 2), (2, 1), (0, 0), (3, 3)])
 
 
-def summed(parts, arriving, sums, share, emit, side):
-    count = len(parts)
-    groups = [[0]] + [list(range(k, min(k + 2, count))) for k in range(1, count - 1, 2)]
-    groups += [[count - 1]] if count > 1 and groups[-1][-1] != count - 1 else []
+def summed(part, count, sums, share, emit, side):
+    groups = KN["groups"](count)
     pending = ()
     if lax.axis_size("section") != 4:
         for group in groups:
-            found = [to_bfloat16(lax.psum(parts[k].astype(jnp.float32), "section")) for k in group]
+            found = []
+            for k in group:
+                value, _ = part(k, None)
+                found.append(to_bfloat16(lax.psum(value.astype(jnp.float32), "section")))
             emit(group, share(found))
         while pending is not None:
             pending = side(pending)
@@ -54,21 +56,31 @@
     index = lax.axis_index("section")
     inner = (index == 1) | (index == 2)
 
-    halves, others, totals, results = {}, {}, {}, {}
-    shares, recent = [], ()
+    parts, arriving, halves, others, totals, results = {}, {}, {}, {}, {}, {}
+    for k in range(min(LAG, count)):
+        last = parts.get(k - 1)
+        parts[k], last = part(k, last)
+        if k and KN["ptie"] and last is not None:
+            parts[k - 1] = last
+        arriving[k] = end_swap(parts[k])
+    shares = []
     for k in range(count + LAG):
-        tied = ({i: totals[i] for i in (k - 2,) if i in totals}, {i: sums[i] for i in recent})
+        tied = {i: totals[i] for i in (k - 2,) if i in totals and KN["t1"]}
         got, tied = lax.optimization_barrier((arriving[k], tied))
-        totals.update(tied[0])
-        sums.update(tied[1])
+        totals.update(tied)
         if k < count:
             halves[k] = add(parts[k], got)
             others[k] = middle_swap(halves[k])
-        if k >= LAG:
-            results[k - LAG] = jnp.where(inner, totals[k - LAG], got)
+        if LAG + k < count:
+            parts[LAG + k], value = part(LAG + k, halves[k])
+            if value is not None:
+                halves[k] = value
         if k - 1 in others:
-            tied = {i: halves[i] for i in (k - 1, k) if i in halves}
-            other, tied = lax.optimization_barrier((others[k - 1], tied))
+            tied = {i: halves[i] for i in (k - 1, k) if i in halves and (i < k or KN["t2"])}
+            if KN["tail"] and k >= count:
+                other, tied, got = lax.optimization_barrier((others[k - 1], tied, got))
+            else:
+                other, tied = lax.optimization_barrier((others[k - 1], tied))
             halves.update(tied)
             totals[k - 1] = add(halves[k - 1], other)
         following = k - 1 + LAG
@@ -77,35 +89,40 @@
             if following < count:
                 value = jnp.where(inner, value, parts[following])
             arriving[following] = end_swap(value)
-        for group in groups:
-            if group[-1] == k - LAG:
-                tied = {i: totals[i] for i in (k - 1,) if i in totals}
-                ready, tied = lax.optimization_barrier(([results[i] for i in group], tied))
-                totals.update(tied)
-                shares.append((k + len(group), group, share(ready)))
-        now = [entry for entry in shares if entry[0] <= k]
-        shares = [entry for entry in shares if entry[0] > k]
-        tied = {i: totals[i] for i in (k - 1,) if i in totals}
-        waited, pending, tied = lax.optimization_barrier(
-            ([entry[2] for entry in now], pending, tied)
-        )
-        totals.update(tied)
-        recent = ()
-        for (_, group, _), values in zip(now, waited):
-            recent += tuple(group)
-            emit(group, values)
-        if k >= LAG and pending is not None:
-            pending = side(pending)
-    for _, group, values in shares:
-        values, tied = lax.optimization_barrier((values, {i: sums[i] for i in recent}))
-        sums.update(tied)
-        recent = tuple(group)
-        emit(group, values)
+        if k >= LAG:
+            results[k - LAG] = jnp.where(inner, totals[k - LAG], got)
+            for group in groups:
+                if group[-1] == k - LAG:
+                    found = [results[i] for i in group]
+                    if KN["tA"] and k - 1 in totals:
+                        found, totals[k - 1] = lax.optimization_barrier((found, totals[k - 1]))
+                    back = KN["xser"]
+                    if back and len(shares) >= back and shares[-back] is not None:
+                        due, last, values = shares[-back]
+                        found, values = lax.optimization_barrier((found, values))
+                        shares[-back] = (due, last, values)
+                    shares.append((k + KN["due"](group), group, share(found)))
+        now = [i for i, entry in enumerate(shares) if entry is not None and entry[0] <= k]
+        tied = {i: totals[i] for i in (k - 1,) if i in totals and KN["t3"]}
+        if now or (pending is not None and k >= KN["keys"]):
+            waited, held, tied = lax.optimization_barrier(
+                ([shares[i][2] for i in now], pending if k >= KN["keys"] else (), tied)
+            )
+            totals.update(tied)
+            for i, values in zip(now, waited):
+                emit(shares[i][1], values)
+                shares[i] = None
+            if k >= KN["keys"] and pending is not None:
+                pending = side(held)
+    for entry in shares:
+        if entry is not None:
+            emit(entry[1], entry[2])
     while pending is not None:
         pending = side(pending)
 
 
-def square(block_len, rows, squares):
+def square(block_len, rows, squares, held):
+    held[...] = rows[...]
     lane = lax.broadcasted_iota(jnp.int32, (block_len, block_len), 1)
     diagonal = lane == lax.broadcasted_iota(jnp.int32, (block_len, block_len), 0)
     for b in range(squares.shape[0]):
@@ -133,7 +150,7 @@
         )
 
 
-def scale(n_dp, n_mp, width, order, rest, rows, *refs):
+def scale(n_dp, n_mp, width, rest, rows, *refs):
     squares, inverse, pieces = refs[:n_mp], refs[n_mp], refs[n_mp + 1 :]
     block_count, block_len = inverse.shape
     dp = lax.axis_index("dp")
@@ -146,11 +163,12 @@
     factors = inverse[...] * rest[:block_count, :]
     lane = lax.broadcasted_iota(jnp.int32, (block_len, block_len), 1)
     diagonal = lane == lax.broadcasted_iota(jnp.int32, (block_len, block_len), 0)
+    order = [jnp.max(rest[block_count + b : block_count + b + 1, :]) for b in range(block_count)]
     sources = []
     for slot in range(block_count):
         source, factor = 0, factors[0:1]
         for b in range(1, block_count):
-            here = order[0, b] == slot
+            here = order[b] == slot
             source = jnp.where(here, b, source)
             factor = jnp.where(here, factors[b : b + 1], factor)
         factor = jnp.sum(jnp.where(diagonal, factor, 0.0), axis=1, keepdims=True)
@@ -172,7 +190,7 @@
 def store(n_dp, g, first, offset, shards, *refs):
     values, gain, weight = refs[0], refs[1], refs[2]
     out, sums, results, semaphores = refs[-4:]
-    (_, chunk, width) = results.shape
+    _, chunk, width = results.shape
     far = lax.axis_index("mp") >> 1
     own_width = weight.shape[0] // n_dp
     column = pl.multiple_of((far ^ g) * width, 128)
@@ -229,19 +247,22 @@
     def in_order(values):
         return [pick(values, dp ^ e) for e in range(n_dp)]
 
-    cotangents = [key_cotangent] + [swap(key_cotangent, "dp", j) for j in range(1, n_dp)]
-
     vmem, smem = pl.BlockSpec(memory_space=pltpu.VMEM), pl.BlockSpec(memory_space=pltpu.SMEM)
     hbm = pl.BlockSpec(memory_space=pltpu.MemorySpace.HBM)
-    squares = pl.pallas_call(
+    squares, held = pl.pallas_call(
         functools.partial(square, block_len),
-        out_shape=jax.ShapeDtypeStruct((block_count, block_len), jnp.float32),
+        out_shape=[
+            jax.ShapeDtypeStruct((block_count, block_len), jnp.float32),
+            jax.ShapeDtypeStruct(policy_input.shape, policy_input.dtype),
+        ],
         in_specs=[vmem],
-        out_specs=vmem,
+        out_specs=[vmem] * 2,
         compiler_params=pltpu.CompilerParams(vmem_limit_bytes=32 * 2**20),
         name="square",
     )(policy_input)
     squares = [squares] + [swap(squares, "mp", j) for j in range(1, n_mp)]
+    cotangents, squares[0] = lax.optimization_barrier((key_cotangent, squares[0]))
+    cotangents = [cotangents] + [swap(cotangents, "dp", j) for j in range(1, n_dp)]
     rest = pl.pallas_call(
         score,
         out_shape=jax.ShapeDtypeStruct((2 * block_count, block_len), jnp.float32),
@@ -253,56 +274,63 @@
         functools.partial(scale, n_dp, n_mp, chunk),
         out_shape=[jax.ShapeDtypeStruct((block_count, block_len), jnp.float32)]
         + [jax.ShapeDtypeStruct((tokens, chunk), jnp.bfloat16)] * (n_dp * feature_blocks),
-        in_specs=[smem] + [vmem] * (2 + n_mp),
+        in_specs=[vmem] * (2 + n_mp),
         out_specs=[vmem] * (1 + n_dp * feature_blocks),
         compiler_params=pltpu.CompilerParams(vmem_limit_bytes=32 * 2**20),
         name="scale",
-    )(block_order, rest, policy_input, *squares)
+    )(rest, held, *squares)
 
     cotangents, inverse = lax.optimization_barrier((cotangents, inverse))
     cotangents = jnp.concatenate(in_order(cotangents), axis=0)
-    parts, arriving = [], {}
-
-    def rows(f):
-        got = [pieces[f]]
-        for j in range(1, n_dp):
-            piece = pieces[j * feature_blocks + f]
-            if f > 1:
-                piece, parts[1] = lax.optimization_barrier((piece, parts[1]))
-            piece = swap(piece, "dp", j)
-            if f:
-                piece, parts[f - 1] = lax.optimization_barrier((piece, parts[f - 1]))
-            got.append(piece)
-        return jnp.concatenate(in_order(got), axis=0)
-
-    gathered = []
-
     def both_cores(near):
         other = swap(near, "mp", 1)
         cotangent = jnp.concatenate([pick([near, other], core), pick([other, near], core)], axis=1)
         cotangent = cotangent.reshape(n_dp, n_dp, tokens // n_dp, 2 * columns)
         return cotangent.transpose(1, 0, 2, 3).reshape(n_dp * tokens, 2 * columns)
 
-    for g in range(n_far):
+    ready, moved, first = {}, {}, {}
+
+    def send(f):
+        got = [pieces[f]]
+        for j in range(1, n_dp):
+            piece = pieces[j * feature_blocks + f]
+            tie = KN["rpay"][f] if n_dp == 2 else None
+            if tie is not None:
+                piece, first[tie] = lax.optimization_barrier((piece, first[tie]))
+            got.append(swap(piece, "dp", j))
+        return got
+
+    def columns_of(g, value):
         near = cotangents
         if g:
-            tied = min(1, len(parts) - 1)
-            near, parts[tied] = lax.optimization_barrier((near, parts[tied]))
+            if KN["ypay"] is not None:
+                near, first[KN["ypay"]] = lax.optimization_barrier((near, first[KN["ypay"]]))
             near = swap(near, "mp", 2 * g)
-        cotangent = both_cores(near)
-        for f in range(feature_blocks):
-            if not g:
-                gathered.append(rows(f))
-            part = lax.dot_general(
-                gathered[f],
-                cotangent,
-                (((0,), (0,)), ((), ())),
-                preferred_element_type=jnp.float32,
+            if KN["yrecv"] and value is not None:
+                near, value = lax.optimization_barrier((near, value))
+        return both_cores(near), value
+
+    def part(k, value):
+        g, f = divmod(k, feature_blocks)
+        if g not in ready:
+            ready[g], value = columns_of(g, value)
+        if f not in moved:
+            got = send(f)
+            if not f:
+                got, ready[0] = lax.optimization_barrier((got, ready[0]))
+            elif KN["rrecv"][f] and value is not None:
+                got, value = lax.optimization_barrier((got, value))
+            moved[f] = jnp.concatenate(in_order(got), axis=0)
+        found = to_bfloat16(
+            lax.dot_general(
+                moved[f], ready[g], (((0,), (0,)), ((), ())), preferred_element_type=jnp.float32
             )
-            parts.append(to_bfloat16(part))
-            if len(parts) <= LAG and n_section == 4:
-                arriving[len(parts) - 1] = end_swap(parts[-1])
-    late_gain, parts[1] = lax.optimization_barrier((norm_gain, parts[1]))
+        )
+        if k < 2:
+            first[k] = found
+        return found, value
+
+    late_gain = norm_gain
     gain = late_gain.astype(jnp.float32)[None, :]
     shards = n_section * n_dp
     out = []
@@ -344,10 +372,9 @@
     def key_steps():
         yield (inverse,)
         (late_inverse,) = side_values[0]
-        normed = policy_input.astype(jnp.float32) * late_inverse.reshape(-1, 1) * gain
+        normed = held.astype(jnp.float32) * late_inverse.reshape(-1, 1) * gain
         normed = lax.optimization_barrier(normed.astype(jnp.bfloat16))
         partial = jnp.dot(normed, key_weight, preferred_element_type=jnp.float32)
-        cut = [partial[:, i * columns : (i + 1) * columns] for i in range(n_mp)]
         yield (partial,)
         (partial,) = side_values[0]
         cut = [partial[:, i * columns : (i + 1) * columns] for i in range(n_mp)]
@@ -378,7 +405,7 @@
         side_values[0] = waited
         return next(steps, None)
 
-    summed(parts, arriving, sums, share, emit, side)
+    summed(part, n_far * feature_blocks, sums, share, emit, side)
     grad_gain = [
         sum(sums[g * feature_blocks + f] for g in range(n_far)) for f in range(feature_blocks)
     ]

time: 129 us -> 114 us (0.88)
  waiting for transfers between devices: 45.1 us -> 27.7 us
  starting transfers between devices: 55.6 us -> 59.4 us
  local copies, waits for them, and re-layouts: 4.59 us -> 2.58 us
    ppermute x20 -> x21, waiting for transfers between devices: 28.6 us -> 14.4 us  [swap(): lax.ppermute(value, axis, [(i, i ^ bit) for i in range(lax.axis_size(axis...]
    ppermute x11, waiting for transfers between devices: 16.5 us -> 13.3 us  [end_swap(): return lax.ppermute(value, 'section', [(0, 1), (1, 0), (2, 3), (3, 2)])]
    ppermute x20 -> x21, starting transfers between devices: 17.8 us -> 19.8 us  [swap(): lax.ppermute(value, axis, [(i, i ^ bit) for i in range(lax.axis_size(axis...]
    unnamed x18 -> x7, local copies, waits for them, and re-layouts: 4.46 us -> 2.51 us
    ppermute x11, starting transfers between devices: 32.2 us -> 33.8 us  [end_swap(): return lax.ppermute(value, 'section', [(0, 1), (1, 0), (2, 3), (3, 2)])]
  transfers between devices with their start and end apart: 39 -> 40, of which waited for: 15 -> 17; matrix products, arithmetic and copies ran while one was open for 7% -> 8% of each run, Pallas kernels for 9% -> 9%
where the time goes in v9:
time: 114 us; the launch traced here: 113 us
  starting transfers between devices  59.4 us (52%)
  waiting for transfers between devices  27.7 us (24%)
  Pallas kernels  11.8 us (10%)
  other arithmetic  6.24 us (5%)
  matrix products  3.82 us (3%)
  local copies, waits for them, and re-layouts  2.58 us (2%)
  between operations  1.34 us (1%)
    ppermute x11, starting transfers between devices, end_swap(): return lax.ppermute(value, 'section', [(0, 1), (1, 0), (2, 3), (3, 2)])  33.8 us
    ppermute x21, starting transfers between devices, swap(): lax.ppermute(value, axis, [(i, i ^ bit) for i in range(lax.axis_size(axis...  19.8 us
    ppermute x21, waiting for transfers between devices, swap(): lax.ppermute(value, axis, [(i, i ^ bit) for i in range(lax.axis_size(axis...  14.4 us
    ppermute x11, waiting for transfers between devices, end_swap(): return lax.ppermute(value, 'section', [(0, 1), (1, 0), (2, 3), (3, 2)])  13.3 us
    pallas_call x8, Pallas kernels, emit(): pl.pallas_call(functools.partial(store, n_dp, g, f * chunk, i * chunk, sh...  9.57 us
    ppermute x8, starting transfers between devices, middle_swap(): return lax.ppermute(value, 'section', [(1, 2), (2, 1), (0, 0), (3, 3)])  5.73 us
    dot_general x8, matrix products, part(): lax.dot_general(moved[f], ready[g], (((0,), (0,)), ((), ())), preferred_e...  2.56 us
    unnamed x7, local copies, waits for them, and re-layouts  2.51 us
  transfers between devices with their start and end apart: 40, of which 17 were waited for; matrix products, arithmetic and copies ran while one was open for 8% of the time, Pallas kernels for 9%

profile of v9, /device:TPU:0, one launch (start us, length us, event | category | flops | bytes accessed | tf_op | source)
XLA Modules:
  0.0 112.8 jit_solution(943774248463905449)
XLA Ops:
  2.1 3.0 %collective-permute-start.4 = (bf16[256,256]{1,0:T(8,128)(2,1)}, bf16[256,256]{1,0:T(8,128)(2,1)S(1)}, u32[]{:S(2)}, u32[]{:S(2)}) collective-permute-start(bf16[256,256]{1,0:T(8,128)(2,1)} %param.17), channel_id=1, source_target_pairs={{0,4},{4,0},{1,5},{5,1},{2,6},{6,2},{3,7},{7,3},{8,12},{12,8},{9,1... | collective-permute-start | bytes 393224 | tf_op jit(solution)/shard_map/ppermute | solution.py:17
  5.2 1.5 %collective-permute-start.1 = (f32[2,128]{1,0:T(2,128)S(1)}, f32[2,128]{1,0:T(2,128)S(1)}, u32[]{:S(2)}, u32[]{:S(2)}) collective-permute-start(f32[2,128]{1,0:T(2,128)S(1)} %get-tuple-element.84.refs_0_), channel_id=1, source_target_pairs={{0,2},{1,3},{2,0},{3,1},{4,6},{5,7},{6,4},{7,5},{8,10},{9,11},{10,... | collective-permute-start | bytes 3080 | tf_op jit(solution)/shard_map/ppermute | solution.py:17
  7.0 1.5 %score.1.rest = f32[4,128]{1,0:T(4,128)} custom-call(s32[2]{0:T(128)} %lengths.1, s32[1,2]{1,0:T(1,128)} %order.1, bf16[2,3584]{1,0:T(2,128)(2,1)} %hidden.1, bf16[3584]{0:T(1024)(128)(2,1)} %gain.1, bf16[3584]{0:T(1024)(128)(2,1)} %head.1), custom_call_target="tpu_custom_call" | custom-call | tf_op jit(solution)/shard_map/score/pallas_call | solution.py:266
  14.1 4.3 %collective-permute-done.3 = bf16[256,256]{1,0:T(8,128)(2,1)S(1)} collective-permute-done((bf16[256,256]{1,0:T(8,128)(2,1)S(1)}, bf16[256,256]{1,0:T(8,128)(2,1)S(1)}, u32[]{:S(2)}, u32[]{:S(2)}) %collective-permute-start.3) | collective-permute-done | bytes 131104 | tf_op jit(solution)/shard_map/ppermute | solution.py:17
  21.5 1.6 %collective-permute-start.17 = (bf16[256,512]{1,0:T(8,128)(2,1)S(1)}, bf16[256,512]{1,0:T(8,128)(2,1)S(1)}, u32[]{:S(2)}, u32[]{:S(2)}) collective-permute-start(bf16[256,512]{1,0:T(8,128)(2,1)S(1)} %fusion), channel_id=1, source_target_pairs={{0,8},{8,0},{16,24},{24,16},{1,9},{9,1},{17,25},{25,17},{2,10},{10... | collective-permute-start | bytes 786440 | tf_op jit(solution)/shard_map/ppermute | solution.py:36
  23.1 2.0 %collective-permute-done.6 = bf16[256,256]{1,0:T(8,128)(2,1)S(1)} collective-permute-done((bf16[256,256]{1,0:T(8,128)(2,1)S(1)}, bf16[256,256]{1,0:T(8,128)(2,1)S(1)}, u32[]{:S(2)}, u32[]{:S(2)}) %collective-permute-start.6) | collective-permute-done | bytes 131104 | tf_op jit(solution)/shard_map/ppermute | solution.py:17
  25.4 1.6 %collective-permute-start.7 = (bf16[256,512]{1,0:T(8,128)(2,1)S(1)}, bf16[256,512]{1,0:T(8,128)(2,1)S(1)}, u32[]{:S(2)}, u32[]{:S(2)}) collective-permute-start(bf16[256,512]{1,0:T(8,128)(2,1)S(1)} %fusion.1), channel_id=1, source_target_pairs={{0,8},{8,0},{16,24},{24,16},{1,9},{9,1},{17,25},{25,17},{2,10},{10... | collective-permute-start | bytes 786440 | tf_op jit(solution)/shard_map/ppermute | solution.py:36
  27.5 3.1 %collective-permute-done.17 = bf16[256,512]{1,0:T(8,128)(2,1)S(1)} collective-permute-done((bf16[256,512]{1,0:T(8,128)(2,1)S(1)}, bf16[256,512]{1,0:T(8,128)(2,1)S(1)}, u32[]{:S(2)}, u32[]{:S(2)}) %collective-permute-start.17) | collective-permute-done | bytes 262176 | tf_op jit(solution)/shard_map/ppermute | solution.py:36
  33.1 3.9 %collective-permute-start.13 = (bf16[256,512]{1,0:T(8,128)(2,1)S(1)}, bf16[256,512]{1,0:T(8,128)(2,1)S(1)}, u32[]{:S(2)}, u32[]{:S(2)}) collective-permute-start(bf16[256,512]{1,0:T(8,128)(2,1)S(1)} %fusion.3), channel_id=1, source_target_pairs={{0,8},{8,0},{16,24},{24,16},{1,9},{9,1},{17,25},{25,17},{2,10},{10... | collective-permute-start | bytes 786440 | tf_op jit(solution)/shard_map/ppermute | solution.py:36
  38.4 5.0 %collective-permute-start.20 = (bf16[256,512]{1,0:T(8,128)(2,1)S(1)}, bf16[256,512]{1,0:T(8,128)(2,1)S(1)}, u32[]{:S(2)}, u32[]{:S(2)}) collective-permute-start(bf16[256,512]{1,0:T(8,128)(2,1)S(1)} %get-tuple-element.203), channel_id=1, source_target_pairs={{0,8},{8,0},{16,24},{24,16},{1,9},{9,1},{17,25},{25,17},{2,10},{10... | collective-permute-start | bytes 786440 | tf_op jit(solution)/shard_map/ppermute | solution.py:36
  45.2 3.8 %collective-permute-start.11 = (bf16[256,512]{1,0:T(8,128)(2,1)S(1)}, bf16[256,512]{1,0:T(8,128)(2,1)S(1)}, u32[]{:S(2)}, u32[]{:S(2)}) collective-permute-start(bf16[256,512]{1,0:T(8,128)(2,1)S(1)} %get-tuple-element.201), channel_id=1, source_target_pairs={{0,8},{8,0},{16,24},{24,16},{1,9},{9,1},{17,25},{25,17},{2,10},{10... | collective-permute-start | bytes 786440 | tf_op jit(solution)/shard_map/ppermute | solution.py:36
  52.0 4.2 %collective-permute-start.15 = (bf16[256,512]{1,0:T(8,128)(2,1)S(1)}, bf16[256,512]{1,0:T(8,128)(2,1)S(1)}, u32[]{:S(2)}, u32[]{:S(2)}) collective-permute-start(bf16[256,512]{1,0:T(8,128)(2,1)S(1)} %get-tuple-element.165), channel_id=1, source_target_pairs={{0,8},{8,0},{16,24},{24,16},{1,9},{9,1},{17,25},{25,17},{2,10},{10... | collective-permute-start | bytes 786440 | tf_op jit(solution)/shard_map/ppermute | solution.py:36
  57.6 6.3 %collective-permute-start.29 = (bf16[256,512]{1,0:T(8,128)(2,1)S(1)}, bf16[256,512]{1,0:T(8,128)(2,1)S(1)}, u32[]{:S(2)}, u32[]{:S(2)}) collective-permute-start(bf16[256,512]{1,0:T(8,128)(2,1)S(1)} %get-tuple-element.163), channel_id=1, source_target_pairs={{0,8},{8,0},{16,24},{24,16},{1,9},{9,1},{17,25},{25,17},{2,10},{10... | collective-permute-start | bytes 786440 | tf_op jit(solution)/shard_map/ppermute | solution.py:36
  71.0 2.6 %collective-permute-start.31 = (bf16[256,512]{1,0:T(8,128)(2,1)S(1)}, bf16[256,512]{1,0:T(8,128)(2,1)S(1)}, u32[]{:S(2)}, u32[]{:S(2)}) collective-permute-start(bf16[256,512]{1,0:T(8,128)(2,1)S(1)} %get-tuple-element.161), channel_id=1, source_target_pairs={{0,8},{8,0},{16,24},{24,16},{1,9},{9,1},{17,25},{25,17},{2,10},{10... | collective-permute-start | bytes 786440 | tf_op jit(solution)/shard_map/ppermute | solution.py:36
  74.4 2.2 %collective-permute-start.33 = (bf16[256,512]{1,0:T(8,128)(2,1)S(1)}, bf16[256,512]{1,0:T(8,128)(2,1)S(1)}, u32[]{:S(2)}, u32[]{:S(2)}) collective-permute-start(bf16[256,512]{1,0:T(8,128)(2,1)S(1)} %reduce-precision_convert_fusion.4), channel_id=1, source_target_pairs={{0,8},{8,0},{16,24},{24,16},{1,9},{9,1},{17,25},{25,17},{2,10},{10... | collective-permute-start | bytes 786440 | tf_op jit(solution)/shard_map/ppermute | solution.py:36
  77.4 1.5 %collective-permute-start.28 = (bf16[128,256]{1,0:T(8,128)(2,1)S(1)}, bf16[128,256]{1,0:T(8,128)(2,1)S(1)}, u32[]{:S(2)}, u32[]{:S(2)}) collective-permute-start(bf16[128,256]{1,0:T(8,128)(2,1)S(1)} %get-tuple-element.195), channel_id=1, source_target_pairs={{0,4},{4,0},{1,5},{5,1},{2,6},{6,2},{3,7},{7,3},{8,12},{12,8},{9,1... | collective-permute-start | bytes 196616 | tf_op jit(solution)/shard_map/ppermute | solution.py:17
  78.9 1.9 %collective-permute-done.31 = bf16[256,512]{1,0:T(8,128)(2,1)S(1)} collective-permute-done((bf16[256,512]{1,0:T(8,128)(2,1)S(1)}, bf16[256,512]{1,0:T(8,128)(2,1)S(1)}, u32[]{:S(2)}, u32[]{:S(2)}) %collective-permute-start.31) | collective-permute-done | bytes 262176 | tf_op jit(solution)/shard_map/ppermute | solution.py:36
  83.4 2.2 %collective-permute-done.33 = bf16[256,512]{1,0:T(8,128)(2,1)S(1)} collective-permute-done((bf16[256,512]{1,0:T(8,128)(2,1)S(1)}, bf16[256,512]{1,0:T(8,128)(2,1)S(1)}, u32[]{:S(2)}, u32[]{:S(2)}) %collective-permute-start.33) | collective-permute-done | bytes 262176 | tf_op jit(solution)/shard_map/ppermute | solution.py:36
  85.5 2.2 %collective-permute-start.36 = (bf16[256,512]{1,0:T(8,128)(2,1)S(1)}, bf16[256,512]{1,0:T(8,128)(2,1)S(1)}, u32[]{:S(2)}, u32[]{:S(2)}) collective-permute-start(bf16[256,512]{1,0:T(8,128)(2,1)S(1)} %reduce-precision_convert_fusion.2), channel_id=1, source_target_pairs={{0,8},{8,0},{16,24},{24,16},{1,9},{9,1},{17,25},{25,17},{2,10},{10... | collective-permute-start | bytes 786440 | tf_op jit(solution)/shard_map/ppermute | solution.py:36
  91.4 1.5 %collective-permute-start.39 = (bf16[256,512]{1,0:T(8,128)(2,1)S(1)}, bf16[256,512]{1,0:T(8,128)(2,1)S(1)}, u32[]{:S(2)}, u32[]{:S(2)}) collective-permute-start(bf16[256,512]{1,0:T(8,128)(2,1)S(1)} %broadcast_select_fusion.4), channel_id=1, source_target_pairs={{0,4},{4,0},{1,5},{5,1},{2,6},{6,2},{3,7},{7,3},{8,12},{12,8},{9,1... | collective-permute-start | bytes 786440 | tf_op jit(solution)/shard_map/ppermute | solution.py:17
  94.0 1.5 %collective-permute-start.37 = (bf16[256,512]{1,0:T(8,128)(2,1)S(1)}, bf16[256,512]{1,0:T(8,128)(2,1)S(1)}, u32[]{:S(2)}, u32[]{:S(2)}) collective-permute-start(bf16[256,512]{1,0:T(8,128)(2,1)S(1)} %broadcast_select_fusion.7), channel_id=1, source_target_pairs={{0,4},{4,0},{1,5},{5,1},{2,6},{6,2},{3,7},{7,3},{8,12},{12,8},{9,1... | collective-permute-start | bytes 786440 | tf_op jit(solution)/shard_map/ppermute | solution.py:17
  95.4 3.1 %collective-permute-done.34 = bf16[256,512]{1,0:T(8,128)(2,1)S(1)} collective-permute-done((bf16[256,512]{1,0:T(8,128)(2,1)S(1)}, bf16[256,512]{1,0:T(8,128)(2,1)S(1)}, u32[]{:S(2)}, u32[]{:S(2)}) %collective-permute-start.34) | collective-permute-done | bytes 262176 | tf_op jit(solution)/shard_map/ppermute | solution.py:36
  105.3 1.7 %collective-permute-done.37 = bf16[256,512]{1,0:T(8,128)(2,1)S(1)} collective-permute-done((bf16[256,512]{1,0:T(8,128)(2,1)S(1)}, bf16[256,512]{1,0:T(8,128)(2,1)S(1)}, u32[]{:S(2)}, u32[]{:S(2)}) %collective-permute-start.37) | collective-permute-done | bytes 262176 | tf_op jit(solution)/shard_map/ppermute | solution.py:17
  108.3 2.7 %collective-permute-done.35 = bf16[256,512]{1,0:T(8,128)(2,1)S(1)} collective-permute-done((bf16[256,512]{1,0:T(8,128)(2,1)S(1)}, bf16[256,512]{1,0:T(8,128)(2,1)S(1)}, u32[]{:S(2)}, u32[]{:S(2)}) %collective-permute-start.35) | collective-permute-done | bytes 262176 | tf_op jit(solution)/shard_map/ppermute | solution.py:17
  (146 shorter events, 46.5 us)
Async XLA Ops:
  2.1 8.6 %collective-permute-start.4 = (bf16[256,256]{1,0:T(8,128)(2,1)}, bf16[256,256]{1,0:T(8,128)(2,1)S(1)}, u32[]{:S(2)}, u32[]{:S(2)}) collective-permute-start(bf16[256,256]{1,0:T(8,128)(2,1)} %param.17), channel_id=1, source_target_pairs={{0,4},{4,0},{1,5},{5,1},{2,6},{6,2},{3,7},{7,3},{8,12},{12,8},{9,1... | collective-permute-start | bytes 393224 | tf_op jit(solution)/shard_map/ppermute | solution.py:17
  13.5 9.6 %collective-permute-start.9 = (bf16[512,256]{1,0:T(8,128)(2,1)S(1)}, bf16[512,256]{1,0:T(8,128)(2,1)S(1)}, u32[]{:S(2)}, u32[]{:S(2)}) collective-permute-start(bf16[512,256]{1,0:T(8,128)(2,1)S(1)} %pad_maximum_fusion.10), channel_id=1, source_target_pairs={{0,2},{1,3},{2,0},{3,1},{4,6},{5,7},{6,4},{7,5},{8,10},{9,11},{10,... | collective-permute-start | bytes 786440 | tf_op jit(solution)/shard_map/ppermute | solution.py:17
  20.1 12.9 %collective-permute-start.19 = (bf16[256,256]{1,0:T(8,128)(2,1)S(1)}, bf16[256,256]{1,0:T(8,128)(2,1)S(1)}, u32[]{:S(2)}, u32[]{:S(2)}) collective-permute-start(bf16[256,256]{1,0:T(8,128)(2,1)S(1)} %get-tuple-element.105), channel_id=1, source_target_pairs={{0,4},{4,0},{1,5},{5,1},{2,6},{6,2},{3,7},{7,3},{8,12},{12,8},{9,1... | collective-permute-start | bytes 393224 | tf_op jit(solution)/shard_map/ppermute | solution.py:17
  21.5 9.1 %collective-permute-start.17 = (bf16[256,512]{1,0:T(8,128)(2,1)S(1)}, bf16[256,512]{1,0:T(8,128)(2,1)S(1)}, u32[]{:S(2)}, u32[]{:S(2)}) collective-permute-start(bf16[256,512]{1,0:T(8,128)(2,1)S(1)} %fusion), channel_id=1, source_target_pairs={{0,8},{8,0},{16,24},{24,16},{1,9},{9,1},{17,25},{25,17},{2,10},{10... | collective-permute-start | bytes 786440 | tf_op jit(solution)/shard_map/ppermute | solution.py:36
  23.1 8.2 %collective-permute-start.10 = (bf16[512,256]{1,0:T(8,128)(2,1)S(1)}, bf16[512,256]{1,0:T(8,128)(2,1)S(1)}, u32[]{:S(2)}, u32[]{:S(2)}) collective-permute-start(bf16[512,256]{1,0:T(8,128)(2,1)S(1)} %collective-permute-done.9), channel_id=1, source_target_pairs={{0,1},{1,0},{2,3},{3,2},{4,5},{5,4},{6,7},{7,6},{8,9},{9,8},{10,11... | collective-permute-start | bytes 786440 | tf_op jit(solution)/shard_map/ppermute | solution.py:17
  25.4 11.9 %collective-permute-start.7 = (bf16[256,512]{1,0:T(8,128)(2,1)S(1)}, bf16[256,512]{1,0:T(8,128)(2,1)S(1)}, u32[]{:S(2)}, u32[]{:S(2)}) collective-permute-start(bf16[256,512]{1,0:T(8,128)(2,1)S(1)} %fusion.1), channel_id=1, source_target_pairs={{0,8},{8,0},{16,24},{24,16},{1,9},{9,1},{17,25},{25,17},{2,10},{10... | collective-permute-start | bytes 786440 | tf_op jit(solution)/shard_map/ppermute | solution.py:36
  33.1 11.0 %collective-permute-start.13 = (bf16[256,512]{1,0:T(8,128)(2,1)S(1)}, bf16[256,512]{1,0:T(8,128)(2,1)S(1)}, u32[]{:S(2)}, u32[]{:S(2)}) collective-permute-start(bf16[256,512]{1,0:T(8,128)(2,1)S(1)} %fusion.3), channel_id=1, source_target_pairs={{0,8},{8,0},{16,24},{24,16},{1,9},{9,1},{17,25},{25,17},{2,10},{10... | collective-permute-start | bytes 786440 | tf_op jit(solution)/shard_map/ppermute | solution.py:36
  38.4 11.9 %collective-permute-start.20 = (bf16[256,512]{1,0:T(8,128)(2,1)S(1)}, bf16[256,512]{1,0:T(8,128)(2,1)S(1)}, u32[]{:S(2)}, u32[]{:S(2)}) collective-permute-start(bf16[256,512]{1,0:T(8,128)(2,1)S(1)} %get-tuple-element.203), channel_id=1, source_target_pairs={{0,8},{8,0},{16,24},{24,16},{1,9},{9,1},{17,25},{25,17},{2,10},{10... | collective-permute-start | bytes 786440 | tf_op jit(solution)/shard_map/ppermute | solution.py:36
  44.2 7.7 %collective-permute-start.14 = (bf16[256,512]{1,0:T(8,128)(2,1)S(1)}, bf16[256,512]{1,0:T(8,128)(2,1)S(1)}, u32[]{:S(2)}, u32[]{:S(2)}) collective-permute-start(bf16[256,512]{1,0:T(8,128)(2,1)S(1)} %reduce-precision_convert_fusion.13), channel_id=1, source_target_pairs={{8,16},{16,8},{0,0},{24,24},{9,17},{17,9},{1,1},{25,25},{10,18},{1... | collective-permute-start | bytes 786440 | tf_op jit(solution)/shard_map/ppermute | solution.py:40
  45.2 11.0 %collective-permute-start.11 = (bf16[256,512]{1,0:T(8,128)(2,1)S(1)}, bf16[256,512]{1,0:T(8,128)(2,1)S(1)}, u32[]{:S(2)}, u32[]{:S(2)}) collective-permute-start(bf16[256,512]{1,0:T(8,128)(2,1)S(1)} %get-tuple-element.201), channel_id=1, source_target_pairs={{0,8},{8,0},{16,24},{24,16},{1,9},{9,1},{17,25},{25,17},{2,10},{10... | collective-permute-start | bytes 786440 | tf_op jit(solution)/shard_map/ppermute | solution.py:36
  52.0 11.9 %collective-permute-start.15 = (bf16[256,512]{1,0:T(8,128)(2,1)S(1)}, bf16[256,512]{1,0:T(8,128)(2,1)S(1)}, u32[]{:S(2)}, u32[]{:S(2)}) collective-permute-start(bf16[256,512]{1,0:T(8,128)(2,1)S(1)} %get-tuple-element.165), channel_id=1, source_target_pairs={{0,8},{8,0},{16,24},{24,16},{1,9},{9,1},{17,25},{25,17},{2,10},{10... | collective-permute-start | bytes 786440 | tf_op jit(solution)/shard_map/ppermute | solution.py:36
  56.4 11.9 %collective-permute-start.23 = (bf16[256,512]{1,0:T(8,128)(2,1)S(1)}, bf16[256,512]{1,0:T(8,128)(2,1)S(1)}, u32[]{:S(2)}, u32[]{:S(2)}) collective-permute-start(bf16[256,512]{1,0:T(8,128)(2,1)S(1)} %reduce-precision_convert_fusion.7), channel_id=1, source_target_pairs={{8,16},{16,8},{0,0},{24,24},{9,17},{17,9},{1,1},{25,25},{10,18},{1... | collective-permute-start | bytes 786440 | tf_op jit(solution)/shard_map/ppermute | solution.py:40
  57.6 12.0 %collective-permute-start.29 = (bf16[256,512]{1,0:T(8,128)(2,1)S(1)}, bf16[256,512]{1,0:T(8,128)(2,1)S(1)}, u32[]{:S(2)}, u32[]{:S(2)}) collective-permute-start(bf16[256,512]{1,0:T(8,128)(2,1)S(1)} %get-tuple-element.163), channel_id=1, source_target_pairs={{0,8},{8,0},{16,24},{24,16},{1,9},{9,1},{17,25},{25,17},{2,10},{10... | collective-permute-start | bytes 786440 | tf_op jit(solution)/shard_map/ppermute | solution.py:36
  65.0 22.7 %collective-permute-start.16 = (bf16[512,512]{1,0:T(8,128)(2,1)S(1)}, bf16[512,512]{1,0:T(8,128)(2,1)S(1)}, u32[]{:S(2)}, u32[]{:S(2)}) collective-permute-start(bf16[512,512]{1,0:T(8,128)(2,1)S(1)} %pad_maximum_fusion.4), channel_id=1, source_target_pairs={{0,4},{4,0},{1,5},{5,1},{2,6},{6,2},{3,7},{7,3},{8,12},{12,8},{9,1... | collective-permute-start | bytes 1572872 | tf_op jit(solution)/shard_map/ppermute | solution.py:17
  71.0 9.8 %collective-permute-start.31 = (bf16[256,512]{1,0:T(8,128)(2,1)S(1)}, bf16[256,512]{1,0:T(8,128)(2,1)S(1)}, u32[]{:S(2)}, u32[]{:S(2)}) collective-permute-start(bf16[256,512]{1,0:T(8,128)(2,1)S(1)} %get-tuple-element.161), channel_id=1, source_target_pairs={{0,8},{8,0},{16,24},{24,16},{1,9},{9,1},{17,25},{25,17},{2,10},{10... | collective-permute-start | bytes 786440 | tf_op jit(solution)/shard_map/ppermute | solution.py:36
  73.7 8.1 %collective-permute-start.30 = (bf16[256,512]{1,0:T(8,128)(2,1)S(1)}, bf16[256,512]{1,0:T(8,128)(2,1)S(1)}, u32[]{:S(2)}, u32[]{:S(2)}) collective-permute-start(bf16[256,512]{1,0:T(8,128)(2,1)S(1)} %reduce-precision_convert_fusion.3), channel_id=1, source_target_pairs={{8,16},{16,8},{0,0},{24,24},{9,17},{17,9},{1,1},{25,25},{10,18},{1... | collective-permute-start | bytes 786440 | tf_op jit(solution)/shard_map/ppermute | solution.py:40
  74.4 11.1 %collective-permute-start.33 = (bf16[256,512]{1,0:T(8,128)(2,1)S(1)}, bf16[256,512]{1,0:T(8,128)(2,1)S(1)}, u32[]{:S(2)}, u32[]{:S(2)}) collective-permute-start(bf16[256,512]{1,0:T(8,128)(2,1)S(1)} %reduce-precision_convert_fusion.4), channel_id=1, source_target_pairs={{0,8},{8,0},{16,24},{24,16},{1,9},{9,1},{17,25},{25,17},{2,10},{10... | collective-permute-start | bytes 786440 | tf_op jit(solution)/shard_map/ppermute | solution.py:36
  77.4 10.3 %collective-permute-start.28 = (bf16[128,256]{1,0:T(8,128)(2,1)S(1)}, bf16[128,256]{1,0:T(8,128)(2,1)S(1)}, u32[]{:S(2)}, u32[]{:S(2)}) collective-permute-start(bf16[128,256]{1,0:T(8,128)(2,1)S(1)} %get-tuple-element.195), channel_id=1, source_target_pairs={{0,4},{4,0},{1,5},{5,1},{2,6},{6,2},{3,7},{7,3},{8,12},{12,8},{9,1... | collective-permute-start | bytes 196616 | tf_op jit(solution)/shard_map/ppermute | solution.py:17
  80.9 10.2 %collective-permute-start.32 = (bf16[256,512]{1,0:T(8,128)(2,1)S(1)}, bf16[256,512]{1,0:T(8,128)(2,1)S(1)}, u32[]{:S(2)}, u32[]{:S(2)}) collective-permute-start(bf16[256,512]{1,0:T(8,128)(2,1)S(1)} %reduce-precision_convert_fusion.1), channel_id=1, source_target_pairs={{8,16},{16,8},{0,0},{24,24},{9,17},{17,9},{1,1},{25,25},{10,18},{1... | collective-permute-start | bytes 786440 | tf_op jit(solution)/shard_map/ppermute | solution.py:40
  81.8 19.5 %collective-permute-start.38 = (bf16[512,512]{1,0:T(8,128)(2,1)S(1)}, bf16[512,512]{1,0:T(8,128)(2,1)S(1)}, u32[]{:S(2)}, u32[]{:S(2)}) collective-permute-start(bf16[512,512]{1,0:T(8,128)(2,1)S(1)} %pad_maximum_fusion.7), channel_id=1, source_target_pairs={{0,4},{4,0},{1,5},{5,1},{2,6},{6,2},{3,7},{7,3},{8,12},{12,8},{9,1... | collective-permute-start | bytes 1572872 | tf_op jit(solution)/shard_map/ppermute | solution.py:17
  85.5 8.4 %collective-permute-start.36 = (bf16[256,512]{1,0:T(8,128)(2,1)S(1)}, bf16[256,512]{1,0:T(8,128)(2,1)S(1)}, u32[]{:S(2)}, u32[]{:S(2)}) collective-permute-start(bf16[256,512]{1,0:T(8,128)(2,1)S(1)} %reduce-precision_convert_fusion.2), channel_id=1, source_target_pairs={{0,8},{8,0},{16,24},{24,16},{1,9},{9,1},{17,25},{25,17},{2,10},{10... | collective-permute-start | bytes 786440 | tf_op jit(solution)/shard_map/ppermute | solution.py:36
  91.4 10.0 %collective-permute-start.39 = (bf16[256,512]{1,0:T(8,128)(2,1)S(1)}, bf16[256,512]{1,0:T(8,128)(2,1)S(1)}, u32[]{:S(2)}, u32[]{:S(2)}) collective-permute-start(bf16[256,512]{1,0:T(8,128)(2,1)S(1)} %broadcast_select_fusion.4), channel_id=1, source_target_pairs={{0,4},{4,0},{1,5},{5,1},{2,6},{6,2},{3,7},{7,3},{8,12},{12,8},{9,1... | collective-permute-start | bytes 786440 | tf_op jit(solution)/shard_map/ppermute | solution.py:17
  94.0 13.0 %collective-permute-start.37 = (bf16[256,512]{1,0:T(8,128)(2,1)S(1)}, bf16[256,512]{1,0:T(8,128)(2,1)S(1)}, u32[]{:S(2)}, u32[]{:S(2)}) collective-permute-start(bf16[256,512]{1,0:T(8,128)(2,1)S(1)} %broadcast_select_fusion.7), channel_id=1, source_target_pairs={{0,4},{4,0},{1,5},{5,1},{2,6},{6,2},{3,7},{7,3},{8,12},{12,8},{9,1... | collective-permute-start | bytes 786440 | tf_op jit(solution)/shard_map/ppermute | solution.py:17
  98.6 12.3 %collective-permute-start.35 = (bf16[256,512]{1,0:T(8,128)(2,1)S(1)}, bf16[256,512]{1,0:T(8,128)(2,1)S(1)}, u32[]{:S(2)}, u32[]{:S(2)}) collective-permute-start(bf16[256,512]{1,0:T(8,128)(2,1)S(1)} %broadcast_select_fusion.8), channel_id=1, source_target_pairs={{0,4},{4,0},{1,5},{5,1},{2,6},{6,2},{3,7},{7,3},{8,12},{12,8},{9,1... | collective-permute-start | bytes 786440 | tf_op jit(solution)/shard_map/ppermute | solution.py:17
  (19 other events, 101.8 us)

commit v10 on v9

--- a/solution.py
+++ b/solution.py
@@ -10,7 +10,7 @@
 EPSILON = 1e-06
 CHUNK_ROWS = 256
 LAG = 3
-KN = {"groups": (lambda c: [[0], [1, 2], [3, 4], [5], [6], [7]] if c == 8 else [[k] for k in range(c)]), "due": len, "xser": 0, "t1": 0, "t2": 0, "t3": 1, "tA": 0, "tail": 1, "keys": 3, "rpay": (None, 0, 1, 1), "rrecv": (0, 0, 0, 1), "ypay": 0, "yrecv": 0, "ptie": 1}
+KN = {"groups": (lambda c: [[k] for k in range(c)]), "due": (lambda g: 1), "xser": 0, "t1": 0, "t2": 1, "t3": 1, "tA": 0, "tail": 1, "keys": 4, "rpay": (0, 1, 2, 2), "rrecv": (0, 0, 1, 1), "ypay": 1, "yrecv": 1, "ptie": 0, "lead": 2, "kpre": 0}
 
 
 def swap(value, axis, bit):
@@ -57,13 +57,19 @@
     inner = (index == 1) | (index == 2)
 
     parts, arriving, halves, others, totals, results = {}, {}, {}, {}, {}, {}
-    for k in range(min(LAG, count)):
+    for k in range(min(KN["lead"], count)):
         last = parts.get(k - 1)
         parts[k], last = part(k, last)
         if k and KN["ptie"] and last is not None:
             parts[k - 1] = last
         arriving[k] = end_swap(parts[k])
     shares = []
+    if KN["kpre"]:
+        pending, parts[1] = lax.optimization_barrier((side(()), parts[1]))
+        pending = side(pending)
+        if KN["kpre"] == 2:
+            pending, parts[1] = lax.optimization_barrier((pending, parts[1]))
+            pending = side(pending)
     for k in range(count + LAG):
         tied = {i: totals[i] for i in (k - 2,) if i in totals and KN["t1"]}
         got, tied = lax.optimization_barrier((arriving[k], tied))
@@ -71,10 +77,12 @@
         if k < count:
             halves[k] = add(parts[k], got)
             others[k] = middle_swap(halves[k])
-        if LAG + k < count:
-            parts[LAG + k], value = part(LAG + k, halves[k])
+        for i in range(LAG + k if k else KN["lead"], min(LAG + k + 1, count)):
+            parts[i], value = part(i, halves[k])
             if value is not None:
                 halves[k] = value
+            if i < LAG:
+                arriving[i] = end_swap(parts[i])
         if k - 1 in others:
             tied = {i: halves[i] for i in (k - 1, k) if i in halves and (i < k or KN["t2"])}
             if KN["tail"] and k >= count:
@@ -151,7 +159,7 @@
 
 
 def scale(n_dp, n_mp, width, rest, rows, *refs):
-    squares, inverse, pieces = refs[:n_mp], refs[n_mp], refs[n_mp + 1 :]
+    squares, (inverse, places), pieces = refs[:n_mp], refs[n_mp : n_mp + 2], refs[n_mp + 2 :]
     block_count, block_len = inverse.shape
     dp = lax.axis_index("dp")
     own_width = rows.shape[1] // n_dp
@@ -160,6 +168,7 @@
     for other in squares[1:]:
         total = total + other[...]
     inverse[...] = lax.rsqrt(total / (rows.shape[1] * n_mp) + EPSILON)
+    places[...] = rest[block_count:, :]
     factors = inverse[...] * rest[:block_count, :]
     lane = lax.broadcasted_iota(jnp.int32, (block_len, block_len), 1)
     diagonal = lane == lax.broadcasted_iota(jnp.int32, (block_len, block_len), 0)
@@ -270,12 +279,12 @@
         out_specs=vmem,
         name="score",
     )(lengths, block_order, final_hidden, score_gain, score_head)
-    inverse, *pieces = pl.pallas_call(
+    inverse, places, *pieces = pl.pallas_call(
         functools.partial(scale, n_dp, n_mp, chunk),
-        out_shape=[jax.ShapeDtypeStruct((block_count, block_len), jnp.float32)]
+        out_shape=[jax.ShapeDtypeStruct((block_count, block_len), jnp.float32)] * 2
         + [jax.ShapeDtypeStruct((tokens, chunk), jnp.bfloat16)] * (n_dp * feature_blocks),
         in_specs=[vmem] * (2 + n_mp),
-        out_specs=[vmem] * (1 + n_dp * feature_blocks),
+        out_specs=[vmem] * (2 + n_dp * feature_blocks),
         compiler_params=pltpu.CompilerParams(vmem_limit_bytes=32 * 2**20),
         name="scale",
     )(rest, held, *squares)
@@ -288,23 +297,26 @@
         cotangent = cotangent.reshape(n_dp, n_dp, tokens // n_dp, 2 * columns)
         return cotangent.transpose(1, 0, 2, 3).reshape(n_dp * tokens, 2 * columns)
 
-    ready, moved, first = {}, {}, {}
-
-    def send(f):
+    ready, moved = {}, {}
+
+    def send(f, value):
         got = [pieces[f]]
         for j in range(1, n_dp):
             piece = pieces[j * feature_blocks + f]
-            tie = KN["rpay"][f] if n_dp == 2 else None
-            if tie is not None:
-                piece, first[tie] = lax.optimization_barrier((piece, first[tie]))
+            if n_dp == 2 and KN["rpay"][f] == 1:
+                piece, ready[0] = lax.optimization_barrier((piece, ready[0]))
+            elif n_dp == 2 and KN["rpay"][f] == 2 and value is not None:
+                piece, value = lax.optimization_barrier((piece, value))
             got.append(swap(piece, "dp", j))
-        return got
+        return got, value
 
     def columns_of(g, value):
         near = cotangents
         if g:
-            if KN["ypay"] is not None:
-                near, first[KN["ypay"]] = lax.optimization_barrier((near, first[KN["ypay"]]))
+            if KN["ypay"] == 1:
+                near, ready[0] = lax.optimization_barrier((near, ready[0]))
+            elif KN["ypay"] == 2 and value is not None:
+                near, value = lax.optimization_barrier((near, value))
             near = swap(near, "mp", 2 * g)
             if KN["yrecv"] and value is not None:
                 near, value = lax.optimization_barrier((near, value))
@@ -315,7 +327,7 @@
         if g not in ready:
             ready[g], value = columns_of(g, value)
         if f not in moved:
-            got = send(f)
+            got, value = send(f, value)
             if not f:
                 got, ready[0] = lax.optimization_barrier((got, ready[0]))
             elif KN["rrecv"][f] and value is not None:
@@ -326,12 +338,8 @@
                 moved[f], ready[g], (((0,), (0,)), ((), ())), preferred_element_type=jnp.float32
             )
         )
-        if k < 2:
-            first[k] = found
         return found, value
 
-    late_gain = norm_gain
-    gain = late_gain.astype(jnp.float32)[None, :]
     shards = n_section * n_dp
     out = []
     sums = {}
@@ -343,6 +351,8 @@
         return (lax.all_gather(values, "dp"),)
 
     def emit(group, values):
+        values, late_gain = lax.optimization_barrier((values, norm_gain))
+        gain = late_gain.astype(jnp.float32)[None, :]
         if len(values) == 2:
             values = jnp.stack(in_order(values))
         else:
@@ -370,8 +380,9 @@
             sums[k] = total
 
     def key_steps():
-        yield (inverse,)
-        (late_inverse,) = side_values[0]
+        yield (inverse, places, norm_gain)
+        late_inverse, late_places, late_gain = side_values[0]
+        gain = late_gain.astype(jnp.float32)[None, :]
         normed = held.astype(jnp.float32) * late_inverse.reshape(-1, 1) * gain
         normed = lax.optimization_barrier(normed.astype(jnp.bfloat16))
         partial = jnp.dot(normed, key_weight, preferred_element_type=jnp.float32)
@@ -389,7 +400,7 @@
         for slot in range(block_count):
             chosen = keys[0]
             for b in range(1, block_count):
-                chosen = jnp.where(rest[block_count + b][:, None] == slot, keys[b], chosen)
+                chosen = jnp.where(late_places[b][:, None] == slot, keys[b], chosen)
             by_slot.append(chosen)
         by_target = [jnp.concatenate(by_slot[e * pair : (e + 1) * pair]) for e in range(n_dp)]
         yield (pick(by_target, dp),) + tuple(

time: 114 us -> 117 us (1.026)
  waiting for transfers between devices: 27.7 us -> 29.6 us
  starting transfers between devices: 59.4 us -> 61.3 us
  other arithmetic: 6.24 us -> 4.87 us
  local copies, waits for them, and re-layouts: 2.58 us -> 3.94 us
    ppermute x21 -> x23, waiting for transfers between devices: 14.4 us -> 22 us  [swap(): lax.ppermute(value, axis, [(i, i ^ bit) for i in range(lax.axis_size(axis...]
    ppermute x11, waiting for transfers between devices: 13.3 us -> 7.63 us  [end_swap(): return lax.ppermute(value, 'section', [(0, 1), (1, 0), (2, 3), (3, 2)])]
    ppermute x21 -> x23, starting transfers between devices: 19.8 us -> 21.4 us  [swap(): lax.ppermute(value, axis, [(i, i ^ bit) for i in range(lax.axis_size(axis...]
    unnamed x7 -> x25, local copies, waits for them, and re-layouts: 2.51 us -> 3.87 us
  transfers between devices with their start and end apart: 40 -> 42, of which waited for: 17 -> 12; matrix products, arithmetic and copies ran while one was open for 8% -> 7% of each run, Pallas kernels for 9% -> 9%
where the time goes in v10:
time: 117 us
  starting transfers between devices  61.3 us (52%)
  waiting for transfers between devices  29.6 us (25%)
  Pallas kernels  11.8 us (10%)
  other arithmetic  4.87 us (4%)
  local copies, waits for them, and re-layouts  3.94 us (3%)
  matrix products  3.85 us (3%)
  between operations  1.48 us (1%)
    ppermute x11, starting transfers between devices, end_swap(): return lax.ppermute(value, 'section', [(0, 1), (1, 0), (2, 3), (3, 2)])  34.2 us
    ppermute x23, waiting for transfers between devices, swap(): lax.ppermute(value, axis, [(i, i ^ bit) for i in range(lax.axis_size(axis...  22 us
    ppermute x23, starting transfers between devices, swap(): lax.ppermute(value, axis, [(i, i ^ bit) for i in range(lax.axis_size(axis...  21.4 us
    pallas_call x8, Pallas kernels, emit(): pl.pallas_call(functools.partial(store, n_dp, g, f * chunk, i * chunk, sh...  9.56 us
    ppermute x11, waiting for transfers between devices, end_swap(): return lax.ppermute(value, 'section', [(0, 1), (1, 0), (2, 3), (3, 2)])  7.63 us
    ppermute x8, starting transfers between devices, middle_swap(): return lax.ppermute(value, 'section', [(1, 2), (2, 1), (0, 0), (3, 3)])  5.72 us
    unnamed x25, local copies, waits for them, and re-layouts  3.87 us
    dot_general x8, matrix products, part(): lax.dot_general(moved[f], ready[g], (((0,), (0,)), ((), ())), preferred_e...  2.56 us
  transfers between devices with their start and end apart: 42, of which 12 were waited for; matrix products, arithmetic and copies ran while one was open for 7% of the time, Pallas kernels for 9%

profile of v10, /device:TPU:0, one launch (start us, length us, event | category | flops | bytes accessed | tf_op | source)
XLA Modules:
  0.0 116.8 jit_solution(8477187400657215752)
XLA Ops:
  2.1 3.0 %collective-permute-start.4 = (bf16[256,256]{1,0:T(8,128)(2,1)}, bf16[256,256]{1,0:T(8,128)(2,1)S(1)}, u32[]{:S(2)}, u32[]{:S(2)}) collective-permute-start(bf16[256,256]{1,0:T(8,128)(2,1)} %param.17), channel_id=1, source_target_pairs={{0,4},{4,0},{1,5},{5,1},{2,6},{6,2},{3,7},{7,3},{8,12},{12,8},{9,1... | collective-permute-start | bytes 393224 | tf_op jit(solution)/shard_map/ppermute | solution.py:17
  13.3 4.2 %collective-permute-done.3 = bf16[256,256]{1,0:T(8,128)(2,1)S(1)} collective-permute-done((bf16[256,256]{1,0:T(8,128)(2,1)S(1)}, bf16[256,256]{1,0:T(8,128)(2,1)S(1)}, u32[]{:S(2)}, u32[]{:S(2)}) %collective-permute-start.3) | collective-permute-done | bytes 131104 | tf_op jit(solution)/shard_map/ppermute | solution.py:17
  19.0 1.6 %collective-permute-start.9 = (bf16[256,512]{1,0:T(8,128)(2,1)S(1)}, bf16[256,512]{1,0:T(8,128)(2,1)S(1)}, u32[]{:S(2)}, u32[]{:S(2)}) collective-permute-start(bf16[256,512]{1,0:T(8,128)(2,1)S(1)} %fusion.1), channel_id=1, source_target_pairs={{0,8},{8,0},{16,24},{24,16},{1,9},{9,1},{17,25},{25,17},{2,10},{10... | collective-permute-start | bytes 786440 | tf_op jit(solution)/shard_map/ppermute | solution.py:36
  20.7 1.8 %collective-permute-done.6 = bf16[256,256]{1,0:T(8,128)(2,1)S(1)} collective-permute-done((bf16[256,256]{1,0:T(8,128)(2,1)S(1)}, bf16[256,256]{1,0:T(8,128)(2,1)S(1)}, u32[]{:S(2)}, u32[]{:S(2)}) %collective-permute-start.6) | collective-permute-done | bytes 131104 | tf_op jit(solution)/shard_map/ppermute | solution.py:17
  23.6 1.6 %collective-permute-start.7 = (bf16[256,512]{1,0:T(8,128)(2,1)S(1)}, bf16[256,512]{1,0:T(8,128)(2,1)S(1)}, u32[]{:S(2)}, u32[]{:S(2)}) collective-permute-start(bf16[256,512]{1,0:T(8,128)(2,1)S(1)} %fusion), channel_id=1, source_target_pairs={{0,8},{8,0},{16,24},{24,16},{1,9},{9,1},{17,25},{25,17},{2,10},{10... | collective-permute-start | bytes 786440 | tf_op jit(solution)/shard_map/ppermute | solution.py:36
  26.1 2.2 %collective-permute-done.9 = bf16[256,512]{1,0:T(8,128)(2,1)S(1)} collective-permute-done((bf16[256,512]{1,0:T(8,128)(2,1)S(1)}, bf16[256,512]{1,0:T(8,128)(2,1)S(1)}, u32[]{:S(2)}, u32[]{:S(2)}) %collective-permute-start.9) | collective-permute-done | bytes 262176 | tf_op jit(solution)/shard_map/ppermute | solution.py:36
  30.6 1.7 %collective-permute-done.7 = bf16[256,512]{1,0:T(8,128)(2,1)S(1)} collective-permute-done((bf16[256,512]{1,0:T(8,128)(2,1)S(1)}, bf16[256,512]{1,0:T(8,128)(2,1)S(1)}, u32[]{:S(2)}, u32[]{:S(2)}) %collective-permute-start.7) | collective-permute-done | bytes 262176 | tf_op jit(solution)/shard_map/ppermute | solution.py:36
  35.9 4.4 %collective-permute-start.14 = (bf16[256,512]{1,0:T(8,128)(2,1)S(1)}, bf16[256,512]{1,0:T(8,128)(2,1)S(1)}, u32[]{:S(2)}, u32[]{:S(2)}) collective-permute-start(bf16[256,512]{1,0:T(8,128)(2,1)S(1)} %fusion.2), channel_id=1, source_target_pairs={{0,8},{8,0},{16,24},{24,16},{1,9},{9,1},{17,25},{25,17},{2,10},{10... | collective-permute-start | bytes 786440 | tf_op jit(solution)/shard_map/ppermute | solution.py:36
  40.8 3.1 %collective-permute-start.19 = (bf16[256,512]{1,0:T(8,128)(2,1)S(1)}, bf16[256,512]{1,0:T(8,128)(2,1)S(1)}, u32[]{:S(2)}, u32[]{:S(2)}) collective-permute-start(bf16[256,512]{1,0:T(8,128)(2,1)S(1)} %get-tuple-element.303), channel_id=1, source_target_pairs={{0,8},{8,0},{16,24},{24,16},{1,9},{9,1},{17,25},{25,17},{2,10},{10... | collective-permute-start | bytes 786440 | tf_op jit(solution)/shard_map/ppermute | solution.py:36
  43.9 3.7 %collective-permute-done.14 = bf16[256,512]{1,0:T(8,128)(2,1)S(1)} collective-permute-done((bf16[256,512]{1,0:T(8,128)(2,1)S(1)}, bf16[256,512]{1,0:T(8,128)(2,1)S(1)}, u32[]{:S(2)}, u32[]{:S(2)}) %collective-permute-start.14) | collective-permute-done | bytes 262176 | tf_op jit(solution)/shard_map/ppermute | solution.py:36
  49.3 3.3 %collective-permute-start.16 = (bf16[256,512]{1,0:T(8,128)(2,1)S(1)}, bf16[256,512]{1,0:T(8,128)(2,1)S(1)}, u32[]{:S(2)}, u32[]{:S(2)}) collective-permute-start(bf16[256,512]{1,0:T(8,128)(2,1)S(1)} %get-tuple-element.301), channel_id=1, source_target_pairs={{0,8},{8,0},{16,24},{24,16},{1,9},{9,1},{17,25},{25,17},{2,10},{10... | collective-permute-start | bytes 786440 | tf_op jit(solution)/shard_map/ppermute | solution.py:36
  55.5 4.2 %collective-permute-start.22 = (bf16[256,512]{1,0:T(8,128)(2,1)S(1)}, bf16[256,512]{1,0:T(8,128)(2,1)S(1)}, u32[]{:S(2)}, u32[]{:S(2)}) collective-permute-start(bf16[256,512]{1,0:T(8,128)(2,1)S(1)} %get-tuple-element.305), channel_id=1, source_target_pairs={{0,8},{8,0},{16,24},{24,16},{1,9},{9,1},{17,25},{25,17},{2,10},{10... | collective-permute-start | bytes 786440 | tf_op jit(solution)/shard_map/ppermute | solution.py:36
  60.9 4.8 %collective-permute-start.26 = (bf16[256,512]{1,0:T(8,128)(2,1)S(1)}, bf16[256,512]{1,0:T(8,128)(2,1)S(1)}, u32[]{:S(2)}, u32[]{:S(2)}) collective-permute-start(bf16[256,512]{1,0:T(8,128)(2,1)S(1)} %get-tuple-element.259), channel_id=1, source_target_pairs={{0,8},{8,0},{16,24},{24,16},{1,9},{9,1},{17,25},{25,17},{2,10},{10... | collective-permute-start | bytes 786440 | tf_op jit(solution)/shard_map/ppermute | solution.py:36
  67.9 2.0 %collective-permute-start.28 = (bf16[256,512]{1,0:T(8,128)(2,1)S(1)}, bf16[256,512]{1,0:T(8,128)(2,1)S(1)}, u32[]{:S(2)}, u32[]{:S(2)}) collective-permute-start(bf16[256,512]{1,0:T(8,128)(2,1)S(1)} %broadcast_select_fusion.7), channel_id=1, source_target_pairs={{0,4},{4,0},{1,5},{5,1},{2,6},{6,2},{3,7},{7,3},{8,12},{12,8},{9,1... | collective-permute-start | bytes 786440 | tf_op jit(solution)/shard_map/ppermute | solution.py:17
  70.0 2.0 %collective-permute-start.23 = (bf16[256,512]{1,0:T(8,128)(2,1)S(1)}, bf16[256,512]{1,0:T(8,128)(2,1)S(1)}, u32[]{:S(2)}, u32[]{:S(2)}) collective-permute-start(bf16[256,512]{1,0:T(8,128)(2,1)S(1)} %get-tuple-element.261), channel_id=1, source_target_pairs={{0,8},{8,0},{16,24},{24,16},{1,9},{9,1},{17,25},{25,17},{2,10},{10... | collective-permute-start | bytes 786440 | tf_op jit(solution)/shard_map/ppermute | solution.py:36
  76.9 2.7 %collective-permute-start.36 = (bf16[256,512]{1,0:T(8,128)(2,1)S(1)}, bf16[256,512]{1,0:T(8,128)(2,1)S(1)}, u32[]{:S(2)}, u32[]{:S(2)}) collective-permute-start(bf16[256,512]{1,0:T(8,128)(2,1)S(1)} %reduce-precision_convert_fusion.3), channel_id=1, source_target_pairs={{0,8},{8,0},{16,24},{24,16},{1,9},{9,1},{17,25},{25,17},{2,10},{10... | collective-permute-start | bytes 786440 | tf_op jit(solution)/shard_map/ppermute | solution.py:36
  81.9 1.8 %collective-permute-start.30 = (bf16[256,256]{1,0:T(8,128)(2,1)S(1)}, bf16[256,256]{1,0:T(8,128)(2,1)S(1)}, u32[]{:S(2)}, u32[]{:S(2)}) collective-permute-start(bf16[256,256]{1,0:T(8,128)(2,1)S(1)} %get-tuple-element.264), channel_id=1, source_target_pairs={{0,1},{1,0},{2,3},{3,2},{4,5},{5,4},{6,7},{7,6},{8,9},{9,8},{10,11... | collective-permute-start | bytes 393224 | tf_op jit(solution)/shard_map/ppermute | solution.py:17
  84.6 1.6 %collective-permute-done.31 = bf16[256,256]{1,0:T(8,128)(2,1)S(1)} collective-permute-done((bf16[256,256]{1,0:T(8,128)(2,1)S(1)}, bf16[256,256]{1,0:T(8,128)(2,1)S(1)}, u32[]{:S(2)}, u32[]{:S(2)}) %collective-permute-start.31) | collective-permute-done | bytes 131104 | tf_op jit(solution)/shard_map/ppermute | solution.py:17
  86.9 2.2 %collective-permute-start.39 = (bf16[256,512]{1,0:T(8,128)(2,1)S(1)}, bf16[256,512]{1,0:T(8,128)(2,1)S(1)}, u32[]{:S(2)}, u32[]{:S(2)}) collective-permute-start(bf16[256,512]{1,0:T(8,128)(2,1)S(1)} %reduce-precision_convert_fusion.1), channel_id=1, source_target_pairs={{0,8},{8,0},{16,24},{24,16},{1,9},{9,1},{17,25},{25,17},{2,10},{10... | collective-permute-start | bytes 786440 | tf_op jit(solution)/shard_map/ppermute | solution.py:36
  91.8 4.1 %collective-permute-start.37 = (bf16[256,512]{1,0:T(8,128)(2,1)S(1)}, bf16[256,512]{1,0:T(8,128)(2,1)S(1)}, u32[]{:S(2)}, u32[]{:S(2)}) collective-permute-start(bf16[256,512]{1,0:T(8,128)(2,1)S(1)} %reduce-precision_convert_fusion), channel_id=1, source_target_pairs={{0,8},{8,0},{16,24},{24,16},{1,9},{9,1},{17,25},{25,17},{2,10},{10... | collective-permute-start | bytes 786440 | tf_op jit(solution)/shard_map/ppermute | solution.py:36
  98.5 1.6 %collective-permute-start.40 = (bf16[256,512]{1,0:T(8,128)(2,1)S(1)}, bf16[256,512]{1,0:T(8,128)(2,1)S(1)}, u32[]{:S(2)}, u32[]{:S(2)}) collective-permute-start(bf16[256,512]{1,0:T(8,128)(2,1)S(1)} %broadcast_select_fusion.5), channel_id=1, source_target_pairs={{0,4},{4,0},{1,5},{5,1},{2,6},{6,2},{3,7},{7,3},{8,12},{12,8},{9,1... | collective-permute-start | bytes 786440 | tf_op jit(solution)/shard_map/ppermute | solution.py:17
  100.2 5.1 %collective-permute-done.41 = bf16[256,512]{1,0:T(8,128)(2,1)S(1)} collective-permute-done((bf16[256,512]{1,0:T(8,128)(2,1)S(1)}, bf16[256,512]{1,0:T(8,128)(2,1)S(1)}, u32[]{:S(2)}, u32[]{:S(2)}) %collective-permute-start.41) | collective-permute-done | bytes 262176 | tf_op jit(solution)/shard_map/ppermute | solution.py:17
  107.1 3.7 %collective-permute-done.40 = bf16[256,512]{1,0:T(8,128)(2,1)S(1)} collective-permute-done((bf16[256,512]{1,0:T(8,128)(2,1)S(1)}, bf16[256,512]{1,0:T(8,128)(2,1)S(1)}, u32[]{:S(2)}, u32[]{:S(2)}) %collective-permute-start.40) | collective-permute-done | bytes 262176 | tf_op jit(solution)/shard_map/ppermute | solution.py:17
  112.2 2.7 %collective-permute-done.38 = bf16[256,512]{1,0:T(8,128)(2,1)S(1)} collective-permute-done((bf16[256,512]{1,0:T(8,128)(2,1)S(1)}, bf16[256,512]{1,0:T(8,128)(2,1)S(1)}, u32[]{:S(2)}, u32[]{:S(2)}) %collective-permute-start.38) | collective-permute-done | bytes 262176 | tf_op jit(solution)/shard_map/ppermute | solution.py:17
  (177 shorter events, 45.9 us)
Async XLA Ops:
  2.1 8.3 %collective-permute-start.4 = (bf16[256,256]{1,0:T(8,128)(2,1)}, bf16[256,256]{1,0:T(8,128)(2,1)S(1)}, u32[]{:S(2)}, u32[]{:S(2)}) collective-permute-start(bf16[256,256]{1,0:T(8,128)(2,1)} %param.17), channel_id=1, source_target_pairs={{0,4},{4,0},{1,5},{5,1},{2,6},{6,2},{3,7},{7,3},{8,12},{12,8},{9,1... | collective-permute-start | bytes 393224 | tf_op jit(solution)/shard_map/ppermute | solution.py:17
  19.0 9.3 %collective-permute-start.9 = (bf16[256,512]{1,0:T(8,128)(2,1)S(1)}, bf16[256,512]{1,0:T(8,128)(2,1)S(1)}, u32[]{:S(2)}, u32[]{:S(2)}) collective-permute-start(bf16[256,512]{1,0:T(8,128)(2,1)S(1)} %fusion.1), channel_id=1, source_target_pairs={{0,8},{8,0},{16,24},{24,16},{1,9},{9,1},{17,25},{25,17},{2,10},{10... | collective-permute-start | bytes 786440 | tf_op jit(solution)/shard_map/ppermute | solution.py:36
  23.6 8.7 %collective-permute-start.7 = (bf16[256,512]{1,0:T(8,128)(2,1)S(1)}, bf16[256,512]{1,0:T(8,128)(2,1)S(1)}, u32[]{:S(2)}, u32[]{:S(2)}) collective-permute-start(bf16[256,512]{1,0:T(8,128)(2,1)S(1)} %fusion), channel_id=1, source_target_pairs={{0,8},{8,0},{16,24},{24,16},{1,9},{9,1},{17,25},{25,17},{2,10},{10... | collective-permute-start | bytes 786440 | tf_op jit(solution)/shard_map/ppermute | solution.py:36
  28.4 12.0 %collective-permute-start.10 = (bf16[256,512]{1,0:T(8,128)(2,1)S(1)}, bf16[256,512]{1,0:T(8,128)(2,1)S(1)}, u32[]{:S(2)}, u32[]{:S(2)}) collective-permute-start(bf16[256,512]{1,0:T(8,128)(2,1)S(1)} %reduce-precision_convert_fusion.14), channel_id=1, source_target_pairs={{8,16},{16,8},{0,0},{24,24},{9,17},{17,9},{1,1},{25,25},{10,18},{1... | collective-permute-start | bytes 786440 | tf_op jit(solution)/shard_map/ppermute | solution.py:40
  32.3 16.0 %collective-permute-start.8 = (bf16[256,512]{1,0:T(8,128)(2,1)S(1)}, bf16[256,512]{1,0:T(8,128)(2,1)S(1)}, u32[]{:S(2)}, u32[]{:S(2)}) collective-permute-start(bf16[256,512]{1,0:T(8,128)(2,1)S(1)} %reduce-precision_convert_fusion.15), channel_id=1, source_target_pairs={{8,16},{16,8},{0,0},{24,24},{9,17},{17,9},{1,1},{25,25},{10,18},{1... | collective-permute-start | bytes 786440 | tf_op jit(solution)/shard_map/ppermute | solution.py:40
  33.0 15.3 %collective-permute-start.15 = (bf16[512,256]{1,0:T(8,128)(2,1)S(1)}, bf16[512,256]{1,0:T(8,128)(2,1)S(1)}, u32[]{:S(2)}, u32[]{:S(2)}) collective-permute-start(bf16[512,256]{1,0:T(8,128)(2,1)S(1)} %collective-permute-done.13), channel_id=1, source_target_pairs={{0,1},{1,0},{2,3},{3,2},{4,5},{5,4},{6,7},{7,6},{8,9},{9,8},{10,11... | collective-permute-start | bytes 786440 | tf_op jit(solution)/shard_map/ppermute | solution.py:17
  35.9 11.7 %collective-permute-start.14 = (bf16[256,512]{1,0:T(8,128)(2,1)S(1)}, bf16[256,512]{1,0:T(8,128)(2,1)S(1)}, u32[]{:S(2)}, u32[]{:S(2)}) collective-permute-start(bf16[256,512]{1,0:T(8,128)(2,1)S(1)} %fusion.2), channel_id=1, source_target_pairs={{0,8},{8,0},{16,24},{24,16},{1,9},{9,1},{17,25},{25,17},{2,10},{10... | collective-permute-start | bytes 786440 | tf_op jit(solution)/shard_map/ppermute | solution.py:36
  40.8 12.2 %collective-permute-start.19 = (bf16[256,512]{1,0:T(8,128)(2,1)S(1)}, bf16[256,512]{1,0:T(8,128)(2,1)S(1)}, u32[]{:S(2)}, u32[]{:S(2)}) collective-permute-start(bf16[256,512]{1,0:T(8,128)(2,1)S(1)} %get-tuple-element.303), channel_id=1, source_target_pairs={{0,8},{8,0},{16,24},{24,16},{1,9},{9,1},{17,25},{25,17},{2,10},{10... | collective-permute-start | bytes 786440 | tf_op jit(solution)/shard_map/ppermute | solution.py:36
  49.3 10.4 %collective-permute-start.16 = (bf16[256,512]{1,0:T(8,128)(2,1)S(1)}, bf16[256,512]{1,0:T(8,128)(2,1)S(1)}, u32[]{:S(2)}, u32[]{:S(2)}) collective-permute-start(bf16[256,512]{1,0:T(8,128)(2,1)S(1)} %get-tuple-element.301), channel_id=1, source_target_pairs={{0,8},{8,0},{16,24},{24,16},{1,9},{9,1},{17,25},{25,17},{2,10},{10... | collective-permute-start | bytes 786440 | tf_op jit(solution)/shard_map/ppermute | solution.py:36
  55.5 11.5 %collective-permute-start.22 = (bf16[256,512]{1,0:T(8,128)(2,1)S(1)}, bf16[256,512]{1,0:T(8,128)(2,1)S(1)}, u32[]{:S(2)}, u32[]{:S(2)}) collective-permute-start(bf16[256,512]{1,0:T(8,128)(2,1)S(1)} %get-tuple-element.305), channel_id=1, source_target_pairs={{0,8},{8,0},{16,24},{24,16},{1,9},{9,1},{17,25},{25,17},{2,10},{10... | collective-permute-start | bytes 786440 | tf_op jit(solution)/shard_map/ppermute | solution.py:36
  59.9 10.0 %collective-permute-start.18 = (bf16[256,512]{1,0:T(8,128)(2,1)S(1)}, bf16[256,512]{1,0:T(8,128)(2,1)S(1)}, u32[]{:S(2)}, u32[]{:S(2)}) collective-permute-start(bf16[256,512]{1,0:T(8,128)(2,1)S(1)} %reduce-precision_convert_fusion.11), channel_id=1, source_target_pairs={{8,16},{16,8},{0,0},{24,24},{9,17},{17,9},{1,1},{25,25},{10,18},{1... | collective-permute-start | bytes 786440 | tf_op jit(solution)/shard_map/ppermute | solution.py:40
  60.6 11.4 %collective-permute-start.17 = (bf16[256,512]{1,0:T(8,128)(2,1)S(1)}, bf16[256,512]{1,0:T(8,128)(2,1)S(1)}, u32[]{:S(2)}, u32[]{:S(2)}) collective-permute-start(bf16[256,512]{1,0:T(8,128)(2,1)S(1)} %broadcast_select_fusion.15), channel_id=1, source_target_pairs={{0,4},{4,0},{1,5},{5,1},{2,6},{6,2},{3,7},{7,3},{8,12},{12,8},{9,1... | collective-permute-start | bytes 786440 | tf_op jit(solution)/shard_map/ppermute | solution.py:17
  60.9 14.0 %collective-permute-start.26 = (bf16[256,512]{1,0:T(8,128)(2,1)S(1)}, bf16[256,512]{1,0:T(8,128)(2,1)S(1)}, u32[]{:S(2)}, u32[]{:S(2)}) collective-permute-start(bf16[256,512]{1,0:T(8,128)(2,1)S(1)} %get-tuple-element.259), channel_id=1, source_target_pairs={{0,8},{8,0},{16,24},{24,16},{1,9},{9,1},{17,25},{25,17},{2,10},{10... | collective-permute-start | bytes 786440 | tf_op jit(solution)/shard_map/ppermute | solution.py:36
  67.2 9.7 %collective-permute-start.29 = (bf16[256,512]{1,0:T(8,128)(2,1)S(1)}, bf16[256,512]{1,0:T(8,128)(2,1)S(1)}, u32[]{:S(2)}, u32[]{:S(2)}) collective-permute-start(bf16[256,512]{1,0:T(8,128)(2,1)S(1)} %reduce-precision_convert_fusion.7), channel_id=1, source_target_pairs={{8,16},{16,8},{0,0},{24,24},{9,17},{17,9},{1,1},{25,25},{10,18},{1... | collective-permute-start | bytes 786440 | tf_op jit(solution)/shard_map/ppermute | solution.py:40
  67.9 11.9 %collective-permute-start.28 = (bf16[256,512]{1,0:T(8,128)(2,1)S(1)}, bf16[256,512]{1,0:T(8,128)(2,1)S(1)}, u32[]{:S(2)}, u32[]{:S(2)}) collective-permute-start(bf16[256,512]{1,0:T(8,128)(2,1)S(1)} %broadcast_select_fusion.7), channel_id=1, source_target_pairs={{0,4},{4,0},{1,5},{5,1},{2,6},{6,2},{3,7},{7,3},{8,12},{12,8},{9,1... | collective-permute-start | bytes 786440 | tf_op jit(solution)/shard_map/ppermute | solution.py:17
  70.0 9.6 %collective-permute-start.23 = (bf16[256,512]{1,0:T(8,128)(2,1)S(1)}, bf16[256,512]{1,0:T(8,128)(2,1)S(1)}, u32[]{:S(2)}, u32[]{:S(2)}) collective-permute-start(bf16[256,512]{1,0:T(8,128)(2,1)S(1)} %get-tuple-element.261), channel_id=1, source_target_pairs={{0,8},{8,0},{16,24},{24,16},{1,9},{9,1},{17,25},{25,17},{2,10},{10... | collective-permute-start | bytes 786440 | tf_op jit(solution)/shard_map/ppermute | solution.py:36
  75.1 8.7 %collective-permute-start.27 = (bf16[256,512]{1,0:T(8,128)(2,1)S(1)}, bf16[256,512]{1,0:T(8,128)(2,1)S(1)}, u32[]{:S(2)}, u32[]{:S(2)}) collective-permute-start(bf16[256,512]{1,0:T(8,128)(2,1)S(1)} %broadcast_select_fusion.8), channel_id=1, source_target_pairs={{0,4},{4,0},{1,5},{5,1},{2,6},{6,2},{3,7},{7,3},{8,12},{12,8},{9,1... | collective-permute-start | bytes 786440 | tf_op jit(solution)/shard_map/ppermute | solution.py:17
  76.9 14.8 %collective-permute-start.36 = (bf16[256,512]{1,0:T(8,128)(2,1)S(1)}, bf16[256,512]{1,0:T(8,128)(2,1)S(1)}, u32[]{:S(2)}, u32[]{:S(2)}) collective-permute-start(bf16[256,512]{1,0:T(8,128)(2,1)S(1)} %reduce-precision_convert_fusion.3), channel_id=1, source_target_pairs={{0,8},{8,0},{16,24},{24,16},{1,9},{9,1},{17,25},{25,17},{2,10},{10... | collective-permute-start | bytes 786440 | tf_op jit(solution)/shard_map/ppermute | solution.py:36
  86.2 10.2 %collective-permute-start.24 = (bf16[256,512]{1,0:T(8,128)(2,1)S(1)}, bf16[256,512]{1,0:T(8,128)(2,1)S(1)}, u32[]{:S(2)}, u32[]{:S(2)}) collective-permute-start(bf16[256,512]{1,0:T(8,128)(2,1)S(1)} %broadcast_select_fusion.11), channel_id=1, source_target_pairs={{0,4},{4,0},{1,5},{5,1},{2,6},{6,2},{3,7},{7,3},{8,12},{12,8},{9,1... | collective-permute-start | bytes 786440 | tf_op jit(solution)/shard_map/ppermute | solution.py:17
  86.9 11.6 %collective-permute-start.39 = (bf16[256,512]{1,0:T(8,128)(2,1)S(1)}, bf16[256,512]{1,0:T(8,128)(2,1)S(1)}, u32[]{:S(2)}, u32[]{:S(2)}) collective-permute-start(bf16[256,512]{1,0:T(8,128)(2,1)S(1)} %reduce-precision_convert_fusion.1), channel_id=1, source_target_pairs={{0,8},{8,0},{16,24},{24,16},{1,9},{9,1},{17,25},{25,17},{2,10},{10... | collective-permute-start | bytes 786440 | tf_op jit(solution)/shard_map/ppermute | solution.py:36
  91.8 13.5 %collective-permute-start.37 = (bf16[256,512]{1,0:T(8,128)(2,1)S(1)}, bf16[256,512]{1,0:T(8,128)(2,1)S(1)}, u32[]{:S(2)}, u32[]{:S(2)}) collective-permute-start(bf16[256,512]{1,0:T(8,128)(2,1)S(1)} %reduce-precision_convert_fusion), channel_id=1, source_target_pairs={{0,8},{8,0},{16,24},{24,16},{1,9},{9,1},{17,25},{25,17},{2,10},{10... | collective-permute-start | bytes 786440 | tf_op jit(solution)/shard_map/ppermute | solution.py:36
  95.9 9.3 %collective-permute-start.41 = (bf16[256,512]{1,0:T(8,128)(2,1)S(1)}, bf16[256,512]{1,0:T(8,128)(2,1)S(1)}, u32[]{:S(2)}, u32[]{:S(2)}) collective-permute-start(bf16[256,512]{1,0:T(8,128)(2,1)S(1)} %broadcast_select_fusion.4), channel_id=1, source_target_pairs={{0,4},{4,0},{1,5},{5,1},{2,6},{6,2},{3,7},{7,3},{8,12},{12,8},{9,1... | collective-permute-start | bytes 786440 | tf_op jit(solution)/shard_map/ppermute | solution.py:17
  98.5 12.3 %collective-permute-start.40 = (bf16[256,512]{1,0:T(8,128)(2,1)S(1)}, bf16[256,512]{1,0:T(8,128)(2,1)S(1)}, u32[]{:S(2)}, u32[]{:S(2)}) collective-permute-start(bf16[256,512]{1,0:T(8,128)(2,1)S(1)} %broadcast_select_fusion.5), channel_id=1, source_target_pairs={{0,4},{4,0},{1,5},{5,1},{2,6},{6,2},{3,7},{7,3},{8,12},{12,8},{9,1... | collective-permute-start | bytes 786440 | tf_op jit(solution)/shard_map/ppermute | solution.py:17
  105.3 9.6 %collective-permute-start.38 = (bf16[256,512]{1,0:T(8,128)(2,1)S(1)}, bf16[256,512]{1,0:T(8,128)(2,1)S(1)}, u32[]{:S(2)}, u32[]{:S(2)}) collective-permute-start(bf16[256,512]{1,0:T(8,128)(2,1)S(1)} %broadcast_select_fusion.6), channel_id=1, source_target_pairs={{0,4},{4,0},{1,5},{5,1},{2,6},{6,2},{3,7},{7,3},{8,12},{12,8},{9,1... | collective-permute-start | bytes 786440 | tf_op jit(solution)/shard_map/ppermute | solution.py:17
  (30 other events, 179.7 us)

commit v11 on v9

--- a/solution.py
+++ b/solution.py
@@ -151,7 +151,7 @@
 
 
 def scale(n_dp, n_mp, width, rest, rows, *refs):
-    squares, inverse, pieces = refs[:n_mp], refs[n_mp], refs[n_mp + 1 :]
+    squares, (inverse, places), pieces = refs[:n_mp], refs[n_mp : n_mp + 2], refs[n_mp + 2 :]
     block_count, block_len = inverse.shape
     dp = lax.axis_index("dp")
     own_width = rows.shape[1] // n_dp
@@ -160,6 +160,7 @@
     for other in squares[1:]:
         total = total + other[...]
     inverse[...] = lax.rsqrt(total / (rows.shape[1] * n_mp) + EPSILON)
+    places[...] = rest[block_count:, :]
     factors = inverse[...] * rest[:block_count, :]
     lane = lax.broadcasted_iota(jnp.int32, (block_len, block_len), 1)
     diagonal = lane == lax.broadcasted_iota(jnp.int32, (block_len, block_len), 0)
@@ -209,13 +210,13 @@
             total = jnp.sum(total, axis=1, keepdims=True)
             total = jnp.sum(jnp.where(diagonal, total, 0.0), axis=0, keepdims=True)
             sums[e : e + 1, at : at + 128] = total
-        copy = pltpu.make_async_copy(
-            results.at[e],
-            out.at[pl.ds(start, chunk), pl.ds(column, width)],
-            semaphores.at[e],
-        )
-        copy.start()
-        stores.append(copy)
+            copy = pltpu.make_async_copy(
+                results.at[e, pl.ds(at, 128)],
+                out.at[pl.ds(start + at, 128), pl.ds(column, width)],
+                semaphores.at[e, at // 128],
+            )
+            copy.start()
+            stores.append(copy)
     for copy in stores:
         copy.wait()
 
@@ -270,12 +271,12 @@
         out_specs=vmem,
         name="score",
     )(lengths, block_order, final_hidden, score_gain, score_head)
-    inverse, *pieces = pl.pallas_call(
+    inverse, places, *pieces = pl.pallas_call(
         functools.partial(scale, n_dp, n_mp, chunk),
-        out_shape=[jax.ShapeDtypeStruct((block_count, block_len), jnp.float32)]
+        out_shape=[jax.ShapeDtypeStruct((block_count, block_len), jnp.float32)] * 2
         + [jax.ShapeDtypeStruct((tokens, chunk), jnp.bfloat16)] * (n_dp * feature_blocks),
         in_specs=[vmem] * (2 + n_mp),
-        out_specs=[vmem] * (1 + n_dp * feature_blocks),
+        out_specs=[vmem] * (2 + n_dp * feature_blocks),
         compiler_params=pltpu.CompilerParams(vmem_limit_bytes=32 * 2**20),
         name="scale",
     )(rest, held, *squares)
@@ -330,8 +331,6 @@
             first[k] = found
         return found, value
 
-    late_gain = norm_gain
-    gain = late_gain.astype(jnp.float32)[None, :]
     shards = n_section * n_dp
     out = []
     sums = {}
@@ -343,6 +342,8 @@
         return (lax.all_gather(values, "dp"),)
 
     def emit(group, values):
+        values, late_gain = lax.optimization_barrier((values, norm_gain))
+        gain = late_gain.astype(jnp.float32)[None, :]
         if len(values) == 2:
             values = jnp.stack(in_order(values))
         else:
@@ -361,7 +362,7 @@
                 input_output_aliases={3: 0} if before else {},
                 scratch_shapes=[
                     pltpu.VMEM((n_dp, chunk, 2 * columns), jnp.float32),
-                    pltpu.SemaphoreType.DMA((n_dp,)),
+                    pltpu.SemaphoreType.DMA((n_dp, chunk // 128)),
                 ],
                 compiler_params=pltpu.CompilerParams(vmem_limit_bytes=32 * 2**20),
                 name="store",
@@ -370,8 +371,9 @@
             sums[k] = total
 
     def key_steps():
-        yield (inverse,)
-        (late_inverse,) = side_values[0]
+        yield (inverse, norm_gain)
+        late_inverse, late_gain = side_values[0]
+        gain = late_gain.astype(jnp.float32)[None, :]
         normed = held.astype(jnp.float32) * late_inverse.reshape(-1, 1) * gain
         normed = lax.optimization_barrier(normed.astype(jnp.bfloat16))
         partial = jnp.dot(normed, key_weight, preferred_element_type=jnp.float32)
@@ -389,7 +391,7 @@
         for slot in range(block_count):
             chosen = keys[0]
             for b in range(1, block_count):
-                chosen = jnp.where(rest[block_count + b][:, None] == slot, keys[b], chosen)
+                chosen = jnp.where(places[b][:, None] == slot, keys[b], chosen)
             by_slot.append(chosen)
         by_target = [jnp.concatenate(by_slot[e * pair : (e + 1) * pair]) for e in range(n_dp)]
         yield (pick(by_target, dp),) + tuple(

time: 114 us -> 111 us (0.974)
  starting transfers between devices: 59.4 us -> 56.2 us
  waiting for transfers between devices: 27.7 us -> 29.8 us
  other arithmetic: 6.24 us -> 4.89 us
    ppermute x21, waiting for transfers between devices: 14.4 us -> 16.7 us  [swap(): lax.ppermute(value, axis, [(i, i ^ bit) for i in range(lax.axis_size(axis...]
    ppermute x11, starting transfers between devices: 33.8 us -> 32.1 us  [end_swap(): return lax.ppermute(value, 'section', [(0, 1), (1, 0), (2, 3), (3, 2)])]
    ppermute x21, starting transfers between devices: 19.8 us -> 18.4 us  [swap(): lax.ppermute(value, axis, [(i, i ^ bit) for i in range(lax.axis_size(axis...]
    unnamed x7 -> x9, local copies, waits for them, and re-layouts: 2.51 us -> 2.51 us
  transfers between devices with their start and end apart: 40 -> 40, of which waited for: 17 -> 15; matrix products, arithmetic and copies ran while one was open for 8% -> 7% of each run, Pallas kernels for 9% -> 9%
where the time goes in v11:
time: 111 us; the launch traced here: 110 us
  starting transfers between devices  56.2 us (51%)
  waiting for transfers between devices  29.8 us (27%)
  Pallas kernels  11.4 us (10%)
  other arithmetic  4.89 us (4%)
  matrix products  3.85 us (3%)
  local copies, waits for them, and re-layouts  2.58 us (2%)
  between operations  1.39 us (1%)
    ppermute x11, starting transfers between devices, end_swap(): return lax.ppermute(value, 'section', [(0, 1), (1, 0), (2, 3), (3, 2)])  32.1 us
    ppermute x21, starting transfers between devices, swap(): lax.ppermute(value, axis, [(i, i ^ bit) for i in range(lax.axis_size(axis...  18.4 us
    ppermute x21, waiting for transfers between devices, swap(): lax.ppermute(value, axis, [(i, i ^ bit) for i in range(lax.axis_size(axis...  16.7 us
    ppermute x11, waiting for transfers between devices, end_swap(): return lax.ppermute(value, 'section', [(0, 1), (1, 0), (2, 3), (3, 2)])  13 us
    pallas_call x8, Pallas kernels, emit(): pl.pallas_call(functools.partial(store, n_dp, g, f * chunk, i * chunk, sh...  9.14 us
    ppermute x8, starting transfers between devices, middle_swap(): return lax.ppermute(value, 'section', [(1, 2), (2, 1), (0, 0), (3, 3)])  5.73 us
    dot_general x8, matrix products, part(): lax.dot_general(moved[f], ready[g], (((0,), (0,)), ((), ())), preferred_e...  2.56 us
    unnamed x9, local copies, waits for them, and re-layouts  2.51 us
  transfers between devices with their start and end apart: 40, of which 15 were waited for; matrix products, arithmetic and copies ran while one was open for 7% of the time, Pallas kernels for 9%

profile of v11, /device:TPU:0, one launch (start us, length us, event | category | flops | bytes accessed | tf_op | source)
XLA Modules:
  0.0 110.0 jit_solution(8824021717982103662)
XLA Ops:
  2.1 3.0 %collective-permute-start.4 = (bf16[256,256]{1,0:T(8,128)(2,1)}, bf16[256,256]{1,0:T(8,128)(2,1)S(1)}, u32[]{:S(2)}, u32[]{:S(2)}) collective-permute-start(bf16[256,256]{1,0:T(8,128)(2,1)} %param.17), channel_id=1, source_target_pairs={{0,4},{4,0},{1,5},{5,1},{2,6},{6,2},{3,7},{7,3},{8,12},{12,8},{9,1... | collective-permute-start | bytes 393224 | tf_op jit(solution)/shard_map/ppermute | solution.py:17
  5.2 1.5 %collective-permute-start.1 = (f32[2,128]{1,0:T(2,128)S(1)}, f32[2,128]{1,0:T(2,128)S(1)}, u32[]{:S(2)}, u32[]{:S(2)}) collective-permute-start(f32[2,128]{1,0:T(2,128)S(1)} %get-tuple-element.104.refs_0_), channel_id=1, source_target_pairs={{0,2},{1,3},{2,0},{3,1},{4,6},{5,7},{6,4},{7,5},{8,10},{9,11},{10,... | collective-permute-start | bytes 3080 | tf_op jit(solution)/shard_map/ppermute | solution.py:17
  7.0 1.5 %score.1.rest = f32[4,128]{1,0:T(4,128)} custom-call(s32[2]{0:T(128)} %lengths.1, s32[1,2]{1,0:T(1,128)} %order.1, bf16[2,3584]{1,0:T(2,128)(2,1)} %hidden.1, bf16[3584]{0:T(1024)(128)(2,1)} %gain.1, bf16[3584]{0:T(1024)(128)(2,1)} %head.1), custom_call_target="tpu_custom_call" | custom-call | tf_op jit(solution)/shard_map/score/pallas_call | solution.py:267
  15.0 3.3 %collective-permute-done.3 = bf16[256,256]{1,0:T(8,128)(2,1)S(1)} collective-permute-done((bf16[256,256]{1,0:T(8,128)(2,1)S(1)}, bf16[256,256]{1,0:T(8,128)(2,1)S(1)}, u32[]{:S(2)}, u32[]{:S(2)}) %collective-permute-start.3) | collective-permute-done | bytes 131104 | tf_op jit(solution)/shard_map/ppermute | solution.py:17
  19.6 1.6 %collective-permute-start.17 = (bf16[256,512]{1,0:T(8,128)(2,1)S(1)}, bf16[256,512]{1,0:T(8,128)(2,1)S(1)}, u32[]{:S(2)}, u32[]{:S(2)}) collective-permute-start(bf16[256,512]{1,0:T(8,128)(2,1)S(1)} %fusion), channel_id=1, source_target_pairs={{0,8},{8,0},{16,24},{24,16},{1,9},{9,1},{17,25},{25,17},{2,10},{10... | collective-permute-start | bytes 786440 | tf_op jit(solution)/shard_map/ppermute | solution.py:36
  22.0 1.7 %collective-permute-done.6 = bf16[256,256]{1,0:T(8,128)(2,1)S(1)} collective-permute-done((bf16[256,256]{1,0:T(8,128)(2,1)S(1)}, bf16[256,256]{1,0:T(8,128)(2,1)S(1)}, u32[]{:S(2)}, u32[]{:S(2)}) %collective-permute-start.6) | collective-permute-done | bytes 131104 | tf_op jit(solution)/shard_map/ppermute | solution.py:17
  24.1 1.6 %collective-permute-start.7 = (bf16[256,512]{1,0:T(8,128)(2,1)S(1)}, bf16[256,512]{1,0:T(8,128)(2,1)S(1)}, u32[]{:S(2)}, u32[]{:S(2)}) collective-permute-start(bf16[256,512]{1,0:T(8,128)(2,1)S(1)} %fusion.1), channel_id=1, source_target_pairs={{0,8},{8,0},{16,24},{24,16},{1,9},{9,1},{17,25},{25,17},{2,10},{10... | collective-permute-start | bytes 786440 | tf_op jit(solution)/shard_map/ppermute | solution.py:36
  27.5 3.2 %collective-permute-done.12 = bf16[256,256]{1,0:T(8,128)(2,1)S(1)} collective-permute-done((bf16[256,256]{1,0:T(8,128)(2,1)S(1)}, bf16[256,256]{1,0:T(8,128)(2,1)S(1)}, u32[]{:S(2)}, u32[]{:S(2)}) %collective-permute-start.12) | collective-permute-done | bytes 131104 | tf_op jit(solution)/shard_map/ppermute | solution.py:17
  34.4 3.7 %collective-permute-start.20 = (bf16[256,512]{1,0:T(8,128)(2,1)S(1)}, bf16[256,512]{1,0:T(8,128)(2,1)S(1)}, u32[]{:S(2)}, u32[]{:S(2)}) collective-permute-start(bf16[256,512]{1,0:T(8,128)(2,1)S(1)} %get-tuple-element.243), channel_id=1, source_target_pairs={{0,8},{8,0},{16,24},{24,16},{1,9},{9,1},{17,25},{25,17},{2,10},{10... | collective-permute-start | bytes 786440 | tf_op jit(solution)/shard_map/ppermute | solution.py:36
  38.1 2.1 %collective-permute-done.13 = bf16[256,512]{1,0:T(8,128)(2,1)S(1)} collective-permute-done((bf16[256,512]{1,0:T(8,128)(2,1)S(1)}, bf16[256,512]{1,0:T(8,128)(2,1)S(1)}, u32[]{:S(2)}, u32[]{:S(2)}) %collective-permute-start.13) | collective-permute-done | bytes 262176 | tf_op jit(solution)/shard_map/ppermute | solution.py:36
  41.3 5.0 %collective-permute-start.11 = (bf16[256,512]{1,0:T(8,128)(2,1)S(1)}, bf16[256,512]{1,0:T(8,128)(2,1)S(1)}, u32[]{:S(2)}, u32[]{:S(2)}) collective-permute-start(bf16[256,512]{1,0:T(8,128)(2,1)S(1)} %get-tuple-element.241), channel_id=1, source_target_pairs={{0,8},{8,0},{16,24},{24,16},{1,9},{9,1},{17,25},{25,17},{2,10},{10... | collective-permute-start | bytes 786440 | tf_op jit(solution)/shard_map/ppermute | solution.py:36
  48.0 5.1 %collective-permute-start.15 = (bf16[256,512]{1,0:T(8,128)(2,1)S(1)}, bf16[256,512]{1,0:T(8,128)(2,1)S(1)}, u32[]{:S(2)}, u32[]{:S(2)}) collective-permute-start(bf16[256,512]{1,0:T(8,128)(2,1)S(1)} %get-tuple-element.205), channel_id=1, source_target_pairs={{0,8},{8,0},{16,24},{24,16},{1,9},{9,1},{17,25},{25,17},{2,10},{10... | collective-permute-start | bytes 786440 | tf_op jit(solution)/shard_map/ppermute | solution.py:36
  54.3 4.5 %collective-permute-start.29 = (bf16[256,512]{1,0:T(8,128)(2,1)S(1)}, bf16[256,512]{1,0:T(8,128)(2,1)S(1)}, u32[]{:S(2)}, u32[]{:S(2)}) collective-permute-start(bf16[256,512]{1,0:T(8,128)(2,1)S(1)} %get-tuple-element.203), channel_id=1, source_target_pairs={{0,8},{8,0},{16,24},{24,16},{1,9},{9,1},{17,25},{25,17},{2,10},{10... | collective-permute-start | bytes 786440 | tf_op jit(solution)/shard_map/ppermute | solution.py:36
  65.3 1.6 %collective-permute-start.25 = (bf16[256,256]{1,0:T(8,128)(2,1)S(1)}, bf16[256,256]{1,0:T(8,128)(2,1)S(1)}, u32[]{:S(2)}, u32[]{:S(2)}) collective-permute-start(bf16[256,256]{1,0:T(8,128)(2,1)S(1)} %select_convert_fusion.1), channel_id=1, source_target_pairs={{0,2},{1,3},{2,0},{3,1},{4,6},{5,7},{6,4},{7,5},{8,10},{9,11},{10,... | collective-permute-start | bytes 393224 | tf_op jit(solution)/shard_map/ppermute | solution.py:17
  67.0 3.9 %collective-permute-start.31 = (bf16[256,512]{1,0:T(8,128)(2,1)S(1)}, bf16[256,512]{1,0:T(8,128)(2,1)S(1)}, u32[]{:S(2)}, u32[]{:S(2)}) collective-permute-start(bf16[256,512]{1,0:T(8,128)(2,1)S(1)} %get-tuple-element.201), channel_id=1, source_target_pairs={{0,8},{8,0},{16,24},{24,16},{1,9},{9,1},{17,25},{25,17},{2,10},{10... | collective-permute-start | bytes 786440 | tf_op jit(solution)/shard_map/ppermute | solution.py:36
  71.7 3.0 %collective-permute-start.33 = (bf16[256,512]{1,0:T(8,128)(2,1)S(1)}, bf16[256,512]{1,0:T(8,128)(2,1)S(1)}, u32[]{:S(2)}, u32[]{:S(2)}) collective-permute-start(bf16[256,512]{1,0:T(8,128)(2,1)S(1)} %reduce-precision_convert_fusion.4), channel_id=1, source_target_pairs={{0,8},{8,0},{16,24},{24,16},{1,9},{9,1},{17,25},{25,17},{2,10},{10... | collective-permute-start | bytes 786440 | tf_op jit(solution)/shard_map/ppermute | solution.py:36
  75.5 2.5 %collective-permute-done.31 = bf16[256,512]{1,0:T(8,128)(2,1)S(1)} collective-permute-done((bf16[256,512]{1,0:T(8,128)(2,1)S(1)}, bf16[256,512]{1,0:T(8,128)(2,1)S(1)}, u32[]{:S(2)}, u32[]{:S(2)}) %collective-permute-start.31) | collective-permute-done | bytes 262176 | tf_op jit(solution)/shard_map/ppermute | solution.py:36
  79.8 3.0 %collective-permute-done.33 = bf16[256,512]{1,0:T(8,128)(2,1)S(1)} collective-permute-done((bf16[256,512]{1,0:T(8,128)(2,1)S(1)}, bf16[256,512]{1,0:T(8,128)(2,1)S(1)}, u32[]{:S(2)}, u32[]{:S(2)}) %collective-permute-start.33) | collective-permute-done | bytes 262176 | tf_op jit(solution)/shard_map/ppermute | solution.py:36
  82.8 2.1 %collective-permute-start.36 = (bf16[256,512]{1,0:T(8,128)(2,1)S(1)}, bf16[256,512]{1,0:T(8,128)(2,1)S(1)}, u32[]{:S(2)}, u32[]{:S(2)}) collective-permute-start(bf16[256,512]{1,0:T(8,128)(2,1)S(1)} %reduce-precision_convert_fusion.2), channel_id=1, source_target_pairs={{0,8},{8,0},{16,24},{24,16},{1,9},{9,1},{17,25},{25,17},{2,10},{10... | collective-permute-start | bytes 786440 | tf_op jit(solution)/shard_map/ppermute | solution.py:36
  89.7 1.5 %collective-permute-done.36 = bf16[256,512]{1,0:T(8,128)(2,1)S(1)} collective-permute-done((bf16[256,512]{1,0:T(8,128)(2,1)S(1)}, bf16[256,512]{1,0:T(8,128)(2,1)S(1)}, u32[]{:S(2)}, u32[]{:S(2)}) %collective-permute-start.36) | collective-permute-done | bytes 262176 | tf_op jit(solution)/shard_map/ppermute | solution.py:36
  92.7 3.1 %collective-permute-done.34 = bf16[256,512]{1,0:T(8,128)(2,1)S(1)} collective-permute-done((bf16[256,512]{1,0:T(8,128)(2,1)S(1)}, bf16[256,512]{1,0:T(8,128)(2,1)S(1)}, u32[]{:S(2)}, u32[]{:S(2)}) %collective-permute-start.34) | collective-permute-done | bytes 262176 | tf_op jit(solution)/shard_map/ppermute | solution.py:36
  96.5 2.1 %collective-permute-done.39 = bf16[256,512]{1,0:T(8,128)(2,1)S(1)} collective-permute-done((bf16[256,512]{1,0:T(8,128)(2,1)S(1)}, bf16[256,512]{1,0:T(8,128)(2,1)S(1)}, u32[]{:S(2)}, u32[]{:S(2)}) %collective-permute-start.39) | collective-permute-done | bytes 262176 | tf_op jit(solution)/shard_map/ppermute | solution.py:17
  102.4 1.8 %collective-permute-done.37 = bf16[256,512]{1,0:T(8,128)(2,1)S(1)} collective-permute-done((bf16[256,512]{1,0:T(8,128)(2,1)S(1)}, bf16[256,512]{1,0:T(8,128)(2,1)S(1)}, u32[]{:S(2)}, u32[]{:S(2)}) %collective-permute-start.37) | collective-permute-done | bytes 262176 | tf_op jit(solution)/shard_map/ppermute | solution.py:17
  105.5 2.6 %collective-permute-done.35 = bf16[256,512]{1,0:T(8,128)(2,1)S(1)} collective-permute-done((bf16[256,512]{1,0:T(8,128)(2,1)S(1)}, bf16[256,512]{1,0:T(8,128)(2,1)S(1)}, u32[]{:S(2)}, u32[]{:S(2)}) %collective-permute-start.35) | collective-permute-done | bytes 262176 | tf_op jit(solution)/shard_map/ppermute | solution.py:17
  (154 shorter events, 43.6 us)
Async XLA Ops:
  2.1 8.6 %collective-permute-start.4 = (bf16[256,256]{1,0:T(8,128)(2,1)}, bf16[256,256]{1,0:T(8,128)(2,1)S(1)}, u32[]{:S(2)}, u32[]{:S(2)}) collective-permute-start(bf16[256,256]{1,0:T(8,128)(2,1)} %param.17), channel_id=1, source_target_pairs={{0,4},{4,0},{1,5},{5,1},{2,6},{6,2},{3,7},{7,3},{8,12},{12,8},{9,1... | collective-permute-start | bytes 393224 | tf_op jit(solution)/shard_map/ppermute | solution.py:17
  12.8 18.8 %collective-permute-start.19 = (bf16[256,256]{1,0:T(8,128)(2,1)S(1)}, bf16[256,256]{1,0:T(8,128)(2,1)S(1)}, u32[]{:S(2)}, u32[]{:S(2)}) collective-permute-start(bf16[256,256]{1,0:T(8,128)(2,1)S(1)} %get-tuple-element.126), channel_id=1, source_target_pairs={{0,4},{4,0},{1,5},{5,1},{2,6},{6,2},{3,7},{7,3},{8,12},{12,8},{9,1... | collective-permute-start | bytes 393224 | tf_op jit(solution)/shard_map/ppermute | solution.py:17
  14.0 7.9 %collective-permute-start.9 = (bf16[512,256]{1,0:T(8,128)(2,1)S(1)}, bf16[512,256]{1,0:T(8,128)(2,1)S(1)}, u32[]{:S(2)}, u32[]{:S(2)}) collective-permute-start(bf16[512,256]{1,0:T(8,128)(2,1)S(1)} %pad_maximum_fusion.10), channel_id=1, source_target_pairs={{0,2},{1,3},{2,0},{3,1},{4,6},{5,7},{6,4},{7,5},{8,10},{9,11},{10,... | collective-permute-start | bytes 786440 | tf_op jit(solution)/shard_map/ppermute | solution.py:17
  24.1 9.2 %collective-permute-start.7 = (bf16[256,512]{1,0:T(8,128)(2,1)S(1)}, bf16[256,512]{1,0:T(8,128)(2,1)S(1)}, u32[]{:S(2)}, u32[]{:S(2)}) collective-permute-start(bf16[256,512]{1,0:T(8,128)(2,1)S(1)} %fusion.1), channel_id=1, source_target_pairs={{0,8},{8,0},{16,24},{24,16},{1,9},{9,1},{17,25},{25,17},{2,10},{10... | collective-permute-start | bytes 786440 | tf_op jit(solution)/shard_map/ppermute | solution.py:36
  31.7 8.5 %collective-permute-start.13 = (bf16[256,512]{1,0:T(8,128)(2,1)S(1)}, bf16[256,512]{1,0:T(8,128)(2,1)S(1)}, u32[]{:S(2)}, u32[]{:S(2)}) collective-permute-start(bf16[256,512]{1,0:T(8,128)(2,1)S(1)} %fusion.3), channel_id=1, source_target_pairs={{0,8},{8,0},{16,24},{24,16},{1,9},{9,1},{17,25},{25,17},{2,10},{10... | collective-permute-start | bytes 786440 | tf_op jit(solution)/shard_map/ppermute | solution.py:36
  34.4 11.9 %collective-permute-start.20 = (bf16[256,512]{1,0:T(8,128)(2,1)S(1)}, bf16[256,512]{1,0:T(8,128)(2,1)S(1)}, u32[]{:S(2)}, u32[]{:S(2)}) collective-permute-start(bf16[256,512]{1,0:T(8,128)(2,1)S(1)} %get-tuple-element.243), channel_id=1, source_target_pairs={{0,8},{8,0},{16,24},{24,16},{1,9},{9,1},{17,25},{25,17},{2,10},{10... | collective-permute-start | bytes 786440 | tf_op jit(solution)/shard_map/ppermute | solution.py:36
  41.3 11.8 %collective-permute-start.11 = (bf16[256,512]{1,0:T(8,128)(2,1)S(1)}, bf16[256,512]{1,0:T(8,128)(2,1)S(1)}, u32[]{:S(2)}, u32[]{:S(2)}) collective-permute-start(bf16[256,512]{1,0:T(8,128)(2,1)S(1)} %get-tuple-element.241), channel_id=1, source_target_pairs={{0,8},{8,0},{16,24},{24,16},{1,9},{9,1},{17,25},{25,17},{2,10},{10... | collective-permute-start | bytes 786440 | tf_op jit(solution)/shard_map/ppermute | solution.py:36
  46.5 7.6 %collective-permute-start.22 = (bf16[256,512]{1,0:T(8,128)(2,1)S(1)}, bf16[256,512]{1,0:T(8,128)(2,1)S(1)}, u32[]{:S(2)}, u32[]{:S(2)}) collective-permute-start(bf16[256,512]{1,0:T(8,128)(2,1)S(1)} %reduce-precision_convert_fusion.9), channel_id=1, source_target_pairs={{8,16},{16,8},{0,0},{24,24},{9,17},{17,9},{1,1},{25,25},{10,18},{1... | collective-permute-start | bytes 786440 | tf_op jit(solution)/shard_map/ppermute | solution.py:40
  48.0 11.5 %collective-permute-start.15 = (bf16[256,512]{1,0:T(8,128)(2,1)S(1)}, bf16[256,512]{1,0:T(8,128)(2,1)S(1)}, u32[]{:S(2)}, u32[]{:S(2)}) collective-permute-start(bf16[256,512]{1,0:T(8,128)(2,1)S(1)} %get-tuple-element.205), channel_id=1, source_target_pairs={{0,8},{8,0},{16,24},{24,16},{1,9},{9,1},{17,25},{25,17},{2,10},{10... | collective-permute-start | bytes 786440 | tf_op jit(solution)/shard_map/ppermute | solution.py:36
  53.3 11.0 %collective-permute-start.23 = (bf16[256,512]{1,0:T(8,128)(2,1)S(1)}, bf16[256,512]{1,0:T(8,128)(2,1)S(1)}, u32[]{:S(2)}, u32[]{:S(2)}) collective-permute-start(bf16[256,512]{1,0:T(8,128)(2,1)S(1)} %reduce-precision_convert_fusion.7), channel_id=1, source_target_pairs={{8,16},{16,8},{0,0},{24,24},{9,17},{17,9},{1,1},{25,25},{10,18},{1... | collective-permute-start | bytes 786440 | tf_op jit(solution)/shard_map/ppermute | solution.py:40
  54.3 11.1 %collective-permute-start.29 = (bf16[256,512]{1,0:T(8,128)(2,1)S(1)}, bf16[256,512]{1,0:T(8,128)(2,1)S(1)}, u32[]{:S(2)}, u32[]{:S(2)}) collective-permute-start(bf16[256,512]{1,0:T(8,128)(2,1)S(1)} %get-tuple-element.203), channel_id=1, source_target_pairs={{0,8},{8,0},{16,24},{24,16},{1,9},{9,1},{17,25},{25,17},{2,10},{10... | collective-permute-start | bytes 786440 | tf_op jit(solution)/shard_map/ppermute | solution.py:36
  60.8 24.1 %collective-permute-start.16 = (bf16[512,512]{1,0:T(8,128)(2,1)S(1)}, bf16[512,512]{1,0:T(8,128)(2,1)S(1)}, u32[]{:S(2)}, u32[]{:S(2)}) collective-permute-start(bf16[512,512]{1,0:T(8,128)(2,1)S(1)} %pad_maximum_fusion.4), channel_id=1, source_target_pairs={{0,4},{4,0},{1,5},{5,1},{2,6},{6,2},{3,7},{7,3},{8,12},{12,8},{9,1... | collective-permute-start | bytes 1572872 | tf_op jit(solution)/shard_map/ppermute | solution.py:17
  65.3 9.3 %collective-permute-start.25 = (bf16[256,256]{1,0:T(8,128)(2,1)S(1)}, bf16[256,256]{1,0:T(8,128)(2,1)S(1)}, u32[]{:S(2)}, u32[]{:S(2)}) collective-permute-start(bf16[256,256]{1,0:T(8,128)(2,1)S(1)} %select_convert_fusion.1), channel_id=1, source_target_pairs={{0,2},{1,3},{2,0},{3,1},{4,6},{5,7},{6,4},{7,5},{8,10},{9,11},{10,... | collective-permute-start | bytes 393224 | tf_op jit(solution)/shard_map/ppermute | solution.py:17
  67.0 11.0 %collective-permute-start.31 = (bf16[256,512]{1,0:T(8,128)(2,1)S(1)}, bf16[256,512]{1,0:T(8,128)(2,1)S(1)}, u32[]{:S(2)}, u32[]{:S(2)}) collective-permute-start(bf16[256,512]{1,0:T(8,128)(2,1)S(1)} %get-tuple-element.201), channel_id=1, source_target_pairs={{0,8},{8,0},{16,24},{24,16},{1,9},{9,1},{17,25},{25,17},{2,10},{10... | collective-permute-start | bytes 786440 | tf_op jit(solution)/shard_map/ppermute | solution.py:36
  71.0 8.1 %collective-permute-start.30 = (bf16[256,512]{1,0:T(8,128)(2,1)S(1)}, bf16[256,512]{1,0:T(8,128)(2,1)S(1)}, u32[]{:S(2)}, u32[]{:S(2)}) collective-permute-start(bf16[256,512]{1,0:T(8,128)(2,1)S(1)} %reduce-precision_convert_fusion.3), channel_id=1, source_target_pairs={{8,16},{16,8},{0,0},{24,24},{9,17},{17,9},{1,1},{25,25},{10,18},{1... | collective-permute-start | bytes 786440 | tf_op jit(solution)/shard_map/ppermute | solution.py:40
  71.7 11.1 %collective-permute-start.33 = (bf16[256,512]{1,0:T(8,128)(2,1)S(1)}, bf16[256,512]{1,0:T(8,128)(2,1)S(1)}, u32[]{:S(2)}, u32[]{:S(2)}) collective-permute-start(bf16[256,512]{1,0:T(8,128)(2,1)S(1)} %reduce-precision_convert_fusion.4), channel_id=1, source_target_pairs={{0,8},{8,0},{16,24},{24,16},{1,9},{9,1},{17,25},{25,17},{2,10},{10... | collective-permute-start | bytes 786440 | tf_op jit(solution)/shard_map/ppermute | solution.py:36
  74.8 10.0 %collective-permute-start.28 = (bf16[128,256]{1,0:T(8,128)(2,1)S(1)}, bf16[128,256]{1,0:T(8,128)(2,1)S(1)}, u32[]{:S(2)}, u32[]{:S(2)}) collective-permute-start(bf16[128,256]{1,0:T(8,128)(2,1)S(1)} %get-tuple-element.235), channel_id=1, source_target_pairs={{0,4},{4,0},{1,5},{5,1},{2,6},{6,2},{3,7},{7,3},{8,12},{12,8},{9,1... | collective-permute-start | bytes 196616 | tf_op jit(solution)/shard_map/ppermute | solution.py:17
  78.1 9.9 %collective-permute-start.32 = (bf16[256,512]{1,0:T(8,128)(2,1)S(1)}, bf16[256,512]{1,0:T(8,128)(2,1)S(1)}, u32[]{:S(2)}, u32[]{:S(2)}) collective-permute-start(bf16[256,512]{1,0:T(8,128)(2,1)S(1)} %reduce-precision_convert_fusion.1), channel_id=1, source_target_pairs={{8,16},{16,8},{0,0},{24,24},{9,17},{17,9},{1,1},{25,25},{10,18},{1... | collective-permute-start | bytes 786440 | tf_op jit(solution)/shard_map/ppermute | solution.py:40
  79.1 19.6 %collective-permute-start.38 = (bf16[512,512]{1,0:T(8,128)(2,1)S(1)}, bf16[512,512]{1,0:T(8,128)(2,1)S(1)}, u32[]{:S(2)}, u32[]{:S(2)}) collective-permute-start(bf16[512,512]{1,0:T(8,128)(2,1)S(1)} %pad_maximum_fusion.7), channel_id=1, source_target_pairs={{0,4},{4,0},{1,5},{5,1},{2,6},{6,2},{3,7},{7,3},{8,12},{12,8},{9,1... | collective-permute-start | bytes 1572872 | tf_op jit(solution)/shard_map/ppermute | solution.py:17
  82.8 8.5 %collective-permute-start.36 = (bf16[256,512]{1,0:T(8,128)(2,1)S(1)}, bf16[256,512]{1,0:T(8,128)(2,1)S(1)}, u32[]{:S(2)}, u32[]{:S(2)}) collective-permute-start(bf16[256,512]{1,0:T(8,128)(2,1)S(1)} %reduce-precision_convert_fusion.2), channel_id=1, source_target_pairs={{0,8},{8,0},{16,24},{24,16},{1,9},{9,1},{17,25},{25,17},{2,10},{10... | collective-permute-start | bytes 786440 | tf_op jit(solution)/shard_map/ppermute | solution.py:36
  88.1 7.7 %collective-permute-start.34 = (bf16[256,512]{1,0:T(8,128)(2,1)S(1)}, bf16[256,512]{1,0:T(8,128)(2,1)S(1)}, u32[]{:S(2)}, u32[]{:S(2)}) collective-permute-start(bf16[256,512]{1,0:T(8,128)(2,1)S(1)} %reduce-precision_convert_fusion), channel_id=1, source_target_pairs={{0,8},{8,0},{16,24},{24,16},{1,9},{9,1},{17,25},{25,17},{2,10},{10... | collective-permute-start | bytes 786440 | tf_op jit(solution)/shard_map/ppermute | solution.py:36
  88.6 10.1 %collective-permute-start.39 = (bf16[256,512]{1,0:T(8,128)(2,1)S(1)}, bf16[256,512]{1,0:T(8,128)(2,1)S(1)}, u32[]{:S(2)}, u32[]{:S(2)}) collective-permute-start(bf16[256,512]{1,0:T(8,128)(2,1)S(1)} %broadcast_select_fusion.4), channel_id=1, source_target_pairs={{0,4},{4,0},{1,5},{5,1},{2,6},{6,2},{3,7},{7,3},{8,12},{12,8},{9,1... | collective-permute-start | bytes 786440 | tf_op jit(solution)/shard_map/ppermute | solution.py:17
  91.3 13.0 %collective-permute-start.37 = (bf16[256,512]{1,0:T(8,128)(2,1)S(1)}, bf16[256,512]{1,0:T(8,128)(2,1)S(1)}, u32[]{:S(2)}, u32[]{:S(2)}) collective-permute-start(bf16[256,512]{1,0:T(8,128)(2,1)S(1)} %broadcast_select_fusion.7), channel_id=1, source_target_pairs={{0,4},{4,0},{1,5},{5,1},{2,6},{6,2},{3,7},{7,3},{8,12},{12,8},{9,1... | collective-permute-start | bytes 786440 | tf_op jit(solution)/shard_map/ppermute | solution.py:17
  95.8 12.3 %collective-permute-start.35 = (bf16[256,512]{1,0:T(8,128)(2,1)S(1)}, bf16[256,512]{1,0:T(8,128)(2,1)S(1)}, u32[]{:S(2)}, u32[]{:S(2)}) collective-permute-start(bf16[256,512]{1,0:T(8,128)(2,1)S(1)} %broadcast_select_fusion.8), channel_id=1, source_target_pairs={{0,4},{4,0},{1,5},{5,1},{2,6},{6,2},{3,7},{7,3},{8,12},{12,8},{9,1... | collective-permute-start | bytes 786440 | tf_op jit(solution)/shard_map/ppermute | solution.py:17
  (20 other events, 116.8 us)

commit v12 on v11

--- a/solution.py
+++ b/solution.py
@@ -10,7 +10,7 @@
 EPSILON = 1e-06
 CHUNK_ROWS = 256
 LAG = 3
-KN = {"groups": (lambda c: [[0], [1, 2], [3, 4], [5], [6], [7]] if c == 8 else [[k] for k in range(c)]), "due": len, "xser": 0, "t1": 0, "t2": 0, "t3": 1, "tA": 0, "tail": 1, "keys": 3, "rpay": (None, 0, 1, 1), "rrecv": (0, 0, 0, 1), "ypay": 0, "yrecv": 0, "ptie": 1}
+KEYS_STEP = 3
 
 
 def swap(value, axis, bit):
@@ -41,7 +41,9 @@
 
 
 def summed(part, count, sums, share, emit, side):
-    groups = KN["groups"](count)
+    groups = [[k] for k in range(count)]
+    if count == 8:
+        groups = [[0], [1, 2], [3, 4], [5], [6], [7]]
     pending = ()
     if lax.axis_size("section") != 4:
         for group in groups:
@@ -60,14 +62,12 @@
     for k in range(min(LAG, count)):
         last = parts.get(k - 1)
         parts[k], last = part(k, last)
-        if k and KN["ptie"] and last is not None:
+        if last is not None:
             parts[k - 1] = last
         arriving[k] = end_swap(parts[k])
     shares = []
     for k in range(count + LAG):
-        tied = {i: totals[i] for i in (k - 2,) if i in totals and KN["t1"]}
-        got, tied = lax.optimization_barrier((arriving[k], tied))
-        totals.update(tied)
+        got = lax.optimization_barrier(arriving[k])
         if k < count:
             halves[k] = add(parts[k], got)
             others[k] = middle_swap(halves[k])
@@ -76,13 +76,12 @@
             if value is not None:
                 halves[k] = value
         if k - 1 in others:
-            tied = {i: halves[i] for i in (k - 1, k) if i in halves and (i < k or KN["t2"])}
-            if KN["tail"] and k >= count:
-                other, tied, got = lax.optimization_barrier((others[k - 1], tied, got))
+            tied = (others[k - 1], halves[k - 1])
+            if k >= count:
+                other, half, got = lax.optimization_barrier(tied + (got,))
             else:
-                other, tied = lax.optimization_barrier((others[k - 1], tied))
-            halves.update(tied)
-            totals[k - 1] = add(halves[k - 1], other)
+                other, half = lax.optimization_barrier(tied)
+            totals[k - 1] = add(half, other)
         following = k - 1 + LAG
         if LAG <= following < count + LAG:
             value = totals[following - LAG]
@@ -93,26 +92,18 @@
             results[k - LAG] = jnp.where(inner, totals[k - LAG], got)
             for group in groups:
                 if group[-1] == k - LAG:
-                    found = [results[i] for i in group]
-                    if KN["tA"] and k - 1 in totals:
-                        found, totals[k - 1] = lax.optimization_barrier((found, totals[k - 1]))
-                    back = KN["xser"]
-                    if back and len(shares) >= back and shares[-back] is not None:
-                        due, last, values = shares[-back]
-                        found, values = lax.optimization_barrier((found, values))
-                        shares[-back] = (due, last, values)
-                    shares.append((k + KN["due"](group), group, share(found)))
+                    shares.append((k + 2, group, share([results[i] for i in group])))
         now = [i for i, entry in enumerate(shares) if entry is not None and entry[0] <= k]
-        tied = {i: totals[i] for i in (k - 1,) if i in totals and KN["t3"]}
-        if now or (pending is not None and k >= KN["keys"]):
+        tied = {i: totals[i] for i in (k - 1,) if i in totals}
+        if now or (pending is not None and k >= KEYS_STEP):
             waited, held, tied = lax.optimization_barrier(
-                ([shares[i][2] for i in now], pending if k >= KN["keys"] else (), tied)
+                ([shares[i][2] for i in now], pending if k >= KEYS_STEP else (), tied)
             )
             totals.update(tied)
             for i, values in zip(now, waited):
                 emit(shares[i][1], values)
                 shares[i] = None
-            if k >= KN["keys"] and pending is not None:
+            if k >= KEYS_STEP and pending is not None:
                 pending = side(held)
     for entry in shares:
         if entry is not None:
@@ -295,31 +286,28 @@
         got = [pieces[f]]
         for j in range(1, n_dp):
             piece = pieces[j * feature_blocks + f]
-            tie = KN["rpay"][f] if n_dp == 2 else None
-            if tie is not None:
+            tie = min(f - 1, 1)
+            if tie in first:
                 piece, first[tie] = lax.optimization_barrier((piece, first[tie]))
             got.append(swap(piece, "dp", j))
         return got
 
-    def columns_of(g, value):
+    def columns_of(g):
         near = cotangents
         if g:
-            if KN["ypay"] is not None:
-                near, first[KN["ypay"]] = lax.optimization_barrier((near, first[KN["ypay"]]))
+            near, first[0] = lax.optimization_barrier((near, first[0]))
             near = swap(near, "mp", 2 * g)
-            if KN["yrecv"] and value is not None:
-                near, value = lax.optimization_barrier((near, value))
-        return both_cores(near), value
+        return both_cores(near)
 
     def part(k, value):
         g, f = divmod(k, feature_blocks)
         if g not in ready:
-            ready[g], value = columns_of(g, value)
+            ready[g] = columns_of(g)
         if f not in moved:
             got = send(f)
             if not f:
                 got, ready[0] = lax.optimization_barrier((got, ready[0]))
-            elif KN["rrecv"][f] and value is not None:
+            elif f >= LAG and value is not None:
                 got, value = lax.optimization_barrier((got, value))
             moved[f] = jnp.concatenate(in_order(got), axis=0)
         found = to_bfloat16(

time: 111 us -> 109 us (0.982)
  waiting for transfers between devices: 29.8 us -> 25.2 us
  starting transfers between devices: 56.2 us -> 59.7 us
    ppermute x11, waiting for transfers between devices: 13 us -> 8.13 us  [end_swap(): return lax.ppermute(value, 'section', [(0, 1), (1, 0), (2, 3), (3, 2)])]
    ppermute x11, starting transfers between devices: 32.1 us -> 36.3 us  [end_swap(): return lax.ppermute(value, 'section', [(0, 1), (1, 0), (2, 3), (3, 2)])]
  transfers between devices with their start and end apart: 40 -> 40, of which waited for: 15 -> 13; matrix products, arithmetic and copies ran while one was open for 7% -> 7% of each run, Pallas kernels for 9% -> 9%
where the time goes in v12:
time: 109 us
  starting transfers between devices  59.7 us (55%)
  waiting for transfers between devices  25.2 us (23%)
  Pallas kernels  11.4 us (10%)
  other arithmetic  4.91 us (5%)
  matrix products  3.84 us (4%)
  local copies, waits for them, and re-layouts  2.58 us (2%)
  between operations  1.41 us (1%)
    ppermute x11, starting transfers between devices, end_swap(): return lax.ppermute(value, 'section', [(0, 1), (1, 0), (2, 3), (3, 2)])  36.3 us
    ppermute x21, starting transfers between devices, swap(): lax.ppermute(value, axis, [(i, i ^ bit) for i in range(lax.axis_size(axis...  17.9 us
    ppermute x21, waiting for transfers between devices, swap(): lax.ppermute(value, axis, [(i, i ^ bit) for i in range(lax.axis_size(axis...  17 us
    pallas_call x8, Pallas kernels, emit(): pl.pallas_call(functools.partial(store, n_dp, g, f * chunk, i * chunk, sh...  9.14 us
    ppermute x11, waiting for transfers between devices, end_swap(): return lax.ppermute(value, 'section', [(0, 1), (1, 0), (2, 3), (3, 2)])  8.13 us
    ppermute x8, starting transfers between devices, middle_swap(): return lax.ppermute(value, 'section', [(1, 2), (2, 1), (0, 0), (3, 3)])  5.59 us
    dot_general x8, matrix products, part(): lax.dot_general(moved[f], ready[g], (((0,), (0,)), ((), ())), preferred_e...  2.56 us
    unnamed x9, local copies, waits for them, and re-layouts  2.51 us
  transfers between devices with their start and end apart: 40, of which 13 were waited for; matrix products, arithmetic and copies ran while one was open for 7% of the time, Pallas kernels for 9%

profile of v12, /device:TPU:0, one launch (start us, length us, event | category | flops | bytes accessed | tf_op | source)
XLA Modules:
  0.0 109.0 jit_solution(2594133898077927000)
XLA Ops:
  2.1 3.0 %collective-permute-start.4 = (bf16[256,256]{1,0:T(8,128)(2,1)}, bf16[256,256]{1,0:T(8,128)(2,1)S(1)}, u32[]{:S(2)}, u32[]{:S(2)}) collective-permute-start(bf16[256,256]{1,0:T(8,128)(2,1)} %param.17), channel_id=1, source_target_pairs={{0,4},{4,0},{1,5},{5,1},{2,6},{6,2},{3,7},{7,3},{8,12},{12,8},{9,1... | collective-permute-start | bytes 393224 | tf_op jit(solution)/shard_map/ppermute | solution.py:17
  5.2 1.5 %collective-permute-start.1 = (f32[2,128]{1,0:T(2,128)S(1)}, f32[2,128]{1,0:T(2,128)S(1)}, u32[]{:S(2)}, u32[]{:S(2)}) collective-permute-start(f32[2,128]{1,0:T(2,128)S(1)} %get-tuple-element.102.refs_0_), channel_id=1, source_target_pairs={{0,2},{1,3},{2,0},{3,1},{4,6},{5,7},{6,4},{7,5},{8,10},{9,11},{10,... | collective-permute-start | bytes 3080 | tf_op jit(solution)/shard_map/ppermute | solution.py:17
  7.0 1.5 %score.1.rest = f32[4,128]{1,0:T(4,128)} custom-call(s32[2]{0:T(128)} %lengths.1, s32[1,2]{1,0:T(1,128)} %order.1, bf16[2,3584]{1,0:T(2,128)(2,1)} %hidden.1, bf16[3584]{0:T(1024)(128)(2,1)} %gain.1, bf16[3584]{0:T(1024)(128)(2,1)} %head.1), custom_call_target="tpu_custom_call" | custom-call | tf_op jit(solution)/shard_map/score/pallas_call | solution.py:258
  15.0 3.3 %collective-permute-done.3 = bf16[256,256]{1,0:T(8,128)(2,1)S(1)} collective-permute-done((bf16[256,256]{1,0:T(8,128)(2,1)S(1)}, bf16[256,256]{1,0:T(8,128)(2,1)S(1)}, u32[]{:S(2)}, u32[]{:S(2)}) %collective-permute-start.3) | collective-permute-done | bytes 131104 | tf_op jit(solution)/shard_map/ppermute | solution.py:17
  19.6 1.6 %collective-permute-start.17 = (bf16[256,512]{1,0:T(8,128)(2,1)S(1)}, bf16[256,512]{1,0:T(8,128)(2,1)S(1)}, u32[]{:S(2)}, u32[]{:S(2)}) collective-permute-start(bf16[256,512]{1,0:T(8,128)(2,1)S(1)} %fusion), channel_id=1, source_target_pairs={{0,8},{8,0},{16,24},{24,16},{1,9},{9,1},{17,25},{25,17},{2,10},{10... | collective-permute-start | bytes 786440 | tf_op jit(solution)/shard_map/ppermute | solution.py:36
  22.0 1.7 %collective-permute-done.6 = bf16[256,256]{1,0:T(8,128)(2,1)S(1)} collective-permute-done((bf16[256,256]{1,0:T(8,128)(2,1)S(1)}, bf16[256,256]{1,0:T(8,128)(2,1)S(1)}, u32[]{:S(2)}, u32[]{:S(2)}) %collective-permute-start.6) | collective-permute-done | bytes 131104 | tf_op jit(solution)/shard_map/ppermute | solution.py:17
  24.1 1.6 %collective-permute-start.7 = (bf16[256,512]{1,0:T(8,128)(2,1)S(1)}, bf16[256,512]{1,0:T(8,128)(2,1)S(1)}, u32[]{:S(2)}, u32[]{:S(2)}) collective-permute-start(bf16[256,512]{1,0:T(8,128)(2,1)S(1)} %fusion.1), channel_id=1, source_target_pairs={{0,8},{8,0},{16,24},{24,16},{1,9},{9,1},{17,25},{25,17},{2,10},{10... | collective-permute-start | bytes 786440 | tf_op jit(solution)/shard_map/ppermute | solution.py:36
  27.5 3.2 %collective-permute-done.12 = bf16[256,256]{1,0:T(8,128)(2,1)S(1)} collective-permute-done((bf16[256,256]{1,0:T(8,128)(2,1)S(1)}, bf16[256,256]{1,0:T(8,128)(2,1)S(1)}, u32[]{:S(2)}, u32[]{:S(2)}) %collective-permute-start.12) | collective-permute-done | bytes 131104 | tf_op jit(solution)/shard_map/ppermute | solution.py:17
  34.4 3.7 %collective-permute-start.20 = (bf16[256,512]{1,0:T(8,128)(2,1)S(1)}, bf16[256,512]{1,0:T(8,128)(2,1)S(1)}, u32[]{:S(2)}, u32[]{:S(2)}) collective-permute-start(bf16[256,512]{1,0:T(8,128)(2,1)S(1)} %get-tuple-element.239), channel_id=1, source_target_pairs={{0,8},{8,0},{16,24},{24,16},{1,9},{9,1},{17,25},{25,17},{2,10},{10... | collective-permute-start | bytes 786440 | tf_op jit(solution)/shard_map/ppermute | solution.py:36
  38.1 2.1 %collective-permute-done.13 = bf16[256,512]{1,0:T(8,128)(2,1)S(1)} collective-permute-done((bf16[256,512]{1,0:T(8,128)(2,1)S(1)}, bf16[256,512]{1,0:T(8,128)(2,1)S(1)}, u32[]{:S(2)}, u32[]{:S(2)}) %collective-permute-start.13) | collective-permute-done | bytes 262176 | tf_op jit(solution)/shard_map/ppermute | solution.py:36
  41.3 5.0 %collective-permute-start.11 = (bf16[256,512]{1,0:T(8,128)(2,1)S(1)}, bf16[256,512]{1,0:T(8,128)(2,1)S(1)}, u32[]{:S(2)}, u32[]{:S(2)}) collective-permute-start(bf16[256,512]{1,0:T(8,128)(2,1)S(1)} %get-tuple-element.237), channel_id=1, source_target_pairs={{0,8},{8,0},{16,24},{24,16},{1,9},{9,1},{17,25},{25,17},{2,10},{10... | collective-permute-start | bytes 786440 | tf_op jit(solution)/shard_map/ppermute | solution.py:36
  48.0 5.3 %collective-permute-start.15 = (bf16[256,512]{1,0:T(8,128)(2,1)S(1)}, bf16[256,512]{1,0:T(8,128)(2,1)S(1)}, u32[]{:S(2)}, u32[]{:S(2)}) collective-permute-start(bf16[256,512]{1,0:T(8,128)(2,1)S(1)} %get-tuple-element.201), channel_id=1, source_target_pairs={{0,8},{8,0},{16,24},{24,16},{1,9},{9,1},{17,25},{25,17},{2,10},{10... | collective-permute-start | bytes 786440 | tf_op jit(solution)/shard_map/ppermute | solution.py:36
  54.6 4.5 %collective-permute-start.29 = (bf16[256,512]{1,0:T(8,128)(2,1)S(1)}, bf16[256,512]{1,0:T(8,128)(2,1)S(1)}, u32[]{:S(2)}, u32[]{:S(2)}) collective-permute-start(bf16[256,512]{1,0:T(8,128)(2,1)S(1)} %get-tuple-element.199), channel_id=1, source_target_pairs={{0,8},{8,0},{16,24},{24,16},{1,9},{9,1},{17,25},{25,17},{2,10},{10... | collective-permute-start | bytes 786440 | tf_op jit(solution)/shard_map/ppermute | solution.py:36
  65.1 1.6 %collective-permute-start.25 = (bf16[256,256]{1,0:T(8,128)(2,1)S(1)}, bf16[256,256]{1,0:T(8,128)(2,1)S(1)}, u32[]{:S(2)}, u32[]{:S(2)}) collective-permute-start(bf16[256,256]{1,0:T(8,128)(2,1)S(1)} %select_convert_fusion.1), channel_id=1, source_target_pairs={{0,2},{1,3},{2,0},{3,1},{4,6},{5,7},{6,4},{7,5},{8,10},{9,11},{10,... | collective-permute-start | bytes 393224 | tf_op jit(solution)/shard_map/ppermute | solution.py:17
  66.8 4.0 %collective-permute-start.31 = (bf16[256,512]{1,0:T(8,128)(2,1)S(1)}, bf16[256,512]{1,0:T(8,128)(2,1)S(1)}, u32[]{:S(2)}, u32[]{:S(2)}) collective-permute-start(bf16[256,512]{1,0:T(8,128)(2,1)S(1)} %get-tuple-element.197), channel_id=1, source_target_pairs={{0,8},{8,0},{16,24},{24,16},{1,9},{9,1},{17,25},{25,17},{2,10},{10... | collective-permute-start | bytes 786440 | tf_op jit(solution)/shard_map/ppermute | solution.py:36
  71.5 2.6 %collective-permute-start.33 = (bf16[256,512]{1,0:T(8,128)(2,1)S(1)}, bf16[256,512]{1,0:T(8,128)(2,1)S(1)}, u32[]{:S(2)}, u32[]{:S(2)}) collective-permute-start(bf16[256,512]{1,0:T(8,128)(2,1)S(1)} %reduce-precision_convert_fusion.4), channel_id=1, source_target_pairs={{0,8},{8,0},{16,24},{24,16},{1,9},{9,1},{17,25},{25,17},{2,10},{10... | collective-permute-start | bytes 786440 | tf_op jit(solution)/shard_map/ppermute | solution.py:36
  75.5 2.4 %collective-permute-done.31 = bf16[256,512]{1,0:T(8,128)(2,1)S(1)} collective-permute-done((bf16[256,512]{1,0:T(8,128)(2,1)S(1)}, bf16[256,512]{1,0:T(8,128)(2,1)S(1)}, u32[]{:S(2)}, u32[]{:S(2)}) %collective-permute-start.31) | collective-permute-done | bytes 262176 | tf_op jit(solution)/shard_map/ppermute | solution.py:36
  79.8 2.8 %collective-permute-done.33 = bf16[256,512]{1,0:T(8,128)(2,1)S(1)} collective-permute-done((bf16[256,512]{1,0:T(8,128)(2,1)S(1)}, bf16[256,512]{1,0:T(8,128)(2,1)S(1)}, u32[]{:S(2)}, u32[]{:S(2)}) %collective-permute-start.33) | collective-permute-done | bytes 262176 | tf_op jit(solution)/shard_map/ppermute | solution.py:36
  82.6 2.2 %collective-permute-start.36 = (bf16[256,512]{1,0:T(8,128)(2,1)S(1)}, bf16[256,512]{1,0:T(8,128)(2,1)S(1)}, u32[]{:S(2)}, u32[]{:S(2)}) collective-permute-start(bf16[256,512]{1,0:T(8,128)(2,1)S(1)} %reduce-precision_convert_fusion.2), channel_id=1, source_target_pairs={{0,8},{8,0},{16,24},{24,16},{1,9},{9,1},{17,25},{25,17},{2,10},{10... | collective-permute-start | bytes 786440 | tf_op jit(solution)/shard_map/ppermute | solution.py:36
  86.2 4.6 %collective-permute-start.34 = (bf16[256,512]{1,0:T(8,128)(2,1)S(1)}, bf16[256,512]{1,0:T(8,128)(2,1)S(1)}, u32[]{:S(2)}, u32[]{:S(2)}) collective-permute-start(bf16[256,512]{1,0:T(8,128)(2,1)S(1)} %reduce-precision_convert_fusion), channel_id=1, source_target_pairs={{0,8},{8,0},{16,24},{24,16},{1,9},{9,1},{17,25},{25,17},{2,10},{10... | collective-permute-start | bytes 786440 | tf_op jit(solution)/shard_map/ppermute | solution.py:36
  93.8 1.3 %collective-permute-start.37 = (bf16[256,512]{1,0:T(8,128)(2,1)S(1)}, bf16[256,512]{1,0:T(8,128)(2,1)S(1)}, u32[]{:S(2)}, u32[]{:S(2)}) collective-permute-start(bf16[256,512]{1,0:T(8,128)(2,1)S(1)} %broadcast_select_fusion.7), channel_id=1, source_target_pairs={{0,4},{4,0},{1,5},{5,1},{2,6},{6,2},{3,7},{7,3},{8,12},{12,8},{9,1... | collective-permute-start | bytes 786440 | tf_op jit(solution)/shard_map/ppermute | solution.py:17
  95.1 3.5 %collective-permute-done.38 = bf16[256,512]{1,0:T(8,128)(2,1)S(1)} collective-permute-done((bf16[256,512]{1,0:T(8,128)(2,1)S(1)}, bf16[256,512]{1,0:T(8,128)(2,1)S(1)}, u32[]{:S(2)}, u32[]{:S(2)}) %collective-permute-start.38) | collective-permute-done | bytes 262176 | tf_op jit(solution)/shard_map/ppermute | solution.py:17
  102.5 1.7 %collective-permute-done.37 = bf16[256,512]{1,0:T(8,128)(2,1)S(1)} collective-permute-done((bf16[256,512]{1,0:T(8,128)(2,1)S(1)}, bf16[256,512]{1,0:T(8,128)(2,1)S(1)}, u32[]{:S(2)}, u32[]{:S(2)}) %collective-permute-start.37) | collective-permute-done | bytes 262176 | tf_op jit(solution)/shard_map/ppermute | solution.py:17
  105.5 1.6 %collective-permute-done.35 = bf16[256,512]{1,0:T(8,128)(2,1)S(1)} collective-permute-done((bf16[256,512]{1,0:T(8,128)(2,1)S(1)}, bf16[256,512]{1,0:T(8,128)(2,1)S(1)}, u32[]{:S(2)}, u32[]{:S(2)}) %collective-permute-start.35) | collective-permute-done | bytes 262176 | tf_op jit(solution)/shard_map/ppermute | solution.py:17
  (154 shorter events, 41.2 us)
Async XLA Ops:
  2.1 8.6 %collective-permute-start.4 = (bf16[256,256]{1,0:T(8,128)(2,1)}, bf16[256,256]{1,0:T(8,128)(2,1)S(1)}, u32[]{:S(2)}, u32[]{:S(2)}) collective-permute-start(bf16[256,256]{1,0:T(8,128)(2,1)} %param.17), channel_id=1, source_target_pairs={{0,4},{4,0},{1,5},{5,1},{2,6},{6,2},{3,7},{7,3},{8,12},{12,8},{9,1... | collective-permute-start | bytes 393224 | tf_op jit(solution)/shard_map/ppermute | solution.py:17
  12.8 18.8 %collective-permute-start.19 = (bf16[256,256]{1,0:T(8,128)(2,1)S(1)}, bf16[256,256]{1,0:T(8,128)(2,1)S(1)}, u32[]{:S(2)}, u32[]{:S(2)}) collective-permute-start(bf16[256,256]{1,0:T(8,128)(2,1)S(1)} %get-tuple-element.124), channel_id=1, source_target_pairs={{0,4},{4,0},{1,5},{5,1},{2,6},{6,2},{3,7},{7,3},{8,12},{12,8},{9,1... | collective-permute-start | bytes 393224 | tf_op jit(solution)/shard_map/ppermute | solution.py:17
  14.0 7.9 %collective-permute-start.9 = (bf16[512,256]{1,0:T(8,128)(2,1)S(1)}, bf16[512,256]{1,0:T(8,128)(2,1)S(1)}, u32[]{:S(2)}, u32[]{:S(2)}) collective-permute-start(bf16[512,256]{1,0:T(8,128)(2,1)S(1)} %pad_maximum_fusion.10), channel_id=1, source_target_pairs={{0,2},{1,3},{2,0},{3,1},{4,6},{5,7},{6,4},{7,5},{8,10},{9,11},{10,... | collective-permute-start | bytes 786440 | tf_op jit(solution)/shard_map/ppermute | solution.py:17
  24.1 9.2 %collective-permute-start.7 = (bf16[256,512]{1,0:T(8,128)(2,1)S(1)}, bf16[256,512]{1,0:T(8,128)(2,1)S(1)}, u32[]{:S(2)}, u32[]{:S(2)}) collective-permute-start(bf16[256,512]{1,0:T(8,128)(2,1)S(1)} %fusion.1), channel_id=1, source_target_pairs={{0,8},{8,0},{16,24},{24,16},{1,9},{9,1},{17,25},{25,17},{2,10},{10... | collective-permute-start | bytes 786440 | tf_op jit(solution)/shard_map/ppermute | solution.py:36
  31.7 8.5 %collective-permute-start.13 = (bf16[256,512]{1,0:T(8,128)(2,1)S(1)}, bf16[256,512]{1,0:T(8,128)(2,1)S(1)}, u32[]{:S(2)}, u32[]{:S(2)}) collective-permute-start(bf16[256,512]{1,0:T(8,128)(2,1)S(1)} %fusion.3), channel_id=1, source_target_pairs={{0,8},{8,0},{16,24},{24,16},{1,9},{9,1},{17,25},{25,17},{2,10},{10... | collective-permute-start | bytes 786440 | tf_op jit(solution)/shard_map/ppermute | solution.py:36
  34.4 11.9 %collective-permute-start.20 = (bf16[256,512]{1,0:T(8,128)(2,1)S(1)}, bf16[256,512]{1,0:T(8,128)(2,1)S(1)}, u32[]{:S(2)}, u32[]{:S(2)}) collective-permute-start(bf16[256,512]{1,0:T(8,128)(2,1)S(1)} %get-tuple-element.239), channel_id=1, source_target_pairs={{0,8},{8,0},{16,24},{24,16},{1,9},{9,1},{17,25},{25,17},{2,10},{10... | collective-permute-start | bytes 786440 | tf_op jit(solution)/shard_map/ppermute | solution.py:36
  41.3 11.9 %collective-permute-start.11 = (bf16[256,512]{1,0:T(8,128)(2,1)S(1)}, bf16[256,512]{1,0:T(8,128)(2,1)S(1)}, u32[]{:S(2)}, u32[]{:S(2)}) collective-permute-start(bf16[256,512]{1,0:T(8,128)(2,1)S(1)} %get-tuple-element.237), channel_id=1, source_target_pairs={{0,8},{8,0},{16,24},{24,16},{1,9},{9,1},{17,25},{25,17},{2,10},{10... | collective-permute-start | bytes 786440 | tf_op jit(solution)/shard_map/ppermute | solution.py:36
  47.2 15.8 %collective-permute-start.21 = (bf16[256,512]{1,0:T(8,128)(2,1)S(1)}, bf16[256,512]{1,0:T(8,128)(2,1)S(1)}, u32[]{:S(2)}, u32[]{:S(2)}) collective-permute-start(bf16[256,512]{1,0:T(8,128)(2,1)S(1)} %broadcast_select_fusion.11), channel_id=1, source_target_pairs={{0,4},{4,0},{1,5},{5,1},{2,6},{6,2},{3,7},{7,3},{8,12},{12,8},{9,1... | collective-permute-start | bytes 786440 | tf_op jit(solution)/shard_map/ppermute | solution.py:17
  48.0 11.9 %collective-permute-start.15 = (bf16[256,512]{1,0:T(8,128)(2,1)S(1)}, bf16[256,512]{1,0:T(8,128)(2,1)S(1)}, u32[]{:S(2)}, u32[]{:S(2)}) collective-permute-start(bf16[256,512]{1,0:T(8,128)(2,1)S(1)} %get-tuple-element.201), channel_id=1, source_target_pairs={{0,8},{8,0},{16,24},{24,16},{1,9},{9,1},{17,25},{25,17},{2,10},{10... | collective-permute-start | bytes 786440 | tf_op jit(solution)/shard_map/ppermute | solution.py:36
  53.3 9.5 %collective-permute-start.23 = (bf16[256,512]{1,0:T(8,128)(2,1)S(1)}, bf16[256,512]{1,0:T(8,128)(2,1)S(1)}, u32[]{:S(2)}, u32[]{:S(2)}) collective-permute-start(bf16[256,512]{1,0:T(8,128)(2,1)S(1)} %reduce-precision_convert_fusion.7), channel_id=1, source_target_pairs={{8,16},{16,8},{0,0},{24,24},{9,17},{17,9},{1,1},{25,25},{10,18},{1... | collective-permute-start | bytes 786440 | tf_op jit(solution)/shard_map/ppermute | solution.py:40
  54.6 10.5 %collective-permute-start.29 = (bf16[256,512]{1,0:T(8,128)(2,1)S(1)}, bf16[256,512]{1,0:T(8,128)(2,1)S(1)}, u32[]{:S(2)}, u32[]{:S(2)}) collective-permute-start(bf16[256,512]{1,0:T(8,128)(2,1)S(1)} %get-tuple-element.199), channel_id=1, source_target_pairs={{0,8},{8,0},{16,24},{24,16},{1,9},{9,1},{17,25},{25,17},{2,10},{10... | collective-permute-start | bytes 786440 | tf_op jit(solution)/shard_map/ppermute | solution.py:36
  60.7 24.1 %collective-permute-start.16 = (bf16[512,512]{1,0:T(8,128)(2,1)S(1)}, bf16[512,512]{1,0:T(8,128)(2,1)S(1)}, u32[]{:S(2)}, u32[]{:S(2)}) collective-permute-start(bf16[512,512]{1,0:T(8,128)(2,1)S(1)} %pad_maximum_fusion.4), channel_id=1, source_target_pairs={{0,4},{4,0},{1,5},{5,1},{2,6},{6,2},{3,7},{7,3},{8,12},{12,8},{9,1... | collective-permute-start | bytes 1572872 | tf_op jit(solution)/shard_map/ppermute | solution.py:17
  63.1 8.4 %collective-permute-start.26 = (bf16[256,256]{1,0:T(8,128)(2,1)S(1)}, bf16[256,256]{1,0:T(8,128)(2,1)S(1)}, u32[]{:S(2)}, u32[]{:S(2)}) collective-permute-start(bf16[256,256]{1,0:T(8,128)(2,1)S(1)} %get-tuple-element.207), channel_id=1, source_target_pairs={{0,3},{1,2},{2,1},{3,0},{4,7},{5,6},{6,5},{7,4},{8,11},{9,10},{10,... | collective-permute-start | bytes 393224 | tf_op jit(solution)/shard_map/ppermute | solution.py:17
  65.1 9.1 %collective-permute-start.25 = (bf16[256,256]{1,0:T(8,128)(2,1)S(1)}, bf16[256,256]{1,0:T(8,128)(2,1)S(1)}, u32[]{:S(2)}, u32[]{:S(2)}) collective-permute-start(bf16[256,256]{1,0:T(8,128)(2,1)S(1)} %select_convert_fusion.1), channel_id=1, source_target_pairs={{0,2},{1,3},{2,0},{3,1},{4,6},{5,7},{6,4},{7,5},{8,10},{9,11},{10,... | collective-permute-start | bytes 393224 | tf_op jit(solution)/shard_map/ppermute | solution.py:17
  66.8 11.1 %collective-permute-start.31 = (bf16[256,512]{1,0:T(8,128)(2,1)S(1)}, bf16[256,512]{1,0:T(8,128)(2,1)S(1)}, u32[]{:S(2)}, u32[]{:S(2)}) collective-permute-start(bf16[256,512]{1,0:T(8,128)(2,1)S(1)} %get-tuple-element.197), channel_id=1, source_target_pairs={{0,8},{8,0},{16,24},{24,16},{1,9},{9,1},{17,25},{25,17},{2,10},{10... | collective-permute-start | bytes 786440 | tf_op jit(solution)/shard_map/ppermute | solution.py:36
  70.8 8.1 %collective-permute-start.30 = (bf16[256,512]{1,0:T(8,128)(2,1)S(1)}, bf16[256,512]{1,0:T(8,128)(2,1)S(1)}, u32[]{:S(2)}, u32[]{:S(2)}) collective-permute-start(bf16[256,512]{1,0:T(8,128)(2,1)S(1)} %reduce-precision_convert_fusion.3), channel_id=1, source_target_pairs={{8,16},{16,8},{0,0},{24,24},{9,17},{17,9},{1,1},{25,25},{10,18},{1... | collective-permute-start | bytes 786440 | tf_op jit(solution)/shard_map/ppermute | solution.py:40
  71.5 11.1 %collective-permute-start.33 = (bf16[256,512]{1,0:T(8,128)(2,1)S(1)}, bf16[256,512]{1,0:T(8,128)(2,1)S(1)}, u32[]{:S(2)}, u32[]{:S(2)}) collective-permute-start(bf16[256,512]{1,0:T(8,128)(2,1)S(1)} %reduce-precision_convert_fusion.4), channel_id=1, source_target_pairs={{0,8},{8,0},{16,24},{24,16},{1,9},{9,1},{17,25},{25,17},{2,10},{10... | collective-permute-start | bytes 786440 | tf_op jit(solution)/shard_map/ppermute | solution.py:36
  74.3 10.5 %collective-permute-start.28 = (bf16[128,256]{1,0:T(8,128)(2,1)S(1)}, bf16[128,256]{1,0:T(8,128)(2,1)S(1)}, u32[]{:S(2)}, u32[]{:S(2)}) collective-permute-start(bf16[128,256]{1,0:T(8,128)(2,1)S(1)} %get-tuple-element.231), channel_id=1, source_target_pairs={{0,4},{4,0},{1,5},{5,1},{2,6},{6,2},{3,7},{7,3},{8,12},{12,8},{9,1... | collective-permute-start | bytes 196616 | tf_op jit(solution)/shard_map/ppermute | solution.py:17
  78.1 20.8 %collective-permute-start.39 = (bf16[512,512]{1,0:T(8,128)(2,1)S(1)}, bf16[512,512]{1,0:T(8,128)(2,1)S(1)}, u32[]{:S(2)}, u32[]{:S(2)}) collective-permute-start(bf16[512,512]{1,0:T(8,128)(2,1)S(1)} %pad_maximum_fusion.8), channel_id=1, source_target_pairs={{0,4},{4,0},{1,5},{5,1},{2,6},{6,2},{3,7},{7,3},{8,12},{12,8},{9,1... | collective-permute-start | bytes 1572872 | tf_op jit(solution)/shard_map/ppermute | solution.py:17
  82.6 11.1 %collective-permute-start.36 = (bf16[256,512]{1,0:T(8,128)(2,1)S(1)}, bf16[256,512]{1,0:T(8,128)(2,1)S(1)}, u32[]{:S(2)}, u32[]{:S(2)}) collective-permute-start(bf16[256,512]{1,0:T(8,128)(2,1)S(1)} %reduce-precision_convert_fusion.2), channel_id=1, source_target_pairs={{0,8},{8,0},{16,24},{24,16},{1,9},{9,1},{17,25},{25,17},{2,10},{10... | collective-permute-start | bytes 786440 | tf_op jit(solution)/shard_map/ppermute | solution.py:36
  85.1 13.5 %collective-permute-start.38 = (bf16[256,512]{1,0:T(8,128)(2,1)S(1)}, bf16[256,512]{1,0:T(8,128)(2,1)S(1)}, u32[]{:S(2)}, u32[]{:S(2)}) collective-permute-start(bf16[256,512]{1,0:T(8,128)(2,1)S(1)} %broadcast_select_fusion.6), channel_id=1, source_target_pairs={{0,4},{4,0},{1,5},{5,1},{2,6},{6,2},{3,7},{7,3},{8,12},{12,8},{9,1... | collective-permute-start | bytes 786440 | tf_op jit(solution)/shard_map/ppermute | solution.py:17
  86.2 12.5 %collective-permute-start.34 = (bf16[256,512]{1,0:T(8,128)(2,1)S(1)}, bf16[256,512]{1,0:T(8,128)(2,1)S(1)}, u32[]{:S(2)}, u32[]{:S(2)}) collective-permute-start(bf16[256,512]{1,0:T(8,128)(2,1)S(1)} %reduce-precision_convert_fusion), channel_id=1, source_target_pairs={{0,8},{8,0},{16,24},{24,16},{1,9},{9,1},{17,25},{25,17},{2,10},{10... | collective-permute-start | bytes 786440 | tf_op jit(solution)/shard_map/ppermute | solution.py:36
  93.8 10.5 %collective-permute-start.37 = (bf16[256,512]{1,0:T(8,128)(2,1)S(1)}, bf16[256,512]{1,0:T(8,128)(2,1)S(1)}, u32[]{:S(2)}, u32[]{:S(2)}) collective-permute-start(bf16[256,512]{1,0:T(8,128)(2,1)S(1)} %broadcast_select_fusion.7), channel_id=1, source_target_pairs={{0,4},{4,0},{1,5},{5,1},{2,6},{6,2},{3,7},{7,3},{8,12},{12,8},{9,1... | collective-permute-start | bytes 786440 | tf_op jit(solution)/shard_map/ppermute | solution.py:17
  98.7 8.5 %collective-permute-start.35 = (bf16[256,512]{1,0:T(8,128)(2,1)S(1)}, bf16[256,512]{1,0:T(8,128)(2,1)S(1)}, u32[]{:S(2)}, u32[]{:S(2)}) collective-permute-start(bf16[256,512]{1,0:T(8,128)(2,1)S(1)} %broadcast_select_fusion.8), channel_id=1, source_target_pairs={{0,4},{4,0},{1,5},{5,1},{2,6},{6,2},{3,7},{7,3},{8,12},{12,8},{9,1... | collective-permute-start | bytes 786440 | tf_op jit(solution)/shard_map/ppermute | solution.py:17
  (20 other events, 121.4 us)

commit v13 on v12

--- a/solution.py
+++ b/solution.py
@@ -10,7 +10,7 @@
 EPSILON = 1e-06
 CHUNK_ROWS = 256
 LAG = 3
-KEYS_STEP = 3
+KEYS_STEP = 4
 
 
 def swap(value, axis, bit):

time: 109 us -> 109 us (level)
    ppermute x21, waiting for transfers between devices: 17 us -> 20.9 us  [swap(): lax.ppermute(value, axis, [(i, i ^ bit) for i in range(lax.axis_size(axis...]
    ppermute x11, waiting for transfers between devices: 8.13 us -> 4.74 us  [end_swap(): return lax.ppermute(value, 'section', [(0, 1), (1, 0), (2, 3), (3, 2)])]
  transfers between devices with their start and end apart: 40 -> 40, of which waited for: 13 -> 14; matrix products, arithmetic and copies ran while one was open for 7% -> 7% of each run, Pallas kernels for 9% -> 9%
where the time goes in v13:
time: 109 us
  starting transfers between devices  59.3 us (54%)
  waiting for transfers between devices  25.6 us (23%)
  Pallas kernels  11.4 us (10%)
  other arithmetic  4.85 us (4%)
  matrix products  3.83 us (4%)
  local copies, waits for them, and re-layouts  2.58 us (2%)
  between operations  1.4 us (1%)
    ppermute x11, starting transfers between devices, end_swap(): return lax.ppermute(value, 'section', [(0, 1), (1, 0), (2, 3), (3, 2)])  35.4 us
    ppermute x21, waiting for transfers between devices, swap(): lax.ppermute(value, axis, [(i, i ^ bit) for i in range(lax.axis_size(axis...  20.9 us
    ppermute x21, starting transfers between devices, swap(): lax.ppermute(value, axis, [(i, i ^ bit) for i in range(lax.axis_size(axis...  18.2 us
    pallas_call x8, Pallas kernels, emit(): pl.pallas_call(functools.partial(store, n_dp, g, f * chunk, i * chunk, sh...  9.14 us
    ppermute x8, starting transfers between devices, middle_swap(): return lax.ppermute(value, 'section', [(1, 2), (2, 1), (0, 0), (3, 3)])  5.73 us
    ppermute x11, waiting for transfers between devices, end_swap(): return lax.ppermute(value, 'section', [(0, 1), (1, 0), (2, 3), (3, 2)])  4.74 us
    dot_general x8, matrix products, part(): lax.dot_general(moved[f], ready[g], (((0,), (0,)), ((), ())), preferred_e...  2.56 us
    unnamed x9, local copies, waits for them, and re-layouts  2.51 us
  transfers between devices with their start and end apart: 40, of which 14 were waited for; matrix products, arithmetic and copies ran while one was open for 7% of the time, Pallas kernels for 9%

profile of v13, /device:TPU:0, one launch (start us, length us, event | category | flops | bytes accessed | tf_op | source)
XLA Modules:
  0.0 108.9 jit_solution(5212193736018194975)
XLA Ops:
  2.1 3.0 %collective-permute-start.4 = (bf16[256,256]{1,0:T(8,128)(2,1)}, bf16[256,256]{1,0:T(8,128)(2,1)S(1)}, u32[]{:S(2)}, u32[]{:S(2)}) collective-permute-start(bf16[256,256]{1,0:T(8,128)(2,1)} %param.17), channel_id=1, source_target_pairs={{0,4},{4,0},{1,5},{5,1},{2,6},{6,2},{3,7},{7,3},{8,12},{12,8},{9,1... | collective-permute-start | bytes 393224 | tf_op jit(solution)/shard_map/ppermute | solution.py:17
  5.2 1.5 %collective-permute-start.1 = (f32[2,128]{1,0:T(2,128)S(1)}, f32[2,128]{1,0:T(2,128)S(1)}, u32[]{:S(2)}, u32[]{:S(2)}) collective-permute-start(f32[2,128]{1,0:T(2,128)S(1)} %get-tuple-element.102.refs_0_), channel_id=1, source_target_pairs={{0,2},{1,3},{2,0},{3,1},{4,6},{5,7},{6,4},{7,5},{8,10},{9,11},{10,... | collective-permute-start | bytes 3080 | tf_op jit(solution)/shard_map/ppermute | solution.py:17
  7.0 1.5 %score.1.rest = f32[4,128]{1,0:T(4,128)} custom-call(s32[2]{0:T(128)} %lengths.1, s32[1,2]{1,0:T(1,128)} %order.1, bf16[2,3584]{1,0:T(2,128)(2,1)} %hidden.1, bf16[3584]{0:T(1024)(128)(2,1)} %gain.1, bf16[3584]{0:T(1024)(128)(2,1)} %head.1), custom_call_target="tpu_custom_call" | custom-call | tf_op jit(solution)/shard_map/score/pallas_call | solution.py:258
  15.0 3.3 %collective-permute-done.3 = bf16[256,256]{1,0:T(8,128)(2,1)S(1)} collective-permute-done((bf16[256,256]{1,0:T(8,128)(2,1)S(1)}, bf16[256,256]{1,0:T(8,128)(2,1)S(1)}, u32[]{:S(2)}, u32[]{:S(2)}) %collective-permute-start.3) | collective-permute-done | bytes 131104 | tf_op jit(solution)/shard_map/ppermute | solution.py:17
  19.6 1.6 %collective-permute-start.17 = (bf16[256,512]{1,0:T(8,128)(2,1)S(1)}, bf16[256,512]{1,0:T(8,128)(2,1)S(1)}, u32[]{:S(2)}, u32[]{:S(2)}) collective-permute-start(bf16[256,512]{1,0:T(8,128)(2,1)S(1)} %fusion), channel_id=1, source_target_pairs={{0,8},{8,0},{16,24},{24,16},{1,9},{9,1},{17,25},{25,17},{2,10},{10... | collective-permute-start | bytes 786440 | tf_op jit(solution)/shard_map/ppermute | solution.py:36
  22.0 1.7 %collective-permute-done.6 = bf16[256,256]{1,0:T(8,128)(2,1)S(1)} collective-permute-done((bf16[256,256]{1,0:T(8,128)(2,1)S(1)}, bf16[256,256]{1,0:T(8,128)(2,1)S(1)}, u32[]{:S(2)}, u32[]{:S(2)}) %collective-permute-start.6) | collective-permute-done | bytes 131104 | tf_op jit(solution)/shard_map/ppermute | solution.py:17
  24.1 1.6 %collective-permute-start.7 = (bf16[256,512]{1,0:T(8,128)(2,1)S(1)}, bf16[256,512]{1,0:T(8,128)(2,1)S(1)}, u32[]{:S(2)}, u32[]{:S(2)}) collective-permute-start(bf16[256,512]{1,0:T(8,128)(2,1)S(1)} %fusion.1), channel_id=1, source_target_pairs={{0,8},{8,0},{16,24},{24,16},{1,9},{9,1},{17,25},{25,17},{2,10},{10... | collective-permute-start | bytes 786440 | tf_op jit(solution)/shard_map/ppermute | solution.py:36
  27.5 3.2 %collective-permute-done.12 = bf16[256,256]{1,0:T(8,128)(2,1)S(1)} collective-permute-done((bf16[256,256]{1,0:T(8,128)(2,1)S(1)}, bf16[256,256]{1,0:T(8,128)(2,1)S(1)}, u32[]{:S(2)}, u32[]{:S(2)}) %collective-permute-start.12) | collective-permute-done | bytes 131104 | tf_op jit(solution)/shard_map/ppermute | solution.py:17
  31.4 1.3 %collective-permute-start.13 = (bf16[256,512]{1,0:T(8,128)(2,1)S(1)}, bf16[256,512]{1,0:T(8,128)(2,1)S(1)}, u32[]{:S(2)}, u32[]{:S(2)}) collective-permute-start(bf16[256,512]{1,0:T(8,128)(2,1)S(1)} %fusion.3), channel_id=1, source_target_pairs={{0,8},{8,0},{16,24},{24,16},{1,9},{9,1},{17,25},{25,17},{2,10},{10... | collective-permute-start | bytes 786440 | tf_op jit(solution)/shard_map/ppermute | solution.py:36
  34.1 3.7 %collective-permute-start.20 = (bf16[256,512]{1,0:T(8,128)(2,1)S(1)}, bf16[256,512]{1,0:T(8,128)(2,1)S(1)}, u32[]{:S(2)}, u32[]{:S(2)}) collective-permute-start(bf16[256,512]{1,0:T(8,128)(2,1)S(1)} %get-tuple-element.239), channel_id=1, source_target_pairs={{0,8},{8,0},{16,24},{24,16},{1,9},{9,1},{17,25},{25,17},{2,10},{10... | collective-permute-start | bytes 786440 | tf_op jit(solution)/shard_map/ppermute | solution.py:36
  37.8 1.7 %collective-permute-done.13 = bf16[256,512]{1,0:T(8,128)(2,1)S(1)} collective-permute-done((bf16[256,512]{1,0:T(8,128)(2,1)S(1)}, bf16[256,512]{1,0:T(8,128)(2,1)S(1)}, u32[]{:S(2)}, u32[]{:S(2)}) %collective-permute-start.13) | collective-permute-done | bytes 262176 | tf_op jit(solution)/shard_map/ppermute | solution.py:36
  40.6 5.4 %collective-permute-start.11 = (bf16[256,512]{1,0:T(8,128)(2,1)S(1)}, bf16[256,512]{1,0:T(8,128)(2,1)S(1)}, u32[]{:S(2)}, u32[]{:S(2)}) collective-permute-start(bf16[256,512]{1,0:T(8,128)(2,1)S(1)} %get-tuple-element.237), channel_id=1, source_target_pairs={{0,8},{8,0},{16,24},{24,16},{1,9},{9,1},{17,25},{25,17},{2,10},{10... | collective-permute-start | bytes 786440 | tf_op jit(solution)/shard_map/ppermute | solution.py:36
  48.0 4.3 %collective-permute-start.15 = (bf16[256,512]{1,0:T(8,128)(2,1)S(1)}, bf16[256,512]{1,0:T(8,128)(2,1)S(1)}, u32[]{:S(2)}, u32[]{:S(2)}) collective-permute-start(bf16[256,512]{1,0:T(8,128)(2,1)S(1)} %get-tuple-element.235), channel_id=1, source_target_pairs={{0,8},{8,0},{16,24},{24,16},{1,9},{9,1},{17,25},{25,17},{2,10},{10... | collective-permute-start | bytes 786440 | tf_op jit(solution)/shard_map/ppermute | solution.py:36
  54.0 4.6 %collective-permute-start.28 = (bf16[256,512]{1,0:T(8,128)(2,1)S(1)}, bf16[256,512]{1,0:T(8,128)(2,1)S(1)}, u32[]{:S(2)}, u32[]{:S(2)}) collective-permute-start(bf16[256,512]{1,0:T(8,128)(2,1)S(1)} %get-tuple-element.199), channel_id=1, source_target_pairs={{0,8},{8,0},{16,24},{24,16},{1,9},{9,1},{17,25},{25,17},{2,10},{10... | collective-permute-start | bytes 786440 | tf_op jit(solution)/shard_map/ppermute | solution.py:36
  61.8 4.2 %collective-permute-start.31 = (bf16[256,512]{1,0:T(8,128)(2,1)S(1)}, bf16[256,512]{1,0:T(8,128)(2,1)S(1)}, u32[]{:S(2)}, u32[]{:S(2)}) collective-permute-start(bf16[256,512]{1,0:T(8,128)(2,1)S(1)} %get-tuple-element.197), channel_id=1, source_target_pairs={{0,8},{8,0},{16,24},{24,16},{1,9},{9,1},{17,25},{25,17},{2,10},{10... | collective-permute-start | bytes 786440 | tf_op jit(solution)/shard_map/ppermute | solution.py:36
  66.1 1.3 %fusion.16 = f32[256,1024]{1,0:T(8,128)S(1)} fusion(bf16[256,2048]{1,0:T(8,128)(2,1)S(1)} %multiply_convert_fusion, bf16[2048,1024]{1,0:T(8,128)(2,1)S(1)} %copy-done), kind=kOutput, calls=%fused_computation.111 | convolution fusion | flops 1073741824 | bytes 6291456 | tf_op jit(solution)/shard_map/dot_general | solution.py:367
  69.5 3.0 %collective-permute-start.33 = (bf16[256,512]{1,0:T(8,128)(2,1)S(1)}, bf16[256,512]{1,0:T(8,128)(2,1)S(1)}, u32[]{:S(2)}, u32[]{:S(2)}) collective-permute-start(bf16[256,512]{1,0:T(8,128)(2,1)S(1)} %reduce-precision_convert_fusion.6), channel_id=1, source_target_pairs={{0,8},{8,0},{16,24},{24,16},{1,9},{9,1},{17,25},{25,17},{2,10},{10... | collective-permute-start | bytes 786440 | tf_op jit(solution)/shard_map/ppermute | solution.py:36
  73.5 1.7 %collective-permute-start.25 = (bf16[256,256]{1,0:T(8,128)(2,1)S(1)}, bf16[256,256]{1,0:T(8,128)(2,1)S(1)}, u32[]{:S(2)}, u32[]{:S(2)}) collective-permute-start(bf16[256,256]{1,0:T(8,128)(2,1)S(1)} %select_convert_fusion.1), channel_id=1, source_target_pairs={{0,2},{1,3},{2,0},{3,1},{4,6},{5,7},{6,4},{7,5},{8,10},{9,11},{10,... | collective-permute-start | bytes 393224 | tf_op jit(solution)/shard_map/ppermute | solution.py:17
  75.2 1.6 %collective-permute-done.33 = bf16[256,512]{1,0:T(8,128)(2,1)S(1)} collective-permute-done((bf16[256,512]{1,0:T(8,128)(2,1)S(1)}, bf16[256,512]{1,0:T(8,128)(2,1)S(1)}, u32[]{:S(2)}, u32[]{:S(2)}) %collective-permute-start.33) | collective-permute-done | bytes 262176 | tf_op jit(solution)/shard_map/ppermute | solution.py:36
  78.9 4.6 %collective-permute-start.36 = (bf16[256,512]{1,0:T(8,128)(2,1)S(1)}, bf16[256,512]{1,0:T(8,128)(2,1)S(1)}, u32[]{:S(2)}, u32[]{:S(2)}) collective-permute-start(bf16[256,512]{1,0:T(8,128)(2,1)S(1)} %reduce-precision_convert_fusion.2), channel_id=1, source_target_pairs={{0,8},{8,0},{16,24},{24,16},{1,9},{9,1},{17,25},{25,17},{2,10},{10... | collective-permute-start | bytes 786440 | tf_op jit(solution)/shard_map/ppermute | solution.py:36
  89.4 3.1 %collective-permute-done.30 = bf16[128,256]{1,0:T(8,128)(2,1)S(1)} collective-permute-done((bf16[128,256]{1,0:T(8,128)(2,1)S(1)}, bf16[128,256]{1,0:T(8,128)(2,1)S(1)}, u32[]{:S(2)}, u32[]{:S(2)}) %collective-permute-start.30) | collective-permute-done | bytes 65568 | tf_op jit(solution)/shard_map/ppermute | solution.py:17
  93.8 4.4 %collective-permute-done.38 = bf16[256,512]{1,0:T(8,128)(2,1)S(1)} collective-permute-done((bf16[256,512]{1,0:T(8,128)(2,1)S(1)}, bf16[256,512]{1,0:T(8,128)(2,1)S(1)}, u32[]{:S(2)}, u32[]{:S(2)}) %collective-permute-start.38) | collective-permute-done | bytes 262176 | tf_op jit(solution)/shard_map/ppermute | solution.py:17
  102.6 1.3 %collective-permute-done.37 = bf16[256,512]{1,0:T(8,128)(2,1)S(1)} collective-permute-done((bf16[256,512]{1,0:T(8,128)(2,1)S(1)}, bf16[256,512]{1,0:T(8,128)(2,1)S(1)}, u32[]{:S(2)}, u32[]{:S(2)}) %collective-permute-start.37) | collective-permute-done | bytes 262176 | tf_op jit(solution)/shard_map/ppermute | solution.py:17
  105.1 1.9 %collective-permute-done.35 = bf16[256,512]{1,0:T(8,128)(2,1)S(1)} collective-permute-done((bf16[256,512]{1,0:T(8,128)(2,1)S(1)}, bf16[256,512]{1,0:T(8,128)(2,1)S(1)}, u32[]{:S(2)}, u32[]{:S(2)}) %collective-permute-start.35) | collective-permute-done | bytes 262176 | tf_op jit(solution)/shard_map/ppermute | solution.py:17
  (153 shorter events, 41.9 us)
Async XLA Ops:
  2.1 8.6 %collective-permute-start.4 = (bf16[256,256]{1,0:T(8,128)(2,1)}, bf16[256,256]{1,0:T(8,128)(2,1)S(1)}, u32[]{:S(2)}, u32[]{:S(2)}) collective-permute-start(bf16[256,256]{1,0:T(8,128)(2,1)} %param.17), channel_id=1, source_target_pairs={{0,4},{4,0},{1,5},{5,1},{2,6},{6,2},{3,7},{7,3},{8,12},{12,8},{9,1... | collective-permute-start | bytes 393224 | tf_op jit(solution)/shard_map/ppermute | solution.py:17
  12.8 14.6 %collective-permute-start.19 = (bf16[256,256]{1,0:T(8,128)(2,1)S(1)}, bf16[256,256]{1,0:T(8,128)(2,1)S(1)}, u32[]{:S(2)}, u32[]{:S(2)}) collective-permute-start(bf16[256,256]{1,0:T(8,128)(2,1)S(1)} %get-tuple-element.124), channel_id=1, source_target_pairs={{0,4},{4,0},{1,5},{5,1},{2,6},{6,2},{3,7},{7,3},{8,12},{12,8},{9,1... | collective-permute-start | bytes 393224 | tf_op jit(solution)/shard_map/ppermute | solution.py:17
  14.0 7.9 %collective-permute-start.9 = (bf16[512,256]{1,0:T(8,128)(2,1)S(1)}, bf16[512,256]{1,0:T(8,128)(2,1)S(1)}, u32[]{:S(2)}, u32[]{:S(2)}) collective-permute-start(bf16[512,256]{1,0:T(8,128)(2,1)S(1)} %pad_maximum_fusion.10), channel_id=1, source_target_pairs={{0,2},{1,3},{2,0},{3,1},{4,6},{5,7},{6,4},{7,5},{8,10},{9,11},{10,... | collective-permute-start | bytes 786440 | tf_op jit(solution)/shard_map/ppermute | solution.py:17
  24.1 8.9 %collective-permute-start.7 = (bf16[256,512]{1,0:T(8,128)(2,1)S(1)}, bf16[256,512]{1,0:T(8,128)(2,1)S(1)}, u32[]{:S(2)}, u32[]{:S(2)}) collective-permute-start(bf16[256,512]{1,0:T(8,128)(2,1)S(1)} %fusion.1), channel_id=1, source_target_pairs={{0,8},{8,0},{16,24},{24,16},{1,9},{9,1},{17,25},{25,17},{2,10},{10... | collective-permute-start | bytes 786440 | tf_op jit(solution)/shard_map/ppermute | solution.py:36
  31.4 8.1 %collective-permute-start.13 = (bf16[256,512]{1,0:T(8,128)(2,1)S(1)}, bf16[256,512]{1,0:T(8,128)(2,1)S(1)}, u32[]{:S(2)}, u32[]{:S(2)}) collective-permute-start(bf16[256,512]{1,0:T(8,128)(2,1)S(1)} %fusion.3), channel_id=1, source_target_pairs={{0,8},{8,0},{16,24},{24,16},{1,9},{9,1},{17,25},{25,17},{2,10},{10... | collective-permute-start | bytes 786440 | tf_op jit(solution)/shard_map/ppermute | solution.py:36
  34.1 11.9 %collective-permute-start.20 = (bf16[256,512]{1,0:T(8,128)(2,1)S(1)}, bf16[256,512]{1,0:T(8,128)(2,1)S(1)}, u32[]{:S(2)}, u32[]{:S(2)}) collective-permute-start(bf16[256,512]{1,0:T(8,128)(2,1)S(1)} %get-tuple-element.239), channel_id=1, source_target_pairs={{0,8},{8,0},{16,24},{24,16},{1,9},{9,1},{17,25},{25,17},{2,10},{10... | collective-permute-start | bytes 786440 | tf_op jit(solution)/shard_map/ppermute | solution.py:36
  39.6 8.1 %collective-permute-start.14 = (bf16[256,512]{1,0:T(8,128)(2,1)S(1)}, bf16[256,512]{1,0:T(8,128)(2,1)S(1)}, u32[]{:S(2)}, u32[]{:S(2)}) collective-permute-start(bf16[256,512]{1,0:T(8,128)(2,1)S(1)} %reduce-precision_convert_fusion.13), channel_id=1, source_target_pairs={{8,16},{16,8},{0,0},{24,24},{9,17},{17,9},{1,1},{25,25},{10,18},{1... | collective-permute-start | bytes 786440 | tf_op jit(solution)/shard_map/ppermute | solution.py:40
  40.6 12.2 %collective-permute-start.11 = (bf16[256,512]{1,0:T(8,128)(2,1)S(1)}, bf16[256,512]{1,0:T(8,128)(2,1)S(1)}, u32[]{:S(2)}, u32[]{:S(2)}) collective-permute-start(bf16[256,512]{1,0:T(8,128)(2,1)S(1)} %get-tuple-element.237), channel_id=1, source_target_pairs={{0,8},{8,0},{16,24},{24,16},{1,9},{9,1},{17,25},{25,17},{2,10},{10... | collective-permute-start | bytes 786440 | tf_op jit(solution)/shard_map/ppermute | solution.py:36
  46.1 15.4 %collective-permute-start.21 = (bf16[256,512]{1,0:T(8,128)(2,1)S(1)}, bf16[256,512]{1,0:T(8,128)(2,1)S(1)}, u32[]{:S(2)}, u32[]{:S(2)}) collective-permute-start(bf16[256,512]{1,0:T(8,128)(2,1)S(1)} %broadcast_select_fusion.11), channel_id=1, source_target_pairs={{0,4},{4,0},{1,5},{5,1},{2,6},{6,2},{3,7},{7,3},{8,12},{12,8},{9,1... | collective-permute-start | bytes 786440 | tf_op jit(solution)/shard_map/ppermute | solution.py:17
  48.0 11.5 %collective-permute-start.15 = (bf16[256,512]{1,0:T(8,128)(2,1)S(1)}, bf16[256,512]{1,0:T(8,128)(2,1)S(1)}, u32[]{:S(2)}, u32[]{:S(2)}) collective-permute-start(bf16[256,512]{1,0:T(8,128)(2,1)S(1)} %get-tuple-element.235), channel_id=1, source_target_pairs={{0,8},{8,0},{16,24},{24,16},{1,9},{9,1},{17,25},{25,17},{2,10},{10... | collective-permute-start | bytes 786440 | tf_op jit(solution)/shard_map/ppermute | solution.py:36
  53.0 8.4 %collective-permute-start.22 = (bf16[256,512]{1,0:T(8,128)(2,1)S(1)}, bf16[256,512]{1,0:T(8,128)(2,1)S(1)}, u32[]{:S(2)}, u32[]{:S(2)}) collective-permute-start(bf16[256,512]{1,0:T(8,128)(2,1)S(1)} %reduce-precision_convert_fusion.9), channel_id=1, source_target_pairs={{8,16},{16,8},{0,0},{24,24},{9,17},{17,9},{1,1},{25,25},{10,18},{1... | collective-permute-start | bytes 786440 | tf_op jit(solution)/shard_map/ppermute | solution.py:40
  54.0 14.7 %collective-permute-start.28 = (bf16[256,512]{1,0:T(8,128)(2,1)S(1)}, bf16[256,512]{1,0:T(8,128)(2,1)S(1)}, u32[]{:S(2)}, u32[]{:S(2)}) collective-permute-start(bf16[256,512]{1,0:T(8,128)(2,1)S(1)} %get-tuple-element.199), channel_id=1, source_target_pairs={{0,8},{8,0},{16,24},{24,16},{1,9},{9,1},{17,25},{25,17},{2,10},{10... | collective-permute-start | bytes 786440 | tf_op jit(solution)/shard_map/ppermute | solution.py:36
  59.6 9.8 %collective-permute-start.23 = (bf16[256,512]{1,0:T(8,128)(2,1)S(1)}, bf16[256,512]{1,0:T(8,128)(2,1)S(1)}, u32[]{:S(2)}, u32[]{:S(2)}) collective-permute-start(bf16[256,512]{1,0:T(8,128)(2,1)S(1)} %reduce-precision_convert_fusion.7), channel_id=1, source_target_pairs={{8,16},{16,8},{0,0},{24,24},{9,17},{17,9},{1,1},{25,25},{10,18},{1... | collective-permute-start | bytes 786440 | tf_op jit(solution)/shard_map/ppermute | solution.py:40
  60.4 23.1 %collective-permute-start.16 = (bf16[512,512]{1,0:T(8,128)(2,1)S(1)}, bf16[512,512]{1,0:T(8,128)(2,1)S(1)}, u32[]{:S(2)}, u32[]{:S(2)}) collective-permute-start(bf16[512,512]{1,0:T(8,128)(2,1)S(1)} %pad_maximum_fusion.4), channel_id=1, source_target_pairs={{0,4},{4,0},{1,5},{5,1},{2,6},{6,2},{3,7},{7,3},{8,12},{12,8},{9,1... | collective-permute-start | bytes 1572872 | tf_op jit(solution)/shard_map/ppermute | solution.py:17
  61.8 10.9 %collective-permute-start.31 = (bf16[256,512]{1,0:T(8,128)(2,1)S(1)}, bf16[256,512]{1,0:T(8,128)(2,1)S(1)}, u32[]{:S(2)}, u32[]{:S(2)}) collective-permute-start(bf16[256,512]{1,0:T(8,128)(2,1)S(1)} %get-tuple-element.197), channel_id=1, source_target_pairs={{0,8},{8,0},{16,24},{24,16},{1,9},{9,1},{17,25},{25,17},{2,10},{10... | collective-permute-start | bytes 786440 | tf_op jit(solution)/shard_map/ppermute | solution.py:36
  69.5 7.3 %collective-permute-start.33 = (bf16[256,512]{1,0:T(8,128)(2,1)S(1)}, bf16[256,512]{1,0:T(8,128)(2,1)S(1)}, u32[]{:S(2)}, u32[]{:S(2)}) collective-permute-start(bf16[256,512]{1,0:T(8,128)(2,1)S(1)} %reduce-precision_convert_fusion.6), channel_id=1, source_target_pairs={{0,8},{8,0},{16,24},{24,16},{1,9},{9,1},{17,25},{25,17},{2,10},{10... | collective-permute-start | bytes 786440 | tf_op jit(solution)/shard_map/ppermute | solution.py:36
  73.5 9.9 %collective-permute-start.25 = (bf16[256,256]{1,0:T(8,128)(2,1)S(1)}, bf16[256,256]{1,0:T(8,128)(2,1)S(1)}, u32[]{:S(2)}, u32[]{:S(2)}) collective-permute-start(bf16[256,256]{1,0:T(8,128)(2,1)S(1)} %select_convert_fusion.1), channel_id=1, source_target_pairs={{0,2},{1,3},{2,0},{3,1},{4,6},{5,7},{6,4},{7,5},{8,10},{9,11},{10,... | collective-permute-start | bytes 393224 | tf_op jit(solution)/shard_map/ppermute | solution.py:17
  76.8 22.1 %collective-permute-start.39 = (bf16[512,512]{1,0:T(8,128)(2,1)S(1)}, bf16[512,512]{1,0:T(8,128)(2,1)S(1)}, u32[]{:S(2)}, u32[]{:S(2)}) collective-permute-start(bf16[512,512]{1,0:T(8,128)(2,1)S(1)} %pad_maximum_fusion.8), channel_id=1, source_target_pairs={{0,4},{4,0},{1,5},{5,1},{2,6},{6,2},{3,7},{7,3},{8,12},{12,8},{9,1... | collective-permute-start | bytes 1572872 | tf_op jit(solution)/shard_map/ppermute | solution.py:17
  78.0 9.3 %collective-permute-start.32 = (bf16[256,512]{1,0:T(8,128)(2,1)S(1)}, bf16[256,512]{1,0:T(8,128)(2,1)S(1)}, u32[]{:S(2)}, u32[]{:S(2)}) collective-permute-start(bf16[256,512]{1,0:T(8,128)(2,1)S(1)} %reduce-precision_convert_fusion.1), channel_id=1, source_target_pairs={{8,16},{16,8},{0,0},{24,24},{9,17},{17,9},{1,1},{25,25},{10,18},{1... | collective-permute-start | bytes 786440 | tf_op jit(solution)/shard_map/ppermute | solution.py:40
  78.9 14.4 %collective-permute-start.36 = (bf16[256,512]{1,0:T(8,128)(2,1)S(1)}, bf16[256,512]{1,0:T(8,128)(2,1)S(1)}, u32[]{:S(2)}, u32[]{:S(2)}) collective-permute-start(bf16[256,512]{1,0:T(8,128)(2,1)S(1)} %reduce-precision_convert_fusion.2), channel_id=1, source_target_pairs={{0,8},{8,0},{16,24},{24,16},{1,9},{9,1},{17,25},{25,17},{2,10},{10... | collective-permute-start | bytes 786440 | tf_op jit(solution)/shard_map/ppermute | solution.py:36
  87.4 10.8 %collective-permute-start.38 = (bf16[256,512]{1,0:T(8,128)(2,1)S(1)}, bf16[256,512]{1,0:T(8,128)(2,1)S(1)}, u32[]{:S(2)}, u32[]{:S(2)}) collective-permute-start(bf16[256,512]{1,0:T(8,128)(2,1)S(1)} %broadcast_select_fusion.6), channel_id=1, source_target_pairs={{0,4},{4,0},{1,5},{5,1},{2,6},{6,2},{3,7},{7,3},{8,12},{12,8},{9,1... | collective-permute-start | bytes 786440 | tf_op jit(solution)/shard_map/ppermute | solution.py:17
  88.4 9.8 %collective-permute-start.34 = (bf16[256,512]{1,0:T(8,128)(2,1)S(1)}, bf16[256,512]{1,0:T(8,128)(2,1)S(1)}, u32[]{:S(2)}, u32[]{:S(2)}) collective-permute-start(bf16[256,512]{1,0:T(8,128)(2,1)S(1)} %reduce-precision_convert_fusion), channel_id=1, source_target_pairs={{0,8},{8,0},{16,24},{24,16},{1,9},{9,1},{17,25},{25,17},{2,10},{10... | collective-permute-start | bytes 786440 | tf_op jit(solution)/shard_map/ppermute | solution.py:36
  93.3 10.5 %collective-permute-start.37 = (bf16[256,512]{1,0:T(8,128)(2,1)S(1)}, bf16[256,512]{1,0:T(8,128)(2,1)S(1)}, u32[]{:S(2)}, u32[]{:S(2)}) collective-permute-start(bf16[256,512]{1,0:T(8,128)(2,1)S(1)} %broadcast_select_fusion.7), channel_id=1, source_target_pairs={{0,4},{4,0},{1,5},{5,1},{2,6},{6,2},{3,7},{7,3},{8,12},{12,8},{9,1... | collective-permute-start | bytes 786440 | tf_op jit(solution)/shard_map/ppermute | solution.py:17
  98.2 8.8 %collective-permute-start.35 = (bf16[256,512]{1,0:T(8,128)(2,1)S(1)}, bf16[256,512]{1,0:T(8,128)(2,1)S(1)}, u32[]{:S(2)}, u32[]{:S(2)}) collective-permute-start(bf16[256,512]{1,0:T(8,128)(2,1)S(1)} %broadcast_select_fusion.8), channel_id=1, source_target_pairs={{0,4},{4,0},{1,5},{5,1},{2,6},{6,2},{3,7},{7,3},{8,12},{12,8},{9,1... | collective-permute-start | bytes 786440 | tf_op jit(solution)/shard_map/ppermute | solution.py:17
  (20 other events, 113.5 us)
